TPU v7x, 32 devices: a whole 2x2x4 slice. The times are simulated.
32 devices in a mesh: dev: 32 (over z, y, x, core).
Axes of the slice: x: 2, y: 2, z: 4, core: 2. Of those that a mesh axis runs over, the one named last changes fastest.
Arguments:
- tokens: bfloat16 [32768, 1024], P('dev'), may hold values from -6 to 6
- segment_ids: int32 [32768], replicated, may hold values from -1 to 52, as said below
- first_gain: float32 [1024], P('dev'), may hold values from 0.5 to 1.5
- first_bias: float32 [1024], P('dev'), may hold values from -1.75 to 1.75
- qkv_weight: float32 [1024, 3072], P('dev'), may hold values from -0.1875 to 0.1875
- query_bias: float32 [1024], P('dev'), may hold values from -1.75 to 1.75
- value_bias: float32 [1024], P('dev'), may hold values from -1.75 to 1.75
- out_weight: float32 [1024, 1024], P('dev'), may hold values from -1.5 to 1.5
- out_bias: float32 [1024], P('dev'), may hold values from -1.75 to 1.75
- second_gain: float32 [1024], P('dev'), may hold values from 0.5 to 1.5
- second_bias: float32 [1024], P('dev'), may hold values from -1.75 to 1.75
- hidden_weight: float32 [1024, 4096], P('dev'), may hold values from -0.1875 to 0.1875
- hidden_bias: float32 [4096], P('dev'), may hold values from -1.75 to 1.75
- final_weight: float32 [4096, 1024], P('dev'), may hold values from -0.09375 to 0.09375
- final_bias: float32 [1024], P('dev'), may hold values from -1.75 to 1.75
- cotangent: bfloat16 [32768, 1024], P('dev'), may hold values from -6 to 6
Outputs:
- block_output: bfloat16 [32768, 1024], P('dev')
- input_grad: bfloat16 [32768, 1024], P('dev')
- first_gain_grad: float32 [1024], P('dev')
- first_bias_grad: float32 [1024], P('dev')
- qkv_weight_grad: float32 [1024, 3072], P('dev')
- query_bias_grad: float32 [1024], P('dev')
- value_bias_grad: float32 [1024], P('dev')
- out_weight_grad: float32 [1024, 1024], P('dev')
- out_bias_grad: float32 [1024], P('dev')
- second_gain_grad: float32 [1024], P('dev')
- second_bias_grad: float32 [1024], P('dev')
- hidden_weight_grad: float32 [1024, 4096], P('dev')
- hidden_bias_grad: float32 [4096], P('dev')
- final_weight_grad: float32 [4096, 1024], P('dev')
- final_bias_grad: float32 [1024], P('dev')
Inputs may be any that keep to these rules, and one draw needn't show every extreme that they name: `segment_ids`: every image is a run of exactly 577 consecutive token slots, numbered 0, 1, ... in order along the slots, every number present once; all slots outside images are -1, in gaps of random length before, between and after images.
All inputs are finite; a program needn't handle non-finite values.
Results may differ from a plain program's by a relative error of at most 0.012.
The roundings to bfloat16 on the way count: a program that leaves them out, or rounds other values in their place, can miss the bound.
Values may be sent and summed in bfloat16 or wider, within the bound.
No kernel may reach another device: no remote copies, remote signals or barrier semaphores. Data moves between devices by JAX's collectives and lax.ppermute only.
A program may use at most 256 MiB of HBM per device.

v0:
```python
import math

import jax
import jax.numpy as jnp
from jax import lax
from jax.sharding import PartitionSpec as P

HEADS = 16
HEAD = 64
HALO = 576


norm_epsilon = 1e-06


def extended(cells, sides, width):
    for axis, dim in sides:
        count = lax.axis_size(axis)
        ends = count - 1
        head = lax.slice_in_dim(cells, 0, width, axis=dim)
        tail = lax.slice_in_dim(cells, cells.shape[dim] - width, cells.shape[dim], axis=dim)
        cells = jnp.concatenate(
            [
                lax.ppermute(tail, axis, [(i, (i + 1) % count) for i in range(ends)]),
                cells,
                lax.ppermute(head, axis, [((i + 1) % count, i) for i in range(ends)]),
            ],
            axis=dim,
        )
    return cells


def layer_norm(values, gain, bias):
    center = values - jnp.mean(values, axis=-1, keepdims=True)
    spread = jnp.mean(center * center, axis=-1, keepdims=True)
    return center * lax.rsqrt(spread + norm_epsilon) * gain + bias


def exact_gelu(values):
    return jax.nn.gelu(values, approximate=False)


def split_heads(matrix):
    return matrix.reshape(matrix.shape[0], HEADS, HEAD).transpose(1, 0, 2)


def join_heads(stacked):
    return stacked.transpose(1, 0, 2).reshape(stacked.shape[1], HEADS * HEAD)


def per_device(
    tokens,
    segment_ids,
    first_gain,
    first_bias,
    qkv_weight,
    query_bias,
    value_bias,
    out_weight,
    out_bias,
    second_gain,
    second_bias,
    hidden_weight,
    hidden_bias,
    final_weight,
    final_bias,
    cotangent,
):
    bfloat = jnp.bfloat16
    single = jnp.float32
    row_count, model_width = tokens.shape
    reach_rows = HALO
    block_rows = math.gcd(row_count, 512)
    key_span = block_rows + 2 * reach_rows
    blocks = row_count // block_rows
    (
        gain_one,
        bias_one,
        weight_qkv,
        bias_query,
        bias_value,
        weight_out,
        bias_out,
        gain_two,
        bias_two,
        weight_hidden,
        bias_hidden,
        weight_final,
        bias_final,
    ) = (
        lax.all_gather(first_gain.astype(bfloat), "dev", axis=0, tiled=True),
        lax.all_gather(first_bias.astype(bfloat), "dev", axis=0, tiled=True),
        lax.all_gather(qkv_weight.astype(bfloat), "dev", axis=0, tiled=True),
        lax.all_gather(query_bias.astype(bfloat), "dev", axis=0, tiled=True),
        lax.all_gather(value_bias.astype(bfloat), "dev", axis=0, tiled=True),
        lax.all_gather(out_weight.astype(bfloat), "dev", axis=0, tiled=True),
        lax.all_gather(out_bias.astype(bfloat), "dev", axis=0, tiled=True),
        lax.all_gather(second_gain.astype(bfloat), "dev", axis=0, tiled=True),
        lax.all_gather(second_bias.astype(bfloat), "dev", axis=0, tiled=True),
        lax.all_gather(hidden_weight.astype(bfloat), "dev", axis=0, tiled=True),
        lax.all_gather(hidden_bias.astype(bfloat), "dev", axis=0, tiled=True),
        lax.all_gather(final_weight.astype(bfloat), "dev", axis=0, tiled=True),
        lax.all_gather(final_bias.astype(bfloat), "dev", axis=0, tiled=True),
    )
    device_index = lax.axis_index("dev")
    segments_padded = jnp.pad(segment_ids, (reach_rows, reach_rows), constant_values=-2)
    key_ids = lax.dynamic_slice_in_dim(
        segments_padded, device_index * row_count, row_count + 2 * reach_rows, 0
    )
    query_ids = lax.dynamic_slice_in_dim(segment_ids, device_index * row_count, row_count, 0)
    columns = jnp.arange(key_span, dtype=jnp.int32)
    diagonal = jnp.arange(block_rows, dtype=jnp.int32)[:, None] + reach_rows == columns[None, :]
    block_masks = []
    for number in range(blocks):
        begin_at = number * block_rows
        ids_query = query_ids[begin_at : begin_at + block_rows]
        ids_keys = key_ids[begin_at : begin_at + key_span]
        block_masks.append(
            (ids_query[:, None] == ids_keys[None, :]) & (ids_query[:, None] >= 0) | diagonal
        )

    def block_scores(query_block, key_block, number):
        products = jnp.einsum("qd,kd->qk", query_block, key_block, preferred_element_type=single)
        return jnp.where(block_masks[number], products * 0.125, -1e30)

    def head_forward(operands):
        query_head, key_head, value_head = operands
        outputs_list = []
        totals_list = []
        for number in range(blocks):
            begin_at = number * block_rows
            query_block = query_head[begin_at : begin_at + block_rows]
            key_block = key_head[begin_at : begin_at + key_span]
            value_block = value_head[begin_at : begin_at + key_span]
            scores = block_scores(query_block, key_block, number)
            maximum = jnp.max(scores, axis=-1, keepdims=True)
            log_total = maximum + jnp.log(
                jnp.sum(jnp.exp(scores - maximum), axis=-1, keepdims=True)
            )
            weights_soft = jnp.exp(scores - log_total).astype(bfloat)
            outputs_list.append(jnp.dot(weights_soft, value_block, preferred_element_type=single))
            totals_list.append(log_total[:, 0])
        return (jnp.concatenate(outputs_list, axis=0), jnp.concatenate(totals_list, axis=0))

    inputs = tokens.astype(single)
    normed_one = layer_norm(inputs, gain_one.astype(single), bias_one.astype(single)).astype(bfloat)
    packed = jnp.dot(normed_one, weight_qkv, preferred_element_type=single)
    queries = (packed[:, :model_width] + bias_query.astype(single)).astype(bfloat)
    key_rows = packed[:, model_width : 2 * model_width].astype(bfloat)
    value_rows = (packed[:, 2 * model_width :] + bias_value.astype(single)).astype(bfloat)
    window = extended(jnp.concatenate([key_rows, value_rows], axis=1), (("dev", 0),), reach_rows)
    query_heads = split_heads(queries)
    key_heads = split_heads(window[:, :model_width])
    value_heads = split_heads(window[:, model_width:])
    head_outputs, log_totals = lax.map(head_forward, (query_heads, key_heads, value_heads))
    mixed_low = join_heads(head_outputs).astype(bfloat)
    middle = inputs + (
        jnp.dot(mixed_low, weight_out, preferred_element_type=single) + bias_out.astype(single)
    )
    normed_two = layer_norm(middle, gain_two.astype(single), bias_two.astype(single)).astype(bfloat)
    hidden_pre = jnp.dot(
        normed_two, weight_hidden, preferred_element_type=single
    ) + bias_hidden.astype(single)
    activated = exact_gelu(hidden_pre).astype(bfloat)
    result = (
        middle
        + jnp.dot(activated, weight_final, preferred_element_type=single)
        + bias_final.astype(single)
    ).astype(bfloat)
    (
        gain_one,
        bias_one,
        weight_qkv,
        bias_query,
        bias_value,
        weight_out,
        bias_out,
        gain_two,
        bias_two,
        weight_hidden,
        bias_hidden,
        weight_final,
        bias_final,
    ) = (
        lax.all_gather(first_gain.astype(bfloat), "dev", axis=0, tiled=True),
        lax.all_gather(first_bias.astype(bfloat), "dev", axis=0, tiled=True),
        lax.all_gather(qkv_weight.astype(bfloat), "dev", axis=0, tiled=True),
        lax.all_gather(query_bias.astype(bfloat), "dev", axis=0, tiled=True),
        lax.all_gather(value_bias.astype(bfloat), "dev", axis=0, tiled=True),
        lax.all_gather(out_weight.astype(bfloat), "dev", axis=0, tiled=True),
        lax.all_gather(out_bias.astype(bfloat), "dev", axis=0, tiled=True),
        lax.all_gather(second_gain.astype(bfloat), "dev", axis=0, tiled=True),
        lax.all_gather(second_bias.astype(bfloat), "dev", axis=0, tiled=True),
        lax.all_gather(hidden_weight.astype(bfloat), "dev", axis=0, tiled=True),
        lax.all_gather(hidden_bias.astype(bfloat), "dev", axis=0, tiled=True),
        lax.all_gather(final_weight.astype(bfloat), "dev", axis=0, tiled=True),
        lax.all_gather(final_bias.astype(bfloat), "dev", axis=0, tiled=True),
    )
    grad_output = cotangent.astype(single)
    final_weight_grad = jnp.einsum("tf,td->fd", activated, cotangent, preferred_element_type=single)
    final_bias_grad = jnp.sum(grad_output, axis=0)
    grad_activated = jnp.einsum("td,fd->tf", cotangent, weight_final, preferred_element_type=single)
    gelu_pull = jax.vjp(exact_gelu, hidden_pre)[1]
    grad_pre = gelu_pull(grad_activated)[0].astype(bfloat)
    hidden_bias_grad = jnp.sum(grad_pre, axis=0, dtype=single)
    hidden_weight_grad = jnp.einsum(
        "tc,tf->cf", normed_two, grad_pre, preferred_element_type=single
    )
    grad_normed_two = jnp.einsum(
        "tf,cf->tc", grad_pre, weight_hidden, preferred_element_type=single
    )
    norm_pull = jax.vjp(layer_norm, middle, gain_two.astype(single), bias_two.astype(single))[1]
    grad_from_norm, second_gain_grad, second_bias_grad = norm_pull(grad_normed_two)
    grad_middle = grad_output + grad_from_norm
    grad_branch = grad_middle.astype(bfloat)
    out_bias_grad = jnp.sum(grad_branch, axis=0, dtype=single)
    out_weight_grad = jnp.einsum("tc,td->cd", mixed_low, grad_branch, preferred_element_type=single)
    grad_mixed = jnp.einsum(
        "td,cd->tc", grad_branch, weight_out, preferred_element_type=single
    ).astype(bfloat)

    def head_backward(operands):
        query_head, key_head, value_head, grad_head, total_head = operands
        grad_query_list = []
        grad_key_window = jnp.zeros((row_count + 2 * reach_rows, HEAD), single)
        grad_value_window = jnp.zeros((row_count + 2 * reach_rows, HEAD), single)
        for number in range(blocks):
            begin_at = number * block_rows
            query_block = query_head[begin_at : begin_at + block_rows]
            key_block = key_head[begin_at : begin_at + key_span]
            value_block = value_head[begin_at : begin_at + key_span]
            grad_block = grad_head[begin_at : begin_at + block_rows]
            scores = block_scores(query_block, key_block, number)
            weights_full = jnp.exp(scores - total_head[begin_at : begin_at + block_rows, None])
            grad_weights = jnp.einsum(
                "qd,kd->qk", grad_block, value_block, preferred_element_type=single
            )
            row_inner = jnp.sum(weights_full * grad_weights, axis=-1, keepdims=True)
            grad_scores = (weights_full * (grad_weights - row_inner) * 0.125).astype(bfloat)
            grad_query_list.append(
                jnp.einsum("qk,kd->qd", grad_scores, key_block, preferred_element_type=single)
            )
            grad_key_window = grad_key_window.at[begin_at : begin_at + key_span].add(
                jnp.einsum("qk,qd->kd", grad_scores, query_block, preferred_element_type=single)
            )
            grad_value_window = grad_value_window.at[begin_at : begin_at + key_span].add(
                jnp.einsum(
                    "qk,qd->kd",
                    weights_full.astype(bfloat),
                    grad_block,
                    preferred_element_type=single,
                )
            )
        return (jnp.concatenate(grad_query_list, axis=0), grad_key_window, grad_value_window)

    grad_query_heads, grad_key_heads, grad_value_heads = lax.map(
        head_backward, (query_heads, key_heads, value_heads, split_heads(grad_mixed), log_totals)
    )
    grad_queries = join_heads(grad_query_heads).astype(bfloat)
    grad_window = jnp.concatenate(
        [join_heads(grad_key_heads), join_heads(grad_value_heads)], axis=1
    )
    edge_rows = jnp.concatenate(
        [grad_window[:reach_rows], grad_window[row_count + reach_rows :]], axis=0
    )
    arrived = extended(edge_rows.astype(jnp.bfloat16), (("dev", 0),), reach_rows).astype(
        edge_rows.dtype
    )
    own_rows = grad_window[reach_rows : reach_rows + row_count]
    own_rows = own_rows.at[:reach_rows].add(arrived[:reach_rows])
    own_rows = own_rows.at[row_count - reach_rows :].add(arrived[3 * reach_rows :])
    grad_keys = own_rows[:, :model_width].astype(bfloat)
    grad_values = own_rows[:, model_width:].astype(bfloat)
    grad_packed = jnp.concatenate([grad_queries, grad_keys, grad_values], axis=1)
    qkv_weight_grad = jnp.einsum(
        "tc,tq->cq", normed_one, grad_packed, preferred_element_type=single
    )
    query_bias_grad = jnp.sum(grad_queries, axis=0, dtype=single)
    value_bias_grad = jnp.sum(grad_values, axis=0, dtype=single)
    grad_normed_one = jnp.einsum(
        "tq,cq->tc", grad_packed, weight_qkv, preferred_element_type=single
    )
    first_pull = jax.vjp(layer_norm, inputs, gain_one.astype(single), bias_one.astype(single))[1]
    grad_from_first, first_gain_grad, first_bias_grad = first_pull(grad_normed_one)
    input_grad = (grad_middle + grad_from_first).astype(bfloat)
    shards = (
        lax.psum_scatter(first_gain_grad, "dev", scatter_dimension=0, tiled=True),
        lax.psum_scatter(first_bias_grad, "dev", scatter_dimension=0, tiled=True),
        lax.psum_scatter(qkv_weight_grad, "dev", scatter_dimension=0, tiled=True),
        lax.psum_scatter(query_bias_grad, "dev", scatter_dimension=0, tiled=True),
        lax.psum_scatter(value_bias_grad, "dev", scatter_dimension=0, tiled=True),
        lax.psum_scatter(out_weight_grad, "dev", scatter_dimension=0, tiled=True),
        lax.psum_scatter(out_bias_grad, "dev", scatter_dimension=0, tiled=True),
        lax.psum_scatter(second_gain_grad, "dev", scatter_dimension=0, tiled=True),
        lax.psum_scatter(second_bias_grad, "dev", scatter_dimension=0, tiled=True),
        lax.psum_scatter(hidden_weight_grad, "dev", scatter_dimension=0, tiled=True),
        lax.psum_scatter(hidden_bias_grad, "dev", scatter_dimension=0, tiled=True),
        lax.psum_scatter(final_weight_grad, "dev", scatter_dimension=0, tiled=True),
        lax.psum_scatter(final_bias_grad, "dev", scatter_dimension=0, tiled=True),
    )
    return (
        result,
        input_grad,
        shards[0],
        shards[1],
        shards[2],
        shards[3],
        shards[4],
        shards[5],
        shards[6],
        shards[7],
        shards[8],
        shards[9],
        shards[10],
        shards[11],
        shards[12],
    )


def solution(mesh):
    return jax.shard_map(
        per_device,
        mesh=mesh,
        in_specs=(
            P("dev", None),
            P(),
            P("dev"),
            P("dev"),
            P("dev", None),
            P("dev"),
            P("dev"),
            P("dev", None),
            P("dev"),
            P("dev"),
            P("dev"),
            P("dev", None),
            P("dev"),
            P("dev", None),
            P("dev"),
            P("dev", None),
        ),
        out_specs=(
            P("dev", None),
            P("dev", None),
            P("dev"),
            P("dev"),
            P("dev", None),
            P("dev"),
            P("dev"),
            P("dev", None),
            P("dev"),
            P("dev"),
            P("dev"),
            P("dev", None),
            P("dev"),
            P("dev", None),
            P("dev"),
        ),
        check_vma=False,
    )
```

profile of v0, /device:TPU:0, one launch (start us, length us, event | category | flops | bytes accessed | tf_op | source)
XLA Modules:
  0.0 1637.9 jit_solution(4876742592519676714)
XLA Ops:
  22.3 42.7 %all-reduce.21 = (bf16[1024]{0:T(1024)(128)(2,1)S(1)}, bf16[1024]{0:T(1024)(128)(2,1)S(1)}, bf16[1024]{0:T(1024)(128)(2,1)S(1)}, bf16[1024]{0:T(1024)(128)(2,1)S...) all-reduce(bf16[1024]{0:T(1024)(128)(2,1)S(1)} %dynamic-update-slic, ...), channel_id=1, replica_groups=mesh['dev'=32] {'dev'}, use_global_device_ids=true, to_apply=%add.7 | all-reduce | flops 8192 | bytes 32768
  66.6 17.5 %all-gather.6.cloned.1.call-done = bf16[1024,3072]{1,0:T(8,128)(2,1)} async-done(((bf16[32,3072]{1,0:T(8,128)(2,1)}), bf16[1024,3072]{1,0:T(8,128)(2,1)}) %all-gather.6.cloned.1.call-update) | async-done | bytes 6291472 | tf_op jit(solution)/shard_map/all_gather | solution.py:93
  84.1 9.3 fusion.77
  96.4 6.2 fusion.70
  109.4 85.2 %all-gather = bf16[32,1,128]{2,1,0:T(2,128)(2,1)S(1)} all-gather(bf16[1,1,128]{2,1,0:T(2,128)(2,1)S(1)} %convert_bitcast_fusion), channel_id=1, replica_groups=mesh['dev'=32] {'dev'}, dimensions={0}, use_global_device_ids=true | all-gather | bytes 8448 | tf_op jit(solution)/shard_map/all_gather | solution.py:101
  217.0 6.6 copy.87
  223.6 9.3 copy.90
  232.9 6.5 copy.88
  239.4 9.3 copy.91
  250.3 190.9 %while.39 = (s32[]{:T(128)}, bf16[16,1024,64]{1,2,0:T(8,128)(2,1)}, f32[16,1024]{1,0:T(8,128)}, bf16[16,1024,64]{2,1,0:T(8,128)(2,1)}, bf16[16,2176,64]{2,1,0:T(...) while((s32[]{:T(128)}, bf16[16,1024,64]{1,2,0:T(8,128)(2,1)}, ...), condition=%wide.region_7.8_spmd.clone.clone, body=%wide.region_2.7_spmd.clone.clone.sunk | while | flops 455213056 | bytes 22877372 | solution.py:155
  449.0 16.9 %fusion.80 = f32[1024,4096]{1,0:T(8,128)} fusion(bf16[1024,4096]{1,0:T(8,128)(2,1)} %all-gather.10.cloned.1.call-done, f32[1024,1024]{0,1:T(8,128)} %copy-done.5, f32[1024]{0:T(1024)S(1)} %convert_element_type.207, f32[1024]{0:T(1024)S(1)} %convert_element_type.205, f32[1024]{0:T(1024)S(1)} %fusion.73, f32[1024]{0:T(1024)S(1)} %broadcast_multiply_fusion), kind=kOutput, calls=%fused_computation.173 | convolution fusion | flops 8595177472 | bytes 29376512 | tf_op jit(solution)/shard_map/dot_general | solution.py:161
  466.0 51.7 %convert_reduce_fusion = (f32[4096]{0:T(1024)}, bf16[1024,4096]{1,0:T(8,128)(2,1)S(1)}, f32[1024,4096]{1,0:T(8,128)}) fusion(f32[1024,4096]{1,0:T(8,128)} %fusion.80, f32[4096]{0:T(1024)S(1)} %bitcast.217, bf16[1024,1024]{1,0:T(8,128)(2,1)S(1)} %copy-done.17, bf16[4096,1024]{1,0:T(8,128)(2,1)} %all-gather.12.cloned.1.call-done), kind=kOutput, calls=%fused_computation.90 | convolution fusion | flops 8904503296 | bytes 52461568 | tf_op jit(solution)/shard_map/td,fd->tf/dot_general | solution.py:202
  517.7 11.0 fusion.91
  558.7 351.4 %while.40 = (s32[]{:T(128)}, bf16[16,1024,64]{1,2,0:T(8,128)(2,1)}, f32[16,2176,64]{1,2,0:T(8,128)}, f32[16,2176,64]{1,2,0:T(8,128)}, bf16[16,1024,64]{2,1,0:T(8...) while((s32[]{:T(128)}, bf16[16,1024,64]{1,2,0:T(8,128)(2,1)}, ...), condition=%wide.region_15.16_spmd.clone.clone, body=%wide.region_12.15_spmd.clone.clone.sunk | while | flops 1114848256 | bytes 61915380 | solution.py:256
  910.1 7.6 fusion.44
  935.3 9.2 fusion.51
  953.4 16.0 concatenate.50
  969.5 11.6 convert_element_type.224
  981.0 8.1 fusion.57
  989.1 25.3 %scatter-add.24 = f32[1024,2048]{0,1:T(8,128)} dynamic-update-slice(f32[1024,2048]{0,1:T(8,128)} %fusion.51, f32[576,2048]{0,1:T(8,128)} %fusion.57, s32[]{:T(128)} %constant.294.clone.1, s32[]{:T(128)} %constant.294.clone.1) | dynamic-update-slice | bytes 9437188 | tf_op jit(solution)/shard_map/scatter-add | solution.py:270
  1014.4 9.2 slice_add_fusion
  1023.6 27.5 %scatter-add.25 = f32[1024,2048]{0,1:T(8,128)} dynamic-update-slice(f32[1024,2048]{0,1:T(8,128)} %scatter-add.24, f32[576,2048]{0,1:T(8,128)} %slice_add_fusion, s32[]{:T(128)} %constant.335.clone.1, s32[]{:T(128)} %constant.294.clone.1) | dynamic-update-slice | bytes 9437188 | tf_op jit(solution)/shard_map/scatter-add | solution.py:271
  1057.4 11.4 fusion.67
  1069.5 16.9 %fusion.79 = f32[1024,4096]{1,0:T(8,128)} fusion(bf16[1024,4096]{1,0:T(8,128)(2,1)} %copy-done.69, f32[1024,1024]{0,1:T(8,128)} %copy-done.5, f32[1024]{0:T(1024)S(1)} %copy-done.55, f32[1024]{0:T(1024)S(1)} %copy-done.36, f32[1024]{0:T(1024)S(1)} %copy-done.39, f32[1024]{0:T(1024)S(1)} %copy-done.29), kind=kOutput, calls=%fused_computation.172 | convolution fusion | flops 8595177472 | bytes 29376512 | tf_op jit(solution)/shard_map/tc,tf->cf/dot_general | solution.py:206
  1087.0 12.2 multiply_convert_fusion.2
  1102.5 11.5 fusion.93
  1114.7 16.1 add_convert_fusion.2
  1137.0 12.6 fusion.90
  1171.1 75.4 %all-reduce.20 = (f32[1024]{0:T(1024)S(1)}, f32[1024]{0:T(1024)S(1)}, f32[1024]{0:T(1024)S(1)}, f32[1024]{0:T(1024)S(1)}, f32[1024]{0:T(1024)S(1)}, /*index=5*/f...) all-reduce(f32[1024]{0:T(1024)S(1)} %get-tuple-element.609, ...), channel_id=2, replica_groups=mesh['dev'=32] {'dev'}, use_global_device_ids=true, to_apply=%region_19.20.clone | all-reduce | flops 12288 | bytes 98304
  1251.8 6.6 reduce-scatter.5.cloned.1.call-done
  1258.4 184.7 %reduce-scatter.9.cloned.1.call-done = f32[32,4096]{1,0:T(8,128)} async-done(((f32[1024,4096]{1,0:T(8,128)}), f32[32,4096]{1,0:T(8,128)}) %reduce-scatter.9.cloned.1.call-update) | async-done | bytes 524304 | tf_op jit(solution)/shard_map/reduce_scatter | solution.py:296
  1443.1 187.6 %reduce-scatter.11.cloned.1.call-done = f32[128,1024]{1,0:T(8,128)} async-done(((f32[4096,1024]{1,0:T(8,128)}), f32[128,1024]{1,0:T(8,128)}) %reduce-scatter.11.cloned.1.call-update) | async-done | bytes 524304 | tf_op jit(solution)/shard_map/reduce_scatter | solution.py:298
  (698 shorter events, 698.3 us)
Async XLA Ops:
  7.2 76.9 %all-gather.6.cloned.1.call-start = ((), (), s32[]{:S(2)}) async-start(), calls=%async_computation.4 | async-start | bytes 6488064 | tf_op jit(solution)/shard_map/all_gather | solution.py:93
  8.9 432.4 %all-gather.8.cloned.1.call-start = ((), (), s32[]{:S(2)}) async-start(), calls=%async_computation.5 | async-start | bytes 2162688 | tf_op jit(solution)/shard_map/all_gather | solution.py:96
  10.6 438.4 %all-gather.10.cloned.1.call-start = ((), (), s32[]{:S(2)}) async-start(), calls=%async_computation.6 | async-start | bytes 8650752 | tf_op jit(solution)/shard_map/all_gather | solution.py:100
  12.4 453.5 %all-gather.12.cloned.1.call-start = ((), (), s32[]{:S(2)}) async-start(), calls=%async_computation.7 | async-start | bytes 8650752 | tf_op jit(solution)/shard_map/all_gather | solution.py:102
  20.6 420.8 %copy-start = (bf16[1024,1024]{0,1:T(8,128)(2,1)}, bf16[1024,1024]{0,1:T(8,128)(2,1)S(1)}, u32[]{:S(2)}) copy-start(bf16[1024,1024]{0,1:T(8,128)(2,1)S(1)} %copy.85) | copy-start | bytes 6291460
  65.0 28.4 %copy-start.52 = (f32[1024]{0:T(1024)}, f32[1024]{0:T(1024)S(1)}, u32[]{:S(2)}) copy-start(f32[1024]{0:T(1024)S(1)} %convert_element_type.189) | copy-start | bytes 12292
  65.0 28.4 %copy-start.25 = (f32[1024]{0:T(1024)}, f32[1024]{0:T(1024)S(1)}, u32[]{:S(2)}) copy-start(f32[1024]{0:T(1024)S(1)} %convert_element_type.187) | copy-start | bytes 12292
  65.4 28.0 %copy-start.21 = (f32[1024]{0:T(1024)}, f32[1024]{0:T(1024)S(1)}, u32[]{:S(2)}) copy-start(f32[1024]{0:T(1024)S(1)} %broadcast_multiply_fusion.1) | copy-start | bytes 12292
  66.6 26.8 %copy-start.32 = (f32[1024]{0:T(1024)}, f32[1024]{0:T(1024)S(1)}, u32[]{:S(2)}) copy-start(f32[1024]{0:T(1024)S(1)} %fusion.72) | copy-start | bytes 12292
  96.4 12.1 copy-start.19
  96.4 13.0 copy-start.68
  102.6 96.0 %copy-start.20 = (s32[32768]{0:T(1024)S(1)}, s32[32768]{0:T(1024)}, u32[]{:S(2)}) copy-start(s32[32768]{0:T(1024)} %param.33) | copy-start | bytes 393220
  102.6 104.9 %collective-permute-start.1 = (bf16[576,2048]{1,0:T(8,128)(2,1)}, bf16[576,2048]{1,0:T(8,128)(2,1)}, u32[]{:S(2)}, u32[]{:S(2)}) collective-permute-start(bf16[576,2048]{1,0:T(8,128)(2,1)} %get-tuple-element.714), channel_id=1, source_target_pairs={{1,0},{2,1},{3,2},{4,3},{5,4},{6,5},{7,6},{8,7},{9,8},{10,9},{11,1... | collective-permute-start | bytes 7077896 | tf_op jit(solution)/shard_map/ppermute | solution.py:26
  104.0 103.4 %collective-permute-start = (bf16[576,2048]{1,0:T(8,128)(2,1)}, bf16[576,2048]{1,0:T(8,128)(2,1)}, u32[]{:S(2)}, u32[]{:S(2)}) collective-permute-start(bf16[576,2048]{1,0:T(8,128)(2,1)} %get-tuple-element.713), channel_id=1, source_target_pairs={{0,1},{1,2},{2,3},{3,4},{4,5},{5,6},{6,7},{7,8},{8,9},{9,10},{10,1... | collective-permute-start | bytes 7077896 | tf_op jit(solution)/shard_map/ppermute | solution.py:24
  109.2 1142.6 %reduce-scatter.7.cloned.1.call-start = ((), (), s32[]{:S(2)}) async-start(), calls=%async_computation.9 | async-start | bytes 4325376 | tf_op jit(solution)/shard_map/reduce_scatter | solution.py:292
  109.3 339.6 %copy-start.54 = (f32[1024]{0:T(1024)}, f32[1024]{0:T(1024)S(1)}, u32[]{:S(2)}) copy-start(f32[1024]{0:T(1024)S(1)} %convert_element_type.207) | copy-start | bytes 12292
  109.4 339.6 %copy-start.34 = (f32[1024]{0:T(1024)}, f32[1024]{0:T(1024)S(1)}, u32[]{:S(2)}) copy-start(f32[1024]{0:T(1024)S(1)} %convert_element_type.205) | copy-start | bytes 12292
  194.7 271.3 %copy-start.23 = (f32[32,1,128]{2,1,0:T(1,128)}, f32[32,1,128]{2,1,0:T(1,128)S(1)}, u32[]{:S(2)}) copy-start(f32[32,1,128]{2,1,0:T(1,128)S(1)} %convert_element_type.230) | copy-start | bytes 49156
  446.5 19.4 %copy-start.27 = (f32[1024]{0:T(1024)}, f32[1024]{0:T(1024)S(1)}, u32[]{:S(2)}) copy-start(f32[1024]{0:T(1024)S(1)} %broadcast_multiply_fusion) | copy-start | bytes 12292
  448.9 17.0 %copy-start.42 = (f32[1024]{0:T(1024)}, f32[1024]{0:T(1024)S(1)}, u32[]{:S(2)}) copy-start(f32[1024]{0:T(1024)S(1)} %multiply_reduce_fusion.4) | copy-start | bytes 12292
  448.9 17.0 %copy-start.37 = (f32[1024]{0:T(1024)}, f32[1024]{0:T(1024)S(1)}, u32[]{:S(2)}) copy-start(f32[1024]{0:T(1024)S(1)} %fusion.73) | copy-start | bytes 12292
  448.9 17.0 %copy-start.17 = (bf16[1024,1024]{1,0:T(8,128)(2,1)S(1)}, bf16[1024,1024]{1,0:T(8,128)(2,1)}, u32[]{:S(2)}) copy-start(bf16[1024,1024]{1,0:T(8,128)(2,1)} %param.47) | copy-start | bytes 6291460
  466.0 51.7 %copy-start.67 = (bf16[1024,4096]{1,0:T(8,128)(2,1)S(1)}, bf16[1024,4096]{1,0:T(8,128)(2,1)}, u32[]{:S(2)}) copy-start(bf16[1024,4096]{1,0:T(8,128)(2,1)} %all-gather.10.cloned.1.call-done) | copy-start | bytes 25165828
  517.7 11.0 copy-start.69
  557.1 701.3 %reduce-scatter.5.cloned.1.call-start = ((), (), s32[]{:S(2)}) async-start(), calls=%async_computation.8 | async-start | bytes 12976128 | tf_op jit(solution)/shard_map/reduce_scatter | solution.py:289
  925.9 18.6 %collective-permute-start.2 = (bf16[576,2048]{1,0:T(8,128)(2,1)}, bf16[576,2048]{1,0:T(8,128)(2,1)}, u32[]{:S(2)}, u32[]{:S(2)}) collective-permute-start(bf16[576,2048]{1,0:T(8,128)(2,1)} %copy.99), channel_id=1, source_target_pairs={{0,1},{1,2},{2,3},{3,4},{4,5},{5,6},{6,7},{7,8},{8,9},{9,10},{10,1... | collective-permute-start | bytes 7077896 | tf_op jit(solution)/shard_map/ppermute | solution.py:24
  934.0 15.1 collective-permute-start.3
  1051.1 6.2 copy-start.14
  1051.1 6.2 copy-start.22
  1068.8 374.3 %reduce-scatter.9.cloned.1.call-start = ((), (), s32[]{:S(2)}) async-start(), calls=%async_computation.10 | async-start | bytes 17301504 | tf_op jit(solution)/shard_map/reduce_scatter | solution.py:296
  1086.3 544.4 %reduce-scatter.11.cloned.1.call-start = ((), (), s32[]{:S(2)}) async-start(), calls=%async_computation.11 | async-start | bytes 17301504 | tf_op jit(solution)/shard_map/reduce_scatter | solution.py:298
  1087.0 15.5 copy-start.18
  (50 other events, 178.7 us)
Sparse Core Ops, SparseCore 0:
  11.5 72.5 all-gather.5
  87.5 79.4 all-gather.7
  170.5 76.3 all-gather.9
  250.2 76.0 all-gather.11
  557.2 137.0 reduce-scatter.6
  1068.9 189.4 reduce-scatter.4
  1261.4 181.6 reduce-scatter.8
  1446.1 184.6 reduce-scatter.10
where the time goes:
time: 1650 us; the launch traced here: 1640 us
  matrix products  600 us (36%)
  waiting for transfers between devices  397 us (24%)
  local copies, waits for them, and re-layouts  244 us (15%)
  blocking collectives  203 us (12%)
  other arithmetic  165 us (10%)
    reduce_scatter x1, waiting for transfers between devices, per_device(): lax.psum_scatter(final_weight_grad, 'dev', scatter_dimension=0, tiled=True)  188 us
    reduce_scatter x1, waiting for transfers between devices, per_device(): lax.psum_scatter(hidden_weight_grad, 'dev', scatter_dimension=0, tiled=True)  185 us
    dot_general x64, matrix products, block_scores(): jnp.einsum('qd,kd->qk', query_block, key_block, preferred_element_type=si...  180 us
    unnamed x2, blocking collectives  118 us
    all_gather x1, blocking collectives, per_device(): lax.all_gather(hidden_bias.astype(bfloat), 'dev', axis=0, tiled=True)  85.2 us
    unnamed x172, local copies, waits for them, and re-layouts  58.8 us
    dot_general x32, matrix products, head_forward(): jnp.dot(weights_soft, value_block, preferred_element_type=single)  56.4 us
    dot_general x32, matrix products, head_backward(): jnp.einsum('qd,kd->qk', grad_block, value_block, preferred_element_type=s...  54.2 us
  transfers between devices with their start and end apart: 12, of which 4 were waited for; matrix products, arithmetic and copies ran while one was open for 55% of the time, Pallas kernels for 0%

commit v1 on v0

v1 whole, which is shorter than its diff:
```python
import functools
import math

import jax
import jax.numpy as jnp
from jax import lax
from jax.experimental import pallas as pl
from jax.experimental.pallas import tpu as pltpu
from jax.sharding import PartitionSpec as P

IMG = 577
REACH = IMG - 1
HEAD = 64
SPAN = 592
LANES = 128
QB = 256
PP = 2
PIECES = 32
VMEM = 60 * 1024 * 1024
f32 = jnp.float32
bf16 = jnp.bfloat16

norm_epsilon = 1e-06

def make_items(img_ref, items_ref, blocks, images):
    count = jnp.int32(0)
    for b in range(blocks):
        for i in range(images):
            start = img_ref[i]
            low = b * QB + REACH
            hit = (start < low + QB) & (start + IMG > low)

            @pl.when(hit)
            def _():
                items_ref[count] = b * 8 + i

            count = count + hit.astype(jnp.int32)
    return count

def item_scalars(img_ref, items_ref, n):
    code = items_ref[n]
    b = code // 8
    start = img_ref[code % 8]
    begin = pl.multiple_of((start // 16) * 16, 16)
    row = pl.multiple_of(b * QB, QB)
    return b, start, begin, row

def halves(x):
    lane = lax.broadcasted_iota(jnp.int32, x.shape, 1)
    zero = jnp.zeros_like(x)
    return jnp.concatenate([jnp.where(lane < HEAD, x, zero), jnp.where(lane >= HEAD, x, zero)], axis=0)

def key_valid(start, begin):
    r = lax.broadcasted_iota(jnp.int32, (SPAN, 1), 0) + (begin - start)
    return (r >= 0) & (r < IMG)

def query_valid(start, row):
    lane = lax.broadcasted_iota(jnp.int32, (1, 2 * QB), 1)
    pos = jnp.where(lane < QB, lane, lane - QB) + (row + REACH - start)
    return (pos >= 0) & (pos < IMG)

def pad_rows(img_ref, images, rows):
    r = lax.broadcasted_iota(jnp.int32, (rows, LANES), 0) + REACH
    inside = jnp.zeros((rows, LANES), jnp.bool_)
    for i in range(images):
        start = img_ref[i]
        inside = inside | ((r >= start) & (r < start + IMG))
    return ~inside

def fwd_kernel(blocks, images, img_ref, q_ref, k_ref, v_ref, o_ref, lse_ref, acc, items):
    rows = blocks * QB
    count = make_items(img_ref, items, blocks, images)
    acc[...] = jnp.zeros_like(acc)
    lse_ref[...] = jnp.zeros_like(lse_ref)

    def body(n, carry):
        b, start, begin, row = item_scalars(img_ref, items, n)
        valid = key_valid(start, begin)
        qm = query_valid(start, row)
        done = []
        for u in range(PP):
            cols = slice(u * LANES, (u + 1) * LANES)
            q2 = halves(q_ref[pl.ds(row, QB), cols])
            kw = k_ref[pl.ds(begin, SPAN), cols]
            vw = v_ref[pl.ds(begin, SPAN), cols]
            s = lax.dot_general(kw, q2, (((1,), (1,)), ((), ())), preferred_element_type=f32)
            s = jnp.where(valid, s, -1e30)
            m = jnp.max(s, axis=0, keepdims=True)
            e = jnp.exp(s - m)
            l = jnp.sum(e, axis=0, keepdims=True)
            p = (e * jnp.where(qm, 1.0 / l, 0.0)).astype(bf16)
            ot = lax.dot_general(vw, p, (((0,), (0,)), ((), ())), preferred_element_type=f32)
            done.append((jnp.concatenate([ot[:HEAD, :QB], ot[HEAD:, QB:]], axis=0).T, m + jnp.log(l)))
        for u in range(PP):
            cols = slice(u * LANES, (u + 1) * LANES)
            o, total = done[u]
            acc[pl.ds(row, QB), cols] += o
            old = lse_ref[u, pl.ds(b, 1), :]
            lse_ref[u, pl.ds(b, 1), :] = jnp.where(qm, total, old)
        return carry

    lax.fori_loop(0, count, body, 0)
    pad = pad_rows(img_ref, images, rows)
    for u in range(PP):
        cols = slice(u * LANES, (u + 1) * LANES)
        own = v_ref[pl.ds(REACH, rows), cols].astype(f32)
        o_ref[:, cols] = jnp.where(pad, own, acc[:, cols]).astype(bf16)

def attention_forward(img, q, k, v, first, pairs):
    rows, width = q.shape
    win = k.shape[0]
    blocks = rows // QB
    images = img.shape[0]
    spec = lambda r: pl.BlockSpec((r, PP * LANES), lambda p, *_: (0, first // PP + p))
    return pl.pallas_call(
        functools.partial(fwd_kernel, blocks, images),
        grid_spec=pltpu.PrefetchScalarGridSpec(
            num_scalar_prefetch=1,
            grid=(pairs // PP,),
            in_specs=[spec(rows), spec(win), spec(win)],
            out_specs=[
                pl.BlockSpec((rows, PP * LANES), lambda p, *_: (0, p)),
                pl.BlockSpec((PP, blocks, 2 * QB), lambda p, *_: (p, 0, 0)),
            ],
            scratch_shapes=[pltpu.VMEM((rows, PP * LANES), f32), pltpu.SMEM((blocks * images,), jnp.int32)],
        ),
        out_shape=[
            jax.ShapeDtypeStruct((rows, pairs * LANES), bf16),
            jax.ShapeDtypeStruct((pairs, blocks, 2 * QB), f32),
        ],
        compiler_params=pltpu.CompilerParams(vmem_limit_bytes=VMEM, dimension_semantics=("arbitrary",)),
        cost_estimate=pl.CostEstimate(flops=pairs * 4 * 1300 * SPAN * 256, bytes_accessed=pairs * 2 * LANES * (2 * rows + 2 * win), transcendentals=pairs * 2 * 1300 * SPAN),
        name="attention_forward",
    )(img, q, k, v)

def bwd_kernel(blocks, images, img_ref, q_ref, k_ref, v_ref, g_ref, lse_ref,
               dq_ref, dk_ref, dv_ref, left_ref, right_ref, dq_acc, dk_acc, dv_acc, items):
    rows = blocks * QB
    count = make_items(img_ref, items, blocks, images)
    dq_acc[...] = jnp.zeros_like(dq_acc)
    dk_acc[...] = jnp.zeros_like(dk_acc)
    dv_acc[...] = jnp.zeros_like(dv_acc)

    def body(n, carry):
        b, start, begin, row = item_scalars(img_ref, items, n)
        valid = key_valid(start, begin)
        qm = query_valid(start, row)
        done = []
        for u in range(PP):
            cols = slice(u * LANES, (u + 1) * LANES)
            q2 = halves(q_ref[pl.ds(row, QB), cols])
            g2 = halves(g_ref[pl.ds(row, QB), cols])
            kw = k_ref[pl.ds(begin, SPAN), cols]
            vw = v_ref[pl.ds(begin, SPAN), cols]
            lse = jnp.where(qm, lse_ref[u, pl.ds(b, 1), :], 1e30)
            s = lax.dot_general(kw, q2, (((1,), (1,)), ((), ())), preferred_element_type=f32)
            dp = lax.dot_general(vw, g2, (((1,), (1,)), ((), ())), preferred_element_type=f32)
            p = jnp.exp(jnp.where(valid, s, -1e30) - lse)
            inner = jnp.sum(p * dp, axis=0, keepdims=True)
            ds = (p * (dp - inner)).astype(bf16)
            dv = jnp.dot(p.astype(bf16), g2, preferred_element_type=f32)
            dk = jnp.dot(ds, q2, preferred_element_type=f32)
            dqt = lax.dot_general(kw, ds, (((0,), (0,)), ((), ())), preferred_element_type=f32)
            done.append((dv, dk, jnp.concatenate([dqt[:HEAD, :QB], dqt[HEAD:, QB:]], axis=0).T))
        for u in range(PP):
            cols = slice(u * LANES, (u + 1) * LANES)
            dv, dk, dq = done[u]
            dv_acc[pl.ds(begin, SPAN), cols] += dv
            dk_acc[pl.ds(begin, SPAN), cols] += dk
            dq_acc[pl.ds(row, QB), cols] += dq
        return carry

    lax.fori_loop(0, count, body, 0)
    pad = pad_rows(img_ref, images, rows)
    dq_ref[...] = (dq_acc[...] * 0.125).astype(bf16)
    dk_ref[...] = dk_acc[pl.ds(REACH, rows), :]
    for u in range(PP):
        cols = slice(u * LANES, (u + 1) * LANES)
        dv_ref[:, cols] = dv_acc[pl.ds(REACH, rows), cols] + jnp.where(pad, g_ref[:, cols].astype(f32), 0.0)
    left_ref[0] = dk_acc[pl.ds(0, REACH), :].astype(bf16)
    left_ref[1] = dv_acc[pl.ds(0, REACH), :].astype(bf16)
    right_ref[0] = dk_acc[pl.ds(REACH + rows, REACH), :].astype(bf16)
    right_ref[1] = dv_acc[pl.ds(REACH + rows, REACH), :].astype(bf16)

def attention_backward(img, q, k, v, g, lse, first, pairs):
    rows, width = q.shape
    win = k.shape[0]
    blocks = rows // QB
    images = img.shape[0]
    C = PP * LANES
    spec = lambda r: pl.BlockSpec((r, C), lambda p, *_: (0, first // PP + p))
    out = lambda r: pl.BlockSpec((r, C), lambda p, *_: (0, p))
    edge = pl.BlockSpec((2, REACH, C), lambda p, *_: (0, 0, p))
    sds = jax.ShapeDtypeStruct
    cols = pairs * LANES
    return pl.pallas_call(
        functools.partial(bwd_kernel, blocks, images),
        grid_spec=pltpu.PrefetchScalarGridSpec(
            num_scalar_prefetch=1,
            grid=(pairs // PP,),
            in_specs=[spec(rows), spec(win), spec(win), spec(rows),
                      pl.BlockSpec((PP, blocks, 2 * QB), lambda p, *_: (first // PP + p, 0, 0))],
            out_specs=[out(rows), out(rows), out(rows), edge, edge],
            scratch_shapes=[pltpu.VMEM((rows, C), f32), pltpu.VMEM((win, C), f32), pltpu.VMEM((win, C), f32),
                            pltpu.SMEM((blocks * images,), jnp.int32)],
        ),
        out_shape=[sds((rows, cols), bf16), sds((rows, cols), f32), sds((rows, cols), f32),
                   sds((2, REACH, cols), bf16), sds((2, REACH, cols), bf16)],
        compiler_params=pltpu.CompilerParams(vmem_limit_bytes=VMEM, dimension_semantics=("arbitrary",)),
        cost_estimate=pl.CostEstimate(flops=pairs * 10 * 1300 * SPAN * 256, bytes_accessed=pairs * 2 * LANES * (8 * rows + 4 * win), transcendentals=pairs * 2 * 1300 * SPAN),
        name="attention_backward",
    )(img, q, k, v, g, lse)

def bit_orders(count):
    bits = [1 << i for i in range(count.bit_length() - 1)]
    return (bits[0], bits[2], bits[1], *reversed(bits[3:])), (bits[0], bits[1], bits[2], *reversed(bits[3:]))


def exchange(x, bit, count):
    return lax.ppermute(x, "dev", [(i, i ^ bit) for i in range(count)])


def owners(order, me):
    table = []
    for place in range(PIECES):
        offset = 0
        for i, bit in enumerate(order):
            if (place >> (len(order) - 1 - i)) & 1:
                offset |= bit
        table.append(offset)
    return jnp.array(table, jnp.int32) ^ me


def gather_pieces(shard, order, count):
    held = shard[None]
    for bit in reversed(order[1:]):
        held = jnp.concatenate([held, exchange(held, bit, count)], axis=0)
    return held, exchange(held, order[0], count)


def place_kernel(rows, table, near, far, out, sems):
    half = PIECES // 2
    copies = []
    for place in range(PIECES):
        source = near if place < half else far
        target = out.at[pl.ds(pl.multiple_of(table[place] * rows, 16), rows), :]
        copies.append(pltpu.make_async_copy(source.at[place % half], target, sems.at[place]))
    for copy in copies:
        copy.start()
    for copy in copies:
        copy.wait()


def place(near, far, table):
    _, rows, cols = near.shape
    return pl.pallas_call(
        functools.partial(place_kernel, rows),
        in_specs=[pl.BlockSpec(memory_space=pltpu.SMEM), pl.BlockSpec(memory_space=pl.ANY), pl.BlockSpec(memory_space=pl.ANY)],
        out_specs=pl.BlockSpec(memory_space=pl.ANY),
        out_shape=jax.ShapeDtypeStruct((PIECES * rows, cols), near.dtype),
        scratch_shapes=[pltpu.SemaphoreType.DMA((PIECES,))],
        name="place_pieces",
    )(table, near, far)


def spread_kernel(rows, table, whole, near, far, sems):
    half = PIECES // 2
    copies = []
    for place in range(PIECES):
        target = near if place < half else far
        source = whole.at[pl.ds(pl.multiple_of(table[place] * rows, 16), rows), :]
        copies.append(pltpu.make_async_copy(source, target.at[place % half], sems.at[place]))
    for copy in copies:
        copy.start()
    for copy in copies:
        copy.wait()


def spread(whole, table):
    rows, cols = whole.shape[0] // PIECES, whole.shape[1]
    piece = jax.ShapeDtypeStruct((PIECES // 2, rows, cols), whole.dtype)
    return pl.pallas_call(
        functools.partial(spread_kernel, rows),
        in_specs=[pl.BlockSpec(memory_space=pltpu.SMEM), pl.BlockSpec(memory_space=pl.ANY)],
        out_specs=[pl.BlockSpec(memory_space=pl.ANY)] * 2,
        out_shape=[piece, piece],
        scratch_shapes=[pltpu.SemaphoreType.DMA((PIECES,))],
        name="spread_pieces",
    )(table, whole)


def scatter_pieces(near, far, order, count):
    for step, bit in enumerate(order):
        arrived = exchange(far, bit, count)
        total = lambda a, b: a.astype(f32) + b.astype(f32)
        half = near.shape[0] // 2
        if step + 1 == len(order):
            return total(near, arrived)[0]
        near, far = (
            total(near[:half], arrived[:half]).astype(bf16),
            total(near[half:], arrived[half:]).astype(bf16),
        )


def all_sum(x, count):
    for bit in bit_orders(count)[0]:
        x = x + exchange(x, bit, count)
    return x


def gather_weight(parts, count, me):
    if count != PIECES:
        return [lax.all_gather(part, "dev", axis=0, tiled=True) for part in parts]
    orders = bit_orders(count)
    wholes = []
    for number, part in enumerate(parts):
        order = orders[number % 2]
        near, far = gather_pieces(part, order, count)
        wholes.append(place(near, far, owners(order, me)))
    return wholes


def scatter_weight(parts, count, me):
    if count != PIECES:
        return [lax.psum_scatter(part.astype(f32), "dev", scatter_dimension=0, tiled=True) for part in parts]
    orders = bit_orders(count)
    shards = []
    for number, part in enumerate(parts):
        order = orders[number % 2]
        near, far = spread(part.astype(bf16), owners(order, me))
        shards.append(scatter_pieces(near, far, order, count))
    return shards


def layer_norm(values, gain, bias):
    center = values - jnp.mean(values, axis=-1, keepdims=True)
    spread_of = jnp.mean(center * center, axis=-1, keepdims=True)
    return center * lax.rsqrt(spread_of + norm_epsilon) * gain + bias


def exact_gelu(values):
    return jax.nn.gelu(values, approximate=False)


def image_starts(segment_ids, me, rows):
    padded = jnp.pad(segment_ids, (REACH, REACH), constant_values=-2)
    window = lax.dynamic_slice_in_dim(padded, me * rows, rows + 2 * REACH, 0)
    own = window[REACH : REACH + rows]
    far = jnp.int32(1 << 20)
    first = jnp.min(jnp.where(own >= 0, own, far))
    places = jnp.arange(rows + 2 * REACH, dtype=jnp.int32)
    images = (rows - 2) // IMG + 2
    starts = []
    for i in range(images):
        start = jnp.min(jnp.where(window == first + i, places, far))
        starts.append(jnp.where(start == far, -far, start))
    return jnp.stack(starts)


def per_device(
    tokens,
    segment_ids,
    first_gain,
    first_bias,
    qkv_weight,
    query_bias,
    value_bias,
    out_weight,
    out_bias,
    second_gain,
    second_bias,
    hidden_weight,
    hidden_bias,
    final_weight,
    final_bias,
    cotangent,
):
    count = lax.axis_size("dev")
    me = lax.axis_index("dev")
    rows, width = tokens.shape
    hidden_width = hidden_weight.shape[1]
    pairs = width // LANES
    part = width // count
    img = image_starts(segment_ids, me, rows)
    to_right = [(i, i + 1) for i in range(count - 1)]
    to_left = [(i + 1, i) for i in range(count - 1)]
    window = jnp.concatenate(
        [lax.ppermute(tokens[rows - REACH :], "dev", to_right), tokens, lax.ppermute(tokens[:REACH], "dev", to_left)], axis=0
    )

    vectors = [first_gain, first_bias, query_bias, value_bias, out_bias, second_gain, second_bias, final_bias]
    small = jnp.concatenate([jnp.stack(vectors, axis=1), hidden_bias.reshape(part, -1)], axis=1).astype(bf16)
    small = jnp.pad(small, ((0, 0), (0, LANES - small.shape[1])))
    qkv_low = qkv_weight.astype(bf16)
    split = 2 * width
    part_one, part_two = gather_weight(
        [qkv_low[:, :split], jnp.concatenate([qkv_low[:, split:], out_weight.astype(bf16), small], axis=1)], count, me
    )
    feed = jnp.concatenate([hidden_weight.astype(bf16), final_weight.astype(bf16).reshape(4, part, width).transpose(1, 0, 2).reshape(part, 4 * width)], axis=1)
    feed = lax.all_gather(feed, "dev", axis=0, tiled=True)
    weight_hidden = feed[:, :hidden_width]
    weight_final = feed[:, hidden_width:].reshape(count, part, 4, width).transpose(0, 2, 1, 3).reshape(hidden_width, width)
    weight_value = part_two[:, :width]
    weight_out = part_two[:, width : 2 * width]
    vectors = part_two[:, 2 * width :].astype(f32)
    gain_one, bias_one, bias_query, bias_value, bias_out, gain_two, bias_two, bias_final = [vectors[:, i] for i in range(8)]
    bias_hidden = vectors[:, 8:12].reshape(hidden_width)

    normed = layer_norm(window.astype(f32), gain_one, bias_one).astype(bf16)
    normed_one = normed[REACH : REACH + rows]
    inputs = tokens.astype(f32)
    queries = (jnp.dot(normed_one, part_one[:, :width], preferred_element_type=f32) + bias_query).astype(bf16)
    queries = queries * jnp.asarray(HEAD**-0.5, bf16)
    key_rows = jnp.dot(normed, part_one[:, width:], preferred_element_type=f32).astype(bf16)
    value_rows = (jnp.dot(normed, weight_value, preferred_element_type=f32) + bias_value).astype(bf16)

    mixed_low, totals = attention_forward(img, queries, key_rows, value_rows, 0, pairs)
    middle = inputs + (jnp.dot(mixed_low, weight_out, preferred_element_type=f32) + bias_out)
    normed_two = layer_norm(middle, gain_two, bias_two).astype(bf16)
    hidden_pre = jnp.dot(normed_two, weight_hidden, preferred_element_type=f32) + bias_hidden
    activated = exact_gelu(hidden_pre).astype(bf16)
    result = (middle + jnp.dot(activated, weight_final, preferred_element_type=f32) + bias_final).astype(bf16)

    grad_output = cotangent.astype(f32)
    final_weight_grad = jnp.einsum("tf,td->fd", activated, cotangent, preferred_element_type=f32)
    final_bias_grad = jnp.sum(grad_output, axis=0)
    grad_activated = jnp.einsum("td,fd->tf", cotangent, weight_final, preferred_element_type=f32)
    gelu_pull = jax.vjp(exact_gelu, hidden_pre)[1]
    grad_pre = gelu_pull(grad_activated)[0].astype(bf16)
    hidden_bias_grad = jnp.sum(grad_pre, axis=0, dtype=f32)
    hidden_weight_grad = jnp.einsum("tc,tf->cf", normed_two, grad_pre, preferred_element_type=f32)
    grad_normed_two = jnp.einsum("tf,cf->tc", grad_pre, weight_hidden, preferred_element_type=f32)
    norm_pull = jax.vjp(layer_norm, middle, gain_two, bias_two)[1]
    grad_from_norm, second_gain_grad, second_bias_grad = norm_pull(grad_normed_two)
    grad_middle = grad_output + grad_from_norm
    grad_branch = grad_middle.astype(bf16)
    out_bias_grad = jnp.sum(grad_branch, axis=0, dtype=f32)
    out_weight_grad = jnp.einsum("tc,td->cd", mixed_low, grad_branch, preferred_element_type=f32)
    grad_mixed = jnp.einsum("td,cd->tc", grad_branch, weight_out, preferred_element_type=f32).astype(bf16)
    final_shard, hidden_shard, out_shard = scatter_weight([final_weight_grad, hidden_weight_grad, out_weight_grad], count, me)

    groups = 2
    step = pairs // groups
    cols = step * LANES
    query_parts, key_parts, value_parts = [], [], []
    for group in range(groups):
        dq, dk, dv, left, right = attention_backward(
            img, queries, key_rows, value_rows, grad_mixed, totals, group * step, step
        )
        from_left = lax.ppermute(right, "dev", to_right).astype(f32)
        from_right = lax.ppermute(left, "dev", to_left).astype(f32)
        rest = ((0, rows - REACH), (0, 0))
        back = ((rows - REACH, 0), (0, 0))
        key_parts.append((dk + jnp.pad(from_left[0], rest) + jnp.pad(from_right[0], back)).astype(bf16))
        value_parts.append((dv + jnp.pad(from_left[1], rest) + jnp.pad(from_right[1], back)).astype(bf16))
        query_parts.append(dq)
    grad_queries, grad_keys, grad_values = [jnp.concatenate(p, axis=1) for p in (query_parts, key_parts, value_parts)]
    grad_qk = jnp.concatenate([grad_queries, grad_keys], axis=1)
    qk_weight_grad = jnp.einsum("tc,tq->cq", normed_one, grad_qk, preferred_element_type=f32)
    value_weight_grad = jnp.einsum("tc,tq->cq", normed_one, grad_values, preferred_element_type=f32)
    query_bias_grad = jnp.sum(grad_queries, axis=0, dtype=f32)
    value_bias_grad = jnp.sum(grad_values, axis=0, dtype=f32)
    qk_shard, value_shard = scatter_weight([qk_weight_grad, value_weight_grad], count, me)
    grad_normed_one = jnp.einsum("tq,cq->tc", grad_qk, part_one, preferred_element_type=f32) + jnp.einsum(
        "tq,cq->tc", grad_values, weight_value, preferred_element_type=f32
    )
    first_pull = jax.vjp(layer_norm, inputs, gain_one, bias_one)[1]
    grad_from_first, first_gain_grad, first_bias_grad = first_pull(grad_normed_one)
    input_grad = (grad_middle + grad_from_first).astype(bf16)

    sums = [first_gain_grad, first_bias_grad, query_bias_grad, value_bias_grad, out_bias_grad, second_gain_grad, second_bias_grad, final_bias_grad]
    sums = jnp.concatenate([jnp.stack(sums), hidden_bias_grad.reshape(-1, width)], axis=0)
    sums = all_sum(sums, count)
    own = lax.dynamic_slice_in_dim(sums[:8], me * part, part, 1)
    own_hidden = lax.dynamic_slice_in_dim(sums[8:].reshape(-1), me * hidden_bias.shape[0], hidden_bias.shape[0], 0)
    return (
        result,
        input_grad,
        own[0],
        own[1],
        jnp.concatenate([qk_shard, value_shard], axis=1),
        own[2],
        own[3],
        out_shard,
        own[4],
        own[5],
        own[6],
        hidden_shard,
        own_hidden,
        final_shard,
        own[7],
    )


def solution(mesh):
    split = P("dev", None)
    line = P("dev")
    return jax.shard_map(
        per_device,
        mesh=mesh,
        in_specs=(split, P(), line, line, split, line, line, split, line, line, line, split, line, split, line, split),
        out_specs=(split, split, line, line, split, line, line, split, line, line, line, split, line, split, line),
        check_vma=False,
    )
```

time: 1650 us -> 1840 us (1.12)
  Pallas kernels: 0 us -> 1130 us
  matrix products: 600 us -> 189 us
  blocking collectives: 203 us -> 0 us
  local copies, waits for them, and re-layouts: 244 us -> 75.4 us
  waiting for transfers between devices: 397 us -> 250 us
  other arithmetic: 165 us -> 73.6 us
  starting transfers between devices: 11.1 us -> 87.8 us
    pallas_call x0 -> x10, Pallas kernels: none -> 1130 us  [the longest x5 773 us: spread(): pl.pallas_call(functools.partial(spread_kernel, rows), in_specs=[pl.Block...]
    dot_general x236 -> x16, matrix products: 600 us -> 189 us  [the longest x1 48 us: per_device(): jnp.dot(normed_two, weight_hidden, preferred_element_type=f32) + bias_hidden]
    reduce_scatter x4 -> x0, waiting for transfers between devices: 379 us -> none  [the longest x1 188 us: per_device(): lax.psum_scatter(final_weight_grad, 'dev', scatter_dimension=0, tiled=True)]
    ppermute x4 -> x46, waiting for transfers between devices: 0.01 us -> 250 us  [the longest x40 250 us: exchange(): return lax.ppermute(x, 'dev', [(i, i ^ bit) for i in range(count)])]
    unnamed x2 -> x0, blocking collectives: 118 us -> none
    all_gather x1 -> x0, blocking collectives: 85.2 us -> none  [per_device(): lax.all_gather(hidden_bias.astype(bfloat), 'dev', axis=0, tiled=True)]
    ppermute x4 -> x46, starting transfers between devices: 10.8 us -> 87.8 us  [the longest x40 74.5 us: exchange(): return lax.ppermute(x, 'dev', [(i, i ^ bit) for i in range(count)])]
    scatter-add x2 -> x0, local copies, waits for them, and re-layouts: 52.8 us -> none  [the longest x1 27.5 us: per_device(): own_rows.at[row_count - reach_rows:].add(arrived[3 * reach_rows:])]
  transfers between devices with their start and end apart: 12 -> 47, of which waited for: 4 -> 19; matrix products, arithmetic and copies ran while one was open for 55% -> 9% of each run, Pallas kernels for 0% -> 59%
where the time goes in v1:
time: 1840 us; the launch traced here: 1820 us
  Pallas kernels  1130 us (61%)
  waiting for transfers between devices  250 us (14%)
  matrix products  189 us (10%)
  starting transfers between devices  87.8 us (5%)
  local copies, waits for them, and re-layouts  75.4 us (4%)
  other arithmetic  73.6 us (4%)
  between operations  20.9 us (1%)
    pallas_call x5, Pallas kernels, spread(): pl.pallas_call(functools.partial(spread_kernel, rows), in_specs=[pl.Block...  773 us
    pallas_call x2, Pallas kernels, place(): pl.pallas_call(functools.partial(place_kernel, rows), in_specs=[pl.BlockS...  266 us
    ppermute x40, waiting for transfers between devices, exchange(): return lax.ppermute(x, 'dev', [(i, i ^ bit) for i in range(count)])  250 us
    ppermute x40, starting transfers between devices, exchange(): return lax.ppermute(x, 'dev', [(i, i ^ bit) for i in range(count)])  74.5 us
    pallas_call x2, Pallas kernels, attention_backward(): pl.pallas_call(functools.partial(bwd_kernel, blocks, images), grid_spec=p...  52.2 us
    dot_general x1, matrix products, per_device(): jnp.dot(normed_two, weight_hidden, preferred_element_type=f32) + bias_hidden  48 us
    pallas_call x1, Pallas kernels, attention_forward(): pl.pallas_call(functools.partial(fwd_kernel, blocks, images), grid_spec=p...  37 us
  transfers between devices with their start and end apart: 47, of which 19 were waited for; matrix products, arithmetic and copies ran while one was open for 9% of the time, Pallas kernels for 59%

profile of v1, /device:TPU:0, one launch (start us, length us, event | category | flops | bytes accessed | tf_op | source)
XLA Modules:
  0.0 1825.0 jit_solution(16685414929112728445)
XLA Ops:
  42.7 29.9 %collective-permute-done.7 = bf16[1,32,2048]{2,1,0:T(8,128)(2,1)} collective-permute-done((bf16[1,32,2048]{2,1,0:T(8,128)(2,1)}, bf16[1,32,2048]{2,1,0:T(8,128)(2,1)}, u32[]{:S(2)}, u32[]{:S(2)}) %collective-permute-start.7) | collective-permute-done | bytes 131104 | tf_op jit(solution)/shard_map/ppermute | solution.py:220
  75.6 18.1 collective-permute-done.3
  98.5 17.2 collective-permute-done.4
  116.0 7.8 collective-permute-done.9
  127.3 25.8 %collective-permute-done.5 = bf16[8,32,2176]{2,1,0:T(8,128)(2,1)S(1)} collective-permute-done((bf16[8,32,2176]{2,1,0:T(8,128)(2,1)S(1)}, bf16[8,32,2176]{2,1,0:T(8,128)(2,1)S(1)}, u32[]{:S(2)}, u32[]{:S(2)}) %collective-permute-start.5) | collective-permute-done | bytes 1114144 | tf_op jit(solution)/shard_map/ppermute | solution.py:220
  172.2 129.1 %place_pieces.3 = bf16[1024,2048]{1,0:T(8,128)(2,1)} custom-call(s32[32]{0:T(128)} %broadcast_xor_fusion.table, bf16[16,32,2048]{2,1,0:T(8,128)(2,1)} %constant_dynamic-update-slice_fusion.5.near, bf16[16,32,2048]{2,1,0:T(8,128)(2,1)} %collective-permute-done.11.far), custom_call_target="tpu_custom_call" | custom-call | tf_op jit(solution)/shard_map/place_pieces/pallas_call | solution.py:256
  301.3 137.1 %place_pieces.2 = bf16[1024,2176]{1,0:T(8,128)(2,1)} custom-call(s32[32]{0:T(128)} %broadcast_xor_fusion.1.table, bf16[16,32,2176]{2,1,0:T(8,128)(2,1)} %constant_dynamic-update-slice_fusion.near, bf16[16,32,2176]{2,1,0:T(8,128)(2,1)} %collective-permute-done.6.far), custom_call_target="tpu_custom_call" | custom-call | tf_op jit(solution)/shard_map/place_pieces/pallas_call | solution.py:256
  456.9 8.0 add_convert_fusion.v_ref
  464.9 37.0 %attention_forward.1 = (bf16[1024,1024]{1,0:T(8,128)(2,1)}, f32[8,4,512]{2,1,0:T(4,128)}) custom-call(s32[3]{0:T(128)} %pad_add_fusion.img_ref, bf16[1024,1024]{1,0:T(8,128)(2,1)} %fusion.32.q_ref, bf16[2176,1024]{1,0:T(8,128)(2,1)} %convolution_convert_fusion.2.k_ref, bf16[2176,1024]{1,0:T(8,128)(2,1)} %add_convert_fusion.v_ref), custom_call_target="tpu_custom_call" | custom-call | flops 6304563200 | bytes 13107200 | tf_op jit(solution)/shard_map/attention_forward/pallas_call | solution.py:115
  509.7 7.7 slice.497
  517.5 14.9 reshape.144
  532.4 10.3 copy.84
  542.8 48.0 %multiply_convert_fusion = (bf16[1024,4096]{1,0:T(8,128)(2,1)}, f32[1024,4096]{1,0:T(8,128)}, f32[1024,4096]{1,0:T(8,128)}) fusion(f32[4096]{0:T(1024)S(1)} %add.348, bf16[1024,8192]{1,0:T(8,128)(2,1)} %all-gather.2.cloned.1.call-done, bf16[1024,1024]{0,1:T(8,128)(2,1)S(1)} %add_convert_fusion.50.clone.5), kind=kOutput, calls=%fused_computation.12 | convolution fusion | flops 8866758656 | bytes 52445184 | tf_op jit(solution)/shard_map/dot_general | solution.py:420
  590.8 23.7 %convert_reduce_fusion = (f32[4096]{0:T(1024)S(1)}, bf16[1024,4096]{1,0:T(8,128)(2,1)}) fusion(f32[1024,4096]{1,0:T(8,128)} %get-tuple-element.127, bf16[4096,1024]{1,0:T(8,128)(2,1)} %bitcast.125, bf16[1024,1024]{1,0:T(8,128)(2,1)S(1)} %copy-done.21, f32[1024,4096]{1,0:T(8,128)} %get-tuple-element.182, f32[4096]{0:T(1024)S(1)} %add.348), kind=kOutput, calls=%fused_computation.11 | convolution fusion | flops 8661233664 | bytes 52461568 | tf_op jit(solution)/shard_map/td,fd->tf/dot_general | solution.py:427
  614.6 15.1 convolution_convert_fusion.1.whole
  629.7 12.7 fusion.63
  663.3 26.2 %attention_backward.2 = (bf16[1024,512]{1,0:T(8,128)(2,1)}, f32[1024,512]{1,0:T(8,128)}, f32[1024,512]{1,0:T(8,128)}, bf16[2,576,512]{2,1,0:T(8,128)(2,1)}, bf16[2,576,512]{2,1,0:T(8,128)(2,1)}) custom-call(s32[3]{0:T(128)} %pad_add_fusion.img_ref, bf16[1024,1024]{1,0:T(8,128)(2,1)} %fusion.32.q_ref, bf16[2176,1024]{1,0:T(8,128)(2,1)} %convolution_convert_fusion.2.k_ref, ...), custom_call_target="tpu_custom_call" | custom-call | flops 7880704000 | bytes 17301504 | tf_op jit(solution)/shard_map/attention_backward/pallas_call | solution.py:196
  689.5 26.1 %attention_backward.3 = (bf16[1024,512]{1,0:T(8,128)(2,1)}, f32[1024,512]{1,0:T(8,128)}, f32[1024,512]{1,0:T(8,128)}, bf16[2,576,512]{2,1,0:T(8,128)(2,1)}, bf16[2,576,512]{2,1,0:T(8,128)(2,1)}) custom-call(s32[3]{0:T(128)} %pad_add_fusion.img_ref, bf16[1024,1024]{1,0:T(8,128)(2,1)} %fusion.32.q_ref, bf16[2176,1024]{1,0:T(8,128)(2,1)} %convolution_convert_fusion.2.k_ref, ...), custom_call_target="tpu_custom_call" | custom-call | flops 7880704000 | bytes 17301504 | tf_op jit(solution)/shard_map/attention_backward/pallas_call | solution.py:196
  726.0 15.2 convolution_convert_fusion.whole
  770.5 34.4 %collective-permute-start.16 = (f32[12,1024]{1,0:T(8,128)S(1)}, f32[12,1024]{1,0:T(8,128)S(1)}, u32[]{:S(2)}, u32[]{:S(2)}) collective-permute-start(f32[12,1024]{1,0:T(8,128)S(1)} %concatenate.74), channel_id=1, source_target_pairs={{0,1},{1,0},{2,3},{3,2},{4,5},{5,4},{6,7},{7,6},{8,9},{9,8},{10,11... | collective-permute-start | bytes 147464 | tf_op jit(solution)/shard_map/ppermute | solution.py:220
  810.9 256.2 %spread_pieces.9 = (bf16[16,128,1024]{2,1,0:T(8,128)(2,1)}, bf16[16,128,1024]{2,1,0:T(8,128)(2,1)}) custom-call(s32[32]{0:T(128)} %broadcast_xor_fusion.table, bf16[4096,1024]{1,0:T(8,128)(2,1)} %convolution_convert_fusion.whole), custom_call_target="tpu_custom_call" | custom-call | tf_op jit(solution)/shard_map/spread_pieces/pallas_call | solution.py:282
  1067.2 256.2 %spread_pieces.8 = (bf16[16,32,4096]{2,1,0:T(8,128)(2,1)}, bf16[16,32,4096]{2,1,0:T(8,128)(2,1)}) custom-call(s32[32]{0:T(128)} %broadcast_xor_fusion.1.table, bf16[1024,4096]{1,0:T(8,128)(2,1)} %convolution_convert_fusion.1.whole), custom_call_target="tpu_custom_call" | custom-call | tf_op jit(solution)/shard_map/spread_pieces/pallas_call | solution.py:282
  1323.9 65.6 %spread_pieces.7 = (bf16[16,32,1024]{2,1,0:T(8,128)(2,1)}, bf16[16,32,1024]{2,1,0:T(8,128)(2,1)}) custom-call(s32[32]{0:T(128)} %broadcast_xor_fusion.table, bf16[1024,1024]{1,0:T(8,128)(2,1)} %convolution_convert_fusion.4.whole), custom_call_target="tpu_custom_call" | custom-call | tf_op jit(solution)/shard_map/spread_pieces/pallas_call | solution.py:282
  1397.2 14.4 add_convert_fusion.6
  1417.3 9.4 convolution_convert_fusion.3.whole
  1426.6 129.3 %spread_pieces.5 = (bf16[16,32,2048]{2,1,0:T(8,128)(2,1)}, bf16[16,32,2048]{2,1,0:T(8,128)(2,1)}) custom-call(s32[32]{0:T(128)} %broadcast_xor_fusion.table, bf16[1024,2048]{1,0:T(8,128)(2,1)} %convolution_convert_fusion.3.whole), custom_call_target="tpu_custom_call" | custom-call | tf_op jit(solution)/shard_map/spread_pieces/pallas_call | solution.py:282
  1568.3 65.7 %spread_pieces.6 = (bf16[16,32,1024]{2,1,0:T(8,128)(2,1)}, bf16[16,32,1024]{2,1,0:T(8,128)(2,1)}) custom-call(s32[32]{0:T(128)} %broadcast_xor_fusion.1.table, bf16[1024,1024]{1,0:T(8,128)(2,1)} %convolution_convert_fusion.5.whole), custom_call_target="tpu_custom_call" | custom-call | tf_op jit(solution)/shard_map/spread_pieces/pallas_call | solution.py:282
  1664.7 15.9 collective-permute-done.22
  1681.6 47.5 %collective-permute-done.28 = bf16[4,32,1024]{2,1,0:T(8,128)(2,1)S(1)} collective-permute-done((bf16[4,32,1024]{2,1,0:T(8,128)(2,1)S(1)}, bf16[4,32,1024]{2,1,0:T(8,128)(2,1)S(1)}, u32[]{:S(2)}, u32[]{:S(2)}) %collective-permute-start.28) | collective-permute-done | bytes 262176 | tf_op jit(solution)/shard_map/ppermute | solution.py:220
  1748.2 13.2 collective-permute-done.43
  1765.1 29.5 %collective-permute-done.44 = bf16[2,128,1024]{2,1,0:T(8,128)(2,1)S(1)} collective-permute-done((bf16[2,128,1024]{2,1,0:T(8,128)(2,1)S(1)}, bf16[2,128,1024]{2,1,0:T(8,128)(2,1)S(1)}, u32[]{:S(2)}, u32[]{:S(2)}) %collective-permute-start.44) | collective-permute-done | bytes 524320 | tf_op jit(solution)/shard_map/ppermute | solution.py:220
  1794.8 11.1 collective-permute-done.39
  (352 shorter events, 245.7 us)
Async XLA Ops:
  7.3 502.4 %all-gather.2.cloned.1.call-start = ((), (), s32[]{:S(2)}) async-start(), calls=%async_computation | async-start | bytes 17301504 | tf_op jit(solution)/shard_map/all_gather | solution.py:400
  13.5 26.1 %collective-permute-start.2 = (bf16[1,32,2176]{2,1,0:T(8,128)(2,1)S(1)}, bf16[1,32,2176]{2,1,0:T(8,128)(2,1)S(1)}, u32[]{:S(2)}, u32[]{:S(2)}) collective-permute-start(bf16[1,32,2176]{2,1,0:T(8,128)(2,1)S(1)} %fusion.49), channel_id=1, source_target_pairs={{0,8},{1,9},{2,10},{3,11},{4,12},{5,13},{6,14},{7,15},{8,0},{9,1},... | collective-permute-start | bytes 417800 | tf_op jit(solution)/shard_map/ppermute | solution.py:220
  18.2 148.7 %collective-permute-start = (bf16[576,1024]{1,0:T(8,128)(2,1)}, bf16[576,1024]{1,0:T(8,128)(2,1)S(1)}, u32[]{:S(2)}, u32[]{:S(2)}) collective-permute-start(bf16[576,1024]{1,0:T(8,128)(2,1)} %get-tuple-element.158), channel_id=1, source_target_pairs={{0,1},{1,2},{2,3},{3,4},{4,5},{5,6},{6,7},{7,8},{8,9},{9,10},{10,1... | collective-permute-start | bytes 3538952 | tf_op jit(solution)/shard_map/ppermute | solution.py:388
  19.8 147.1 %collective-permute-start.1 = (bf16[576,1024]{1,0:T(8,128)(2,1)}, bf16[576,1024]{1,0:T(8,128)(2,1)}, u32[]{:S(2)}, u32[]{:S(2)}) collective-permute-start(bf16[576,1024]{1,0:T(8,128)(2,1)} %get-tuple-element.159), channel_id=1, source_target_pairs={{1,0},{2,1},{3,2},{4,3},{5,4},{6,5},{7,6},{8,7},{9,8},{10,9},{11,1... | collective-permute-start | bytes 3538952 | tf_op jit(solution)/shard_map/ppermute | solution.py:388
  21.8 50.8 %collective-permute-start.7 = (bf16[1,32,2048]{2,1,0:T(8,128)(2,1)}, bf16[1,32,2048]{2,1,0:T(8,128)(2,1)}, u32[]{:S(2)}, u32[]{:S(2)}) collective-permute-start(bf16[1,32,2048]{2,1,0:T(8,128)(2,1)} %slice_bitcast_fusion.8), channel_id=1, source_target_pairs={{0,8},{1,9},{2,10},{3,11},{4,12},{5,13},{6,14},{7,15},{8,0},{9,1},... | collective-permute-start | bytes 393224 | tf_op jit(solution)/shard_map/ppermute | solution.py:220
  39.6 54.2 %collective-permute-start.3 = (bf16[2,32,2176]{2,1,0:T(8,128)(2,1)S(1)}, bf16[2,32,2176]{2,1,0:T(8,128)(2,1)S(1)}, u32[]{:S(2)}, u32[]{:S(2)}) collective-permute-start(bf16[2,32,2176]{2,1,0:T(8,128)(2,1)S(1)} %pad_maximum_fusion.13), channel_id=1, source_target_pairs={{0,16},{1,17},{2,18},{3,19},{4,20},{5,21},{6,22},{7,23},{8,24},{9,... | collective-permute-start | bytes 835592 | tf_op jit(solution)/shard_map/ppermute | solution.py:220
  73.6 23.0 %collective-permute-start.8 = (bf16[2,32,2048]{2,1,0:T(8,128)(2,1)S(1)}, bf16[2,32,2048]{2,1,0:T(8,128)(2,1)S(1)}, u32[]{:S(2)}, u32[]{:S(2)}) collective-permute-start(bf16[2,32,2048]{2,1,0:T(8,128)(2,1)S(1)} %pad_maximum_fusion.14), channel_id=1, source_target_pairs={{0,16},{1,17},{2,18},{3,19},{4,20},{5,21},{6,22},{7,23},{8,24},{9,... | collective-permute-start | bytes 786440 | tf_op jit(solution)/shard_map/ppermute | solution.py:220
  97.7 26.0 %collective-permute-start.9 = (bf16[4,32,2048]{2,1,0:T(8,128)(2,1)S(1)}, bf16[4,32,2048]{2,1,0:T(8,128)(2,1)S(1)}, u32[]{:S(2)}, u32[]{:S(2)}) collective-permute-start(bf16[4,32,2048]{2,1,0:T(8,128)(2,1)S(1)} %pad_maximum_fusion.10), channel_id=1, source_target_pairs={{0,2},{1,3},{2,0},{3,1},{4,6},{5,7},{6,4},{7,5},{8,10},{9,11},{10,... | collective-permute-start | bytes 1572872 | tf_op jit(solution)/shard_map/ppermute | solution.py:220
  115.9 37.3 %collective-permute-start.5 = (bf16[8,32,2176]{2,1,0:T(8,128)(2,1)S(1)}, bf16[8,32,2176]{2,1,0:T(8,128)(2,1)S(1)}, u32[]{:S(2)}, u32[]{:S(2)}) collective-permute-start(bf16[8,32,2176]{2,1,0:T(8,128)(2,1)S(1)} %pad_maximum_fusion.3), channel_id=1, source_target_pairs={{0,2},{1,3},{2,0},{3,1},{4,6},{5,7},{6,4},{7,5},{8,10},{9,11},{10,... | collective-permute-start | bytes 3342344 | tf_op jit(solution)/shard_map/ppermute | solution.py:220
  124.8 30.9 %collective-permute-start.10 = (bf16[8,32,2048]{2,1,0:T(8,128)(2,1)S(1)}, bf16[8,32,2048]{2,1,0:T(8,128)(2,1)S(1)}, u32[]{:S(2)}, u32[]{:S(2)}) collective-permute-start(bf16[8,32,2048]{2,1,0:T(8,128)(2,1)S(1)} %pad_maximum_fusion.4), channel_id=1, source_target_pairs={{0,4},{1,5},{2,6},{3,7},{4,0},{5,1},{6,2},{7,3},{8,12},{9,13},{10,... | collective-permute-start | bytes 3145736 | tf_op jit(solution)/shard_map/ppermute | solution.py:220
  154.2 147.1 %collective-permute-start.6 = (bf16[16,32,2176]{2,1,0:T(8,128)(2,1)}, bf16[16,32,2176]{2,1,0:T(8,128)(2,1)}, u32[]{:S(2)}, u32[]{:S(2)}) collective-permute-start(bf16[16,32,2176]{2,1,0:T(8,128)(2,1)} %constant_dynamic-update-slice_fusion.near), channel_id=1, source_target_pairs={{0,1},{1,0},{2,3},{3,2},{4,5},{5,4},{6,7},{7,6},{8,9},{9,8},{10,11... | collective-permute-start | bytes 6684680 | tf_op jit(solution)/shard_map/ppermute | solution.py:220
  715.6 27.6 %collective-permute-start.12 = (bf16[2,576,512]{2,1,0:T(8,128)(2,1)}, bf16[2,576,512]{2,1,0:T(8,128)(2,1)}, u32[]{:S(2)}, u32[]{:S(2)}) collective-permute-start(bf16[2,576,512]{2,1,0:T(8,128)(2,1)} %get-tuple-element.42), channel_id=1, source_target_pairs={{0,1},{1,2},{2,3},{3,4},{4,5},{5,6},{6,7},{7,8},{8,9},{9,10},{10,1... | collective-permute-start | bytes 3538952 | tf_op jit(solution)/shard_map/ppermute | solution.py:450
  719.4 25.4 %collective-permute-start.13 = (bf16[2,576,512]{2,1,0:T(8,128)(2,1)}, bf16[2,576,512]{2,1,0:T(8,128)(2,1)}, u32[]{:S(2)}, u32[]{:S(2)}) collective-permute-start(bf16[2,576,512]{2,1,0:T(8,128)(2,1)} %get-tuple-element.43), channel_id=1, source_target_pairs={{1,0},{2,1},{3,2},{4,3},{5,4},{6,5},{7,6},{8,7},{9,8},{10,9},{11,1... | collective-permute-start | bytes 3538952 | tf_op jit(solution)/shard_map/ppermute | solution.py:451
  720.6 25.7 %collective-permute-start.14 = (bf16[2,576,512]{2,1,0:T(8,128)(2,1)}, bf16[2,576,512]{2,1,0:T(8,128)(2,1)}, u32[]{:S(2)}, u32[]{:S(2)}) collective-permute-start(bf16[2,576,512]{2,1,0:T(8,128)(2,1)} %get-tuple-element.45), channel_id=1, source_target_pairs={{0,1},{1,2},{2,3},{3,4},{4,5},{5,6},{6,7},{7,8},{8,9},{9,10},{10,1... | collective-permute-start | bytes 3538952 | tf_op jit(solution)/shard_map/ppermute | solution.py:450
  724.7 23.8 %collective-permute-start.15 = (bf16[2,576,512]{2,1,0:T(8,128)(2,1)}, bf16[2,576,512]{2,1,0:T(8,128)(2,1)S(1)}, u32[]{:S(2)}, u32[]{:S(2)}) collective-permute-start(bf16[2,576,512]{2,1,0:T(8,128)(2,1)} %get-tuple-element.46), channel_id=1, source_target_pairs={{1,0},{2,1},{3,2},{4,3},{5,4},{6,5},{7,6},{8,7},{9,8},{10,9},{11,1... | collective-permute-start | bytes 3538952 | tf_op jit(solution)/shard_map/ppermute | solution.py:451
  770.5 619.1 %collective-permute-start.16 = (f32[12,1024]{1,0:T(8,128)S(1)}, f32[12,1024]{1,0:T(8,128)S(1)}, u32[]{:S(2)}, u32[]{:S(2)}) collective-permute-start(f32[12,1024]{1,0:T(8,128)S(1)} %concatenate.74), channel_id=1, source_target_pairs={{0,1},{1,0},{2,3},{3,2},{4,5},{5,4},{6,7},{7,6},{8,9},{9,8},{10,11... | collective-permute-start | bytes 147464 | tf_op jit(solution)/shard_map/ppermute | solution.py:220
  1067.1 587.5 %collective-permute-start.41 = (bf16[16,128,1024]{2,1,0:T(8,128)(2,1)}, bf16[16,128,1024]{2,1,0:T(8,128)(2,1)}, u32[]{:S(2)}, u32[]{:S(2)}) collective-permute-start(bf16[16,128,1024]{2,1,0:T(8,128)(2,1)} %get-tuple-element.58), channel_id=1, source_target_pairs={{0,1},{1,0},{2,3},{3,2},{4,5},{5,4},{6,7},{7,6},{8,9},{9,8},{10,11... | collective-permute-start | bytes 12582920 | tf_op jit(solution)/shard_map/ppermute | solution.py:220
  1323.3 336.9 %collective-permute-start.36 = (bf16[16,32,4096]{2,1,0:T(8,128)(2,1)}, bf16[16,32,4096]{2,1,0:T(8,128)(2,1)}, u32[]{:S(2)}, u32[]{:S(2)}) collective-permute-start(bf16[16,32,4096]{2,1,0:T(8,128)(2,1)} %get-tuple-element.56), channel_id=1, source_target_pairs={{0,1},{1,0},{2,3},{3,2},{4,5},{5,4},{6,7},{7,6},{8,9},{9,8},{10,11... | collective-permute-start | bytes 12582920 | tf_op jit(solution)/shard_map/ppermute | solution.py:220
  1389.5 166.6 %collective-permute-start.31 = (bf16[16,32,1024]{2,1,0:T(8,128)(2,1)}, bf16[16,32,1024]{2,1,0:T(8,128)(2,1)}, u32[]{:S(2)}, u32[]{:S(2)}) collective-permute-start(bf16[16,32,1024]{2,1,0:T(8,128)(2,1)} %get-tuple-element.54), channel_id=1, source_target_pairs={{0,1},{1,0},{2,3},{3,2},{4,5},{5,4},{6,7},{7,6},{8,9},{9,8},{10,11... | collective-permute-start | bytes 3145736 | tf_op jit(solution)/shard_map/ppermute | solution.py:220
  1389.6 24.7 %collective-permute-start.17 = (f32[12,1024]{1,0:T(8,128)S(1)}, f32[12,1024]{1,0:T(8,128)S(1)}, u32[]{:S(2)}, u32[]{:S(2)}) collective-permute-start(f32[12,1024]{1,0:T(8,128)S(1)} %add.367), channel_id=1, source_target_pairs={{0,4},{1,5},{2,6},{3,7},{4,0},{5,1},{6,2},{7,3},{8,12},{9,13},{10,... | collective-permute-start | bytes 147464 | tf_op jit(solution)/shard_map/ppermute | solution.py:220
  1414.3 141.6 %collective-permute-start.18 = (f32[12,1024]{1,0:T(8,128)S(1)}, f32[12,1024]{1,0:T(8,128)S(1)}, u32[]{:S(2)}, u32[]{:S(2)}) collective-permute-start(f32[12,1024]{1,0:T(8,128)S(1)} %add.368), channel_id=1, source_target_pairs={{0,2},{1,3},{2,0},{3,1},{4,6},{5,7},{6,4},{7,5},{8,10},{9,11},{10,... | collective-permute-start | bytes 147464 | tf_op jit(solution)/shard_map/ppermute | solution.py:220
  1555.9 96.2 %collective-permute-start.21 = (bf16[16,32,2048]{2,1,0:T(8,128)(2,1)}, bf16[16,32,2048]{2,1,0:T(8,128)(2,1)}, u32[]{:S(2)}, u32[]{:S(2)}) collective-permute-start(bf16[16,32,2048]{2,1,0:T(8,128)(2,1)} %get-tuple-element.50), channel_id=1, source_target_pairs={{0,1},{1,0},{2,3},{3,2},{4,5},{5,4},{6,7},{7,6},{8,9},{9,8},{10,11... | collective-permute-start | bytes 6291464 | tf_op jit(solution)/shard_map/ppermute | solution.py:220
  1558.7 78.0 %collective-permute-start.32 = (bf16[8,32,1024]{2,1,0:T(8,128)(2,1)}, bf16[8,32,1024]{2,1,0:T(8,128)(2,1)}, u32[]{:S(2)}, u32[]{:S(2)}) collective-permute-start(bf16[8,32,1024]{2,1,0:T(8,128)(2,1)} %get-tuple-element.151), channel_id=1, source_target_pairs={{0,4},{1,5},{2,6},{3,7},{4,0},{5,1},{6,2},{7,3},{8,12},{9,13},{10,... | collective-permute-start | bytes 1572872 | tf_op jit(solution)/shard_map/ppermute | solution.py:220
  1562.4 74.1 %collective-permute-start.20 = (f32[12,1024]{1,0:T(8,128)S(1)}, f32[12,1024]{1,0:T(8,128)S(1)}, u32[]{:S(2)}, u32[]{:S(2)}) collective-permute-start(f32[12,1024]{1,0:T(8,128)S(1)} %add.370), channel_id=1, source_target_pairs={{0,8},{1,9},{2,10},{3,11},{4,12},{5,13},{6,14},{7,15},{8,0},{9,1},... | collective-permute-start | bytes 147464 | tf_op jit(solution)/shard_map/ppermute | solution.py:220
  1646.8 82.8 %collective-permute-start.34 = (bf16[2,32,1024]{2,1,0:T(8,128)(2,1)S(1)}, bf16[2,32,1024]{2,1,0:T(8,128)(2,1)S(1)}, u32[]{:S(2)}, u32[]{:S(2)}) collective-permute-start(bf16[2,32,1024]{2,1,0:T(8,128)(2,1)S(1)} %get-tuple-element.167), channel_id=1, source_target_pairs={{0,16},{1,17},{2,18},{3,19},{4,20},{5,21},{6,22},{7,23},{8,24},{9,... | collective-permute-start | bytes 393224 | tf_op jit(solution)/shard_map/ppermute | solution.py:220
  1654.4 26.2 %collective-permute-start.22 = (bf16[8,32,2048]{2,1,0:T(8,128)(2,1)S(1)}, bf16[8,32,2048]{2,1,0:T(8,128)(2,1)S(1)}, u32[]{:S(2)}, u32[]{:S(2)}) collective-permute-start(bf16[8,32,2048]{2,1,0:T(8,128)(2,1)S(1)} %get-tuple-element.137), channel_id=1, source_target_pairs={{0,4},{1,5},{2,6},{3,7},{4,0},{5,1},{6,2},{7,3},{8,12},{9,13},{10,... | collective-permute-start | bytes 3145736 | tf_op jit(solution)/shard_map/ppermute | solution.py:220
  1658.2 80.5 %collective-permute-start.42 = (bf16[8,128,1024]{2,1,0:T(8,128)(2,1)S(1)}, bf16[8,128,1024]{2,1,0:T(8,128)(2,1)S(1)}, u32[]{:S(2)}, u32[]{:S(2)}) collective-permute-start(bf16[8,128,1024]{2,1,0:T(8,128)(2,1)S(1)} %get-tuple-element.129), channel_id=1, source_target_pairs={{0,4},{1,5},{2,6},{3,7},{4,0},{5,1},{6,2},{7,3},{8,12},{9,13},{10,... | collective-permute-start | bytes 6291464 | tf_op jit(solution)/shard_map/ppermute | solution.py:220
  1663.7 77.4 %collective-permute-start.37 = (bf16[8,32,4096]{2,1,0:T(8,128)(2,1)S(1)}, bf16[8,32,4096]{2,1,0:T(8,128)(2,1)S(1)}, u32[]{:S(2)}, u32[]{:S(2)}) collective-permute-start(bf16[8,32,4096]{2,1,0:T(8,128)(2,1)S(1)} %get-tuple-element.131), channel_id=1, source_target_pairs={{0,2},{1,3},{2,0},{3,1},{4,6},{5,7},{6,4},{7,5},{8,10},{9,11},{10,... | collective-permute-start | bytes 6291464 | tf_op jit(solution)/shard_map/ppermute | solution.py:220
  1664.6 64.6 %collective-permute-start.28 = (bf16[4,32,1024]{2,1,0:T(8,128)(2,1)S(1)}, bf16[4,32,1024]{2,1,0:T(8,128)(2,1)S(1)}, u32[]{:S(2)}, u32[]{:S(2)}) collective-permute-start(bf16[4,32,1024]{2,1,0:T(8,128)(2,1)S(1)} %get-tuple-element.165), channel_id=1, source_target_pairs={{0,4},{1,5},{2,6},{3,7},{4,0},{5,1},{6,2},{7,3},{8,12},{9,13},{10,... | collective-permute-start | bytes 786440 | tf_op jit(solution)/shard_map/ppermute | solution.py:220
  1681.0 55.3 %collective-permute-start.23 = (bf16[4,32,2048]{2,1,0:T(8,128)(2,1)S(1)}, bf16[4,32,2048]{2,1,0:T(8,128)(2,1)S(1)}, u32[]{:S(2)}, u32[]{:S(2)}) collective-permute-start(bf16[4,32,2048]{2,1,0:T(8,128)(2,1)S(1)} %get-tuple-element.153), channel_id=1, source_target_pairs={{0,2},{1,3},{2,0},{3,1},{4,6},{5,7},{6,4},{7,5},{8,10},{9,11},{10,... | collective-permute-start | bytes 1572872 | tf_op jit(solution)/shard_map/ppermute | solution.py:220
  1761.8 32.9 %collective-permute-start.44 = (bf16[2,128,1024]{2,1,0:T(8,128)(2,1)S(1)}, bf16[2,128,1024]{2,1,0:T(8,128)(2,1)S(1)}, u32[]{:S(2)}, u32[]{:S(2)}) collective-permute-start(bf16[2,128,1024]{2,1,0:T(8,128)(2,1)S(1)} %get-tuple-element.147), channel_id=1, source_target_pairs={{0,16},{1,17},{2,18},{3,19},{4,20},{5,21},{6,22},{7,23},{8,24},{9,... | collective-permute-start | bytes 1572872 | tf_op jit(solution)/shard_map/ppermute | solution.py:220
  1763.4 42.4 %collective-permute-start.39 = (bf16[2,32,4096]{2,1,0:T(8,128)(2,1)S(1)}, bf16[2,32,4096]{2,1,0:T(8,128)(2,1)S(1)}, u32[]{:S(2)}, u32[]{:S(2)}) collective-permute-start(bf16[2,32,4096]{2,1,0:T(8,128)(2,1)S(1)} %get-tuple-element.149), channel_id=1, source_target_pairs={{0,16},{1,17},{2,18},{3,19},{4,20},{5,21},{6,22},{7,23},{8,24},{9,... | collective-permute-start | bytes 1572872 | tf_op jit(solution)/shard_map/ppermute | solution.py:220
  (80 other events, 1498.7 us)
Sparse Core Ops, SparseCore 0:
  11.6 159.3 all-gather.1

commit v2 on v1

--- a/solution.py
+++ b/solution.py
@@ -211,9 +211,132 @@
         name="attention_backward",
     )(img, q, k, v, g, lse)
 
+
+FT = 512
+ROWS = 256
+
+
+def contract(a, b, dims):
+    return lax.dot_general(a, b, (dims, ((), ())), preferred_element_type=f32)
+
+
+def feed_kernel(
+    tiles, places, table, home, normed, cot, middle, bias_final, wide, tall, bias_hidden,
+    result, grad_normed, bias_grad, hidden_near, hidden_far, final_near, final_far,
+    total, normed_t, final, active, grad_pre, hidden_grad, final_grad, sems,
+):
+    step = pl.program_id(0)
+    slot = lax.rem(step, 2)
+    rows, width = normed.shape
+    devices = tall.shape[0] // 32
+    depth = FT // devices
+    half = places // 2
+
+    @pl.when(step == 0)
+    def _():
+        total[...] = middle[...] + bias_final[...]
+        grad_normed[...] = jnp.zeros_like(grad_normed)
+        normed_t[...] = normed[...].T
+
+    for d in range(devices):
+        for i in range(4):
+            final[d * depth + i * 32 : d * depth + (i + 1) * 32, :] = tall[d * 32 : (d + 1) * 32, i * width : (i + 1) * width]
+    for r in range(0, rows, ROWS):
+        cut = slice(r, r + ROWS)
+        pre = contract(normed[cut, :], wide[...], ((1,), (0,))) + bias_hidden[...]
+        grad = contract(cot[cut, :], final[...], ((1,), (1,)))
+        phi = 0.5 + 0.5 * lax.erf(pre * (0.5**0.5))
+        slope = phi + pre * jnp.exp(pre * pre * -0.5) * ((0.5 / math.pi) ** 0.5)
+        active[cut, :] = (pre * phi).astype(bf16)
+        grad_pre[cut, :] = (grad * slope).astype(bf16)
+        total[cut, :] += contract(active[cut, :], final[...], ((1,), (0,)))
+        grad_normed[cut, :] += contract(grad_pre[cut, :], wide[...], ((1,), (1,)))
+    bias_grad[...] = jnp.sum(grad_pre[...].astype(f32), axis=0, keepdims=True)
+
+    hidden_grad[...] = contract(normed_t[...], grad_pre[...], ((1,), (0,)))
+    piece = width // places
+    for place in range(places):
+        rows_of = hidden_grad[pl.ds(pl.multiple_of(table[place] * piece, piece), piece), :].astype(bf16)
+        if place < half:
+            hidden_near[place] = rows_of
+        else:
+            hidden_far[place - half] = rows_of
+
+    def copy_out(slot, d, target):
+        return pltpu.make_async_copy(final_grad.at[slot, d], target, sems.at[slot, d])
+
+    @pl.when(step >= 2)
+    def _():
+        for d in range(devices):
+            copy_out(slot, d, final_near.at[0]).wait()
+
+    final_grad[slot] = contract(active[...], cot[...], ((0,), (0,))).astype(bf16).reshape(devices, depth, width)
+    for d in range(devices):
+        at = home[step * devices + d]
+
+        @pl.when(at < half)
+        def _():
+            copy_out(slot, d, final_near.at[at]).start()
+
+        @pl.when(at >= half)
+        def _():
+            copy_out(slot, d, final_far.at[at - half]).start()
+
+    @pl.when(step == tiles - 1)
+    def _():
+        result[...] = total[...].astype(bf16)
+        for d in range(devices):
+            copy_out(1 - slot, d, final_near.at[0]).wait()
+            copy_out(slot, d, final_near.at[0]).wait()
+
+
+def feed_forward(normed, cot, middle, bias_final, feed, bias_hidden, table, home):
+    rows, width = normed.shape
+    hidden_width = bias_hidden.shape[1]
+    tiles = hidden_width // FT
+    places = PIECES
+    whole = lambda *shape: pl.BlockSpec(shape, lambda t, *_: (0,) * len(shape), pipeline_mode=pl.Buffered(1))
+    sds = jax.ShapeDtypeStruct
+    final_rows = hidden_width // places
+    devices = FT // final_rows
+    edge = pl.BlockSpec((places // 2, width // places, FT), lambda t, *_: (0, 0, t))
+    anywhere = pl.BlockSpec(memory_space=pl.ANY)
+    flops = 12 * rows * width * hidden_width
+    return pl.pallas_call(
+        functools.partial(feed_kernel, tiles, places),
+        grid_spec=pltpu.PrefetchScalarGridSpec(
+            num_scalar_prefetch=2,
+            grid=(tiles,),
+            in_specs=[
+                whole(rows, width), whole(rows, width), whole(rows, width), whole(1, width),
+                pl.BlockSpec((width, FT), lambda t, *_: (0, t)),
+                pl.BlockSpec((devices * 32, 4 * width), lambda t, *_: (t, 1)),
+                pl.BlockSpec((1, FT), lambda t, *_: (0, t)),
+            ],
+            out_specs=[
+                whole(rows, width), whole(rows, width), pl.BlockSpec((1, FT), lambda t, *_: (0, t)),
+                edge, edge, anywhere, anywhere,
+            ],
+            scratch_shapes=[
+                pltpu.VMEM((rows, width), f32), pltpu.VMEM((width, rows), bf16), pltpu.VMEM((FT, width), bf16),
+                pltpu.VMEM((rows, FT), bf16), pltpu.VMEM((rows, FT), bf16), pltpu.VMEM((width, FT), f32),
+                pltpu.VMEM((2, devices, final_rows, width), bf16), pltpu.SemaphoreType.DMA((2, devices)),
+            ],
+        ),
+        out_shape=[
+            sds((rows, width), bf16), sds((rows, width), f32), sds((1, hidden_width), f32),
+            sds((places // 2, width // places, hidden_width), bf16), sds((places // 2, width // places, hidden_width), bf16),
+            sds((places // 2, final_rows, width), bf16), sds((places // 2, final_rows, width), bf16),
+        ],
+        compiler_params=pltpu.CompilerParams(vmem_limit_bytes=VMEM, dimension_semantics=("arbitrary",)),
+        cost_estimate=pl.CostEstimate(flops=flops, bytes_accessed=60 * 1024 * 1024, transcendentals=2 * rows * hidden_width),
+        name="feed_forward",
+    )(table, home, normed, cot, middle, bias_final, feed, feed, bias_hidden)
+
+
 def bit_orders(count):
     bits = [1 << i for i in range(count.bit_length() - 1)]
-    return (bits[0], bits[2], bits[1], *reversed(bits[3:])), (bits[0], bits[1], bits[2], *reversed(bits[3:]))
+    return (bits[0], bits[2], bits[1], *bits[3:]), (bits[0], bits[1], bits[2], *bits[3:])
 
 
 def exchange(x, bit, count):
@@ -238,68 +361,77 @@
     return held, exchange(held, order[0], count)
 
 
-def place_kernel(rows, table, near, far, out, sems):
-    half = PIECES // 2
-    copies = []
-    for place in range(PIECES):
-        source = near if place < half else far
-        target = out.at[pl.ds(pl.multiple_of(table[place] * rows, 16), rows), :]
-        copies.append(pltpu.make_async_copy(source.at[place % half], target, sems.at[place]))
-    for copy in copies:
-        copy.start()
-    for copy in copies:
-        copy.wait()
+def place_kernel(table, near, far, out):
+    half, rows, _ = near.shape
+    for place in range(2 * half):
+        piece = near[place] if place < half else far[place - half]
+        out[pl.ds(pl.multiple_of(table[place] * rows, rows), rows), :] = piece
 
 
 def place(near, far, table):
-    _, rows, cols = near.shape
+    half, rows, cols = near.shape
+    step = max(c for c in range(LANES, 1024, LANES) if cols % c == 0)
     return pl.pallas_call(
-        functools.partial(place_kernel, rows),
-        in_specs=[pl.BlockSpec(memory_space=pltpu.SMEM), pl.BlockSpec(memory_space=pl.ANY), pl.BlockSpec(memory_space=pl.ANY)],
-        out_specs=pl.BlockSpec(memory_space=pl.ANY),
-        out_shape=jax.ShapeDtypeStruct((PIECES * rows, cols), near.dtype),
-        scratch_shapes=[pltpu.SemaphoreType.DMA((PIECES,))],
+        place_kernel,
+        grid_spec=pltpu.PrefetchScalarGridSpec(
+            num_scalar_prefetch=1,
+            grid=(cols // step,),
+            in_specs=[pl.BlockSpec((half, rows, step), lambda c, *_: (0, 0, c))] * 2,
+            out_specs=pl.BlockSpec((2 * half * rows, step), lambda c, *_: (0, c)),
+        ),
+        out_shape=jax.ShapeDtypeStruct((2 * half * rows, cols), near.dtype),
+        compiler_params=pltpu.CompilerParams(vmem_limit_bytes=VMEM, dimension_semantics=("arbitrary",)),
+        cost_estimate=pl.CostEstimate(flops=0, bytes_accessed=8 * half * rows * cols, transcendentals=0),
         name="place_pieces",
     )(table, near, far)
 
 
-def spread_kernel(rows, table, whole, near, far, sems):
-    half = PIECES // 2
-    copies = []
-    for place in range(PIECES):
-        target = near if place < half else far
-        source = whole.at[pl.ds(pl.multiple_of(table[place] * rows, 16), rows), :]
-        copies.append(pltpu.make_async_copy(source, target.at[place % half], sems.at[place]))
-    for copy in copies:
-        copy.start()
-    for copy in copies:
-        copy.wait()
+def spread_kernel(table, whole, near, far):
+    half, rows, _ = near.shape
+    for place in range(2 * half):
+        piece = whole[pl.ds(pl.multiple_of(table[place] * rows, rows), rows), :]
+        if place < half:
+            near[place] = piece
+        else:
+            far[place - half] = piece
 
 
 def spread(whole, table):
-    rows, cols = whole.shape[0] // PIECES, whole.shape[1]
-    piece = jax.ShapeDtypeStruct((PIECES // 2, rows, cols), whole.dtype)
+    total, cols = whole.shape
+    half, rows = PIECES // 2, total // PIECES
+    step = max(c for c in range(LANES, 1024, LANES) if cols % c == 0)
+    piece = jax.ShapeDtypeStruct((half, rows, cols), whole.dtype)
     return pl.pallas_call(
-        functools.partial(spread_kernel, rows),
-        in_specs=[pl.BlockSpec(memory_space=pltpu.SMEM), pl.BlockSpec(memory_space=pl.ANY)],
-        out_specs=[pl.BlockSpec(memory_space=pl.ANY)] * 2,
+        spread_kernel,
+        grid_spec=pltpu.PrefetchScalarGridSpec(
+            num_scalar_prefetch=1,
+            grid=(cols // step,),
+            in_specs=[pl.BlockSpec((total, step), lambda c, *_: (0, c))],
+            out_specs=[pl.BlockSpec((half, rows, step), lambda c, *_: (0, 0, c))] * 2,
+        ),
         out_shape=[piece, piece],
-        scratch_shapes=[pltpu.SemaphoreType.DMA((PIECES,))],
+        compiler_params=pltpu.CompilerParams(vmem_limit_bytes=VMEM, dimension_semantics=("arbitrary",)),
+        cost_estimate=pl.CostEstimate(flops=0, bytes_accessed=4 * total * cols, transcendentals=0),
         name="spread_pieces",
     )(table, whole)
 
 
-def scatter_pieces(near, far, order, count):
-    for step, bit in enumerate(order):
-        arrived = exchange(far, bit, count)
-        total = lambda a, b: a.astype(f32) + b.astype(f32)
-        half = near.shape[0] // 2
-        if step + 1 == len(order):
-            return total(near, arrived)[0]
-        near, far = (
-            total(near[:half], arrived[:half]).astype(bf16),
-            total(near[half:], arrived[half:]).astype(bf16),
-        )
+def add_low(a, b):
+    return (a.astype(f32) + b.astype(f32)).astype(bf16)
+
+
+def scatter_step(near, far, bit, count):
+    arrived = exchange(far, bit, count)
+    half = near.shape[0] // 2
+    if half == 0:
+        return near[0].astype(f32) + arrived[0].astype(f32), None
+    return add_low(near[:half], arrived[:half]), add_low(near[half:], arrived[half:])
+
+
+def scatter_steps(near, far, order, count):
+    for bit in order:
+        near, far = scatter_step(near, far, bit, count)
+    return near
 
 
 def all_sum(x, count):
@@ -320,26 +452,15 @@
     return wholes
 
 
-def scatter_weight(parts, count, me):
-    if count != PIECES:
-        return [lax.psum_scatter(part.astype(f32), "dev", scatter_dimension=0, tiled=True) for part in parts]
-    orders = bit_orders(count)
-    shards = []
-    for number, part in enumerate(parts):
-        order = orders[number % 2]
-        near, far = spread(part.astype(bf16), owners(order, me))
-        shards.append(scatter_pieces(near, far, order, count))
-    return shards
+def scatter_whole(near, far, count):
+    whole = jnp.concatenate([near, far], axis=0).reshape(-1, near.shape[2])
+    return lax.psum_scatter(whole.astype(f32), "dev", scatter_dimension=0, tiled=True)
 
 
 def layer_norm(values, gain, bias):
     center = values - jnp.mean(values, axis=-1, keepdims=True)
     spread_of = jnp.mean(center * center, axis=-1, keepdims=True)
     return center * lax.rsqrt(spread_of + norm_epsilon) * gain + bias
-
-
-def exact_gelu(values):
-    return jax.nn.gelu(values, approximate=False)
 
 
 def image_starts(segment_ids, me, rows):
@@ -377,10 +498,15 @@
 ):
     count = lax.axis_size("dev")
     me = lax.axis_index("dev")
+    direct = count == PIECES
     rows, width = tokens.shape
     hidden_width = hidden_weight.shape[1]
     pairs = width // LANES
     part = width // count
+    order_one, order_two = bit_orders(PIECES)
+    table_one = owners(order_one, me if direct else 0)
+    table_two = owners(order_two, me if direct else 0)
+    home_two = jnp.argsort(table_two).astype(jnp.int32)
     img = image_starts(segment_ids, me, rows)
     to_right = [(i, i + 1) for i in range(count - 1)]
     to_left = [(i + 1, i) for i in range(count - 1)]
@@ -390,21 +516,26 @@
 
     vectors = [first_gain, first_bias, query_bias, value_bias, out_bias, second_gain, second_bias, final_bias]
     small = jnp.concatenate([jnp.stack(vectors, axis=1), hidden_bias.reshape(part, -1)], axis=1).astype(bf16)
-    small = jnp.pad(small, ((0, 0), (0, LANES - small.shape[1])))
+    small = jnp.pad(small, ((0, 0), (0, 2 * LANES - small.shape[1])))
     qkv_low = qkv_weight.astype(bf16)
     split = 2 * width
     part_one, part_two = gather_weight(
         [qkv_low[:, :split], jnp.concatenate([qkv_low[:, split:], out_weight.astype(bf16), small], axis=1)], count, me
     )
-    feed = jnp.concatenate([hidden_weight.astype(bf16), final_weight.astype(bf16).reshape(4, part, width).transpose(1, 0, 2).reshape(part, 4 * width)], axis=1)
-    feed = lax.all_gather(feed, "dev", axis=0, tiled=True)
-    weight_hidden = feed[:, :hidden_width]
-    weight_final = feed[:, hidden_width:].reshape(count, part, 4, width).transpose(0, 2, 1, 3).reshape(hidden_width, width)
+    final_low = final_weight.astype(bf16)
+    if direct:
+        feed = jnp.concatenate([hidden_weight.astype(bf16)] + [final_low[32 * i : 32 * (i + 1)] for i in range(4)], axis=1)
+        feed = lax.all_gather(feed, "dev", axis=0, tiled=True)
+    else:
+        hidden_low = lax.all_gather(hidden_weight.astype(bf16), "dev", axis=0, tiled=True)
+        final_low = lax.all_gather(final_low, "dev", axis=0, tiled=True)
+        final_low = final_low.reshape(PIECES, 4, 32, width).transpose(0, 2, 1, 3).reshape(width, 4 * width)
+        feed = jnp.concatenate([hidden_low, final_low], axis=1)
     weight_value = part_two[:, :width]
     weight_out = part_two[:, width : 2 * width]
     vectors = part_two[:, 2 * width :].astype(f32)
     gain_one, bias_one, bias_query, bias_value, bias_out, gain_two, bias_two, bias_final = [vectors[:, i] for i in range(8)]
-    bias_hidden = vectors[:, 8:12].reshape(hidden_width)
+    bias_hidden = vectors[:, 8 : 8 + hidden_width // width].reshape(1, hidden_width)
 
     normed = layer_norm(window.astype(f32), gain_one, bias_one).astype(bf16)
     normed_one = normed[REACH : REACH + rows]
@@ -417,53 +548,68 @@
     mixed_low, totals = attention_forward(img, queries, key_rows, value_rows, 0, pairs)
     middle = inputs + (jnp.dot(mixed_low, weight_out, preferred_element_type=f32) + bias_out)
     normed_two = layer_norm(middle, gain_two, bias_two).astype(bf16)
-    hidden_pre = jnp.dot(normed_two, weight_hidden, preferred_element_type=f32) + bias_hidden
-    activated = exact_gelu(hidden_pre).astype(bf16)
-    result = (middle + jnp.dot(activated, weight_final, preferred_element_type=f32) + bias_final).astype(bf16)
-
     grad_output = cotangent.astype(f32)
-    final_weight_grad = jnp.einsum("tf,td->fd", activated, cotangent, preferred_element_type=f32)
     final_bias_grad = jnp.sum(grad_output, axis=0)
-    grad_activated = jnp.einsum("td,fd->tf", cotangent, weight_final, preferred_element_type=f32)
-    gelu_pull = jax.vjp(exact_gelu, hidden_pre)[1]
-    grad_pre = gelu_pull(grad_activated)[0].astype(bf16)
-    hidden_bias_grad = jnp.sum(grad_pre, axis=0, dtype=f32)
-    hidden_weight_grad = jnp.einsum("tc,tf->cf", normed_two, grad_pre, preferred_element_type=f32)
-    grad_normed_two = jnp.einsum("tf,cf->tc", grad_pre, weight_hidden, preferred_element_type=f32)
+    result, grad_normed_two, hidden_bias_grad, hidden_near, hidden_far, final_near, final_far = feed_forward(
+        normed_two, cotangent, middle, bias_final[None], feed, bias_hidden, table_one, home_two
+    )
+
     norm_pull = jax.vjp(layer_norm, middle, gain_two, bias_two)[1]
     grad_from_norm, second_gain_grad, second_bias_grad = norm_pull(grad_normed_two)
     grad_middle = grad_output + grad_from_norm
     grad_branch = grad_middle.astype(bf16)
     out_bias_grad = jnp.sum(grad_branch, axis=0, dtype=f32)
-    out_weight_grad = jnp.einsum("tc,td->cd", mixed_low, grad_branch, preferred_element_type=f32)
     grad_mixed = jnp.einsum("td,cd->tc", grad_branch, weight_out, preferred_element_type=f32).astype(bf16)
-    final_shard, hidden_shard, out_shard = scatter_weight([final_weight_grad, hidden_weight_grad, out_weight_grad], count, me)
+    if direct:
+        hidden_near, hidden_far = scatter_step(hidden_near, hidden_far, order_one[0], count)
+        final_near, final_far = scatter_step(final_near, final_far, order_two[0], count)
+        grad_mixed, hidden_near, hidden_far, final_near, final_far = lax.optimization_barrier(
+            (grad_mixed, hidden_near, hidden_far, final_near, final_far)
+        )
+    else:
+        hidden_shard = scatter_whole(hidden_near, hidden_far, count)
+        final_shard = scatter_whole(final_near, final_far, count)
 
     groups = 2
     step = pairs // groups
     cols = step * LANES
-    query_parts, key_parts, value_parts = [], [], []
+    query_parts, key_parts, value_parts, shards = [], [], [], []
     for group in range(groups):
         dq, dk, dv, left, right = attention_backward(
             img, queries, key_rows, value_rows, grad_mixed, totals, group * step, step
         )
+        if direct and group == groups - 1:
+            hidden_near, hidden_far = scatter_step(hidden_near, hidden_far, order_one[1], count)
+            final_near, final_far = scatter_step(final_near, final_far, order_two[1], count)
+            dq, hidden_near, hidden_far, final_near, final_far = lax.optimization_barrier(
+                (dq, hidden_near, hidden_far, final_near, final_far)
+            )
+            hidden_shard = scatter_steps(hidden_near, hidden_far, order_one[2:], count)
+            final_shard = scatter_steps(final_near, final_far, order_two[2:], count)
         from_left = lax.ppermute(right, "dev", to_right).astype(f32)
         from_right = lax.ppermute(left, "dev", to_left).astype(f32)
         rest = ((0, rows - REACH), (0, 0))
         back = ((rows - REACH, 0), (0, 0))
+        query_parts.append(dq)
         key_parts.append((dk + jnp.pad(from_left[0], rest) + jnp.pad(from_right[0], back)).astype(bf16))
         value_parts.append((dv + jnp.pad(from_left[1], rest) + jnp.pad(from_right[1], back)).astype(bf16))
-        query_parts.append(dq)
+        packed = jnp.concatenate([query_parts[-1], key_parts[-1], value_parts[-1]], axis=1)
+        share = jnp.einsum("tc,tq->cq", normed_one, packed, preferred_element_type=f32).astype(bf16)
+        pieces = [share[:, : share.shape[1] // 2], share[:, share.shape[1] // 2 :]]
+        if group == 0:
+            pieces = [share, jnp.einsum("tc,td->cd", mixed_low, grad_branch, preferred_element_type=f32).astype(bf16)]
+        for piece, order, table in zip(pieces, (order_one, order_two), (table_one, table_two)):
+            near, far = spread(piece, table)
+            shards.append(scatter_steps(near, far, order, count) if direct else scatter_whole(near, far, count))
     grad_queries, grad_keys, grad_values = [jnp.concatenate(p, axis=1) for p in (query_parts, key_parts, value_parts)]
-    grad_qk = jnp.concatenate([grad_queries, grad_keys], axis=1)
-    qk_weight_grad = jnp.einsum("tc,tq->cq", normed_one, grad_qk, preferred_element_type=f32)
-    value_weight_grad = jnp.einsum("tc,tq->cq", normed_one, grad_values, preferred_element_type=f32)
+    out_shard = shards[1]
+    halves_of = [shards[0], jnp.concatenate(shards[2:], axis=1)]
+    qkv_shard = jnp.concatenate([h[:, i * cols : (i + 1) * cols] for i in range(3) for h in halves_of], axis=1)
     query_bias_grad = jnp.sum(grad_queries, axis=0, dtype=f32)
     value_bias_grad = jnp.sum(grad_values, axis=0, dtype=f32)
-    qk_shard, value_shard = scatter_weight([qk_weight_grad, value_weight_grad], count, me)
-    grad_normed_one = jnp.einsum("tq,cq->tc", grad_qk, part_one, preferred_element_type=f32) + jnp.einsum(
-        "tq,cq->tc", grad_values, weight_value, preferred_element_type=f32
-    )
+    grad_normed_one = jnp.einsum(
+        "tq,cq->tc", jnp.concatenate([grad_queries, grad_keys], axis=1), part_one, preferred_element_type=f32
+    ) + jnp.einsum("tq,cq->tc", grad_values, weight_value, preferred_element_type=f32)
     first_pull = jax.vjp(layer_norm, inputs, gain_one, bias_one)[1]
     grad_from_first, first_gain_grad, first_bias_grad = first_pull(grad_normed_one)
     input_grad = (grad_middle + grad_from_first).astype(bf16)
@@ -478,7 +624,7 @@
         input_grad,
         own[0],
         own[1],
-        jnp.concatenate([qk_shard, value_shard], axis=1),
+        qkv_shard,
         own[2],
         own[3],
         out_shard,

time: 1840 us -> 687 us (0.37)
  Pallas kernels: 1130 us -> 187 us
  matrix products: 189 us -> 58.9 us
  waiting for transfers between devices: 250 us -> 196 us
  local copies, waits for them, and re-layouts: 75.4 us -> 30.9 us
  starting transfers between devices: 87.8 us -> 107 us
    pallas_call x7, Pallas kernels: 1040 us -> 96.6 us  [the longest x1 70.7 us: feed_forward(): pl.pallas_call(functools.partial(feed_kernel, tiles, places), grid_spec=p...]
    dot_general x9 -> x3, matrix products: 149 us -> 20.5 us  [the longest x2 12.9 us: per_device(): jnp.einsum('tc,tq->cq', normed_one, packed, preferred_element_type=f32)]
    ppermute x40 -> x45, waiting for transfers between devices: 250 us -> 196 us  [exchange(): return lax.ppermute(x, 'dev', [(i, i ^ bit) for i in range(count)])]
    ppermute x40 -> x45, starting transfers between devices: 74.5 us -> 94.7 us  [exchange(): return lax.ppermute(x, 'dev', [(i, i ^ bit) for i in range(count)])]
  transfers between devices with their start and end apart: 47 -> 52, of which waited for: 19 -> 22; matrix products, arithmetic and copies ran while one was open for 9% -> 23% of each run, Pallas kernels for 59% -> 17%
where the time goes in v2:
time: 687 us; the launch traced here: 677 us
  waiting for transfers between devices  196 us (29%)
  Pallas kernels  187 us (27%)
  starting transfers between devices  107 us (16%)
  other arithmetic  77 us (11%)
  matrix products  58.9 us (9%)
  local copies, waits for them, and re-layouts  30.9 us (4%)
  between operations  20.6 us (3%)
    ppermute x45, waiting for transfers between devices, exchange(): return lax.ppermute(x, 'dev', [(i, i ^ bit) for i in range(count)])  196 us
    ppermute x45, starting transfers between devices, exchange(): return lax.ppermute(x, 'dev', [(i, i ^ bit) for i in range(count)])  94.7 us
    pallas_call x1, Pallas kernels, feed_forward(): pl.pallas_call(functools.partial(feed_kernel, tiles, places), grid_spec=p...  70.7 us
    pallas_call x2, Pallas kernels, attention_backward(): pl.pallas_call(functools.partial(bwd_kernel, blocks, images), grid_spec=p...  52.6 us
    pallas_call x1, Pallas kernels, attention_forward(): pl.pallas_call(functools.partial(fwd_kernel, blocks, images), grid_spec=p...  37.7 us
    convert_element_type x24, other arithmetic, add_low(): return (a.astype(f32) + b.astype(f32)).astype(bf16)  24.4 us
    unnamed x138, local copies, waits for them, and re-layouts  15.6 us
    pallas_call x4, Pallas kernels, spread(): pl.pallas_call(spread_kernel, grid_spec=pltpu.PrefetchScalarGridSpec(num_...  14.2 us
  transfers between devices with their start and end apart: 52, of which 22 were waited for; matrix products, arithmetic and copies ran while one was open for 23% of the time, Pallas kernels for 17%

profile of v2, /device:TPU:0, one launch (start us, length us, event | category | flops | bytes accessed | tf_op | source)
XLA Modules:
  0.0 677.4 jit_solution(13325043866415473912)
XLA Ops:
  21.4 5.2 collective-permute-start.7
  30.2 24.9 %collective-permute-done.7 = bf16[1,32,2048]{2,1,0:T(8,128)(2,1)S(1)} collective-permute-done((bf16[1,32,2048]{2,1,0:T(8,128)(2,1)S(1)}, bf16[1,32,2048]{2,1,0:T(8,128)(2,1)S(1)}, u32[]{:S(2)}, u32[]{:S(2)}) %collective-permute-start.7) | collective-permute-done | bytes 131104 | tf_op jit(solution)/shard_map/ppermute | solution.py:343
  55.2 13.5 %collective-permute-start.8 = (bf16[2,32,2048]{2,1,0:T(8,128)(2,1)S(1)}, bf16[2,32,2048]{2,1,0:T(8,128)(2,1)S(1)}, u32[]{:S(2)}, u32[]{:S(2)}) collective-permute-start(bf16[2,32,2048]{2,1,0:T(8,128)(2,1)S(1)} %pad_maximum_fusion.8), channel_id=1, source_target_pairs={{0,8},{1,9},{2,10},{3,11},{4,12},{5,13},{6,14},{7,15},{8,0},{9,1},... | collective-permute-start | bytes 786440 | tf_op jit(solution)/shard_map/ppermute | solution.py:343
  68.6 15.6 %collective-permute-done.3 = bf16[2,32,2304]{2,1,0:T(8,128)(2,1)S(1)} collective-permute-done((bf16[2,32,2304]{2,1,0:T(8,128)(2,1)S(1)}, bf16[2,32,2304]{2,1,0:T(8,128)(2,1)S(1)}, u32[]{:S(2)}, u32[]{:S(2)}) %collective-permute-start.3) | collective-permute-done | bytes 294944 | tf_op jit(solution)/shard_map/ppermute | solution.py:343
  87.2 19.4 %collective-permute-done.4 = bf16[4,32,2304]{2,1,0:T(8,128)(2,1)S(1)} collective-permute-done((bf16[4,32,2304]{2,1,0:T(8,128)(2,1)S(1)}, bf16[4,32,2304]{2,1,0:T(8,128)(2,1)S(1)}, u32[]{:S(2)}, u32[]{:S(2)}) %collective-permute-start.4) | collective-permute-done | bytes 589856 | tf_op jit(solution)/shard_map/ppermute | solution.py:343
  112.5 29.7 %collective-permute-done.5 = bf16[8,32,2304]{2,1,0:T(8,128)(2,1)S(1)} collective-permute-done((bf16[8,32,2304]{2,1,0:T(8,128)(2,1)S(1)}, bf16[8,32,2304]{2,1,0:T(8,128)(2,1)S(1)}, u32[]{:S(2)}, u32[]{:S(2)}) %collective-permute-start.5) | collective-permute-done | bytes 1179680 | tf_op jit(solution)/shard_map/ppermute | solution.py:343
  162.9 5.5 place_pieces.3
  168.5 6.1 place_pieces.2
  188.7 6.7 convolution_convert_fusion.k_ref
  195.4 8.0 %add_convert_fusion.v_ref = bf16[2176,1024]{1,0:T(8,128)(2,1)} fusion(bf16[2176,1024]{1,0:T(8,128)(2,1)S(1)} %fusion.5, f32[1024]{0:T(1024)S(1)} %get-tuple-element.103, bf16[1024,2304]{1,0:T(8,128)(2,1)} %place_pieces.2), kind=kOutput, calls=%fused_computation.8 | convolution fusion | flops 4567859200 | bytes 11014144 | tf_op jit(solution)/shard_map/dot_general | solution.py:546
  203.4 37.7 %attention_forward.1 = (bf16[1024,1024]{1,0:T(8,128)(2,1)}, f32[8,4,512]{2,1,0:T(4,128)}) custom-call(s32[3]{0:T(128)} %pad_add_fusion.img_ref, bf16[1024,1024]{1,0:T(8,128)(2,1)} %fusion.33.q_ref, bf16[2176,1024]{1,0:T(8,128)(2,1)} %convolution_convert_fusion.k_ref, bf16[2176,1024]{1,0:T(8,128)(2,1)} %add_convert_fusion.v_ref), custom_call_target="tpu_custom_call" | custom-call | flops 6304563200 | bytes 13107200 | tf_op jit(solution)/shard_map/attention_forward/pallas_call | solution.py:115
  241.0 4.7 fusion.67
  249.8 70.7 %feed_forward.1 = (bf16[1024,1024]{1,0:T(8,128)(2,1)}, f32[1024,1024]{1,0:T(8,128)}, f32[1,4096]{1,0:T(1,128)}, bf16[16,32,4096]{2,1,0:T(8,128)(2,1)}, bf16[16,3...) custom-call(s32[32]{0:T(128)} %broadcast_xor_fusion.1.table, ...), custom_call_target="tpu_custom_call" | custom-call | flops 51539607552 | bytes 62914560 | tf_op jit(solution)/shard_map/feed_forward/pallas_call | solution.py:305
  321.1 5.3 multiply_reduce_fusion
  343.9 5.7 collective-permute-start.41
  349.6 5.5 convolution_convert_fusion.4.g_ref
  355.1 7.0 %collective-permute-done.41 = bf16[8,32,1024]{2,1,0:T(8,128)(2,1)S(1)} collective-permute-done((bf16[8,32,1024]{2,1,0:T(8,128)(2,1)S(1)}, bf16[8,32,1024]{2,1,0:T(8,128)(2,1)S(1)}, u32[]{:S(2)}, u32[]{:S(2)}) %collective-permute-start.41) | collective-permute-done | bytes 524320 | tf_op jit(solution)/shard_map/ppermute | solution.py:343
  362.2 6.8 collective-permute-start.42
  369.0 5.0 add_convert_fusion.2
  378.4 26.3 %attention_backward.3 = (bf16[1024,512]{1,0:T(8,128)(2,1)}, f32[1024,512]{1,0:T(8,128)}, f32[1024,512]{1,0:T(8,128)}, bf16[2,576,512]{2,1,0:T(8,128)(2,1)}, bf16[2,576,512]{2,1,0:T(8,128)(2,1)}) custom-call(s32[3]{0:T(128)} %pad_add_fusion.img_ref, bf16[1024,1024]{1,0:T(8,128)(2,1)} %fusion.33.q_ref, bf16[2176,1024]{1,0:T(8,128)(2,1)} %convolution_convert_fusion.k_ref, ...), custom_call_target="tpu_custom_call" | custom-call | flops 7880704000 | bytes 17301504 | tf_op jit(solution)/shard_map/attention_backward/pallas_call | solution.py:196
  408.5 26.3 %attention_backward.2 = (bf16[1024,512]{1,0:T(8,128)(2,1)}, f32[1024,512]{1,0:T(8,128)}, f32[1024,512]{1,0:T(8,128)}, bf16[2,576,512]{2,1,0:T(8,128)(2,1)}, bf16[2,576,512]{2,1,0:T(8,128)(2,1)}) custom-call(s32[3]{0:T(128)} %pad_add_fusion.img_ref, bf16[1024,1024]{1,0:T(8,128)(2,1)} %fusion.33.q_ref, bf16[2176,1024]{1,0:T(8,128)(2,1)} %convolution_convert_fusion.k_ref, ...), custom_call_target="tpu_custom_call" | custom-call | flops 7880704000 | bytes 17301504 | tf_op jit(solution)/shard_map/attention_backward/pallas_call | solution.py:196
  449.3 15.8 %collective-permute-start.44 = (bf16[1,32,1024]{2,1,0:T(8,128)(2,1)}, bf16[1,32,1024]{2,1,0:T(8,128)(2,1)}, u32[]{:S(2)}, u32[]{:S(2)}) collective-permute-start(bf16[1,32,1024]{2,1,0:T(8,128)(2,1)} %add_convert_fusion.50), channel_id=1, source_target_pairs={{0,16},{1,17},{2,18},{3,19},{4,20},{5,21},{6,22},{7,23},{8,24},{9,... | collective-permute-start | bytes 196616 | tf_op jit(solution)/shard_map/ppermute | solution.py:343
  478.0 6.2 fusion.42
  484.2 36.0 %collective-permute-done.15 = bf16[8,128,1024]{2,1,0:T(8,128)(2,1)S(1)} collective-permute-done((bf16[8,128,1024]{2,1,0:T(8,128)(2,1)}, bf16[8,128,1024]{2,1,0:T(8,128)(2,1)S(1)}, u32[]{:S(2)}, u32[]{:S(2)}) %collective-permute-start.15) | collective-permute-done | bytes 2097184 | tf_op jit(solution)/shard_map/ppermute | solution.py:343
  525.7 7.6 %fusion.62 = (f32[1024]{0:T(1024)S(1)}, f32[1024]{0:T(1024)S(1)}, f32[1024]{0:T(1024)S(1)}, f32[1024,1024]{1,0:T(8,128)S(1)}) fusion(f32[1024]{0:T(1024)S(1)} %copy-done.39, f32[1024]{0:T(1024)S(1)} %copy-done.42, bf16[1024,1024]{1,0:T(8,128)(2,1)S(1)} %copy-done, f32[1024,1024]{1,0:T(8,128)} %fusion.42, bf16[1024,2048]{1,0:T(8,128)(2,1)S(1)} %copy-done.16, ...), kind=kOutput, calls=%fused_computation.226 | convolution fusion | flops 4321178624 | bytes 18894848 | tf_op jit(solution)/shard_map/tq,cq->tc/dot_general | solution.py:610
  547.7 7.6 %convolution_convert_fusion.2.whole = bf16[1024,1536]{1,0:T(8,128)(2,1)} fusion(bf16[1024,512]{1,0:T(8,128)(2,1)} %copy-done.20, bf16[1024,512]{1,0:T(8,128)(2,1)} %get-tuple-element.180, bf16[1024,512]{1,0:T(8,128)(2,1)} %get-tuple-element.63, bf16[2176,1024]{1,0:T(8,128)(2,1)} %copy-done.12), kind=kOutput, calls=%fused_computation.48 | convolution fusion | flops 3232235520 | bytes 8388608 | tf_op jit(solution)/shard_map/tc,tq->cq/dot_general | solution.py:597
  560.8 5.3 convolution_convert_fusion.1
  566.4 9.4 %collective-permute-start.24 = (f32[12,1024]{1,0:T(8,128)S(1)}, f32[12,1024]{1,0:T(8,128)S(1)}, u32[]{:S(2)}, u32[]{:S(2)}) collective-permute-start(f32[12,1024]{1,0:T(8,128)S(1)} %add.393), channel_id=1, source_target_pairs={{0,16},{1,17},{2,18},{3,19},{4,20},{5,21},{6,22},{7,23},{8,24},{9,... | collective-permute-start | bytes 147464 | tf_op jit(solution)/shard_map/ppermute | solution.py:343
  603.0 14.5 %collective-permute-done.31 = bf16[8,32,768]{2,1,0:T(8,128)(2,1)S(1)} collective-permute-done((bf16[8,32,768]{2,1,0:T(8,128)(2,1)S(1)}, bf16[8,32,768]{2,1,0:T(8,128)(2,1)S(1)}, u32[]{:S(2)}, u32[]{:S(2)}) %collective-permute-start.31) | collective-permute-done | bytes 393248 | tf_op jit(solution)/shard_map/ppermute | solution.py:343
  626.7 7.0 %collective-permute-start.39 = (bf16[1,32,768]{2,1,0:T(8,128)(2,1)S(1)}, bf16[1,32,768]{2,1,0:T(8,128)(2,1)S(1)}, u32[]{:S(2)}, u32[]{:S(2)}) collective-permute-start(bf16[1,32,768]{2,1,0:T(8,128)(2,1)S(1)} %add_convert_fusion.52), channel_id=1, source_target_pairs={{0,16},{1,17},{2,18},{3,19},{4,20},{5,21},{6,22},{7,23},{8,24},{9,... | collective-permute-start | bytes 147464 | tf_op jit(solution)/shard_map/ppermute | solution.py:343
  636.7 10.1 %collective-permute-done.34 = bf16[1,32,768]{2,1,0:T(8,128)(2,1)S(1)} collective-permute-done((bf16[1,32,768]{2,1,0:T(8,128)(2,1)S(1)}, bf16[1,32,768]{2,1,0:T(8,128)(2,1)S(1)}, u32[]{:S(2)}, u32[]{:S(2)}) %collective-permute-start.34) | collective-permute-done | bytes 49184 | tf_op jit(solution)/shard_map/ppermute | solution.py:343
  650.2 11.6 %collective-permute-done.47 = bf16[1,32,4096]{2,1,0:T(8,128)(2,1)S(1)} collective-permute-done((bf16[1,32,4096]{2,1,0:T(8,128)(2,1)S(1)}, bf16[1,32,4096]{2,1,0:T(8,128)(2,1)S(1)}, u32[]{:S(2)}, u32[]{:S(2)}) %collective-permute-start.47) | collective-permute-done | bytes 262176 | tf_op jit(solution)/shard_map/ppermute | solution.py:343
  (357 shorter events, 190.4 us)
Async XLA Ops:
  7.3 242.5 %all-gather.2.cloned.1.call-start = ((), (), s32[]{:S(2)}) async-start(), calls=%async_computation | async-start | bytes 17301504 | tf_op jit(solution)/shard_map/all_gather | solution.py:528
  18.6 139.1 %collective-permute-start = (bf16[576,1024]{1,0:T(8,128)(2,1)}, bf16[576,1024]{1,0:T(8,128)(2,1)S(1)}, u32[]{:S(2)}, u32[]{:S(2)}) collective-permute-start(bf16[576,1024]{1,0:T(8,128)(2,1)} %get-tuple-element.142), channel_id=1, source_target_pairs={{0,1},{1,2},{2,3},{3,4},{4,5},{5,6},{6,7},{7,8},{8,9},{9,10},{10,1... | collective-permute-start | bytes 3538952 | tf_op jit(solution)/shard_map/ppermute | solution.py:514
  20.1 137.6 %collective-permute-start.1 = (bf16[576,1024]{1,0:T(8,128)(2,1)}, bf16[576,1024]{1,0:T(8,128)(2,1)}, u32[]{:S(2)}, u32[]{:S(2)}) collective-permute-start(bf16[576,1024]{1,0:T(8,128)(2,1)} %get-tuple-element.143), channel_id=1, source_target_pairs={{1,0},{2,1},{3,2},{4,3},{5,4},{6,5},{7,6},{8,7},{9,8},{10,9},{11,1... | collective-permute-start | bytes 3538952 | tf_op jit(solution)/shard_map/ppermute | solution.py:514
  21.4 33.7 %collective-permute-start.7 = (bf16[1,32,2048]{2,1,0:T(8,128)(2,1)S(1)}, bf16[1,32,2048]{2,1,0:T(8,128)(2,1)S(1)}, u32[]{:S(2)}, u32[]{:S(2)}) collective-permute-start(bf16[1,32,2048]{2,1,0:T(8,128)(2,1)S(1)} %slice_bitcast_fusion.8), channel_id=1, source_target_pairs={{0,16},{1,17},{2,18},{3,19},{4,20},{5,21},{6,22},{7,23},{8,24},{9,... | collective-permute-start | bytes 393224 | tf_op jit(solution)/shard_map/ppermute | solution.py:343
  27.3 57.0 %collective-permute-start.3 = (bf16[2,32,2304]{2,1,0:T(8,128)(2,1)S(1)}, bf16[2,32,2304]{2,1,0:T(8,128)(2,1)S(1)}, u32[]{:S(2)}, u32[]{:S(2)}) collective-permute-start(bf16[2,32,2304]{2,1,0:T(8,128)(2,1)S(1)} %pad_maximum_fusion.7), channel_id=1, source_target_pairs={{0,8},{1,9},{2,10},{3,11},{4,12},{5,13},{6,14},{7,15},{8,0},{9,1},... | collective-permute-start | bytes 884744 | tf_op jit(solution)/shard_map/ppermute | solution.py:343
  55.2 31.9 %collective-permute-start.8 = (bf16[2,32,2048]{2,1,0:T(8,128)(2,1)S(1)}, bf16[2,32,2048]{2,1,0:T(8,128)(2,1)S(1)}, u32[]{:S(2)}, u32[]{:S(2)}) collective-permute-start(bf16[2,32,2048]{2,1,0:T(8,128)(2,1)S(1)} %pad_maximum_fusion.8), channel_id=1, source_target_pairs={{0,8},{1,9},{2,10},{3,11},{4,12},{5,13},{6,14},{7,15},{8,0},{9,1},... | collective-permute-start | bytes 786440 | tf_op jit(solution)/shard_map/ppermute | solution.py:343
  84.3 22.2 %collective-permute-start.4 = (bf16[4,32,2304]{2,1,0:T(8,128)(2,1)S(1)}, bf16[4,32,2304]{2,1,0:T(8,128)(2,1)S(1)}, u32[]{:S(2)}, u32[]{:S(2)}) collective-permute-start(bf16[4,32,2304]{2,1,0:T(8,128)(2,1)S(1)} %pad_maximum_fusion.5), channel_id=1, source_target_pairs={{0,4},{1,5},{2,6},{3,7},{4,0},{5,1},{6,2},{7,3},{8,12},{9,13},{10,... | collective-permute-start | bytes 1769480 | tf_op jit(solution)/shard_map/ppermute | solution.py:343
  87.1 21.1 %collective-permute-start.9 = (bf16[4,32,2048]{2,1,0:T(8,128)(2,1)S(1)}, bf16[4,32,2048]{2,1,0:T(8,128)(2,1)S(1)}, u32[]{:S(2)}, u32[]{:S(2)}) collective-permute-start(bf16[4,32,2048]{2,1,0:T(8,128)(2,1)S(1)} %pad_maximum_fusion.6), channel_id=1, source_target_pairs={{0,2},{1,3},{2,0},{3,1},{4,6},{5,7},{6,4},{7,5},{8,10},{9,11},{10,... | collective-permute-start | bytes 1572872 | tf_op jit(solution)/shard_map/ppermute | solution.py:343
  106.7 35.5 %collective-permute-start.5 = (bf16[8,32,2304]{2,1,0:T(8,128)(2,1)S(1)}, bf16[8,32,2304]{2,1,0:T(8,128)(2,1)S(1)}, u32[]{:S(2)}, u32[]{:S(2)}) collective-permute-start(bf16[8,32,2304]{2,1,0:T(8,128)(2,1)S(1)} %pad_maximum_fusion.3), channel_id=1, source_target_pairs={{0,2},{1,3},{2,0},{3,1},{4,6},{5,7},{6,4},{7,5},{8,10},{9,11},{10,... | collective-permute-start | bytes 3538952 | tf_op jit(solution)/shard_map/ppermute | solution.py:343
  108.4 38.2 %collective-permute-start.10 = (bf16[8,32,2048]{2,1,0:T(8,128)(2,1)S(1)}, bf16[8,32,2048]{2,1,0:T(8,128)(2,1)S(1)}, u32[]{:S(2)}, u32[]{:S(2)}) collective-permute-start(bf16[8,32,2048]{2,1,0:T(8,128)(2,1)S(1)} %pad_maximum_fusion.4), channel_id=1, source_target_pairs={{0,4},{1,5},{2,6},{3,7},{4,0},{5,1},{6,2},{7,3},{8,12},{9,13},{10,... | collective-permute-start | bytes 3145736 | tf_op jit(solution)/shard_map/ppermute | solution.py:343
  143.3 25.2 %collective-permute-start.6 = (bf16[16,32,2304]{2,1,0:T(8,128)(2,1)}, bf16[16,32,2304]{2,1,0:T(8,128)(2,1)}, u32[]{:S(2)}, u32[]{:S(2)}) collective-permute-start(bf16[16,32,2304]{2,1,0:T(8,128)(2,1)} %constant_dynamic-update-slice_fusion.near), channel_id=1, source_target_pairs={{0,1},{1,0},{2,3},{3,2},{4,5},{5,4},{6,7},{7,6},{8,9},{9,8},{10,11... | collective-permute-start | bytes 7077896 | tf_op jit(solution)/shard_map/ppermute | solution.py:343
  320.5 48.5 %collective-permute-start.13 = (bf16[16,128,1024]{2,1,0:T(8,128)(2,1)}, bf16[16,128,1024]{2,1,0:T(8,128)(2,1)}, u32[]{:S(2)}, u32[]{:S(2)}) collective-permute-start(bf16[16,128,1024]{2,1,0:T(8,128)(2,1)} %get-tuple-element.60), channel_id=1, source_target_pairs={{0,1},{1,0},{2,3},{3,2},{4,5},{5,4},{6,7},{7,6},{8,9},{9,8},{10,11... | collective-permute-start | bytes 12582920 | tf_op jit(solution)/shard_map/ppermute | solution.py:343
  320.8 53.2 %collective-permute-start.12 = (bf16[16,32,4096]{2,1,0:T(8,128)(2,1)}, bf16[16,32,4096]{2,1,0:T(8,128)(2,1)}, u32[]{:S(2)}, u32[]{:S(2)}) collective-permute-start(bf16[16,32,4096]{2,1,0:T(8,128)(2,1)} %get-tuple-element.58), channel_id=1, source_target_pairs={{0,1},{1,0},{2,3},{3,2},{4,5},{5,4},{6,7},{7,6},{8,9},{9,8},{10,11... | collective-permute-start | bytes 12582920 | tf_op jit(solution)/shard_map/ppermute | solution.py:343
  343.9 18.1 %collective-permute-start.41 = (bf16[8,32,1024]{2,1,0:T(8,128)(2,1)S(1)}, bf16[8,32,1024]{2,1,0:T(8,128)(2,1)S(1)}, u32[]{:S(2)}, u32[]{:S(2)}) collective-permute-start(bf16[8,32,1024]{2,1,0:T(8,128)(2,1)S(1)} %get-tuple-element.139), channel_id=1, source_target_pairs={{0,2},{1,3},{2,0},{3,1},{4,6},{5,7},{6,4},{7,5},{8,10},{9,11},{10,... | collective-permute-start | bytes 1572872 | tf_op jit(solution)/shard_map/ppermute | solution.py:343
  362.2 77.2 %collective-permute-start.42 = (bf16[4,32,1024]{2,1,0:T(8,128)(2,1)S(1)}, bf16[4,32,1024]{2,1,0:T(8,128)(2,1)S(1)}, u32[]{:S(2)}, u32[]{:S(2)}) collective-permute-start(bf16[4,32,1024]{2,1,0:T(8,128)(2,1)S(1)} %get-tuple-element.151), channel_id=1, source_target_pairs={{0,4},{1,5},{2,6},{3,7},{4,0},{5,1},{6,2},{7,3},{8,12},{9,13},{10,... | collective-permute-start | bytes 786440 | tf_op jit(solution)/shard_map/ppermute | solution.py:343
  404.7 60.3 %collective-permute-start.18 = (bf16[2,576,512]{2,1,0:T(8,128)(2,1)}, bf16[2,576,512]{2,1,0:T(8,128)(2,1)}, u32[]{:S(2)}, u32[]{:S(2)}) collective-permute-start(bf16[2,576,512]{2,1,0:T(8,128)(2,1)} %get-tuple-element.74), channel_id=1, source_target_pairs={{0,1},{1,2},{2,3},{3,4},{4,5},{5,6},{6,7},{7,8},{8,9},{9,10},{10,1... | collective-permute-start | bytes 3538952 | tf_op jit(solution)/shard_map/ppermute | solution.py:589
  407.1 59.6 %collective-permute-start.19 = (bf16[2,576,512]{2,1,0:T(8,128)(2,1)}, bf16[2,576,512]{2,1,0:T(8,128)(2,1)S(1)}, u32[]{:S(2)}, u32[]{:S(2)}) collective-permute-start(bf16[2,576,512]{2,1,0:T(8,128)(2,1)} %get-tuple-element.75), channel_id=1, source_target_pairs={{1,0},{2,1},{3,2},{4,3},{5,4},{6,5},{7,6},{8,7},{9,8},{10,9},{11,1... | collective-permute-start | bytes 3538952 | tf_op jit(solution)/shard_map/ppermute | solution.py:590
  434.8 32.7 %collective-permute-start.16 = (bf16[2,576,512]{2,1,0:T(8,128)(2,1)}, bf16[2,576,512]{2,1,0:T(8,128)(2,1)}, u32[]{:S(2)}, u32[]{:S(2)}) collective-permute-start(bf16[2,576,512]{2,1,0:T(8,128)(2,1)} %get-tuple-element.71), channel_id=1, source_target_pairs={{0,1},{1,2},{2,3},{3,4},{4,5},{5,6},{6,7},{7,8},{8,9},{9,10},{10,1... | collective-permute-start | bytes 3538952 | tf_op jit(solution)/shard_map/ppermute | solution.py:589
  444.2 25.1 %collective-permute-start.17 = (bf16[2,576,512]{2,1,0:T(8,128)(2,1)}, bf16[2,576,512]{2,1,0:T(8,128)(2,1)}, u32[]{:S(2)}, u32[]{:S(2)}) collective-permute-start(bf16[2,576,512]{2,1,0:T(8,128)(2,1)} %get-tuple-element.72), channel_id=1, source_target_pairs={{1,0},{2,1},{3,2},{4,3},{5,4},{6,5},{7,6},{8,7},{9,8},{10,9},{11,1... | collective-permute-start | bytes 3538952 | tf_op jit(solution)/shard_map/ppermute | solution.py:590
  449.3 92.0 %collective-permute-start.44 = (bf16[1,32,1024]{2,1,0:T(8,128)(2,1)}, bf16[1,32,1024]{2,1,0:T(8,128)(2,1)}, u32[]{:S(2)}, u32[]{:S(2)}) collective-permute-start(bf16[1,32,1024]{2,1,0:T(8,128)(2,1)} %add_convert_fusion.50), channel_id=1, source_target_pairs={{0,16},{1,17},{2,18},{3,19},{4,20},{5,21},{6,22},{7,23},{8,24},{9,... | collective-permute-start | bytes 196616 | tf_op jit(solution)/shard_map/ppermute | solution.py:343
  465.1 55.1 %collective-permute-start.15 = (bf16[8,128,1024]{2,1,0:T(8,128)(2,1)}, bf16[8,128,1024]{2,1,0:T(8,128)(2,1)S(1)}, u32[]{:S(2)}, u32[]{:S(2)}) collective-permute-start(bf16[8,128,1024]{2,1,0:T(8,128)(2,1)} %get-tuple-element.68), channel_id=1, source_target_pairs={{0,2},{1,3},{2,0},{3,1},{4,6},{5,7},{6,4},{7,5},{8,10},{9,11},{10,... | collective-permute-start | bytes 6291464 | tf_op jit(solution)/shard_map/ppermute | solution.py:343
  466.7 55.9 %collective-permute-start.14 = (bf16[8,32,4096]{2,1,0:T(8,128)(2,1)S(1)}, bf16[8,32,4096]{2,1,0:T(8,128)(2,1)S(1)}, u32[]{:S(2)}, u32[]{:S(2)}) collective-permute-start(bf16[8,32,4096]{2,1,0:T(8,128)(2,1)S(1)} %copy-done.23), channel_id=1, source_target_pairs={{0,4},{1,5},{2,6},{3,7},{4,0},{5,1},{6,2},{7,3},{8,12},{9,13},{10,... | collective-permute-start | bytes 6291464 | tf_op jit(solution)/shard_map/ppermute | solution.py:343
  559.6 26.6 %collective-permute-start.25 = (bf16[16,32,1536]{2,1,0:T(8,128)(2,1)}, bf16[16,32,1536]{2,1,0:T(8,128)(2,1)}, u32[]{:S(2)}, u32[]{:S(2)}) collective-permute-start(bf16[16,32,1536]{2,1,0:T(8,128)(2,1)} %get-tuple-element.80), channel_id=1, source_target_pairs={{0,1},{1,0},{2,3},{3,2},{4,5},{5,4},{6,7},{7,6},{8,9},{9,8},{10,11... | collective-permute-start | bytes 4718600 | tf_op jit(solution)/shard_map/ppermute | solution.py:343
  566.1 26.2 %collective-permute-start.48 = (bf16[4,128,1024]{2,1,0:T(8,128)(2,1)}, bf16[4,128,1024]{2,1,0:T(8,128)(2,1)}, u32[]{:S(2)}, u32[]{:S(2)}) collective-permute-start(bf16[4,128,1024]{2,1,0:T(8,128)(2,1)} %get-tuple-element.90), channel_id=1, source_target_pairs={{0,4},{1,5},{2,6},{3,7},{4,0},{5,1},{6,2},{7,3},{8,12},{9,13},{10,... | collective-permute-start | bytes 3145736 | tf_op jit(solution)/shard_map/ppermute | solution.py:343
  566.4 29.6 %collective-permute-start.45 = (bf16[4,32,4096]{2,1,0:T(8,128)(2,1)}, bf16[4,32,4096]{2,1,0:T(8,128)(2,1)}, u32[]{:S(2)}, u32[]{:S(2)}) collective-permute-start(bf16[4,32,4096]{2,1,0:T(8,128)(2,1)} %get-tuple-element.88), channel_id=1, source_target_pairs={{0,2},{1,3},{2,0},{3,1},{4,6},{5,7},{6,4},{7,5},{8,10},{9,11},{10,... | collective-permute-start | bytes 3145736 | tf_op jit(solution)/shard_map/ppermute | solution.py:343
  566.4 18.0 %collective-permute-start.24 = (f32[12,1024]{1,0:T(8,128)S(1)}, f32[12,1024]{1,0:T(8,128)S(1)}, u32[]{:S(2)}, u32[]{:S(2)}) collective-permute-start(f32[12,1024]{1,0:T(8,128)S(1)} %add.393), channel_id=1, source_target_pairs={{0,16},{1,17},{2,18},{3,19},{4,20},{5,21},{6,22},{7,23},{8,24},{9,... | collective-permute-start | bytes 147464 | tf_op jit(solution)/shard_map/ppermute | solution.py:343
  588.5 36.9 %collective-permute-start.26 = (bf16[8,32,1536]{2,1,0:T(8,128)(2,1)S(1)}, bf16[8,32,1536]{2,1,0:T(8,128)(2,1)S(1)}, u32[]{:S(2)}, u32[]{:S(2)}) collective-permute-start(bf16[8,32,1536]{2,1,0:T(8,128)(2,1)S(1)} %get-tuple-element.125), channel_id=1, source_target_pairs={{0,4},{1,5},{2,6},{3,7},{4,0},{5,1},{6,2},{7,3},{8,12},{9,13},{10,... | collective-permute-start | bytes 2359304 | tf_op jit(solution)/shard_map/ppermute | solution.py:343
  590.5 26.9 %collective-permute-start.31 = (bf16[8,32,768]{2,1,0:T(8,128)(2,1)S(1)}, bf16[8,32,768]{2,1,0:T(8,128)(2,1)S(1)}, u32[]{:S(2)}, u32[]{:S(2)}) collective-permute-start(bf16[8,32,768]{2,1,0:T(8,128)(2,1)S(1)} %get-tuple-element.147), channel_id=1, source_target_pairs={{0,4},{1,5},{2,6},{3,7},{4,0},{5,1},{6,2},{7,3},{8,12},{9,13},{10,... | collective-permute-start | bytes 1179656 | tf_op jit(solution)/shard_map/ppermute | solution.py:343
  593.9 52.9 %collective-permute-start.49 = (bf16[2,128,1024]{2,1,0:T(8,128)(2,1)S(1)}, bf16[2,128,1024]{2,1,0:T(8,128)(2,1)S(1)}, u32[]{:S(2)}, u32[]{:S(2)}) collective-permute-start(bf16[2,128,1024]{2,1,0:T(8,128)(2,1)S(1)} %get-tuple-element.135), channel_id=1, source_target_pairs={{0,8},{1,9},{2,10},{3,11},{4,12},{5,13},{6,14},{7,15},{8,0},{9,1},... | collective-permute-start | bytes 1572872 | tf_op jit(solution)/shard_map/ppermute | solution.py:343
  597.4 49.5 %collective-permute-start.46 = (bf16[2,32,4096]{2,1,0:T(8,128)(2,1)S(1)}, bf16[2,32,4096]{2,1,0:T(8,128)(2,1)S(1)}, u32[]{:S(2)}, u32[]{:S(2)}) collective-permute-start(bf16[2,32,4096]{2,1,0:T(8,128)(2,1)S(1)} %get-tuple-element.137), channel_id=1, source_target_pairs={{0,8},{1,9},{2,10},{3,11},{4,12},{5,13},{6,14},{7,15},{8,0},{9,1},... | collective-permute-start | bytes 1572872 | tf_op jit(solution)/shard_map/ppermute | solution.py:343
  601.2 19.9 %collective-permute-start.37 = (bf16[4,32,768]{2,1,0:T(8,128)(2,1)S(1)}, bf16[4,32,768]{2,1,0:T(8,128)(2,1)S(1)}, u32[]{:S(2)}, u32[]{:S(2)}) collective-permute-start(bf16[4,32,768]{2,1,0:T(8,128)(2,1)S(1)} %get-tuple-element.153), channel_id=1, source_target_pairs={{0,4},{1,5},{2,6},{3,7},{4,0},{5,1},{6,2},{7,3},{8,12},{9,13},{10,... | collective-permute-start | bytes 589832 | tf_op jit(solution)/shard_map/ppermute | solution.py:343
  625.6 24.4 %collective-permute-start.27 = (bf16[4,32,1536]{2,1,0:T(8,128)(2,1)S(1)}, bf16[4,32,1536]{2,1,0:T(8,128)(2,1)S(1)}, u32[]{:S(2)}, u32[]{:S(2)}) collective-permute-start(bf16[4,32,1536]{2,1,0:T(8,128)(2,1)S(1)} %get-tuple-element.149), channel_id=1, source_target_pairs={{0,2},{1,3},{2,0},{3,1},{4,6},{5,7},{6,4},{7,5},{8,10},{9,11},{10,... | collective-permute-start | bytes 1179656 | tf_op jit(solution)/shard_map/ppermute | solution.py:343
  (81 other events, 687.8 us)
Sparse Core Ops, SparseCore 0:
  11.6 162.6 all-gather.1

commit v3 on v2

v3 whole, which is shorter than its diff:
```python
import functools
import math

import jax
import jax.numpy as jnp
from jax import lax
from jax.experimental import pallas as pl
from jax.experimental.pallas import tpu as pltpu
from jax.sharding import PartitionSpec as P

IMG = 577
REACH = IMG - 1
HEAD = 64
SPAN = 592
LANES = 128
QB = 256
PP = 2
PIECES = 32
PACE = 1.0e5
FEED_AFTER = 2
GROUPS = 2
VMEM = 60 * 1024 * 1024
f32 = jnp.float32
bf16 = jnp.bfloat16

norm_epsilon = 1e-06


def spent(us):
    return pl.CostEstimate(flops=0, bytes_accessed=int(us * PACE), transcendentals=0)


def make_items(img_ref, items_ref, blocks, images):
    count = jnp.int32(0)
    for b in range(blocks):
        for i in range(images):
            start = img_ref[i]
            low = b * QB + REACH
            hit = (start < low + QB) & (start + IMG > low)

            @pl.when(hit)
            def _():
                items_ref[count] = b * 8 + i

            count = count + hit.astype(jnp.int32)
    return count

def item_scalars(img_ref, items_ref, n):
    code = items_ref[n]
    b = code // 8
    start = img_ref[code % 8]
    begin = pl.multiple_of((start // 16) * 16, 16)
    row = pl.multiple_of(b * QB, QB)
    return b, start, begin, row

def halves(x):
    lane = lax.broadcasted_iota(jnp.int32, x.shape, 1)
    zero = jnp.zeros_like(x)
    return jnp.concatenate([jnp.where(lane < HEAD, x, zero), jnp.where(lane >= HEAD, x, zero)], axis=0)

def key_valid(start, begin):
    r = lax.broadcasted_iota(jnp.int32, (SPAN, 1), 0) + (begin - start)
    return (r >= 0) & (r < IMG)

def query_valid(start, row):
    lane = lax.broadcasted_iota(jnp.int32, (1, 2 * QB), 1)
    pos = jnp.where(lane < QB, lane, lane - QB) + (row + REACH - start)
    return (pos >= 0) & (pos < IMG)

def pad_rows(img_ref, images, rows):
    r = lax.broadcasted_iota(jnp.int32, (rows, LANES), 0) + REACH
    inside = jnp.zeros((rows, LANES), jnp.bool_)
    for i in range(images):
        start = img_ref[i]
        inside = inside | ((r >= start) & (r < start + IMG))
    return ~inside

def fwd_kernel(blocks, images, img_ref, q_ref, k_ref, v_ref, o_ref, lse_ref, acc, items):
    rows = blocks * QB
    count = make_items(img_ref, items, blocks, images)
    acc[...] = jnp.zeros_like(acc)
    lse_ref[...] = jnp.zeros_like(lse_ref)

    def body(n, carry):
        b, start, begin, row = item_scalars(img_ref, items, n)
        valid = key_valid(start, begin)
        qm = query_valid(start, row)
        done = []
        for u in range(PP):
            cols = slice(u * LANES, (u + 1) * LANES)
            q2 = halves(q_ref[pl.ds(pl.multiple_of(row + REACH, 16), QB), cols])
            kw = k_ref[pl.ds(begin, SPAN), cols]
            vw = v_ref[pl.ds(begin, SPAN), cols]
            s = lax.dot_general(kw, q2, (((1,), (1,)), ((), ())), preferred_element_type=f32)
            s = jnp.where(valid, s, -1e30)
            m = jnp.max(s, axis=0, keepdims=True)
            e = jnp.exp(s - m)
            l = jnp.sum(e, axis=0, keepdims=True)
            p = (e * jnp.where(qm, 1.0 / l, 0.0)).astype(bf16)
            ot = lax.dot_general(vw, p, (((0,), (0,)), ((), ())), preferred_element_type=f32)
            done.append((jnp.concatenate([ot[:HEAD, :QB], ot[HEAD:, QB:]], axis=0).T, m + jnp.log(l)))
        for u in range(PP):
            cols = slice(u * LANES, (u + 1) * LANES)
            o, total = done[u]
            acc[pl.ds(row, QB), cols] += o
            old = lse_ref[u, pl.ds(b, 1), :]
            lse_ref[u, pl.ds(b, 1), :] = jnp.where(qm, total, old)
        return carry

    lax.fori_loop(0, count, body, 0)
    pad = pad_rows(img_ref, images, rows)
    for u in range(PP):
        cols = slice(u * LANES, (u + 1) * LANES)
        own = v_ref[pl.ds(REACH, rows), cols].astype(f32)
        o_ref[:, cols] = jnp.where(pad, own, acc[:, cols]).astype(bf16)

def attention_forward(img, q, k, v, first, pairs):
    win = k.shape[0]
    rows = win - 2 * REACH
    blocks = rows // QB
    images = img.shape[0]
    spec = lambda r: pl.BlockSpec((r, PP * LANES), lambda p, *_: (0, first // PP + p))
    return pl.pallas_call(
        functools.partial(fwd_kernel, blocks, images),
        grid_spec=pltpu.PrefetchScalarGridSpec(
            num_scalar_prefetch=1,
            grid=(pairs // PP,),
            in_specs=[spec(win), spec(win), spec(win)],
            out_specs=[
                pl.BlockSpec((rows, PP * LANES), lambda p, *_: (0, p)),
                pl.BlockSpec((PP, blocks, 2 * QB), lambda p, *_: (p, 0, 0)),
            ],
            scratch_shapes=[pltpu.VMEM((rows, PP * LANES), f32), pltpu.SMEM((blocks * images,), jnp.int32)],
        ),
        out_shape=[
            jax.ShapeDtypeStruct((rows, pairs * LANES), bf16),
            jax.ShapeDtypeStruct((pairs, blocks, 2 * QB), f32),
        ],
        compiler_params=pltpu.CompilerParams(vmem_limit_bytes=VMEM, dimension_semantics=("arbitrary",)),
        cost_estimate=spent(5 * pairs),
        name="attention_forward",
    )(img, q, k, v)

def bwd_kernel(blocks, images, img_ref, q_ref, k_ref, v_ref, g_ref, lse_ref,
               dq_ref, dk_ref, dv_ref, left_ref, right_ref, dq_acc, dk_acc, dv_acc, items):
    rows = blocks * QB
    count = make_items(img_ref, items, blocks, images)
    dq_acc[...] = jnp.zeros_like(dq_acc)
    dk_acc[...] = jnp.zeros_like(dk_acc)
    dv_acc[...] = jnp.zeros_like(dv_acc)

    def body(n, carry):
        b, start, begin, row = item_scalars(img_ref, items, n)
        valid = key_valid(start, begin)
        qm = query_valid(start, row)
        done = []
        for u in range(PP):
            cols = slice(u * LANES, (u + 1) * LANES)
            q2 = halves(q_ref[pl.ds(pl.multiple_of(row + REACH, 16), QB), cols])
            g2 = halves(g_ref[pl.ds(row, QB), cols])
            kw = k_ref[pl.ds(begin, SPAN), cols]
            vw = v_ref[pl.ds(begin, SPAN), cols]
            lse = jnp.where(qm, lse_ref[u, pl.ds(b, 1), :], 1e30)
            s = lax.dot_general(kw, q2, (((1,), (1,)), ((), ())), preferred_element_type=f32)
            dp = lax.dot_general(vw, g2, (((1,), (1,)), ((), ())), preferred_element_type=f32)
            p = jnp.exp(jnp.where(valid, s, -1e30) - lse)
            inner = jnp.sum(p * dp, axis=0, keepdims=True)
            ds = (p * (dp - inner)).astype(bf16)
            dv = jnp.dot(p.astype(bf16), g2, preferred_element_type=f32)
            dk = jnp.dot(ds, q2, preferred_element_type=f32)
            dqt = lax.dot_general(kw, ds, (((0,), (0,)), ((), ())), preferred_element_type=f32)
            done.append((dv, dk, jnp.concatenate([dqt[:HEAD, :QB], dqt[HEAD:, QB:]], axis=0).T))
        for u in range(PP):
            cols = slice(u * LANES, (u + 1) * LANES)
            dv, dk, dq = done[u]
            dv_acc[pl.ds(begin, SPAN), cols] += dv
            dk_acc[pl.ds(begin, SPAN), cols] += dk
            dq_acc[pl.ds(row, QB), cols] += dq
        return carry

    lax.fori_loop(0, count, body, 0)
    pad = pad_rows(img_ref, images, rows)
    dq_ref[...] = (dq_acc[...] * 0.125).astype(bf16)
    dk_ref[...] = dk_acc[pl.ds(REACH, rows), :]
    for u in range(PP):
        cols = slice(u * LANES, (u + 1) * LANES)
        dv_ref[:, cols] = dv_acc[pl.ds(REACH, rows), cols] + jnp.where(pad, g_ref[:, cols].astype(f32), 0.0)
    left_ref[0] = dk_acc[pl.ds(0, REACH), :].astype(bf16)
    left_ref[1] = dv_acc[pl.ds(0, REACH), :].astype(bf16)
    right_ref[0] = dk_acc[pl.ds(REACH + rows, REACH), :].astype(bf16)
    right_ref[1] = dv_acc[pl.ds(REACH + rows, REACH), :].astype(bf16)

def attention_backward(img, q, k, v, g, lse, first, pairs):
    win = k.shape[0]
    rows = win - 2 * REACH
    blocks = rows // QB
    images = img.shape[0]
    C = PP * LANES
    spec = lambda r: pl.BlockSpec((r, C), lambda p, *_: (0, first // PP + p))
    out = lambda r: pl.BlockSpec((r, C), lambda p, *_: (0, p))
    edge = pl.BlockSpec((2, REACH, C), lambda p, *_: (0, 0, p))
    sds = jax.ShapeDtypeStruct
    cols = pairs * LANES
    return pl.pallas_call(
        functools.partial(bwd_kernel, blocks, images),
        grid_spec=pltpu.PrefetchScalarGridSpec(
            num_scalar_prefetch=1,
            grid=(pairs // PP,),
            in_specs=[spec(win), spec(win), spec(win), spec(rows),
                      pl.BlockSpec((PP, blocks, 2 * QB), lambda p, *_: (first // PP + p, 0, 0))],
            out_specs=[out(rows), out(rows), out(rows), edge, edge],
            scratch_shapes=[pltpu.VMEM((rows, C), f32), pltpu.VMEM((win, C), f32), pltpu.VMEM((win, C), f32),
                            pltpu.SMEM((blocks * images,), jnp.int32)],
        ),
        out_shape=[sds((rows, cols), bf16), sds((rows, cols), f32), sds((rows, cols), f32),
                   sds((2, REACH, cols), bf16), sds((2, REACH, cols), bf16)],
        compiler_params=pltpu.CompilerParams(vmem_limit_bytes=VMEM, dimension_semantics=("arbitrary",)),
        cost_estimate=spent(6.5 * pairs),
        name="attention_backward",
    )(img, q, k, v, g, lse)


FT = 512
ROWS = 256


def contract(a, b, dims):
    return lax.dot_general(a, b, (dims, ((), ())), preferred_element_type=f32)


def feed_kernel(
    table, home, normed, cot, middle, bias_final, wide, tall, bias_hidden,
    result, grad_normed, bias_grad, hidden_near, hidden_far, final_near, final_far,
    total, normed_t, final, active, grad_pre, hidden_grad, final_grad, sems,
):
    step = pl.program_id(0)
    tiles = pl.num_programs(0)
    slot = lax.rem(step, 2)
    rows, width = normed.shape
    half, piece, _ = hidden_near.shape
    devices = tall.shape[0] // 32
    depth = FT // devices

    @pl.when(step == 0)
    def _():
        total[...] = middle[...] + bias_final[...]
        grad_normed[...] = jnp.zeros_like(grad_normed)
        normed_t[...] = normed[...].T

    for d in range(devices):
        for i in range(4):
            final[d * depth + i * 32 : d * depth + (i + 1) * 32, :] = tall[d * 32 : (d + 1) * 32, i * width : (i + 1) * width]
    for r in range(0, rows, ROWS):
        cut = slice(r, r + ROWS)
        pre = contract(normed[cut, :], wide[...], ((1,), (0,))) + bias_hidden[...]
        grad = contract(cot[cut, :], final[...], ((1,), (1,)))
        phi = 0.5 + 0.5 * lax.erf(pre * (0.5**0.5))
        slope = phi + pre * jnp.exp(pre * pre * -0.5) * ((0.5 / math.pi) ** 0.5)
        active[cut, :] = (pre * phi).astype(bf16)
        grad_pre[cut, :] = (grad * slope).astype(bf16)
        total[cut, :] += contract(active[cut, :], final[...], ((1,), (0,)))
        grad_normed[cut, :] += contract(grad_pre[cut, :], wide[...], ((1,), (1,)))
    bias_grad[...] = jnp.sum(grad_pre[...].astype(f32), axis=0, keepdims=True)
    hidden_grad[...] = contract(normed_t[...], grad_pre[...], ((1,), (0,)))
    for place in range(2 * half):
        rows_of = hidden_grad[pl.ds(pl.multiple_of(table[place] * piece, piece), piece), :].astype(bf16)
        if place < half:
            hidden_near[place] = rows_of
        else:
            hidden_far[place - half] = rows_of

    def copy_out(slot, d, target):
        return pltpu.make_async_copy(final_grad.at[slot, d], target, sems.at[slot, d])

    def wait_out(slot):
        for d in range(devices):
            copy_out(slot, d, final_near.at[0]).wait()

    @pl.when(step >= 2)
    def _():
        wait_out(slot)

    final_grad[slot] = contract(active[...], cot[...], ((0,), (0,))).astype(bf16).reshape(devices, depth, width)
    for d in range(devices):
        at = home[step * devices + d]

        @pl.when(at < half)
        def _():
            copy_out(slot, d, final_near.at[at]).start()

        @pl.when(at >= half)
        def _():
            copy_out(slot, d, final_far.at[at - half]).start()

    @pl.when(step == tiles - 1)
    def _():
        result[...] = total[...].astype(bf16)
        wait_out(1 - slot)
        wait_out(slot)


def feed_forward(normed, cot, middle, bias_final, feed, bias_hidden, table, home):
    rows, width = normed.shape
    units = bias_hidden.shape[1]
    whole = lambda *shape: pl.BlockSpec(shape, lambda t, *_: (0,) * len(shape), pipeline_mode=pl.Buffered(1))
    sds = jax.ShapeDtypeStruct
    depth = units // PIECES
    devices = FT // depth
    line = pl.BlockSpec((1, FT), lambda t, *_: (0, t))
    square = whole(rows, width)
    wide_piece = sds((PIECES // 2, width // PIECES, units), bf16)
    tall_piece = sds((PIECES // 2, depth, width), bf16)
    edge = pl.BlockSpec((PIECES // 2, width // PIECES, FT), lambda t, *_: (0, 0, t))
    return pl.pallas_call(
        feed_kernel,
        grid_spec=pltpu.PrefetchScalarGridSpec(
            num_scalar_prefetch=2,
            grid=(units // FT,),
            in_specs=[
                square, square, square, whole(1, width),
                pl.BlockSpec((width, FT), lambda t, *_: (0, t)),
                pl.BlockSpec((devices * 32, 4 * width), lambda t, *_: (t, 1)),
                line,
            ],
            out_specs=[square, square, line, edge, edge] + [pl.BlockSpec(memory_space=pl.ANY)] * 2,
            scratch_shapes=[
                pltpu.VMEM((rows, width), f32), pltpu.VMEM((width, rows), bf16), pltpu.VMEM((FT, width), bf16),
                pltpu.VMEM((rows, FT), bf16), pltpu.VMEM((rows, FT), bf16), pltpu.VMEM((width, FT), f32),
                pltpu.VMEM((2, devices, depth, width), bf16), pltpu.SemaphoreType.DMA((2, devices)),
            ],
        ),
        out_shape=[
            sds((rows, width), bf16), sds((rows, width), f32), sds((1, units), f32),
            wide_piece, wide_piece, tall_piece, tall_piece,
        ],
        compiler_params=pltpu.CompilerParams(vmem_limit_bytes=VMEM, dimension_semantics=("arbitrary",)),
        cost_estimate=spent(70),
        name="feed_forward",
    )(table, home, normed, cot, middle, bias_final, feed, feed, bias_hidden)


def project_kernel(
    table_one, table_two, x, one_near, one_far, two_near, two_far,
    q_out, k_out, v_out, normed_out, weight, weight_out, vectors, small,
):
    half, piece, split = one_near.shape
    width = x.shape[1]
    wide = weight.shape[1]

    @pl.when(pl.program_id(0) == 0)
    def _():
        for place in range(2 * half):
            a, b, at = (one_near, two_near, place) if place < half else (one_far, two_far, place - half)
            rows = pl.ds(pl.multiple_of(table_one[place] * piece, piece), piece)
            weight[rows, :split] = a[at]
            rows = pl.ds(pl.multiple_of(table_two[place] * piece, piece), piece)
            weight[rows, split:] = b[at, :, : wide - split]
            weight_out[rows, :] = b[at, :, wide - split : wide - split + width]
            small[rows, :] = b[at, :, wide - split + width : wide - split + width + LANES].astype(f32)
        vectors[...] = small[...].T[: vectors.shape[0]]

    values = x[...].astype(f32)
    center = values - jnp.mean(values, axis=-1, keepdims=True)
    spread_of = jnp.mean(center * center, axis=-1, keepdims=True)
    normed = (center * lax.rsqrt(spread_of + norm_epsilon) * vectors[0:1, :] + vectors[1:2, :]).astype(bf16)
    normed_out[...] = normed
    cols = width // GROUPS
    for group in range(GROUPS):
        out = slice(group * cols, (group + 1) * cols)
        begin = 3 * group * cols
        product = [
            jnp.dot(normed, weight[:, begin + i * cols : begin + (i + 1) * cols], preferred_element_type=f32) for i in range(3)
        ]
        q_out[:, out] = (product[0] + vectors[2:3, out]).astype(bf16) * jnp.asarray(HEAD**-0.5, bf16)
        k_out[:, out] = product[1].astype(bf16)
        v_out[:, out] = (product[2] + vectors[3:4, out]).astype(bf16)


def project(window, one, two, tables):
    rows, width = window.shape
    half, piece, split = one[0].shape
    block = rows // 4
    whole = lambda *shape: pl.BlockSpec(shape, lambda t, *_: (0,) * len(shape), pipeline_mode=pl.Buffered(1))
    strip = pl.BlockSpec((block, width), lambda t, *_: (t, 0))
    sds = jax.ShapeDtypeStruct
    return pl.pallas_call(
        project_kernel,
        grid_spec=pltpu.PrefetchScalarGridSpec(
            num_scalar_prefetch=2,
            grid=(4,),
            in_specs=[strip] + [whole(half, piece, split)] * 2 + [whole(*two[0].shape)] * 2,
            out_specs=[strip] * 4 + [whole(width, 3 * width), whole(width, width), whole(16, width)],
            scratch_shapes=[pltpu.VMEM((width, LANES), f32)],
        ),
        out_shape=[sds((rows, width), bf16)] * 4 + [sds((width, 3 * width), bf16), sds((width, width), bf16), sds((16, width), f32)],
        compiler_params=pltpu.CompilerParams(vmem_limit_bytes=VMEM, dimension_semantics=("arbitrary",)),
        cost_estimate=spent(24),
        name="project",
    )(*tables, window, *one, *two)


CW = 256


def share_kernel(
    extra, table_one, table_two, normed, dq, dk, dv, left, right, *refs,
):
    mixed, branch = refs[:2] if extra else (None, None)
    packed, sums, near_one, far_one, near_two, far_two, normed_t, mixed_t, x = refs[2 if extra else 0 :]
    step = pl.program_id(0)
    steps = pl.num_programs(0)
    rows = dq.shape[0]
    half, piece, _ = near_one.shape
    per = dq.shape[1] // CW if dq.shape[1] > CW else None

    @pl.when(step == 0)
    def _():
        normed_t[...] = normed[pl.ds(REACH, rows), :].T

    def halo(own, number):
        x[...] = own[...].astype(bf16)
        edge = rows - REACH
        x[:edge, :] = (own[:edge, :] + left[number, :edge, :].astype(f32)).astype(bf16)
        x[edge:REACH, :] = (own[edge:REACH, :] + left[number, edge:, :].astype(f32) + right[number, : REACH - edge, :].astype(f32)).astype(bf16)
        x[REACH:, :] = (own[REACH:, :] + right[number, REACH - edge :, :].astype(f32)).astype(bf16)

    @pl.when(step < 2)
    def _():
        x[...] = dq[...]

    @pl.when((step >= 2) & (step < 4))
    def _():
        halo(dk, 0)

    @pl.when((step >= 4) & (step < 6))
    def _():
        halo(dv, 1)

    if extra:
        @pl.when(step == 6)
        def _():
            normed_t[...] = mixed[...].T

        @pl.when(step >= 6)
        def _():
            x[...] = branch[...]

    @pl.when(step < 6)
    def _():
        packed[...] = x[...]

    sums[...] = jnp.sum(x[...].astype(f32), axis=0, keepdims=True)
    mixed_t[...] = jnp.dot(normed_t[...], x[...], preferred_element_type=f32)

    def put(table, near, far):
        for place in range(2 * half):
            rows_of = mixed_t[pl.ds(pl.multiple_of(table[place] * piece, piece), piece), :].astype(bf16)
            if place < half:
                near[place] = rows_of
            else:
                far[place - half] = rows_of

    @pl.when(step < steps // 2)
    def _():
        put(table_one, near_one, far_one)

    @pl.when(step >= steps // 2)
    def _():
        put(table_two, near_two, far_two)


def weight_share(normed, dq, dk, dv, left, right, tables, extra=()):
    rows, cols = dq.shape
    win, width = normed.shape
    steps = 6 + (4 if extra else 0)
    whole = lambda *shape: pl.BlockSpec(shape, lambda t, *_: (0,) * len(shape), pipeline_mode=pl.Buffered(1))
    clip = lambda t, low, top: jnp.minimum(jnp.maximum(t - low, 0), top)
    tall = lambda low, top: pl.BlockSpec((rows, CW), lambda t, *_: (0, clip(t, low, top)))
    edge = pl.BlockSpec((2, REACH, CW), lambda t, *_: (0, 0, jnp.where(t < 4, clip(t, 2, 1), clip(t, 4, 1))))
    piece = lambda low, top: pl.BlockSpec((PIECES // 2, width // PIECES, CW), lambda t, *_: (0, 0, clip(t, low, top)))
    sds = jax.ShapeDtypeStruct
    hold = steps // 2
    pieces = sds((PIECES // 2, width // PIECES, hold * CW), bf16)
    return pl.pallas_call(
        functools.partial(share_kernel, bool(extra)),
        grid_spec=pltpu.PrefetchScalarGridSpec(
            num_scalar_prefetch=2,
            grid=(steps,),
            in_specs=[whole(win, width), tall(0, 1), tall(2, 1), tall(4, 1), edge, edge]
            + ([whole(rows, width), tall(6, 3)] if extra else []),
            out_specs=[tall(0, 5), pl.BlockSpec((1, CW), lambda t, *_: (0, t))]
            + [piece(0, hold - 1)] * 2 + [piece(hold, hold - 1)] * 2,
            scratch_shapes=[pltpu.VMEM((width, rows), bf16), pltpu.VMEM((width, CW), f32), pltpu.VMEM((rows, CW), bf16)],
        ),
        out_shape=[sds((rows, 6 * CW), bf16), sds((1, steps * CW), f32), pieces, pieces, pieces, pieces],
        compiler_params=pltpu.CompilerParams(vmem_limit_bytes=VMEM, dimension_semantics=("arbitrary",)),
        cost_estimate=spent(10 if extra else 7),
        name="weight_share",
    )(*tables, normed, dq, dk, dv, left, right, *extra)


def norm_backward(values, gain, grad):
    center = values - jnp.mean(values, axis=-1, keepdims=True)
    scale = lax.rsqrt(jnp.mean(center * center, axis=-1, keepdims=True) + norm_epsilon)
    unit = center * scale
    scaled = grad * gain
    moved = scaled - jnp.mean(scaled, axis=-1, keepdims=True) - unit * jnp.mean(scaled * unit, axis=-1, keepdims=True)
    column = lambda x: jnp.sum(x, axis=0, keepdims=True)
    return scale * moved, column(grad * unit), column(grad)


def branch_kernel(grad, middle, cot, weight_out, vectors, total, branch, mixed, sums):
    @pl.when(pl.program_id(0) == 0)
    def _():
        sums[...] = jnp.zeros_like(sums)

    up = cot[...].astype(f32)
    moved, gain_sum, bias_sum = norm_backward(middle[...], vectors[5:6, :], grad[...])
    total[...] = up + moved
    branch[...] = total[...].astype(bf16)
    mixed[...] = contract(branch[...], weight_out[...], ((1,), (1,))).astype(bf16)
    sums[0:1, :] += gain_sum
    sums[1:2, :] += bias_sum
    sums[2:3, :] += jnp.sum(up, axis=0, keepdims=True)


def input_kernel(one, two, weight, tokens, middle_grad, vectors, out, sums):
    @pl.when(pl.program_id(0) == 0)
    def _():
        sums[...] = jnp.zeros_like(sums)

    cols = one.shape[1]
    grad = contract(one[...], weight[:, :cols], ((1,), (1,))) + contract(two[...], weight[:, cols:], ((1,), (1,)))
    moved, gain_sum, bias_sum = norm_backward(tokens[...].astype(f32), vectors[0:1, :], grad)
    out[...] = (middle_grad[...] + moved).astype(bf16)
    sums[0:1, :] += gain_sum
    sums[1:2, :] += bias_sum


def row_blocks(kernel, name, blocked, whole, outs, us):
    rows, width = blocked[0].shape[0], outs[0][0]
    block = rows // 4
    strip = lambda cols: pl.BlockSpec((block, cols), lambda t: (t, 0))
    fixed = lambda *shape: pl.BlockSpec(shape, lambda t: (0,) * len(shape), pipeline_mode=pl.Buffered(1))
    return pl.pallas_call(
        kernel,
        grid=(4,),
        in_specs=[strip(a.shape[1]) for a in blocked] + [fixed(*a.shape) for a in whole],
        out_specs=[strip(cols) for cols, _ in outs] + [fixed(8, width)],
        out_shape=[jax.ShapeDtypeStruct((rows, cols), kind) for cols, kind in outs] + [jax.ShapeDtypeStruct((8, width), f32)],
        compiler_params=pltpu.CompilerParams(vmem_limit_bytes=VMEM, dimension_semantics=("arbitrary",)),
        cost_estimate=spent(us),
        name=name,
    )(*blocked, *whole)


def branch_gradient(grad, middle, cot, weight_out, vectors):
    width = middle.shape[1]
    outs = [(width, f32), (width, bf16), (width, bf16)]
    return row_blocks(branch_kernel, "branch_gradient", [grad, middle, cot], [weight_out, vectors], outs, 10)


def input_gradient(one, two, tokens, middle_grad, weight, vectors):
    def kernel(one, two, tokens, middle_grad, weight, vectors, out, sums):
        input_kernel(one, two, weight, tokens, middle_grad, vectors, out, sums)

    return row_blocks(kernel, "input_gradient", [one, two, tokens, middle_grad], [weight, vectors], [(tokens.shape[1], bf16)], 12)


def bit_orders(count):
    bits = [1 << i for i in range(count.bit_length() - 1)]
    return (bits[0], bits[2], bits[1], *bits[3:]), (bits[0], bits[1], bits[2], *bits[3:])


def exchange(x, bit, count):
    return lax.ppermute(x, "dev", [(i, i ^ bit) for i in range(count)])


def owners(order, me):
    table = []
    for place in range(PIECES):
        offset = 0
        for i, bit in enumerate(order):
            if (place >> (len(order) - 1 - i)) & 1:
                offset |= bit
        table.append(offset)
    return jnp.array(table, jnp.int32) ^ me


def gather_step(held, order, step, count):
    bit = order[len(order) - 1 - step]
    arrived = exchange(held, bit, count)
    return (held, arrived) if bit == order[0] else jnp.concatenate([held, arrived], axis=0)


def add_low(a, b):
    return (a.astype(f32) + b.astype(f32)).astype(bf16)


def near_whole(near, arrived):
    return add_low(near, arrived)


def add_halves(near, arrived):
    half = near.shape[0] // 2
    return add_low(near[:half], arrived[:half]), add_low(near[half:], arrived[half:])


near_halves = near_whole


def line_swap(held, order, count):
    near, middle, far = order[3], order[4], order[3] | order[4]
    return held[0], (exchange(held[2], near, count), exchange(held[1], middle, count), exchange(held[3], far, count))


def line_sum(own, parts):
    one, two, three = [p.astype(f32) for p in parts]
    return (own.astype(f32) + one) + (two + three)


def plane_swap(held, order, count):
    quarter = held.shape[0] // 4
    cut = lambda i: held[i * quarter : (i + 1) * quarter]
    bits = order[2], order[1], order[1] | order[2]
    return cut(0), [exchange(cut(i + 1), bit, count) for i, bit in enumerate(bits)]


def plane_sum(own, parts):
    one, two, three = [p.astype(f32) for p in parts]
    return ((own.astype(f32) + one) + (two + three)).astype(bf16)


def scatter_whole(near, far, count):
    whole = jnp.concatenate([near, far], axis=0).reshape(-1, near.shape[2])
    return lax.psum_scatter(whole.astype(f32), "dev", scatter_dimension=0, tiled=True)


def layer_norm(values, gain, bias):
    center = values - jnp.mean(values, axis=-1, keepdims=True)
    spread_of = jnp.mean(center * center, axis=-1, keepdims=True)
    return center * lax.rsqrt(spread_of + norm_epsilon) * gain + bias


def exact_gelu(values):
    return jax.nn.gelu(values, approximate=False)


def image_starts(segment_ids, me, rows):
    padded = jnp.pad(segment_ids, (REACH, REACH), constant_values=-2)
    window = lax.dynamic_slice_in_dim(padded, me * rows, rows + 2 * REACH, 0)
    own = window[REACH : REACH + rows]
    far = jnp.int32(1 << 20)
    first = jnp.min(jnp.where(own >= 0, own, far))
    places = jnp.arange(rows + 2 * REACH, dtype=jnp.int32)
    images = (rows - 2) // IMG + 2
    starts = []
    for i in range(images):
        start = jnp.min(jnp.where(window == first + i, places, far))
        starts.append(jnp.where(start == far, -far, start))
    return jnp.stack(starts)


def per_device(
    tokens,
    segment_ids,
    first_gain,
    first_bias,
    qkv_weight,
    query_bias,
    value_bias,
    out_weight,
    out_bias,
    second_gain,
    second_bias,
    hidden_weight,
    hidden_bias,
    final_weight,
    final_bias,
    cotangent,
):
    count = lax.axis_size("dev")
    me = lax.axis_index("dev")
    direct = count == PIECES
    rows, width = tokens.shape
    hidden_width = hidden_weight.shape[1]
    pairs = width // LANES
    part = width // count
    half = PIECES // 2
    unit = hidden_width // PIECES
    orders = bit_orders(PIECES)
    tables = [owners(order, me if direct else 0) for order in orders]
    homes = [jnp.argsort(table).astype(jnp.int32) for table in tables]
    sync = lax.optimization_barrier
    img = image_starts(segment_ids, me, rows)
    to_right = [(i, i + 1) for i in range(count - 1)]
    to_left = [(i + 1, i) for i in range(count - 1)]
    send = lambda left, right: (lax.ppermute(right, "dev", to_right), lax.ppermute(left, "dev", to_left))

    vectors = [first_gain, first_bias, query_bias, value_bias, out_bias, second_gain, second_bias, final_bias]
    small = jnp.concatenate([jnp.stack(vectors, axis=1), hidden_bias.reshape(part, -1)], axis=1).astype(bf16)
    small = jnp.pad(small, ((0, 0), (0, 2 * LANES - small.shape[1])))
    cols = width // GROUPS
    qkv_low = qkv_weight.astype(bf16)
    qkv_low = jnp.concatenate(
        [qkv_low[:, i * width + g * cols : i * width + (g + 1) * cols] for g in range(GROUPS) for i in range(3)], axis=1
    )
    split = 2 * width
    early = [qkv_low[:, :split], jnp.concatenate([qkv_low[:, split:], out_weight.astype(bf16), small], axis=1)]
    hidden_low = hidden_weight.astype(bf16)
    final_low = final_weight.astype(bf16)
    if direct:
        feed = jnp.concatenate([hidden_low] + [final_low[32 * i : 32 * (i + 1)] for i in range(4)], axis=1)
        held = [p[None] for p in early]
        halo = send(tokens[:REACH], tokens[rows - REACH :])
        lines = [[exchange(h, o[3], count), exchange(h, o[4], count), exchange(h, o[3] | o[4], count)] for h, o in zip(held, orders)]
        lines, held, halo = sync((lines, held, halo))
        held = [jnp.concatenate([h, line[1], line[0], line[2]], axis=0) for h, line in zip(held, lines)]
        held = [gather_step(h, o, 2, count) for h, o in zip(held, orders)]
        if FEED_AFTER == 2:
            held, feed = sync((held, feed))
        held = [gather_step(h, o, 3, count) for h, o in zip(held, orders)]
        if FEED_AFTER == 3:
            held, feed = sync((held, feed))
        held = [gather_step(h, o, 4, count) for h, o in zip(held, orders)]
        feed = lax.all_gather(feed, "dev", axis=0, tiled=True)
        one, two = held
    else:
        one, two = [jnp.split(lax.all_gather(p, "dev", axis=0, tiled=True).reshape(PIECES, width // PIECES, -1), 2) for p in early]
        hidden_low = lax.all_gather(hidden_low, "dev", axis=0, tiled=True)
        final_low = lax.all_gather(final_low, "dev", axis=0, tiled=True)
        final_low = final_low.reshape(PIECES, 4, 32, width).transpose(0, 2, 1, 3).reshape(width, 4 * width)
        feed = jnp.concatenate([hidden_low, final_low], axis=1)
        halo = send(tokens[:REACH], tokens[rows - REACH :])
    window = jnp.concatenate([halo[0], tokens, halo[1]], axis=0)
    inputs = tokens.astype(f32)
    queries, key_rows, value_rows, normed, weight_qkv, weight_out, vectors = project(window, one, two, tables)
    gain_one, bias_one, bias_query, bias_value, bias_out, gain_two, bias_two, bias_final = [vectors[i] for i in range(8)]
    bias_hidden = vectors[8 : 8 + hidden_width // width].T.reshape(1, hidden_width)
    mixed_low, totals = attention_forward(img, queries, key_rows, value_rows, 0, pairs)
    middle = inputs + (jnp.dot(mixed_low, weight_out, preferred_element_type=f32) + bias_out)
    normed_two = layer_norm(middle, gain_two, bias_two).astype(bf16)
    result, grad_normed_two, hidden_bias_grad, *grads = feed_forward(
        normed_two, cotangent, middle, bias_final[None], feed, bias_hidden, tables[0], homes[1]
    )
    grads = [grads[:2], grads[2:]]
    swap = lambda state, step: [exchange(far, o[step], count) for (_, far), o in zip(state, orders)]
    take = lambda state, arrived: [add_halves(near, a) for (near, _), a in zip(state, arrived)]
    step = pairs // GROUPS
    if direct:
        moving = swap(grads, 0)
    middle_grad, grad_branch, grad_mixed, sums_mid = branch_gradient(grad_normed_two, middle, cotangent, weight_out, vectors)
    if direct:
        grads, moving, grad_mixed = sync((grads, moving, grad_mixed))
        grads = take(grads, moving)
        grads, grad_mixed = sync((grads, grad_mixed))
        moving = swap(grads, 1)
    first = attention_backward(img, queries, key_rows, value_rows, grad_mixed, totals, 0, step)
    if direct:
        grad_mixed, first = sync((grad_mixed, first))
    halo = send(*first[3:])
    second = attention_backward(img, queries, key_rows, value_rows, grad_mixed, totals, step, step)
    if direct:
        moving, first, second, halo, normed, grad_branch = sync((moving, first, second, halo, normed, grad_branch))
        grads = take(grads, moving)
        grads, first, second, halo, normed, grad_branch = sync((grads, first, second, halo, normed, grad_branch))
        moving = swap(grads, 2)
    next_halo = send(*second[3:])
    packed_one, sums_one, *share_one = weight_share(normed, *first[:3], *halo, tables, (mixed_low, grad_branch))
    share_one = [share_one[:2], share_one[2:]]
    if direct:
        moving, grads, second, next_halo, normed, share_one = sync((moving, grads, second, next_halo, normed, share_one))
        lines = [line_swap(near_halves(near, a), order, count) for (near, _), a, order in zip(grads, moving, orders)]
        moving = swap(share_one, 0)
    packed_two, sums_two, *share_two = weight_share(normed, *second[:3], *next_halo, tables)
    share_two = [share_two[:2], share_two[2:]]
    if direct:
        moving, share_one, share_two, packed_one, packed_two = sync((moving, share_one, share_two, packed_one, packed_two))
        planes = [plane_swap(near_whole(near, a), order, count) for (near, _), a, order in zip(share_one, moving, orders)]
        moving = swap(share_two, 0)
    input_grad, sums_first = input_gradient(packed_one, packed_two, tokens, middle_grad, weight_qkv, vectors)
    pick = lambda i: jnp.concatenate([s[:, i * cols : (i + 1) * cols] for s in (sums_one, sums_two)], axis=1)
    sums = jnp.concatenate(
        [sums_first[:2], pick(0), pick(2), sums_one[:, 3 * cols :], sums_mid[:3], hidden_bias_grad.reshape(-1, width)], axis=0
    )
    if direct:
        lines, planes, share_two, moving, input_grad, sums = sync((lines, planes, share_two, moving, input_grad, sums))
        hidden_shard, final_shard = [line_sum(*line) for line in lines]
        lines = [line_swap(plane_sum(*plane), order, count) for plane, order in zip(planes, orders)]
        planes = [plane_swap(near_whole(near, a), order, count) for (near, _), a, order in zip(share_two, moving, orders)]
        parts = [exchange(sums, bit, count) for bit in range(1, 8)]
        lines, planes, sums, parts, hidden_shard, final_shard = sync((lines, planes, sums, parts, hidden_shard, final_shard))
        shards_one = jnp.concatenate([line_sum(*line) for line in lines], axis=1)
        lines = [line_swap(plane_sum(*plane), order, count) for plane, order in zip(planes, orders)]
        sums = functools.reduce(lambda a, b: a + b, parts, sums)
        parts = [exchange(sums, bit, count) for bit in (8, 16, 24)]
        shards_two = jnp.concatenate([line_sum(*line) for line in lines], axis=1)
        sums = sums + parts[0] + (parts[1] + parts[2])
    else:
        sums = lax.psum(sums, "dev")
        shards_one = jnp.concatenate([scatter_whole(*s, count) for s in share_one], axis=1)
        shards_two = jnp.concatenate([scatter_whole(*s, count) for s in share_two], axis=1)
        hidden_shard, final_shard = [scatter_whole(*s, count) for s in grads]
    out_shard = shards_one[:, 3 * cols :]
    qkv_shard = jnp.concatenate([h[:, i * cols : (i + 1) * cols] for i in range(3) for h in (shards_one, shards_two)], axis=1)
    own = lax.dynamic_slice_in_dim(sums[:8], me * part, part, 1)
    own_hidden = lax.dynamic_slice_in_dim(sums[8:].reshape(-1), me * hidden_bias.shape[0], hidden_bias.shape[0], 0)
    return (
        result,
        input_grad,
        own[0],
        own[1],
        qkv_shard,
        own[2],
        own[3],
        out_shard,
        own[4],
        own[5],
        own[6],
        hidden_shard,
        own_hidden,
        final_shard,
        own[7],
    )


def solution(mesh):
    split = P("dev", None)
    line = P("dev")
    return jax.shard_map(
        per_device,
        mesh=mesh,
        in_specs=(split, P(), line, line, split, line, line, split, line, line, line, split, line, split, line, split),
        out_specs=(split, split, line, line, split, line, line, split, line, line, line, split, line, split, line),
        check_vma=False,
    )
```

time: 687 us -> 577 us (0.84)
  waiting for transfers between devices: 196 us -> 112 us
  Pallas kernels: 187 us -> 245 us
  matrix products: 58.9 us -> 4.68 us
  other arithmetic: 77 us -> 44.1 us
  starting transfers between devices: 107 us -> 115 us
    ppermute x45 -> x62, waiting for transfers between devices: 196 us -> 112 us  [exchange(): return lax.ppermute(x, 'dev', [(i, i ^ bit) for i in range(count)])]
    pallas_call x7 -> x6, Pallas kernels: 96.6 us -> 154 us  [the longest x1 70.9 us: feed_forward(): pl.pallas_call(feed_kernel, grid_spec=pltpu.PrefetchScalarGridSpec(num_sc...]
    dot_general x9 -> x0, matrix products: 54.2 us -> none  [the longest x2 12.9 us: per_device(): jnp.einsum('tc,tq->cq', normed_one, packed, preferred_element_type=f32)]
    reduce_sum x9 -> x0, other arithmetic: 17.4 us -> none  [the longest x2 7.75 us: layer_norm(): return center * lax.rsqrt(spread_of + norm_epsilon) * gain + bias]
    convert_element_type x8 -> x4, other arithmetic: 14.2 us -> 1.71 us  [plane_sum(): return (own.astype(f32) + one + (two + three)).astype(bf16)]
    ppermute x6, starting transfers between devices: 12.5 us -> 23.2 us  [the longest x3 19.3 us: per_device(): lax.ppermute(right, 'dev', to_right)]
    unnamed x138 -> x112, local copies, waits for them, and re-layouts: 15.6 us -> 10.2 us
    ppermute x45 -> x62, starting transfers between devices: 94.7 us -> 91.7 us  [exchange(): return lax.ppermute(x, 'dev', [(i, i ^ bit) for i in range(count)])]
  transfers between devices with their start and end apart: 52 -> 69, of which waited for: 22 -> 17; matrix products, arithmetic and copies ran while one was open for 23% -> 10% of each run, Pallas kernels for 17% -> 30%
where the time goes in v3:
time: 577 us; the launch traced here: 571 us
  Pallas kernels  245 us (42%)
  starting transfers between devices  115 us (20%)
  waiting for transfers between devices  112 us (19%)
  other arithmetic  44.1 us (8%)
  local copies, waits for them, and re-layouts  30.4 us (5%)
  between operations  20.6 us (4%)
    ppermute x62, waiting for transfers between devices, exchange(): return lax.ppermute(x, 'dev', [(i, i ^ bit) for i in range(count)])  112 us
    ppermute x62, starting transfers between devices, exchange(): return lax.ppermute(x, 'dev', [(i, i ^ bit) for i in range(count)])  91.7 us
    pallas_call x1, Pallas kernels, feed_forward(): pl.pallas_call(feed_kernel, grid_spec=pltpu.PrefetchScalarGridSpec(num_sc...  70.9 us
    pallas_call x2, Pallas kernels, attention_backward(): pl.pallas_call(functools.partial(bwd_kernel, blocks, images), grid_spec=p...  53.3 us
    pallas_call x1, Pallas kernels, attention_forward(): pl.pallas_call(functools.partial(fwd_kernel, blocks, images), grid_spec=p...  37.4 us
    pallas_call x2, Pallas kernels, weight_share(): pl.pallas_call(functools.partial(share_kernel, bool(extra)), grid_spec=pl...  33.1 us
    pallas_call x1, Pallas kernels, project(): pl.pallas_call(project_kernel, grid_spec=pltpu.PrefetchScalarGridSpec(num...  25.6 us
    pallas_call x2, Pallas kernels, row_blocks(): pl.pallas_call(kernel, grid=(4,), in_specs=[strip(a.shape[1]) for a in bl...  24.4 us
  transfers between devices with their start and end apart: 69, of which 17 were waited for; matrix products, arithmetic and copies ran while one was open for 10% of the time, Pallas kernels for 30%

profile of v3, /device:TPU:0, one launch (start us, length us, event | category | flops | bytes accessed | tf_op | source)
XLA Modules:
  0.0 571.4 jit_solution(3701454334414279880)
XLA Ops:
  9.0 3.1 collective-permute-start
  27.6 4.7 collective-permute-start.3
  32.3 3.5 collective-permute-start.4
  35.8 9.6 %collective-permute-done.3 = bf16[1,32,2304]{2,1,0:T(8,128)(2,1)} collective-permute-done((bf16[1,32,2304]{2,1,0:T(8,128)(2,1)S(1)}, bf16[1,32,2304]{2,1,0:T(8,128)(2,1)}, u32[]{:S(2)}, u32[]{:S(2)}) %collective-permute-start.3) | collective-permute-done | bytes 147488 | tf_op jit(solution)/shard_map/ppermute | solution.py:576
  48.0 3.6 collective-permute-done.5
  59.6 6.6 %collective-permute-done.8 = bf16[4,32,2048]{2,1,0:T(8,128)(2,1)S(1)} collective-permute-done((bf16[4,32,2048]{2,1,0:T(8,128)(2,1)S(1)}, bf16[4,32,2048]{2,1,0:T(8,128)(2,1)S(1)}, u32[]{:S(2)}, u32[]{:S(2)}) %collective-permute-start.8) | collective-permute-done | bytes 524320 | tf_op jit(solution)/shard_map/ppermute | solution.py:576
  70.7 25.0 %collective-permute-done.12 = bf16[8,32,2304]{2,1,0:T(8,128)(2,1)S(1)} collective-permute-done((bf16[8,32,2304]{2,1,0:T(8,128)(2,1)S(1)}, bf16[8,32,2304]{2,1,0:T(8,128)(2,1)S(1)}, u32[]{:S(2)}, u32[]{:S(2)}) %collective-permute-start.12) | collective-permute-done | bytes 1179680 | tf_op jit(solution)/shard_map/ppermute | solution.py:576
  109.5 3.7 pad_maximum_fusion.x
  113.3 25.6 %project.1 = (bf16[2176,1024]{1,0:T(8,128)(2,1)}, bf16[2176,1024]{1,0:T(8,128)(2,1)}, bf16[2176,1024]{1,0:T(8,128)(2,1)}, bf16[2176,1024]{1,0:T(8,128)(2,1)}, bf...) custom-call(s32[32]{0:T(128)} %broadcast_xor_fusion.1.table_one.table, s32[32]{0:T(128)} %copy-done.34, ...), custom_call_target="tpu_custom_call" | custom-call | bytes 2400000 | tf_op jit(solution)/shard_map/project/pallas_call | solution.py:386
  140.8 37.4 %attention_forward.1 = (bf16[1024,1024]{1,0:T(8,128)(2,1)}, f32[8,4,512]{2,1,0:T(4,128)}) custom-call(s32[3]{0:T(128)} %pad_add_fusion.img_ref, bf16[2176,1024]{1,0:T(8,128)(2,1)} %get-tuple-element.204.q_ref, bf16[2176,1024]{1,0:T(8,128)(2,1)} %get-tuple-element.205.k_ref, bf16[2176,1024]{1,0:T(8,128)(2,1)} %get-tuple-element.206.v_ref), custom_call_target="tpu_custom_call" | custom-call | bytes 4000000 | tf_op jit(solution)/shard_map/attention_forward/pallas_call | solution.py:123
  179.7 4.7 fusion.17
  188.4 70.9 %feed_forward.1 = (bf16[1024,1024]{1,0:T(8,128)(2,1)}, f32[1024,1024]{1,0:T(8,128)}, f32[1,4096]{1,0:T(1,128)}, bf16[16,32,4096]{2,1,0:T(8,128)(2,1)}, bf16[16,3...) custom-call(s32[32]{0:T(128)} %broadcast_xor_fusion.1.table_one.table, ...), custom_call_target="tpu_custom_call" | custom-call | bytes 7000000 | tf_op jit(solution)/shard_map/feed_forward/pallas_call | solution.py:314
  259.8 10.2 %branch_gradient.1 = (f32[1024,1024]{1,0:T(8,128)}, bf16[1024,1024]{1,0:T(8,128)(2,1)}, bf16[1024,1024]{1,0:T(8,128)(2,1)}, f32[8,1024]{1,0:T(8,128)}) custom-call(f32[1024,1024]{1,0:T(8,128)} %get-tuple-element.216.grad, f32[1024,1024]{1,0:T(8,128)} %copy-done, bf16[1024,1024]{1,0:T(8,128)(2,1)} %cot.3, bf16[1024,1024]{1,0:T(8,128)(2,1)} %get-tuple-element.208.weight_out, ...), custom_call_target="tpu_custom_call" | custom-call | bytes 1000000 | tf_op jit(solution)/shard_map/branch_gradient/pallas_call | solution.py:545
  272.8 5.6 add_convert_fusion
  278.4 4.5 add_convert_fusion.2
  282.9 7.6 %collective-permute-start.16 = (bf16[8,32,4096]{2,1,0:T(8,128)(2,1)}, bf16[8,32,4096]{2,1,0:T(8,128)(2,1)}, u32[]{:S(2)}, u32[]{:S(2)}) collective-permute-start(bf16[8,32,4096]{2,1,0:T(8,128)(2,1)} %get-tuple-element.224), channel_id=1, source_target_pairs={{0,4},{1,5},{2,6},{3,7},{4,0},{5,1},{6,2},{7,3},{8,12},{9,13},{10,... | collective-permute-start | bytes 6291464 | tf_op jit(solution)/shard_map/ppermute | solution.py:576
  291.7 26.9 %attention_backward.2 = (bf16[1024,512]{1,0:T(8,128)(2,1)}, f32[1024,512]{1,0:T(8,128)}, f32[1024,512]{1,0:T(8,128)}, bf16[2,576,512]{2,1,0:T(8,128)(2,1)}, bf16[2,576,512]{2,1,0:T(8,128)(2,1)}) custom-call(s32[3]{0:T(128)} %pad_add_fusion.img_ref, bf16[2176,1024]{1,0:T(8,128)(2,1)} %get-tuple-element.204.q_ref, ...), custom_call_target="tpu_custom_call" | custom-call | bytes 2600000 | tf_op jit(solution)/shard_map/attention_backward/pallas_call | solution.py:204
  321.4 26.4 %attention_backward.3 = (bf16[1024,512]{1,0:T(8,128)(2,1)}, f32[1024,512]{1,0:T(8,128)}, f32[1024,512]{1,0:T(8,128)}, bf16[2,576,512]{2,1,0:T(8,128)(2,1)}, bf16[2,576,512]{2,1,0:T(8,128)(2,1)}) custom-call(s32[3]{0:T(128)} %pad_add_fusion.img_ref, bf16[2176,1024]{1,0:T(8,128)(2,1)} %get-tuple-element.204.q_ref, ...), custom_call_target="tpu_custom_call" | custom-call | bytes 2600000 | tf_op jit(solution)/shard_map/attention_backward/pallas_call | solution.py:204
  350.7 3.7 add_convert_fusion.9
  354.5 3.3 add_convert_fusion.11
  357.8 15.6 %collective-permute-start.22 = (bf16[2,576,512]{2,1,0:T(8,128)(2,1)}, bf16[2,576,512]{2,1,0:T(8,128)(2,1)}, u32[]{:S(2)}, u32[]{:S(2)}) collective-permute-start(bf16[2,576,512]{2,1,0:T(8,128)(2,1)} %get-tuple-element.269), channel_id=1, source_target_pairs={{0,1},{1,2},{2,3},{3,4},{4,5},{5,6},{6,7},{7,8},{8,9},{9,10},{10,1... | collective-permute-start | bytes 3538952 | tf_op jit(solution)/shard_map/ppermute | solution.py:698
  374.6 3.7 collective-permute-start.20
  379.8 19.3 %weight_share.2 = (bf16[1024,1536]{1,0:T(8,128)(2,1)}, f32[1,2560]{1,0:T(1,128)}, bf16[16,32,1280]{2,1,0:T(8,128)(2,1)}, bf16[16,32,1280]{2,1,0:T(8,128)(2,1)}, ...) custom-call(s32[32]{0:T(128)} %broadcast_xor_fusion.1.table_one.table, s32[32]{0:T(128)} %copy-done.34, ...), custom_call_target="tpu_custom_call" | custom-call | bytes 1000000 | tf_op jit(solution)/shard_map/weight_share/pallas_call | solution.py:484
  400.6 23.7 %collective-permute-done.20 = bf16[4,32,4096]{2,1,0:T(8,128)(2,1)} collective-permute-done((bf16[4,32,4096]{2,1,0:T(8,128)(2,1)}, bf16[4,32,4096]{2,1,0:T(8,128)(2,1)}, u32[]{:S(2)}, u32[]{:S(2)}) %collective-permute-start.20) | collective-permute-done | bytes 1048608 | tf_op jit(solution)/shard_map/ppermute | solution.py:576
  427.3 6.6 %collective-permute-start.27 = (bf16[128,1024]{1,0:T(8,128)(2,1)}, bf16[128,1024]{1,0:T(8,128)(2,1)S(1)}, u32[]{:S(2)}, u32[]{:S(2)}) collective-permute-start(bf16[128,1024]{1,0:T(8,128)(2,1)} %get-tuple-element.390), channel_id=1, source_target_pairs={{0,8},{1,9},{2,10},{3,11},{4,12},{5,13},{6,14},{7,15},{8,0},{9,1},... | collective-permute-start | bytes 786440 | tf_op jit(solution)/shard_map/ppermute | solution.py:576
  437.7 13.8 %weight_share.3 = (bf16[1024,1536]{1,0:T(8,128)(2,1)}, f32[1,1536]{1,0:T(1,128)}, bf16[16,32,768]{2,1,0:T(8,128)(2,1)}, bf16[16,32,768]{2,1,0:T(8,128)(2,1)}, bf...) custom-call(s32[32]{0:T(128)} %broadcast_xor_fusion.1.table_one.table, s32[32]{0:T(128)} %copy-done.34, ...), custom_call_target="tpu_custom_call" | custom-call | bytes 700000 | tf_op jit(solution)/shard_map/weight_share/pallas_call | solution.py:484
  462.5 15.4 %collective-permute-done.25 = bf16[32,4096]{1,0:T(8,128)(2,1)S(1)} collective-permute-done((bf16[32,4096]{1,0:T(8,128)(2,1)S(1)}, bf16[32,4096]{1,0:T(8,128)(2,1)S(1)}, u32[]{:S(2)}, u32[]{:S(2)}) %collective-permute-start.25) | collective-permute-done | bytes 262176 | tf_op jit(solution)/shard_map/ppermute | solution.py:576
  483.1 14.2 %input_gradient.1 = (bf16[1024,1024]{1,0:T(8,128)(2,1)}, f32[8,1024]{1,0:T(8,128)}) custom-call(bf16[1024,1536]{1,0:T(8,128)(2,1)} %get-tuple-element.309.one, bf16[1024,1536]{1,0:T(8,128)(2,1)} %get-tuple-element.310.two, bf16[1024,1024]{1,0:T(8,128)(2,1)} %tokens.1, f32[1024,1024]{1,0:T(8,128)} %get-tuple-element.311.middle_grad, ...), custom_call_target="tpu_custom_call" | custom-call | bytes 1200000 | tf_op jit(solution)/shard_map/input_gradient/pallas_call | solution.py:545
  508.3 4.9 collective-permute-start.43
  518.9 4.0 collective-permute-done.44
  541.9 3.3 collective-permute-start.59
  560.1 2.9 collective-permute-done.67
  (328 shorter events, 137.0 us)
Async XLA Ops:
  7.2 181.2 %all-gather.2.cloned.1.call-start = ((), (), s32[]{:S(2)}) async-start(), calls=%async_computation | async-start | bytes 17301504 | tf_op jit(solution)/shard_map/all_gather | solution.py:726
  9.0 18.6 %collective-permute-start = (bf16[1,32,2048]{2,1,0:T(8,128)(2,1)S(1)}, bf16[1,32,2048]{2,1,0:T(8,128)(2,1)}, u32[]{:S(2)}, u32[]{:S(2)}) collective-permute-start(bf16[1,32,2048]{2,1,0:T(8,128)(2,1)S(1)} %maximum_bitcast_fusion), channel_id=1, source_target_pairs={{0,8},{1,9},{2,10},{3,11},{4,12},{5,13},{6,14},{7,15},{8,0},{9,1},... | collective-permute-start | bytes 393224 | tf_op jit(solution)/shard_map/ppermute | solution.py:576
  12.1 20.2 %collective-permute-start.1 = (bf16[1,32,2048]{2,1,0:T(8,128)(2,1)S(1)}, bf16[1,32,2048]{2,1,0:T(8,128)(2,1)}, u32[]{:S(2)}, u32[]{:S(2)}) collective-permute-start(bf16[1,32,2048]{2,1,0:T(8,128)(2,1)S(1)} %maximum_bitcast_fusion), channel_id=1, source_target_pairs={{0,16},{1,17},{2,18},{3,19},{4,20},{5,21},{6,22},{7,23},{8,24},{9,... | collective-permute-start | bytes 393224 | tf_op jit(solution)/shard_map/ppermute | solution.py:576
  14.7 21.1 %collective-permute-start.2 = (bf16[1,32,2048]{2,1,0:T(8,128)(2,1)S(1)}, bf16[1,32,2048]{2,1,0:T(8,128)(2,1)}, u32[]{:S(2)}, u32[]{:S(2)}) collective-permute-start(bf16[1,32,2048]{2,1,0:T(8,128)(2,1)S(1)} %maximum_bitcast_fusion), channel_id=1, source_target_pairs={{0,24},{1,25},{2,26},{3,27},{4,28},{5,29},{6,30},{7,31},{8,16},{9,... | collective-permute-start | bytes 393224 | tf_op jit(solution)/shard_map/ppermute | solution.py:576
  16.5 35.1 %collective-permute-start.6 = (bf16[576,1024]{1,0:T(8,128)(2,1)S(1)}, bf16[576,1024]{1,0:T(8,128)(2,1)}, u32[]{:S(2)}, u32[]{:S(2)}) collective-permute-start(bf16[576,1024]{1,0:T(8,128)(2,1)S(1)} %get-tuple-element.379), channel_id=1, source_target_pairs={{0,1},{1,2},{2,3},{3,4},{4,5},{5,6},{6,7},{7,8},{8,9},{9,10},{10,1... | collective-permute-start | bytes 3538952 | tf_op jit(solution)/shard_map/ppermute | solution.py:698
  18.9 32.8 %collective-permute-start.7 = (bf16[576,1024]{1,0:T(8,128)(2,1)S(1)}, bf16[576,1024]{1,0:T(8,128)(2,1)}, u32[]{:S(2)}, u32[]{:S(2)}) collective-permute-start(bf16[576,1024]{1,0:T(8,128)(2,1)S(1)} %get-tuple-element.378), channel_id=1, source_target_pairs={{1,0},{2,1},{3,2},{4,3},{5,4},{6,5},{7,6},{8,7},{9,8},{10,9},{11,1... | collective-permute-start | bytes 3538952 | tf_op jit(solution)/shard_map/ppermute | solution.py:698
  27.6 17.8 %collective-permute-start.3 = (bf16[1,32,2304]{2,1,0:T(8,128)(2,1)S(1)}, bf16[1,32,2304]{2,1,0:T(8,128)(2,1)}, u32[]{:S(2)}, u32[]{:S(2)}) collective-permute-start(bf16[1,32,2304]{2,1,0:T(8,128)(2,1)S(1)} %fusion.2), channel_id=1, source_target_pairs={{0,8},{1,9},{2,10},{3,11},{4,12},{5,13},{6,14},{7,15},{8,0},{9,1},... | collective-permute-start | bytes 442376 | tf_op jit(solution)/shard_map/ppermute | solution.py:576
  66.3 29.4 %collective-permute-start.12 = (bf16[8,32,2304]{2,1,0:T(8,128)(2,1)S(1)}, bf16[8,32,2304]{2,1,0:T(8,128)(2,1)S(1)}, u32[]{:S(2)}, u32[]{:S(2)}) collective-permute-start(bf16[8,32,2304]{2,1,0:T(8,128)(2,1)S(1)} %constant_dynamic-update-slice_fusion.5), channel_id=1, source_target_pairs={{0,2},{1,3},{2,0},{3,1},{4,6},{5,7},{6,4},{7,5},{8,10},{9,11},{10,... | collective-permute-start | bytes 3538952 | tf_op jit(solution)/shard_map/ppermute | solution.py:576
  67.6 30.3 %collective-permute-start.10 = (bf16[8,32,2048]{2,1,0:T(8,128)(2,1)S(1)}, bf16[8,32,2048]{2,1,0:T(8,128)(2,1)S(1)}, u32[]{:S(2)}, u32[]{:S(2)}) collective-permute-start(bf16[8,32,2048]{2,1,0:T(8,128)(2,1)S(1)} %constant_dynamic-update-slice_fusion), channel_id=1, source_target_pairs={{0,4},{1,5},{2,6},{3,7},{4,0},{5,1},{6,2},{7,3},{8,12},{9,13},{10,... | collective-permute-start | bytes 3145736 | tf_op jit(solution)/shard_map/ppermute | solution.py:576
  282.9 64.9 %collective-permute-start.16 = (bf16[8,32,4096]{2,1,0:T(8,128)(2,1)}, bf16[8,32,4096]{2,1,0:T(8,128)(2,1)}, u32[]{:S(2)}, u32[]{:S(2)}) collective-permute-start(bf16[8,32,4096]{2,1,0:T(8,128)(2,1)} %get-tuple-element.224), channel_id=1, source_target_pairs={{0,4},{1,5},{2,6},{3,7},{4,0},{5,1},{6,2},{7,3},{8,12},{9,13},{10,... | collective-permute-start | bytes 6291464 | tf_op jit(solution)/shard_map/ppermute | solution.py:576
  290.6 60.2 %collective-permute-start.17 = (bf16[8,128,1024]{2,1,0:T(8,128)(2,1)}, bf16[8,128,1024]{2,1,0:T(8,128)(2,1)}, u32[]{:S(2)}, u32[]{:S(2)}) collective-permute-start(bf16[8,128,1024]{2,1,0:T(8,128)(2,1)} %get-tuple-element.225), channel_id=1, source_target_pairs={{0,2},{1,3},{2,0},{3,1},{4,6},{5,7},{6,4},{7,5},{8,10},{9,11},{10,... | collective-permute-start | bytes 6291464 | tf_op jit(solution)/shard_map/ppermute | solution.py:576
  318.6 29.2 %collective-permute-start.18 = (bf16[2,576,512]{2,1,0:T(8,128)(2,1)}, bf16[2,576,512]{2,1,0:T(8,128)(2,1)S(1)}, u32[]{:S(2)}, u32[]{:S(2)}) collective-permute-start(bf16[2,576,512]{2,1,0:T(8,128)(2,1)} %get-tuple-element.237), channel_id=1, source_target_pairs={{0,1},{1,2},{2,3},{3,4},{4,5},{5,6},{6,7},{7,8},{8,9},{9,10},{10,1... | collective-permute-start | bytes 3538952 | tf_op jit(solution)/shard_map/ppermute | solution.py:698
  320.1 27.7 %collective-permute-start.19 = (bf16[2,576,512]{2,1,0:T(8,128)(2,1)}, bf16[2,576,512]{2,1,0:T(8,128)(2,1)}, u32[]{:S(2)}, u32[]{:S(2)}) collective-permute-start(bf16[2,576,512]{2,1,0:T(8,128)(2,1)} %get-tuple-element.236), channel_id=1, source_target_pairs={{1,0},{2,1},{3,2},{4,3},{5,4},{6,5},{7,6},{8,7},{9,8},{10,9},{11,1... | collective-permute-start | bytes 3538952 | tf_op jit(solution)/shard_map/ppermute | solution.py:698
  357.8 66.4 %collective-permute-start.22 = (bf16[2,576,512]{2,1,0:T(8,128)(2,1)}, bf16[2,576,512]{2,1,0:T(8,128)(2,1)}, u32[]{:S(2)}, u32[]{:S(2)}) collective-permute-start(bf16[2,576,512]{2,1,0:T(8,128)(2,1)} %get-tuple-element.269), channel_id=1, source_target_pairs={{0,1},{1,2},{2,3},{3,4},{4,5},{5,6},{6,7},{7,8},{8,9},{9,10},{10,1... | collective-permute-start | bytes 3538952 | tf_op jit(solution)/shard_map/ppermute | solution.py:698
  373.4 50.9 %collective-permute-start.23 = (bf16[2,576,512]{2,1,0:T(8,128)(2,1)}, bf16[2,576,512]{2,1,0:T(8,128)(2,1)}, u32[]{:S(2)}, u32[]{:S(2)}) collective-permute-start(bf16[2,576,512]{2,1,0:T(8,128)(2,1)} %get-tuple-element.268), channel_id=1, source_target_pairs={{1,0},{2,1},{3,2},{4,3},{5,4},{6,5},{7,6},{8,7},{9,8},{10,9},{11,1... | collective-permute-start | bytes 3538952 | tf_op jit(solution)/shard_map/ppermute | solution.py:698
  374.6 49.6 %collective-permute-start.20 = (bf16[4,32,4096]{2,1,0:T(8,128)(2,1)}, bf16[4,32,4096]{2,1,0:T(8,128)(2,1)}, u32[]{:S(2)}, u32[]{:S(2)}) collective-permute-start(bf16[4,32,4096]{2,1,0:T(8,128)(2,1)} %get-tuple-element.261), channel_id=1, source_target_pairs={{0,2},{1,3},{2,0},{3,1},{4,6},{5,7},{6,4},{7,5},{8,10},{9,11},{10,... | collective-permute-start | bytes 3145736 | tf_op jit(solution)/shard_map/ppermute | solution.py:576
  378.3 45.9 %collective-permute-start.21 = (bf16[4,128,1024]{2,1,0:T(8,128)(2,1)}, bf16[4,128,1024]{2,1,0:T(8,128)(2,1)}, u32[]{:S(2)}, u32[]{:S(2)}) collective-permute-start(bf16[4,128,1024]{2,1,0:T(8,128)(2,1)} %get-tuple-element.262), channel_id=1, source_target_pairs={{0,4},{1,5},{2,6},{3,7},{4,0},{5,1},{6,2},{7,3},{8,12},{9,13},{10,... | collective-permute-start | bytes 3145736 | tf_op jit(solution)/shard_map/ppermute | solution.py:576
  424.2 27.4 %collective-permute-start.30 = (bf16[16,32,1280]{2,1,0:T(8,128)(2,1)}, bf16[16,32,1280]{2,1,0:T(8,128)(2,1)}, u32[]{:S(2)}, u32[]{:S(2)}) collective-permute-start(bf16[16,32,1280]{2,1,0:T(8,128)(2,1)} %get-tuple-element.285), channel_id=1, source_target_pairs={{0,1},{1,0},{2,3},{3,2},{4,5},{5,4},{6,7},{7,6},{8,9},{9,8},{10,11... | collective-permute-start | bytes 3932168 | tf_op jit(solution)/shard_map/ppermute | solution.py:576
  424.3 28.5 %collective-permute-start.31 = (bf16[16,32,1280]{2,1,0:T(8,128)(2,1)}, bf16[16,32,1280]{2,1,0:T(8,128)(2,1)}, u32[]{:S(2)}, u32[]{:S(2)}) collective-permute-start(bf16[16,32,1280]{2,1,0:T(8,128)(2,1)} %get-tuple-element.286), channel_id=1, source_target_pairs={{0,1},{1,0},{2,3},{3,2},{4,5},{5,4},{6,7},{7,6},{8,9},{9,8},{10,11... | collective-permute-start | bytes 3932168 | tf_op jit(solution)/shard_map/ppermute | solution.py:576
  427.3 30.1 %collective-permute-start.27 = (bf16[128,1024]{1,0:T(8,128)(2,1)}, bf16[128,1024]{1,0:T(8,128)(2,1)S(1)}, u32[]{:S(2)}, u32[]{:S(2)}) collective-permute-start(bf16[128,1024]{1,0:T(8,128)(2,1)} %get-tuple-element.390), channel_id=1, source_target_pairs={{0,8},{1,9},{2,10},{3,11},{4,12},{5,13},{6,14},{7,15},{8,0},{9,1},... | collective-permute-start | bytes 786440 | tf_op jit(solution)/shard_map/ppermute | solution.py:576
  433.9 25.0 %collective-permute-start.28 = (bf16[128,1024]{1,0:T(8,128)(2,1)}, bf16[128,1024]{1,0:T(8,128)(2,1)S(1)}, u32[]{:S(2)}, u32[]{:S(2)}) collective-permute-start(bf16[128,1024]{1,0:T(8,128)(2,1)} %get-tuple-element.389), channel_id=1, source_target_pairs={{0,16},{1,17},{2,18},{3,19},{4,20},{5,21},{6,22},{7,23},{8,24},{9,... | collective-permute-start | bytes 786440 | tf_op jit(solution)/shard_map/ppermute | solution.py:576
  434.9 24.8 %collective-permute-start.29 = (bf16[128,1024]{1,0:T(8,128)(2,1)S(1)}, bf16[128,1024]{1,0:T(8,128)(2,1)S(1)}, u32[]{:S(2)}, u32[]{:S(2)}) collective-permute-start(bf16[128,1024]{1,0:T(8,128)(2,1)S(1)} %get-tuple-element.388), channel_id=1, source_target_pairs={{0,24},{1,25},{2,26},{3,27},{4,28},{5,29},{6,30},{7,31},{8,16},{9,... | collective-permute-start | bytes 786440 | tf_op jit(solution)/shard_map/ppermute | solution.py:576
  452.8 25.1 %collective-permute-start.25 = (bf16[32,4096]{1,0:T(8,128)(2,1)S(1)}, bf16[32,4096]{1,0:T(8,128)(2,1)S(1)}, u32[]{:S(2)}, u32[]{:S(2)}) collective-permute-start(bf16[32,4096]{1,0:T(8,128)(2,1)S(1)} %get-tuple-element.393), channel_id=1, source_target_pairs={{0,16},{1,17},{2,18},{3,19},{4,20},{5,21},{6,22},{7,23},{8,24},{9,... | collective-permute-start | bytes 786440 | tf_op jit(solution)/shard_map/ppermute | solution.py:576
  457.4 20.5 %collective-permute-start.26 = (bf16[32,4096]{1,0:T(8,128)(2,1)S(1)}, bf16[32,4096]{1,0:T(8,128)(2,1)S(1)}, u32[]{:S(2)}, u32[]{:S(2)}) collective-permute-start(bf16[32,4096]{1,0:T(8,128)(2,1)S(1)} %get-tuple-element.392), channel_id=1, source_target_pairs={{0,24},{1,25},{2,26},{3,27},{4,28},{5,29},{6,30},{7,31},{8,16},{9,... | collective-permute-start | bytes 786440 | tf_op jit(solution)/shard_map/ppermute | solution.py:576
  458.9 20.6 %collective-permute-start.32 = (bf16[4,32,1280]{2,1,0:T(8,128)(2,1)S(1)}, bf16[4,32,1280]{2,1,0:T(8,128)(2,1)S(1)}, u32[]{:S(2)}, u32[]{:S(2)}) collective-permute-start(bf16[4,32,1280]{2,1,0:T(8,128)(2,1)S(1)} %get-tuple-element.386), channel_id=1, source_target_pairs={{0,2},{1,3},{2,0},{3,1},{4,6},{5,7},{6,4},{7,5},{8,10},{9,11},{10,... | collective-permute-start | bytes 983048 | tf_op jit(solution)/shard_map/ppermute | solution.py:576
  459.7 19.8 %collective-permute-start.33 = (bf16[4,32,1280]{2,1,0:T(8,128)(2,1)S(1)}, bf16[4,32,1280]{2,1,0:T(8,128)(2,1)S(1)}, u32[]{:S(2)}, u32[]{:S(2)}) collective-permute-start(bf16[4,32,1280]{2,1,0:T(8,128)(2,1)S(1)} %get-tuple-element.385), channel_id=1, source_target_pairs={{0,4},{1,5},{2,6},{3,7},{4,0},{5,1},{6,2},{7,3},{8,12},{9,13},{10,... | collective-permute-start | bytes 983048 | tf_op jit(solution)/shard_map/ppermute | solution.py:576
  460.9 20.5 %collective-permute-start.34 = (bf16[4,32,1280]{2,1,0:T(8,128)(2,1)S(1)}, bf16[4,32,1280]{2,1,0:T(8,128)(2,1)S(1)}, u32[]{:S(2)}, u32[]{:S(2)}) collective-permute-start(bf16[4,32,1280]{2,1,0:T(8,128)(2,1)S(1)} %get-tuple-element.384), channel_id=1, source_target_pairs={{0,6},{1,7},{2,4},{3,5},{4,2},{5,3},{6,0},{7,1},{8,14},{9,15},{10,... | collective-permute-start | bytes 983048 | tf_op jit(solution)/shard_map/ppermute | solution.py:576
  477.9 20.3 %collective-permute-start.38 = (bf16[16,32,768]{2,1,0:T(8,128)(2,1)}, bf16[16,32,768]{2,1,0:T(8,128)(2,1)S(1)}, u32[]{:S(2)}, u32[]{:S(2)}) collective-permute-start(bf16[16,32,768]{2,1,0:T(8,128)(2,1)} %get-tuple-element.306), channel_id=1, source_target_pairs={{0,1},{1,0},{2,3},{3,2},{4,5},{5,4},{6,7},{7,6},{8,9},{9,8},{10,11... | collective-permute-start | bytes 2359304 | tf_op jit(solution)/shard_map/ppermute | solution.py:576
  477.9 20.3 %collective-permute-start.39 = (bf16[16,32,768]{2,1,0:T(8,128)(2,1)}, bf16[16,32,768]{2,1,0:T(8,128)(2,1)S(1)}, u32[]{:S(2)}, u32[]{:S(2)}) collective-permute-start(bf16[16,32,768]{2,1,0:T(8,128)(2,1)} %get-tuple-element.308), channel_id=1, source_target_pairs={{0,1},{1,0},{2,3},{3,2},{4,5},{5,4},{6,7},{7,6},{8,9},{9,8},{10,11... | collective-permute-start | bytes 2359304 | tf_op jit(solution)/shard_map/ppermute | solution.py:576
  479.5 18.6 %collective-permute-start.35 = (bf16[4,32,1280]{2,1,0:T(8,128)(2,1)}, bf16[4,32,1280]{2,1,0:T(8,128)(2,1)}, u32[]{:S(2)}, u32[]{:S(2)}) collective-permute-start(bf16[4,32,1280]{2,1,0:T(8,128)(2,1)} %get-tuple-element.382), channel_id=1, source_target_pairs={{0,4},{1,5},{2,6},{3,7},{4,0},{5,1},{6,2},{7,3},{8,12},{9,13},{10,... | collective-permute-start | bytes 983048 | tf_op jit(solution)/shard_map/ppermute | solution.py:576
  479.6 18.6 %collective-permute-start.36 = (bf16[4,32,1280]{2,1,0:T(8,128)(2,1)S(1)}, bf16[4,32,1280]{2,1,0:T(8,128)(2,1)}, u32[]{:S(2)}, u32[]{:S(2)}) collective-permute-start(bf16[4,32,1280]{2,1,0:T(8,128)(2,1)S(1)} %get-tuple-element.381), channel_id=1, source_target_pairs={{0,2},{1,3},{2,0},{3,1},{4,6},{5,7},{6,4},{7,5},{8,10},{9,11},{10,... | collective-permute-start | bytes 983048 | tf_op jit(solution)/shard_map/ppermute | solution.py:576
  513.8 16.8 %collective-permute-start.49 = (bf16[4,32,768]{2,1,0:T(8,128)(2,1)S(1)}, bf16[4,32,768]{2,1,0:T(8,128)(2,1)S(1)}, u32[]{:S(2)}, u32[]{:S(2)}) collective-permute-start(bf16[4,32,768]{2,1,0:T(8,128)(2,1)S(1)} %get-tuple-element.398), channel_id=1, source_target_pairs={{0,4},{1,5},{2,6},{3,7},{4,0},{5,1},{6,2},{7,3},{8,12},{9,13},{10,... | collective-permute-start | bytes 589832 | tf_op jit(solution)/shard_map/ppermute | solution.py:576
  (84 other events, 913.5 us)
Sparse Core Ops, SparseCore 0:
  66.4 119.4 all-gather.1

commit v4 on v3

--- a/solution.py
+++ b/solution.py
@@ -13,7 +13,6 @@
 HEAD = 64
 SPAN = 592
 LANES = 128
-QB = 256
 PP = 2
 PIECES = 32
 PACE = 1.0e5
@@ -30,42 +29,81 @@
     return pl.CostEstimate(flops=0, bytes_accessed=int(us * PACE), transcendentals=0)
 
 
-def make_items(img_ref, items_ref, blocks, images):
-    count = jnp.int32(0)
-    for b in range(blocks):
-        for i in range(images):
-            start = img_ref[i]
-            low = b * QB + REACH
-            hit = (start < low + QB) & (start + IMG > low)
-
-            @pl.when(hit)
-            def _():
-                items_ref[count] = b * 8 + i
-
-            count = count + hit.astype(jnp.int32)
-    return count
-
-def item_scalars(img_ref, items_ref, n):
-    code = items_ref[n]
-    b = code // 8
-    start = img_ref[code % 8]
+FP = 4
+SLOTS = 8
+CHUNKS = (384, 256, 128)
+
+
+def make_items(img_ref, lists, counts, rows, images):
+    for kind in range(len(CHUNKS)):
+        counts[kind] = 0
+
+    def add(kind, first, begin, end, start):
+        size = CHUNKS[kind]
+        n = counts[kind]
+        base = (kind * SLOTS + n) * 4
+        lists[base] = jnp.minimum(first, rows - size)
+        lists[base + 1] = jnp.maximum(first, begin)
+        lists[base + 2] = jnp.minimum(first + size, end)
+        lists[base + 3] = start
+        counts[kind] = n + 1
+
+    for i in range(images):
+        start = img_ref[i]
+        begin = jnp.maximum(start - REACH, 0)
+        end = jnp.minimum(start - REACH + IMG, rows)
+        low = (begin // 16) * 16
+        left = jnp.where(end > begin, end - low, 0)
+
+        @pl.when(left > 512)
+        def _():
+            add(0, low, begin, end, start)
+            add(1, low + 384, begin, end, start)
+
+        @pl.when((left > 384) & (left <= 512))
+        def _():
+            add(1, low, begin, end, start)
+            add(1, low + 256, begin, end, start)
+
+        @pl.when((left > 256) & (left <= 384))
+        def _():
+            add(0, low, begin, end, start)
+
+        @pl.when((left > 128) & (left <= 256))
+        def _():
+            add(1, low, begin, end, start)
+
+        @pl.when((left > 0) & (left <= 128))
+        def _():
+            add(2, low, begin, end, start)
+
+
+def item_scalars(lists, kind, n):
+    base = (kind * SLOTS + n) * 4
+    start = lists[base + 3]
     begin = pl.multiple_of((start // 16) * 16, 16)
-    row = pl.multiple_of(b * QB, QB)
-    return b, start, begin, row
+    return pl.multiple_of(lists[base], 16), lists[base + 1], lists[base + 2], start, begin
+
 
 def halves(x):
     lane = lax.broadcasted_iota(jnp.int32, x.shape, 1)
     zero = jnp.zeros_like(x)
     return jnp.concatenate([jnp.where(lane < HEAD, x, zero), jnp.where(lane >= HEAD, x, zero)], axis=0)
 
-def key_valid(start, begin):
-    r = lax.broadcasted_iota(jnp.int32, (SPAN, 1), 0) + (begin - start)
-    return (r >= 0) & (r < IMG)
-
-def query_valid(start, row):
-    lane = lax.broadcasted_iota(jnp.int32, (1, 2 * QB), 1)
-    pos = jnp.where(lane < QB, lane, lane - QB) + (row + REACH - start)
-    return (pos >= 0) & (pos < IMG)
+
+def mask_keys(scores, start, begin):
+    def masked(low, top):
+        r = lax.broadcasted_iota(jnp.int32, (top - low, 1), 0) + (low + begin - start)
+        return jnp.where((r >= 0) & (r < IMG), scores[low:top], -1e30)
+
+    return jnp.concatenate([masked(0, 16), scores[16 : SPAN - 16], masked(SPAN - 16, SPAN)], axis=0)
+
+
+def query_valid(size, row, low, top):
+    lane = lax.broadcasted_iota(jnp.int32, (1, 2 * size), 1)
+    pos = jnp.where(lane < size, lane, lane - size) + row
+    return (pos >= low) & (pos < top)
+
 
 def pad_rows(img_ref, images, rows):
     r = lax.broadcasted_iota(jnp.int32, (rows, LANES), 0) + REACH
@@ -75,110 +113,111 @@
         inside = inside | ((r >= start) & (r < start + IMG))
     return ~inside
 
-def fwd_kernel(blocks, images, img_ref, q_ref, k_ref, v_ref, o_ref, lse_ref, acc, items):
-    rows = blocks * QB
-    count = make_items(img_ref, items, blocks, images)
+
+def fwd_kernel(images, img_ref, q_ref, k_ref, v_ref, o_ref, lse_ref, acc, lists, counts):
+    rows = acc.shape[0]
+    make_items(img_ref, lists, counts, rows, images)
     acc[...] = jnp.zeros_like(acc)
-    lse_ref[...] = jnp.zeros_like(lse_ref)
-
-    def body(n, carry):
-        b, start, begin, row = item_scalars(img_ref, items, n)
-        valid = key_valid(start, begin)
-        qm = query_valid(start, row)
+
+    def body(kind, size, n, carry):
+        row, low, top, start, begin = item_scalars(lists, kind, n)
+        qm = query_valid(size, row, low, top)
         done = []
-        for u in range(PP):
+        for u in range(FP):
             cols = slice(u * LANES, (u + 1) * LANES)
-            q2 = halves(q_ref[pl.ds(pl.multiple_of(row + REACH, 16), QB), cols])
+            q2 = halves(q_ref[pl.ds(pl.multiple_of(row + REACH, 16), size), cols])
             kw = k_ref[pl.ds(begin, SPAN), cols]
             vw = v_ref[pl.ds(begin, SPAN), cols]
             s = lax.dot_general(kw, q2, (((1,), (1,)), ((), ())), preferred_element_type=f32)
-            s = jnp.where(valid, s, -1e30)
+            s = mask_keys(s, start, begin)
             m = jnp.max(s, axis=0, keepdims=True)
             e = jnp.exp(s - m)
             l = jnp.sum(e, axis=0, keepdims=True)
-            p = (e * jnp.where(qm, 1.0 / l, 0.0)).astype(bf16)
-            ot = lax.dot_general(vw, p, (((0,), (0,)), ((), ())), preferred_element_type=f32)
-            done.append((jnp.concatenate([ot[:HEAD, :QB], ot[HEAD:, QB:]], axis=0).T, m + jnp.log(l)))
-        for u in range(PP):
+            ot = lax.dot_general(vw, e.astype(bf16), (((0,), (0,)), ((), ())), preferred_element_type=f32)
+            ot = ot * jnp.where(qm, 1.0 / l, 0.0)
+            done.append((jnp.concatenate([ot[:HEAD, :size], ot[HEAD:, size:]], axis=0).T, m + jnp.log(l)))
+        for u in range(FP):
             cols = slice(u * LANES, (u + 1) * LANES)
-            o, total = done[u]
-            acc[pl.ds(row, QB), cols] += o
-            old = lse_ref[u, pl.ds(b, 1), :]
-            lse_ref[u, pl.ds(b, 1), :] = jnp.where(qm, total, old)
+            acc[pl.ds(row, size), cols] += done[u][0]
+            lse_ref[u, pl.ds(kind * SLOTS + n, 1), : 2 * size] = done[u][1]
         return carry
 
-    lax.fori_loop(0, count, body, 0)
+    for kind, size in enumerate(CHUNKS):
+        lax.fori_loop(0, counts[kind], functools.partial(body, kind, size), 0)
     pad = pad_rows(img_ref, images, rows)
-    for u in range(PP):
+    for u in range(FP):
         cols = slice(u * LANES, (u + 1) * LANES)
         own = v_ref[pl.ds(REACH, rows), cols].astype(f32)
         o_ref[:, cols] = jnp.where(pad, own, acc[:, cols]).astype(bf16)
 
+
 def attention_forward(img, q, k, v, first, pairs):
     win = k.shape[0]
     rows = win - 2 * REACH
-    blocks = rows // QB
     images = img.shape[0]
-    spec = lambda r: pl.BlockSpec((r, PP * LANES), lambda p, *_: (0, first // PP + p))
+    spec = lambda r: pl.BlockSpec((r, FP * LANES), lambda p, *_: (0, first // FP + p))
     return pl.pallas_call(
-        functools.partial(fwd_kernel, blocks, images),
+        functools.partial(fwd_kernel, images),
         grid_spec=pltpu.PrefetchScalarGridSpec(
             num_scalar_prefetch=1,
-            grid=(pairs // PP,),
+            grid=(pairs // FP,),
             in_specs=[spec(win), spec(win), spec(win)],
             out_specs=[
-                pl.BlockSpec((rows, PP * LANES), lambda p, *_: (0, p)),
-                pl.BlockSpec((PP, blocks, 2 * QB), lambda p, *_: (p, 0, 0)),
+                pl.BlockSpec((rows, FP * LANES), lambda p, *_: (0, p)),
+                pl.BlockSpec((FP, 3 * SLOTS, 2 * CHUNKS[0]), lambda p, *_: (p, 0, 0)),
             ],
-            scratch_shapes=[pltpu.VMEM((rows, PP * LANES), f32), pltpu.SMEM((blocks * images,), jnp.int32)],
+            scratch_shapes=[
+                pltpu.VMEM((rows, FP * LANES), f32), pltpu.SMEM((3 * SLOTS * 4,), jnp.int32), pltpu.SMEM((3,), jnp.int32)
+            ],
         ),
         out_shape=[
             jax.ShapeDtypeStruct((rows, pairs * LANES), bf16),
-            jax.ShapeDtypeStruct((pairs, blocks, 2 * QB), f32),
+            jax.ShapeDtypeStruct((pairs, 3 * SLOTS, 2 * CHUNKS[0]), f32),
         ],
         compiler_params=pltpu.CompilerParams(vmem_limit_bytes=VMEM, dimension_semantics=("arbitrary",)),
         cost_estimate=spent(5 * pairs),
         name="attention_forward",
     )(img, q, k, v)
 
-def bwd_kernel(blocks, images, img_ref, q_ref, k_ref, v_ref, g_ref, lse_ref,
-               dq_ref, dk_ref, dv_ref, left_ref, right_ref, dq_acc, dk_acc, dv_acc, items):
-    rows = blocks * QB
-    count = make_items(img_ref, items, blocks, images)
+
+def bwd_kernel(images, img_ref, q_ref, k_ref, v_ref, g_ref, lse_ref,
+               dq_ref, dk_ref, dv_ref, left_ref, right_ref, dq_acc, dk_acc, dv_acc, lists, counts):
+    rows = dq_acc.shape[0]
+    make_items(img_ref, lists, counts, rows, images)
     dq_acc[...] = jnp.zeros_like(dq_acc)
     dk_acc[...] = jnp.zeros_like(dk_acc)
     dv_acc[...] = jnp.zeros_like(dv_acc)
 
-    def body(n, carry):
-        b, start, begin, row = item_scalars(img_ref, items, n)
-        valid = key_valid(start, begin)
-        qm = query_valid(start, row)
+    def body(kind, size, n, carry):
+        row, low, top, start, begin = item_scalars(lists, kind, n)
+        qm = query_valid(size, row, low, top)
         done = []
         for u in range(PP):
             cols = slice(u * LANES, (u + 1) * LANES)
-            q2 = halves(q_ref[pl.ds(pl.multiple_of(row + REACH, 16), QB), cols])
-            g2 = halves(g_ref[pl.ds(row, QB), cols])
+            q2 = halves(q_ref[pl.ds(pl.multiple_of(row + REACH, 16), size), cols])
+            g2 = halves(g_ref[pl.ds(row, size), cols])
             kw = k_ref[pl.ds(begin, SPAN), cols]
             vw = v_ref[pl.ds(begin, SPAN), cols]
-            lse = jnp.where(qm, lse_ref[u, pl.ds(b, 1), :], 1e30)
+            lse = jnp.where(qm, lse_ref[u, pl.ds(kind * SLOTS + n, 1), : 2 * size], 1e30)
             s = lax.dot_general(kw, q2, (((1,), (1,)), ((), ())), preferred_element_type=f32)
             dp = lax.dot_general(vw, g2, (((1,), (1,)), ((), ())), preferred_element_type=f32)
-            p = jnp.exp(jnp.where(valid, s, -1e30) - lse)
+            p = jnp.exp(mask_keys(s, start, begin) - lse)
             inner = jnp.sum(p * dp, axis=0, keepdims=True)
             ds = (p * (dp - inner)).astype(bf16)
             dv = jnp.dot(p.astype(bf16), g2, preferred_element_type=f32)
             dk = jnp.dot(ds, q2, preferred_element_type=f32)
             dqt = lax.dot_general(kw, ds, (((0,), (0,)), ((), ())), preferred_element_type=f32)
-            done.append((dv, dk, jnp.concatenate([dqt[:HEAD, :QB], dqt[HEAD:, QB:]], axis=0).T))
+            done.append((dv, dk, jnp.concatenate([dqt[:HEAD, :size], dqt[HEAD:, size:]], axis=0).T))
         for u in range(PP):
             cols = slice(u * LANES, (u + 1) * LANES)
             dv, dk, dq = done[u]
             dv_acc[pl.ds(begin, SPAN), cols] += dv
             dk_acc[pl.ds(begin, SPAN), cols] += dk
-            dq_acc[pl.ds(row, QB), cols] += dq
+            dq_acc[pl.ds(row, size), cols] += dq
         return carry
 
-    lax.fori_loop(0, count, body, 0)
+    for kind, size in enumerate(CHUNKS):
+        lax.fori_loop(0, counts[kind], functools.partial(body, kind, size), 0)
     pad = pad_rows(img_ref, images, rows)
     dq_ref[...] = (dq_acc[...] * 0.125).astype(bf16)
     dk_ref[...] = dk_acc[pl.ds(REACH, rows), :]
@@ -190,10 +229,10 @@
     right_ref[0] = dk_acc[pl.ds(REACH + rows, REACH), :].astype(bf16)
     right_ref[1] = dv_acc[pl.ds(REACH + rows, REACH), :].astype(bf16)
 
+
 def attention_backward(img, q, k, v, g, lse, first, pairs):
     win = k.shape[0]
     rows = win - 2 * REACH
-    blocks = rows // QB
     images = img.shape[0]
     C = PP * LANES
     spec = lambda r: pl.BlockSpec((r, C), lambda p, *_: (0, first // PP + p))
@@ -202,15 +241,15 @@
     sds = jax.ShapeDtypeStruct
     cols = pairs * LANES
     return pl.pallas_call(
-        functools.partial(bwd_kernel, blocks, images),
+        functools.partial(bwd_kernel, images),
         grid_spec=pltpu.PrefetchScalarGridSpec(
             num_scalar_prefetch=1,
             grid=(pairs // PP,),
             in_specs=[spec(win), spec(win), spec(win), spec(rows),
-                      pl.BlockSpec((PP, blocks, 2 * QB), lambda p, *_: (first // PP + p, 0, 0))],
+                      pl.BlockSpec((PP, 3 * SLOTS, 2 * CHUNKS[0]), lambda p, *_: (first // PP + p, 0, 0))],
             out_specs=[out(rows), out(rows), out(rows), edge, edge],
             scratch_shapes=[pltpu.VMEM((rows, C), f32), pltpu.VMEM((win, C), f32), pltpu.VMEM((win, C), f32),
-                            pltpu.SMEM((blocks * images,), jnp.int32)],
+                            pltpu.SMEM((3 * SLOTS * 4,), jnp.int32), pltpu.SMEM((3,), jnp.int32)],
         ),
         out_shape=[sds((rows, cols), bf16), sds((rows, cols), f32), sds((rows, cols), f32),
                    sds((2, REACH, cols), bf16), sds((2, REACH, cols), bf16)],
@@ -221,7 +260,7 @@
 
 
 FT = 512
-ROWS = 256
+ROWS = 1024
 
 
 def contract(a, b, dims):
@@ -237,7 +276,7 @@
     tiles = pl.num_programs(0)
     slot = lax.rem(step, 2)
     rows, width = normed.shape
-    half, piece, _ = hidden_near.shape
+    half, _, piece, _ = hidden_near.shape
     devices = tall.shape[0] // 32
     depth = FT // devices
 
@@ -265,9 +304,9 @@
     for place in range(2 * half):
         rows_of = hidden_grad[pl.ds(pl.multiple_of(table[place] * piece, piece), piece), :].astype(bf16)
         if place < half:
-            hidden_near[place] = rows_of
+            hidden_near[place, 0] = rows_of
         else:
-            hidden_far[place - half] = rows_of
+            hidden_far[place - half, 0] = rows_of
 
     def copy_out(slot, d, target):
         return pltpu.make_async_copy(final_grad.at[slot, d], target, sems.at[slot, d])
@@ -308,9 +347,10 @@
     devices = FT // depth
     line = pl.BlockSpec((1, FT), lambda t, *_: (0, t))
     square = whole(rows, width)
-    wide_piece = sds((PIECES // 2, width // PIECES, units), bf16)
+    wide_piece = sds((PIECES // 2, units // width, width // PIECES, width), bf16)
     tall_piece = sds((PIECES // 2, depth, width), bf16)
-    edge = pl.BlockSpec((PIECES // 2, width // PIECES, FT), lambda t, *_: (0, 0, t))
+    blocks = width // FT
+    edge = pl.BlockSpec((PIECES // 2, 1, width // PIECES, FT), lambda t, *_: (0, t // blocks, 0, t % blocks))
     return pl.pallas_call(
         feed_kernel,
         grid_spec=pltpu.PrefetchScalarGridSpec(
@@ -365,15 +405,19 @@
     normed = (center * lax.rsqrt(spread_of + norm_epsilon) * vectors[0:1, :] + vectors[1:2, :]).astype(bf16)
     normed_out[...] = normed
     cols = width // GROUPS
+    needs_queries = (pl.program_id(0) == 1) | (pl.program_id(0) == 2)
     for group in range(GROUPS):
         out = slice(group * cols, (group + 1) * cols)
         begin = 3 * group * cols
-        product = [
-            jnp.dot(normed, weight[:, begin + i * cols : begin + (i + 1) * cols], preferred_element_type=f32) for i in range(3)
-        ]
-        q_out[:, out] = (product[0] + vectors[2:3, out]).astype(bf16) * jnp.asarray(HEAD**-0.5, bf16)
-        k_out[:, out] = product[1].astype(bf16)
-        v_out[:, out] = (product[2] + vectors[3:4, out]).astype(bf16)
+        keys = jnp.dot(normed, weight[:, begin + cols : begin + 2 * cols], preferred_element_type=f32)
+        values = jnp.dot(normed, weight[:, begin + 2 * cols : begin + 3 * cols], preferred_element_type=f32)
+        k_out[:, out] = keys.astype(bf16)
+        v_out[:, out] = (values + vectors[3:4, out]).astype(bf16)
+
+        @pl.when(needs_queries)
+        def _():
+            queries = jnp.dot(normed, weight[:, begin : begin + cols], preferred_element_type=f32)
+            q_out[:, out] = (queries + vectors[2:3, out]).astype(bf16) * jnp.asarray(HEAD**-0.5, bf16)
 
 
 def project(window, one, two, tables):
@@ -403,15 +447,13 @@
 
 
 def share_kernel(
-    extra, table_one, table_two, normed, dq, dk, dv, left, right, *refs,
+    extra, table, normed, dq, dk, dv, left, right, *refs,
 ):
     mixed, branch = refs[:2] if extra else (None, None)
-    packed, sums, near_one, far_one, near_two, far_two, normed_t, mixed_t, x = refs[2 if extra else 0 :]
+    packed, sums, near, far, normed_t, product, x = refs[2 if extra else 0 :]
     step = pl.program_id(0)
-    steps = pl.num_programs(0)
     rows = dq.shape[0]
-    half, piece, _ = near_one.shape
-    per = dq.shape[1] // CW if dq.shape[1] > CW else None
+    half, piece, _ = near.shape
 
     @pl.when(step == 0)
     def _():
@@ -450,26 +492,16 @@
         packed[...] = x[...]
 
     sums[...] = jnp.sum(x[...].astype(f32), axis=0, keepdims=True)
-    mixed_t[...] = jnp.dot(normed_t[...], x[...], preferred_element_type=f32)
-
-    def put(table, near, far):
-        for place in range(2 * half):
-            rows_of = mixed_t[pl.ds(pl.multiple_of(table[place] * piece, piece), piece), :].astype(bf16)
-            if place < half:
-                near[place] = rows_of
-            else:
-                far[place - half] = rows_of
-
-    @pl.when(step < steps // 2)
-    def _():
-        put(table_one, near_one, far_one)
-
-    @pl.when(step >= steps // 2)
-    def _():
-        put(table_two, near_two, far_two)
-
-
-def weight_share(normed, dq, dk, dv, left, right, tables, extra=()):
+    product[...] = jnp.dot(normed_t[...], x[...], preferred_element_type=f32)
+    for place in range(2 * half):
+        rows_of = product[pl.ds(pl.multiple_of(table[place] * piece, piece), piece), :].astype(bf16)
+        if place < half:
+            near[place] = rows_of
+        else:
+            far[place - half] = rows_of
+
+
+def weight_share(normed, dq, dk, dv, left, right, table, extra=()):
     rows, cols = dq.shape
     win, width = normed.shape
     steps = 6 + (4 if extra else 0)
@@ -477,26 +509,25 @@
     clip = lambda t, low, top: jnp.minimum(jnp.maximum(t - low, 0), top)
     tall = lambda low, top: pl.BlockSpec((rows, CW), lambda t, *_: (0, clip(t, low, top)))
     edge = pl.BlockSpec((2, REACH, CW), lambda t, *_: (0, 0, jnp.where(t < 4, clip(t, 2, 1), clip(t, 4, 1))))
-    piece = lambda low, top: pl.BlockSpec((PIECES // 2, width // PIECES, CW), lambda t, *_: (0, 0, clip(t, low, top)))
+    piece = pl.BlockSpec((PIECES // 2, width // PIECES, CW), lambda t, *_: (0, 0, t))
     sds = jax.ShapeDtypeStruct
-    hold = steps // 2
-    pieces = sds((PIECES // 2, width // PIECES, hold * CW), bf16)
+    pieces = sds((PIECES // 2, width // PIECES, steps * CW), bf16)
     return pl.pallas_call(
         functools.partial(share_kernel, bool(extra)),
         grid_spec=pltpu.PrefetchScalarGridSpec(
-            num_scalar_prefetch=2,
+            num_scalar_prefetch=1,
             grid=(steps,),
             in_specs=[whole(win, width), tall(0, 1), tall(2, 1), tall(4, 1), edge, edge]
             + ([whole(rows, width), tall(6, 3)] if extra else []),
             out_specs=[tall(0, 5), pl.BlockSpec((1, CW), lambda t, *_: (0, t))]
-            + [piece(0, hold - 1)] * 2 + [piece(hold, hold - 1)] * 2,
+            + [piece] * 2,
             scratch_shapes=[pltpu.VMEM((width, rows), bf16), pltpu.VMEM((width, CW), f32), pltpu.VMEM((rows, CW), bf16)],
         ),
-        out_shape=[sds((rows, 6 * CW), bf16), sds((1, steps * CW), f32), pieces, pieces, pieces, pieces],
+        out_shape=[sds((rows, 6 * CW), bf16), sds((1, steps * CW), f32), pieces, pieces],
         compiler_params=pltpu.CompilerParams(vmem_limit_bytes=VMEM, dimension_semantics=("arbitrary",)),
         cost_estimate=spent(10 if extra else 7),
         name="weight_share",
-    )(*tables, normed, dq, dk, dv, left, right, *extra)
+    )(table, normed, dq, dk, dv, left, right, *extra)
 
 
 def norm_backward(values, gain, grad):
@@ -587,48 +618,24 @@
     return jnp.array(table, jnp.int32) ^ me
 
 
+def places(order, me):
+    offset = jnp.arange(PIECES, dtype=jnp.int32) ^ me
+    return sum(jnp.where(offset & bit != 0, 1 << (len(order) - 1 - i), 0) for i, bit in enumerate(order)).astype(jnp.int32)
+
+
 def gather_step(held, order, step, count):
     bit = order[len(order) - 1 - step]
     arrived = exchange(held, bit, count)
     return (held, arrived) if bit == order[0] else jnp.concatenate([held, arrived], axis=0)
 
 
-def add_low(a, b):
-    return (a.astype(f32) + b.astype(f32)).astype(bf16)
-
-
-def near_whole(near, arrived):
-    return add_low(near, arrived)
-
-
-def add_halves(near, arrived):
-    half = near.shape[0] // 2
-    return add_low(near[:half], arrived[:half]), add_low(near[half:], arrived[half:])
-
-
-near_halves = near_whole
-
-
-def line_swap(held, order, count):
-    near, middle, far = order[3], order[4], order[3] | order[4]
-    return held[0], (exchange(held[2], near, count), exchange(held[1], middle, count), exchange(held[3], far, count))
-
-
-def line_sum(own, parts):
-    one, two, three = [p.astype(f32) for p in parts]
-    return (own.astype(f32) + one) + (two + three)
-
-
-def plane_swap(held, order, count):
-    quarter = held.shape[0] // 4
-    cut = lambda i: held[i * quarter : (i + 1) * quarter]
-    bits = order[2], order[1], order[1] | order[2]
-    return cut(0), [exchange(cut(i + 1), bit, count) for i, bit in enumerate(bits)]
-
-
-def plane_sum(own, parts):
-    one, two, three = [p.astype(f32) for p in parts]
-    return ((own.astype(f32) + one) + (two + three)).astype(bf16)
+def total(parts, kind=bf16):
+    return functools.reduce(lambda a, b: a + b, [p.astype(f32) for p in parts]).astype(kind)
+
+
+def straight(parts, bits, count):
+    size = parts[0].shape[0] // (len(bits) + 1)
+    return [exchange(total([p[(i + 1) * size : (i + 2) * size] for p in parts]), bit, count) for i, bit in enumerate(bits)]
 
 
 def scatter_whole(near, far, count):
@@ -686,11 +693,12 @@
     hidden_width = hidden_weight.shape[1]
     pairs = width // LANES
     part = width // count
+    part_rows = width // PIECES
     half = PIECES // 2
     unit = hidden_width // PIECES
     orders = bit_orders(PIECES)
     tables = [owners(order, me if direct else 0) for order in orders]
-    homes = [jnp.argsort(table).astype(jnp.int32) for table in tables]
+    home = places(orders[1], me if direct else 0)
     sync = lax.optimization_barrier
     img = image_starts(segment_ids, me, rows)
     to_right = [(i, i + 1) for i in range(count - 1)]
@@ -698,24 +706,23 @@
     send = lambda left, right: (lax.ppermute(right, "dev", to_right), lax.ppermute(left, "dev", to_left))
 
     vectors = [first_gain, first_bias, query_bias, value_bias, out_bias, second_gain, second_bias, final_bias]
-    small = jnp.concatenate([jnp.stack(vectors, axis=1), hidden_bias.reshape(part, -1)], axis=1).astype(bf16)
-    small = jnp.pad(small, ((0, 0), (0, 2 * LANES - small.shape[1])))
+    small = sync(jnp.concatenate([jnp.stack(vectors, axis=1), hidden_bias.reshape(part, -1)], axis=1)).astype(bf16)
+    small = jnp.pad(small, ((0, 0), (0, LANES - small.shape[1])))
     cols = width // GROUPS
     qkv_low = qkv_weight.astype(bf16)
     qkv_low = jnp.concatenate(
         [qkv_low[:, i * width + g * cols : i * width + (g + 1) * cols] for g in range(GROUPS) for i in range(3)], axis=1
     )
     split = 2 * width
-    early = [qkv_low[:, :split], jnp.concatenate([qkv_low[:, split:], out_weight.astype(bf16), small], axis=1)]
+    early = jnp.concatenate([qkv_low, out_weight.astype(bf16), small], axis=1)
     hidden_low = hidden_weight.astype(bf16)
     final_low = final_weight.astype(bf16)
     if direct:
         feed = jnp.concatenate([hidden_low] + [final_low[32 * i : 32 * (i + 1)] for i in range(4)], axis=1)
-        held = [p[None] for p in early]
         halo = send(tokens[:REACH], tokens[rows - REACH :])
-        lines = [[exchange(h, o[3], count), exchange(h, o[4], count), exchange(h, o[3] | o[4], count)] for h, o in zip(held, orders)]
-        lines, held, halo = sync((lines, held, halo))
-        held = [jnp.concatenate([h, line[1], line[0], line[2]], axis=0) for h, line in zip(held, lines)]
+        line = [exchange(early[None], bit, count) for bit in (orders[0][4], orders[0][3], orders[0][3] | orders[0][4])]
+        line, halo, feed = sync((line, halo, feed)) if FEED_AFTER == 1 else (*sync((line, halo)), feed)
+        held = [jnp.concatenate([p[..., cut] for p in (early[None], *line)], axis=0) for cut in (slice(0, split), slice(split, None))]
         held = [gather_step(h, o, 2, count) for h, o in zip(held, orders)]
         if FEED_AFTER == 2:
             held, feed = sync((held, feed))
@@ -726,7 +733,8 @@
         feed = lax.all_gather(feed, "dev", axis=0, tiled=True)
         one, two = held
     else:
-        one, two = [jnp.split(lax.all_gather(p, "dev", axis=0, tiled=True).reshape(PIECES, width // PIECES, -1), 2) for p in early]
+        early = lax.all_gather(early, "dev", axis=0, tiled=True).reshape(PIECES, width // PIECES, -1)
+        one, two = [jnp.split(p, 2) for p in (early[..., :split], early[..., split:])]
         hidden_low = lax.all_gather(hidden_low, "dev", axis=0, tiled=True)
         final_low = lax.all_gather(final_low, "dev", axis=0, tiled=True)
         final_low = final_low.reshape(PIECES, 4, 32, width).transpose(0, 2, 1, 3).reshape(width, 4 * width)
@@ -741,20 +749,18 @@
     middle = inputs + (jnp.dot(mixed_low, weight_out, preferred_element_type=f32) + bias_out)
     normed_two = layer_norm(middle, gain_two, bias_two).astype(bf16)
     result, grad_normed_two, hidden_bias_grad, *grads = feed_forward(
-        normed_two, cotangent, middle, bias_final[None], feed, bias_hidden, tables[0], homes[1]
+        normed_two, cotangent, middle, bias_final[None], feed, bias_hidden, tables[0], home
     )
-    grads = [grads[:2], grads[2:]]
-    swap = lambda state, step: [exchange(far, o[step], count) for (_, far), o in zip(state, orders)]
-    take = lambda state, arrived: [add_halves(near, a) for (near, _), a in zip(state, arrived)]
+    grads = [[g.reshape(g.shape[0], -1, part_rows, width) for g in grads[i : i + 2]] for i in (0, 2)]
     step = pairs // GROUPS
     if direct:
-        moving = swap(grads, 0)
+        got = [[near, exchange(far, order[0], count)] for (near, far), order in zip(grads, orders)]
     middle_grad, grad_branch, grad_mixed, sums_mid = branch_gradient(grad_normed_two, middle, cotangent, weight_out, vectors)
     if direct:
-        grads, moving, grad_mixed = sync((grads, moving, grad_mixed))
-        grads = take(grads, moving)
-        grads, grad_mixed = sync((grads, grad_mixed))
-        moving = swap(grads, 1)
+        got, grad_mixed = sync((got, grad_mixed))
+        away = [total([p[8:] for p in parts]) for parts in got]
+        away, grad_mixed = sync((away, grad_mixed))
+        moving = [exchange(a, order[1], count) for a, order in zip(away, orders)]
     first = attention_backward(img, queries, key_rows, value_rows, grad_mixed, totals, 0, step)
     if direct:
         grad_mixed, first = sync((grad_mixed, first))
@@ -762,49 +768,62 @@
     second = attention_backward(img, queries, key_rows, value_rows, grad_mixed, totals, step, step)
     if direct:
         moving, first, second, halo, normed, grad_branch = sync((moving, first, second, halo, normed, grad_branch))
-        grads = take(grads, moving)
-        grads, first, second, halo, normed, grad_branch = sync((grads, first, second, halo, normed, grad_branch))
-        moving = swap(grads, 2)
+        got = [parts + [m] for parts, m in zip(got, moving)]
+        away = [total([p[4:8] for p in parts]) for parts in got]
+        away, first, second, halo, normed, grad_branch = sync((away, first, second, halo, normed, grad_branch))
+        moving = [exchange(a, order[2], count) for a, order in zip(away, orders)]
     next_halo = send(*second[3:])
-    packed_one, sums_one, *share_one = weight_share(normed, *first[:3], *halo, tables, (mixed_low, grad_branch))
-    share_one = [share_one[:2], share_one[2:]]
+    packed_one, sums_one, *share_one = weight_share(normed, *first[:3], *halo, tables[0], (mixed_low, grad_branch))
     if direct:
-        moving, grads, second, next_halo, normed, share_one = sync((moving, grads, second, next_halo, normed, share_one))
-        lines = [line_swap(near_halves(near, a), order, count) for (near, _), a, order in zip(grads, moving, orders)]
-        moving = swap(share_one, 0)
-    packed_two, sums_two, *share_two = weight_share(normed, *second[:3], *next_halo, tables)
-    share_two = [share_two[:2], share_two[2:]]
+        moving, second, next_halo, normed, share_one = sync((moving, second, next_halo, normed, share_one))
+        got = [parts + [m] for parts, m in zip(got, moving)]
+        away = jnp.concatenate([total([p[2:4] for p in parts]) for parts in got], axis=0)
+        away, second, next_halo, normed, share_one = sync((away, second, next_halo, normed, share_one))
+        lined = exchange(away, orders[0][3], count)
+        share_one = [share_one[0], exchange(share_one[1], orders[0][0], count)]
+    packed_two, sums_two, *share_two = weight_share(normed, *second[:3], *next_halo, tables[0])
+    plane = (orders[0][2], orders[0][1], orders[0][1] | orders[0][2])
+    line = (orders[0][4], orders[0][3], orders[0][3] | orders[0][4])
     if direct:
-        moving, share_one, share_two, packed_one, packed_two = sync((moving, share_one, share_two, packed_one, packed_two))
-        planes = [plane_swap(near_whole(near, a), order, count) for (near, _), a, order in zip(share_one, moving, orders)]
-        moving = swap(share_two, 0)
+        share_one, share_two, packed_one, packed_two = sync((share_one, share_two, packed_one, packed_two))
+        plane_one = straight(share_one, plane, count)
+        share_two = [share_two[0], exchange(share_two[1], orders[0][0], count)]
     input_grad, sums_first = input_gradient(packed_one, packed_two, tokens, middle_grad, weight_qkv, vectors)
     pick = lambda i: jnp.concatenate([s[:, i * cols : (i + 1) * cols] for s in (sums_one, sums_two)], axis=1)
+    sums = jnp.concatenate([sums_first[:2], pick(0), pick(2), sums_one[:, 3 * cols :], sums_mid[:3]], axis=0)
     sums = jnp.concatenate(
-        [sums_first[:2], pick(0), pick(2), sums_one[:, 3 * cols :], sums_mid[:3], hidden_bias_grad.reshape(-1, width)], axis=0
+        [sums.reshape(8, count, part).transpose(1, 0, 2).reshape(count, 8 * part), hidden_bias_grad.reshape(count, -1)], axis=1
     )
     if direct:
-        lines, planes, share_two, moving, input_grad, sums = sync((lines, planes, share_two, moving, input_grad, sums))
-        hidden_shard, final_shard = [line_sum(*line) for line in lines]
-        lines = [line_swap(plane_sum(*plane), order, count) for plane, order in zip(planes, orders)]
-        planes = [plane_swap(near_whole(near, a), order, count) for (near, _), a, order in zip(share_two, moving, orders)]
-        parts = [exchange(sums, bit, count) for bit in range(1, 8)]
-        lines, planes, sums, parts, hidden_shard, final_shard = sync((lines, planes, sums, parts, hidden_shard, final_shard))
-        shards_one = jnp.concatenate([line_sum(*line) for line in lines], axis=1)
-        lines = [line_swap(plane_sum(*plane), order, count) for plane, order in zip(planes, orders)]
-        sums = functools.reduce(lambda a, b: a + b, parts, sums)
-        parts = [exchange(sums, bit, count) for bit in (8, 16, 24)]
-        shards_two = jnp.concatenate([line_sum(*line) for line in lines], axis=1)
-        sums = sums + parts[0] + (parts[1] + parts[2])
+        lined, plane_one, share_one, share_two, input_grad, sums = sync((lined, plane_one, share_one, share_two, input_grad, sums))
+        got = [parts + [lined[2 * i : 2 * i + 2]] for i, parts in enumerate(got)]
+        ended = exchange(jnp.concatenate([total([p[1:2] for p in parts]) for parts in got], axis=0), orders[0][4], count)
+        plane_two = straight(share_two, plane, count)
+        share_one = [p[:4] for p in share_one] + plane_one
+        lined = exchange(total([p[2:4] for p in share_one]), orders[0][3], count)
+        sums = lax.all_to_all(sums, "dev", 0, 0, tiled=True)
+        lined, plane_two, share_two, sums, ended = sync((lined, plane_two, share_two, sums, ended))
+        share_one = [p[:2] for p in share_one] + [lined]
+        share_two = [p[:4] for p in share_two] + plane_two
+        last_one = exchange(total([p[1:2] for p in share_one]), orders[0][4], count)
+        last_two = straight(share_two, line, count)
+        finals = [total([p[0] for p in parts] + [ended[i]], f32) for i, parts in enumerate(got)]
+        hidden_shard = finals[0].transpose(1, 0, 2).reshape(part, hidden_width)
+        final_shard = finals[1].reshape(-1, width)
+        shards_one = total([p[0] for p in share_one] + [last_one[0]], f32)
+        shards_two = total([p[0] for p in share_two] + [p[0] for p in last_two], f32)
     else:
-        sums = lax.psum(sums, "dev")
-        shards_one = jnp.concatenate([scatter_whole(*s, count) for s in share_one], axis=1)
-        shards_two = jnp.concatenate([scatter_whole(*s, count) for s in share_two], axis=1)
-        hidden_shard, final_shard = [scatter_whole(*s, count) for s in grads]
+        sums = lax.all_to_all(sums, "dev", 0, 0, tiled=True)
+        shards_one, shards_two = scatter_whole(*share_one, count), scatter_whole(*share_two, count)
+        finals = [jnp.concatenate(g, axis=0) for g in grads]
+        finals[0] = finals[0].transpose(0, 2, 1, 3).reshape(width, hidden_width)
+        finals[1] = finals[1].reshape(hidden_width, width)
+        hidden_shard, final_shard = [lax.psum_scatter(p.astype(f32), "dev", scatter_dimension=0, tiled=True) for p in finals]
+    sums = jnp.sum(sums, axis=0)
+    own = [sums[i * part : (i + 1) * part] for i in range(8)]
+    own_hidden = sums[8 * part :]
     out_shard = shards_one[:, 3 * cols :]
     qkv_shard = jnp.concatenate([h[:, i * cols : (i + 1) * cols] for i in range(3) for h in (shards_one, shards_two)], axis=1)
-    own = lax.dynamic_slice_in_dim(sums[:8], me * part, part, 1)
-    own_hidden = lax.dynamic_slice_in_dim(sums[8:].reshape(-1), me * hidden_bias.shape[0], hidden_bias.shape[0], 0)
     return (
         result,
         input_grad,

time: 577 us -> 545 us (0.945)
  starting transfers between devices: 115 us -> 75.6 us
  Pallas kernels: 245 us -> 220 us
  blocking collectives: 0 us -> 19.2 us
  waiting for transfers between devices: 112 us -> 119 us
    ppermute x62 -> x30, starting transfers between devices: 91.7 us -> 43.4 us  [exchange(): return lax.ppermute(x, 'dev', [(i, i ^ bit) for i in range(count)])]
    pallas_call x3, Pallas kernels: 90.7 us -> 69.5 us  [the longest x2 44.4 us: attention_backward(): pl.pallas_call(functools.partial(bwd_kernel, images), grid_spec=pltpu.Pre...]
    all_to_all x0 -> x1, blocking collectives: none -> 19.2 us  [per_device(): sums = lax.all_to_all(sums, 'dev', 0, 0, tiled=True)]
    all_gather x1, waiting for transfers between devices: 0.01 us -> 9.37 us  [per_device(): feed = lax.all_gather(feed, 'dev', axis=0, tiled=True)]
    ppermute x3, starting transfers between devices: 19.3 us -> 28.3 us  [per_device(): lax.ppermute(right, 'dev', to_right)]
    convert_element_type x14 -> x11, other arithmetic: 25 us -> 28.5 us  [total(): functools.reduce(lambda a, b: a + b, [p.astype(f32) for p in parts])]
    ppermute x62 -> x30, waiting for transfers between devices: 112 us -> 110 us  [exchange(): return lax.ppermute(x, 'dev', [(i, i ^ bit) for i in range(count)])]
  transfers between devices with their start and end apart: 69 -> 37, of which waited for: 17 -> 13; matrix products, arithmetic and copies ran while one was open for 10% -> 7% of each run, Pallas kernels for 30% -> 28%
where the time goes in v4:
time: 545 us; the launch traced here: 538 us
  Pallas kernels  220 us (40%)
  waiting for transfers between devices  119 us (22%)
  starting transfers between devices  75.6 us (14%)
  other arithmetic  48.9 us (9%)
  local copies, waits for them, and re-layouts  29.8 us (5%)
  between operations  20.1 us (4%)
  blocking collectives  19.2 us (4%)
    ppermute x30, waiting for transfers between devices, exchange(): return lax.ppermute(x, 'dev', [(i, i ^ bit) for i in range(count)])  110 us
    pallas_call x1, Pallas kernels, feed_forward(): pl.pallas_call(feed_kernel, grid_spec=pltpu.PrefetchScalarGridSpec(num_sc...  68.4 us
    pallas_call x2, Pallas kernels, attention_backward(): pl.pallas_call(functools.partial(bwd_kernel, images), grid_spec=pltpu.Pre...  44.4 us
    ppermute x30, starting transfers between devices, exchange(): return lax.ppermute(x, 'dev', [(i, i ^ bit) for i in range(count)])  43.4 us
    pallas_call x2, Pallas kernels, weight_share(): pl.pallas_call(functools.partial(share_kernel, bool(extra)), grid_spec=pl...  31.8 us
    convert_element_type x11, other arithmetic, total(): functools.reduce(lambda a, b: a + b, [p.astype(f32) for p in parts])  28.5 us
    ppermute x3, starting transfers between devices, per_device(): lax.ppermute(right, 'dev', to_right)  28.3 us
    pallas_call x1, Pallas kernels, project(): pl.pallas_call(project_kernel, grid_spec=pltpu.PrefetchScalarGridSpec(num...  26.2 us
  transfers between devices with their start and end apart: 37, of which 13 were waited for; matrix products, arithmetic and copies ran while one was open for 7% of the time, Pallas kernels for 28%

profile of v4, /device:TPU:0, one launch (start us, length us, event | category | flops | bytes accessed | tf_op | source)
XLA Modules:
  0.0 537.6 jit_solution(17394759926109224829)
XLA Ops:
  16.1 5.1 collective-permute-start.2
  28.9 5.7 %collective-permute-done.1 = bf16[1,32,4224]{2,1,0:T(8,128)(2,1)S(1)} collective-permute-done((bf16[1,32,4224]{2,1,0:T(8,128)(2,1)S(1)}, bf16[1,32,4224]{2,1,0:T(8,128)(2,1)S(1)}, u32[]{:S(2)}, u32[]{:S(2)}) %collective-permute-start.1) | collective-permute-done | bytes 270368 | tf_op jit(solution)/shard_map/ppermute | solution.py:607
  34.6 9.7 %collective-permute-done = bf16[1,32,4224]{2,1,0:T(8,128)(2,1)S(1)} collective-permute-done((bf16[1,32,4224]{2,1,0:T(8,128)(2,1)S(1)}, bf16[1,32,4224]{2,1,0:T(8,128)(2,1)S(1)}, u32[]{:S(2)}, u32[]{:S(2)}) %collective-permute-start) | collective-permute-done | bytes 270368 | tf_op jit(solution)/shard_map/ppermute | solution.py:607
  47.5 13.0 %collective-permute-start.5 = (bf16[4,32,2048]{2,1,0:T(8,128)(2,1)}, bf16[4,32,2048]{2,1,0:T(8,128)(2,1)}, u32[]{:S(2)}, u32[]{:S(2)}) collective-permute-start(bf16[4,32,2048]{2,1,0:T(8,128)(2,1)} %pad_maximum_fusion.3), channel_id=1, source_target_pairs={{0,2},{1,3},{2,0},{3,1},{4,6},{5,7},{6,4},{7,5},{8,10},{9,11},{10,... | collective-permute-start | bytes 1572872 | tf_op jit(solution)/shard_map/ppermute | solution.py:607
  60.7 11.6 %collective-permute-done.5 = bf16[4,32,2048]{2,1,0:T(8,128)(2,1)} collective-permute-done((bf16[4,32,2048]{2,1,0:T(8,128)(2,1)}, bf16[4,32,2048]{2,1,0:T(8,128)(2,1)}, u32[]{:S(2)}, u32[]{:S(2)}) %collective-permute-start.5) | collective-permute-done | bytes 524320 | tf_op jit(solution)/shard_map/ppermute | solution.py:607
  79.5 24.8 %collective-permute-done.9 = bf16[8,32,2176]{2,1,0:T(8,128)(2,1)S(1)} collective-permute-done((bf16[8,32,2176]{2,1,0:T(8,128)(2,1)S(1)}, bf16[8,32,2176]{2,1,0:T(8,128)(2,1)S(1)}, u32[]{:S(2)}, u32[]{:S(2)}) %collective-permute-start.9) | collective-permute-done | bytes 1114144 | tf_op jit(solution)/shard_map/ppermute | solution.py:607
  116.5 3.4 pad_maximum_fusion.x
  119.9 26.2 %project.1 = (bf16[2176,1024]{1,0:T(8,128)(2,1)}, bf16[2176,1024]{1,0:T(8,128)(2,1)}, bf16[2176,1024]{1,0:T(8,128)(2,1)}, bf16[2176,1024]{1,0:T(8,128)(2,1)}, bf...) custom-call(s32[32]{0:T(128)} %broadcast_xor_fusion.1.table_one.table, ...), custom_call_target="tpu_custom_call" | custom-call | bytes 2400000 | tf_op jit(solution)/shard_map/project/pallas_call | solution.py:430
  148.0 25.0 %attention_forward.1 = (bf16[1024,1024]{1,0:T(8,128)(2,1)}, f32[8,24,768]{2,1,0:T(8,128)}) custom-call(s32[3]{0:T(128)} %pad_add_fusion.img_ref, bf16[2176,1024]{1,0:T(8,128)(2,1)} %get-tuple-element.155.q_ref, bf16[2176,1024]{1,0:T(8,128)(2,1)} %get-tuple-element.156.k_ref, bf16[2176,1024]{1,0:T(8,128)(2,1)} %get-tuple-element.157.v_ref), custom_call_target="tpu_custom_call" | custom-call | bytes 4000000 | tf_op jit(solution)/shard_map/attention_forward/pallas_call | solution.py:159
  174.6 4.7 fusion.18
  183.3 9.4 %all-gather.2.cloned.1.call-done.wide.tall = bf16[1024,8192]{1,0:T(8,128)(2,1)} async-done(((bf16[32,8192]{1,0:T(8,128)(2,1)}), bf16[1024,8192]{1,0:T(8,128)(2,1)}) %all-gather.2.cloned.1.call-update) | async-done | bytes 16777232 | tf_op jit(solution)/shard_map/all_gather | solution.py:733
  192.7 68.4 %feed_forward.1 = (bf16[1024,1024]{1,0:T(8,128)(2,1)}, f32[1024,1024]{1,0:T(8,128)}, f32[1,4096]{1,0:T(1,128)}, bf16[16,4,32,1024]{3,2,1,0:T(8,128)(2,1)}, bf16[...) custom-call(s32[32]{0:T(128)} %broadcast_xor_fusion.1.table_one.table, ...), custom_call_target="tpu_custom_call" | custom-call | bytes 7000000 | tf_op jit(solution)/shard_map/feed_forward/pallas_call | solution.py:354
  261.7 10.2 %branch_gradient.1 = (f32[1024,1024]{1,0:T(8,128)}, bf16[1024,1024]{1,0:T(8,128)(2,1)}, bf16[1024,1024]{1,0:T(8,128)(2,1)}, f32[8,1024]{1,0:T(8,128)}) custom-call(f32[1024,1024]{1,0:T(8,128)} %get-tuple-element.167.grad, f32[1024,1024]{1,0:T(8,128)} %copy-done, bf16[1024,1024]{1,0:T(8,128)(2,1)} %cot.3, bf16[1024,1024]{1,0:T(8,128)(2,1)} %get-tuple-element.159.weight_out, ...), custom_call_target="tpu_custom_call" | custom-call | bytes 1000000 | tf_op jit(solution)/shard_map/branch_gradient/pallas_call | solution.py:576
  274.7 5.8 %add_convert_fusion = (bf16[8,4,32,1024]{3,2,1,0:T(8,128)(2,1)}, bf16[8,4,32,1024]{3,2,1,0:T(8,128)(2,1)}) fusion(bf16[16,4,32,1024]{3,2,1,0:T(8,128)(2,1)} %collective-permute-done.12, bf16[16,4,32,1024]{3,2,1,0:T(8,128)(2,1)} %bitcast.40, bf16[16,4,32,1024]{3,2,1,0:T(8,128)(2,1)} %collective-permute-done.11, bf16[16,4,32,1024]{3,2,1,0:T(8,128)(2,1)} %get-tuple-element.169), kind=kLoop, calls=%fused_computation.1 | loop fusion | flops 8388608 | bytes 12582912 | tf_op jit(solution)/shard_map/convert_element_type | solution.py:633
  282.6 22.1 %attention_backward.2 = (bf16[1024,512]{1,0:T(8,128)(2,1)}, f32[1024,512]{1,0:T(8,128)}, f32[1024,512]{1,0:T(8,128)}, bf16[2,576,512]{2,1,0:T(8,128)(2,1)}, bf16[2,576,512]{2,1,0:T(8,128)(2,1)}) custom-call(s32[3]{0:T(128)} %pad_add_fusion.img_ref, bf16[2176,1024]{1,0:T(8,128)(2,1)} %get-tuple-element.155.q_ref, ...), custom_call_target="tpu_custom_call" | custom-call | bytes 2600000 | tf_op jit(solution)/shard_map/attention_backward/pallas_call | solution.py:243
  305.9 7.2 %collective-permute-start.15 = (bf16[2,576,512]{2,1,0:T(8,128)(2,1)}, bf16[2,576,512]{2,1,0:T(8,128)(2,1)}, u32[]{:S(2)}, u32[]{:S(2)}) collective-permute-start(bf16[2,576,512]{2,1,0:T(8,128)(2,1)} %get-tuple-element.187), channel_id=1, source_target_pairs={{0,1},{1,2},{2,3},{3,4},{4,5},{5,6},{6,7},{7,8},{8,9},{9,10},{10,1... | collective-permute-start | bytes 3538952 | tf_op jit(solution)/shard_map/ppermute | solution.py:706
  313.1 22.4 %attention_backward.3 = (bf16[1024,512]{1,0:T(8,128)(2,1)}, f32[1024,512]{1,0:T(8,128)}, f32[1024,512]{1,0:T(8,128)}, bf16[2,576,512]{2,1,0:T(8,128)(2,1)}, bf16[2,576,512]{2,1,0:T(8,128)(2,1)}) custom-call(s32[3]{0:T(128)} %pad_add_fusion.img_ref, bf16[2176,1024]{1,0:T(8,128)(2,1)} %get-tuple-element.155.q_ref, ...), custom_call_target="tpu_custom_call" | custom-call | bytes 2600000 | tf_op jit(solution)/shard_map/attention_backward/pallas_call | solution.py:243
  335.5 6.1 %collective-permute-done.14 = bf16[8,4,32,1024]{3,2,1,0:T(8,128)(2,1)} collective-permute-done((bf16[8,4,32,1024]{3,2,1,0:T(8,128)(2,1)}, bf16[8,4,32,1024]{3,2,1,0:T(8,128)(2,1)}, u32[]{:S(2)}, u32[]{:S(2)}) %collective-permute-start.14) | collective-permute-done | bytes 2097184 | tf_op jit(solution)/shard_map/ppermute | solution.py:607
  341.6 3.2 add_convert_fusion.4
  344.8 3.5 add_convert_fusion.3
  349.5 18.0 %collective-permute-start.19 = (bf16[2,576,512]{2,1,0:T(8,128)(2,1)}, bf16[2,576,512]{2,1,0:T(8,128)(2,1)}, u32[]{:S(2)}, u32[]{:S(2)}) collective-permute-start(bf16[2,576,512]{2,1,0:T(8,128)(2,1)} %get-tuple-element.216), channel_id=1, source_target_pairs={{0,1},{1,2},{2,3},{3,4},{4,5},{5,6},{6,7},{7,8},{8,9},{9,10},{10,1... | collective-permute-start | bytes 3538952 | tf_op jit(solution)/shard_map/ppermute | solution.py:706
  369.0 18.6 %weight_share.2 = (bf16[1024,1536]{1,0:T(8,128)(2,1)}, f32[1,2560]{1,0:T(1,128)}, bf16[16,32,2560]{2,1,0:T(8,128)(2,1)}, bf16[16,32,2560]{2,1,0:T(8,128)(2,1)}) custom-call(s32[32]{0:T(128)} %broadcast_xor_fusion.1.table_one.table, bf16[2176,1024]{1,0:T(8,128)(2,1)} %get-tuple-element.239.normed, bf16[1024,512]{1,0:T(8,128)(2,1)} %get-tuple-element.218.dq, ...), custom_call_target="tpu_custom_call" | custom-call | bytes 1000000 | tf_op jit(solution)/shard_map/weight_share/pallas_call | solution.py:515
  387.6 24.7 %collective-permute-done.17 = bf16[4,4,32,1024]{3,2,1,0:T(8,128)(2,1)} collective-permute-done((bf16[4,4,32,1024]{3,2,1,0:T(8,128)(2,1)}, bf16[4,4,32,1024]{3,2,1,0:T(8,128)(2,1)}, u32[]{:S(2)}, u32[]{:S(2)}) %collective-permute-start.17) | collective-permute-done | bytes 1048608 | tf_op jit(solution)/shard_map/ppermute | solution.py:607
  417.5 3.4 collective-permute-start.22
  420.9 13.2 %weight_share.3 = (bf16[1024,1536]{1,0:T(8,128)(2,1)}, f32[1,1536]{1,0:T(1,128)}, bf16[16,32,1536]{2,1,0:T(8,128)(2,1)}, bf16[16,32,1536]{2,1,0:T(8,128)(2,1)}) custom-call(s32[32]{0:T(128)} %broadcast_xor_fusion.1.table_one.table, bf16[2176,1024]{1,0:T(8,128)(2,1)} %get-tuple-element.239.normed, bf16[1024,512]{1,0:T(8,128)(2,1)} %get-tuple-element.240.dq, ...), custom_call_target="tpu_custom_call" | custom-call | bytes 700000 | tf_op jit(solution)/shard_map/weight_share/pallas_call | solution.py:515
  441.4 14.0 %input_gradient.1 = (bf16[1024,1024]{1,0:T(8,128)(2,1)}, f32[8,1024]{1,0:T(8,128)}) custom-call(bf16[1024,1536]{1,0:T(8,128)(2,1)} %get-tuple-element.253.one, bf16[1024,1536]{1,0:T(8,128)(2,1)} %get-tuple-element.254.two, bf16[1024,1024]{1,0:T(8,128)(2,1)} %tokens.1, f32[1024,1024]{1,0:T(8,128)} %get-tuple-element.255.middle_grad, ...), custom_call_target="tpu_custom_call" | custom-call | bytes 1200000 | tf_op jit(solution)/shard_map/input_gradient/pallas_call | solution.py:576
  456.5 3.6 collective-permute-done.21
  460.2 9.7 %collective-permute-done.24 = bf16[4,32,2560]{2,1,0:T(8,128)(2,1)} collective-permute-done((bf16[4,32,2560]{2,1,0:T(8,128)(2,1)}, bf16[4,32,2560]{2,1,0:T(8,128)(2,1)}, u32[]{:S(2)}, u32[]{:S(2)}) %collective-permute-start.24) | collective-permute-done | bytes 655392 | tf_op jit(solution)/shard_map/ppermute | solution.py:607
  482.0 19.2 %all_to_all.12 = f32[32,1,384]{2,1,0:T(1,128)S(1)} all-to-all(f32[32,1,384]{2,1,0:T(1,128)S(1)} %copy.66), channel_id=1, replica_groups=mesh['dev'=32] {'dev'}, dimensions={0} | all-to-all | bytes 98304 | tf_op jit(solution)/shard_map/all_to_all | solution.py:804
  501.3 3.4 add_add_fusion.1
  515.2 4.1 collective-permute-done.33
  521.4 6.4 %collective-permute-done.32 = bf16[1,32,2560]{2,1,0:T(8,128)(2,1)S(1)} collective-permute-done((bf16[1,32,2560]{2,1,0:T(8,128)(2,1)}, bf16[1,32,2560]{2,1,0:T(8,128)(2,1)S(1)}, u32[]{:S(2)}, u32[]{:S(2)}) %collective-permute-start.32) | collective-permute-done | bytes 163872 | tf_op jit(solution)/shard_map/ppermute | solution.py:607
  (202 shorter events, 91.9 us)
Async XLA Ops:
  7.2 185.5 %all-gather.2.cloned.1.call-start = ((), (), s32[]{:S(2)}) async-start(), calls=%async_computation.1 | async-start | bytes 17301504 | tf_op jit(solution)/shard_map/all_gather | solution.py:733
  21.2 13.4 %collective-permute-start.1 = (bf16[1,32,4224]{2,1,0:T(8,128)(2,1)S(1)}, bf16[1,32,4224]{2,1,0:T(8,128)(2,1)S(1)}, u32[]{:S(2)}, u32[]{:S(2)}) collective-permute-start(bf16[1,32,4224]{2,1,0:T(8,128)(2,1)S(1)} %bitcast.49), channel_id=1, source_target_pairs={{0,8},{1,9},{2,10},{3,11},{4,12},{5,13},{6,14},{7,15},{8,0},{9,1},... | collective-permute-start | bytes 811016 | tf_op jit(solution)/shard_map/ppermute | solution.py:607
  21.2 23.1 %collective-permute-start = (bf16[1,32,4224]{2,1,0:T(8,128)(2,1)S(1)}, bf16[1,32,4224]{2,1,0:T(8,128)(2,1)S(1)}, u32[]{:S(2)}, u32[]{:S(2)}) collective-permute-start(bf16[1,32,4224]{2,1,0:T(8,128)(2,1)S(1)} %bitcast.50), channel_id=1, source_target_pairs={{0,16},{1,17},{2,18},{3,19},{4,20},{5,21},{6,22},{7,23},{8,24},{9,... | collective-permute-start | bytes 811016 | tf_op jit(solution)/shard_map/ppermute | solution.py:607
  23.7 20.6 %collective-permute-start.4 = (bf16[576,1024]{1,0:T(8,128)(2,1)S(1)}, bf16[576,1024]{1,0:T(8,128)(2,1)S(1)}, u32[]{:S(2)}, u32[]{:S(2)}) collective-permute-start(bf16[576,1024]{1,0:T(8,128)(2,1)S(1)} %get-tuple-element.293), channel_id=1, source_target_pairs={{1,0},{2,1},{3,2},{4,3},{5,4},{6,5},{7,6},{8,7},{9,8},{10,9},{11,1... | collective-permute-start | bytes 3538952 | tf_op jit(solution)/shard_map/ppermute | solution.py:706
  25.0 19.3 %collective-permute-start.3 = (bf16[576,1024]{1,0:T(8,128)(2,1)S(1)}, bf16[576,1024]{1,0:T(8,128)(2,1)S(1)}, u32[]{:S(2)}, u32[]{:S(2)}) collective-permute-start(bf16[576,1024]{1,0:T(8,128)(2,1)S(1)} %get-tuple-element.294), channel_id=1, source_target_pairs={{0,1},{1,2},{2,3},{3,4},{4,5},{5,6},{6,7},{7,8},{8,9},{9,10},{10,1... | collective-permute-start | bytes 3538952 | tf_op jit(solution)/shard_map/ppermute | solution.py:706
  47.5 24.8 %collective-permute-start.5 = (bf16[4,32,2048]{2,1,0:T(8,128)(2,1)}, bf16[4,32,2048]{2,1,0:T(8,128)(2,1)}, u32[]{:S(2)}, u32[]{:S(2)}) collective-permute-start(bf16[4,32,2048]{2,1,0:T(8,128)(2,1)} %pad_maximum_fusion.3), channel_id=1, source_target_pairs={{0,2},{1,3},{2,0},{3,1},{4,6},{5,7},{6,4},{7,5},{8,10},{9,11},{10,... | collective-permute-start | bytes 1572872 | tf_op jit(solution)/shard_map/ppermute | solution.py:607
  60.6 13.6 %collective-permute-start.6 = (bf16[4,32,2176]{2,1,0:T(8,128)(2,1)S(1)}, bf16[4,32,2176]{2,1,0:T(8,128)(2,1)}, u32[]{:S(2)}, u32[]{:S(2)}) collective-permute-start(bf16[4,32,2176]{2,1,0:T(8,128)(2,1)S(1)} %pad_maximum_fusion.2), channel_id=1, source_target_pairs={{0,4},{1,5},{2,6},{3,7},{4,0},{5,1},{6,2},{7,3},{8,12},{9,13},{10,... | collective-permute-start | bytes 1671176 | tf_op jit(solution)/shard_map/ppermute | solution.py:607
  75.3 29.0 %collective-permute-start.9 = (bf16[8,32,2176]{2,1,0:T(8,128)(2,1)S(1)}, bf16[8,32,2176]{2,1,0:T(8,128)(2,1)S(1)}, u32[]{:S(2)}, u32[]{:S(2)}) collective-permute-start(bf16[8,32,2176]{2,1,0:T(8,128)(2,1)S(1)} %constant_dynamic-update-slice_fusion.13), channel_id=1, source_target_pairs={{0,2},{1,3},{2,0},{3,1},{4,6},{5,7},{6,4},{7,5},{8,10},{9,11},{10,... | collective-permute-start | bytes 3342344 | tf_op jit(solution)/shard_map/ppermute | solution.py:607
  75.9 29.6 %collective-permute-start.7 = (bf16[8,32,2048]{2,1,0:T(8,128)(2,1)}, bf16[8,32,2048]{2,1,0:T(8,128)(2,1)S(1)}, u32[]{:S(2)}, u32[]{:S(2)}) collective-permute-start(bf16[8,32,2048]{2,1,0:T(8,128)(2,1)} %constant_dynamic-update-slice_fusion.8), channel_id=1, source_target_pairs={{0,4},{1,5},{2,6},{3,7},{4,0},{5,1},{6,2},{7,3},{8,12},{9,13},{10,... | collective-permute-start | bytes 3145736 | tf_op jit(solution)/shard_map/ppermute | solution.py:607
  105.4 14.4 %collective-permute-start.10 = (bf16[16,32,2176]{2,1,0:T(8,128)(2,1)}, bf16[16,32,2176]{2,1,0:T(8,128)(2,1)}, u32[]{:S(2)}, u32[]{:S(2)}) collective-permute-start(bf16[16,32,2176]{2,1,0:T(8,128)(2,1)} %constant_dynamic-update-slice_fusion.24.two_near), channel_id=1, source_target_pairs={{0,1},{1,0},{2,3},{3,2},{4,5},{5,4},{6,7},{7,6},{8,9},{9,8},{10,11... | collective-permute-start | bytes 6684680 | tf_op jit(solution)/shard_map/ppermute | solution.py:607
  106.5 13.3 %collective-permute-start.8 = (bf16[16,32,2048]{2,1,0:T(8,128)(2,1)}, bf16[16,32,2048]{2,1,0:T(8,128)(2,1)}, u32[]{:S(2)}, u32[]{:S(2)}) collective-permute-start(bf16[16,32,2048]{2,1,0:T(8,128)(2,1)} %constant_dynamic-update-slice_fusion.22.one_near), channel_id=1, source_target_pairs={{0,1},{1,0},{2,3},{3,2},{4,5},{5,4},{6,7},{7,6},{8,9},{9,8},{10,11... | collective-permute-start | bytes 6291464 | tf_op jit(solution)/shard_map/ppermute | solution.py:607
  261.5 13.2 %collective-permute-start.12 = (bf16[16,4,32,1024]{3,2,1,0:T(8,128)(2,1)}, bf16[16,4,32,1024]{3,2,1,0:T(8,128)(2,1)}, u32[]{:S(2)}, u32[]{:S(2)}) collective-permute-start(bf16[16,4,32,1024]{3,2,1,0:T(8,128)(2,1)} %bitcast.67), channel_id=1, source_target_pairs={{0,1},{1,0},{2,3},{3,2},{4,5},{5,4},{6,7},{7,6},{8,9},{9,8},{10,11... | collective-permute-start | bytes 12582920 | tf_op jit(solution)/shard_map/ppermute | solution.py:607
  280.5 55.0 %collective-permute-start.13 = (bf16[8,4,32,1024]{3,2,1,0:T(8,128)(2,1)}, bf16[8,4,32,1024]{3,2,1,0:T(8,128)(2,1)S(1)}, u32[]{:S(2)}, u32[]{:S(2)}) collective-permute-start(bf16[8,4,32,1024]{3,2,1,0:T(8,128)(2,1)} %get-tuple-element.174), channel_id=1, source_target_pairs={{0,4},{1,5},{2,6},{3,7},{4,0},{5,1},{6,2},{7,3},{8,12},{9,13},{10,... | collective-permute-start | bytes 6291464 | tf_op jit(solution)/shard_map/ppermute | solution.py:607
  282.0 59.5 %collective-permute-start.14 = (bf16[8,4,32,1024]{3,2,1,0:T(8,128)(2,1)}, bf16[8,4,32,1024]{3,2,1,0:T(8,128)(2,1)}, u32[]{:S(2)}, u32[]{:S(2)}) collective-permute-start(bf16[8,4,32,1024]{3,2,1,0:T(8,128)(2,1)} %get-tuple-element.175), channel_id=1, source_target_pairs={{0,2},{1,3},{2,0},{3,1},{4,6},{5,7},{6,4},{7,5},{8,10},{9,11},{10,... | collective-permute-start | bytes 6291464 | tf_op jit(solution)/shard_map/ppermute | solution.py:607
  304.6 30.8 %collective-permute-start.16 = (bf16[2,576,512]{2,1,0:T(8,128)(2,1)}, bf16[2,576,512]{2,1,0:T(8,128)(2,1)S(1)}, u32[]{:S(2)}, u32[]{:S(2)}) collective-permute-start(bf16[2,576,512]{2,1,0:T(8,128)(2,1)} %get-tuple-element.186), channel_id=1, source_target_pairs={{1,0},{2,1},{3,2},{4,3},{5,4},{6,5},{7,6},{8,7},{9,8},{10,9},{11,1... | collective-permute-start | bytes 3538952 | tf_op jit(solution)/shard_map/ppermute | solution.py:706
  305.9 29.6 %collective-permute-start.15 = (bf16[2,576,512]{2,1,0:T(8,128)(2,1)}, bf16[2,576,512]{2,1,0:T(8,128)(2,1)}, u32[]{:S(2)}, u32[]{:S(2)}) collective-permute-start(bf16[2,576,512]{2,1,0:T(8,128)(2,1)} %get-tuple-element.187), channel_id=1, source_target_pairs={{0,1},{1,2},{2,3},{3,4},{4,5},{5,6},{6,7},{7,8},{8,9},{9,10},{10,1... | collective-permute-start | bytes 3538952 | tf_op jit(solution)/shard_map/ppermute | solution.py:706
  348.3 64.1 %collective-permute-start.20 = (bf16[2,576,512]{2,1,0:T(8,128)(2,1)}, bf16[2,576,512]{2,1,0:T(8,128)(2,1)S(1)}, u32[]{:S(2)}, u32[]{:S(2)}) collective-permute-start(bf16[2,576,512]{2,1,0:T(8,128)(2,1)} %get-tuple-element.215), channel_id=1, source_target_pairs={{1,0},{2,1},{3,2},{4,3},{5,4},{6,5},{7,6},{8,7},{9,8},{10,9},{11,1... | collective-permute-start | bytes 3538952 | tf_op jit(solution)/shard_map/ppermute | solution.py:706
  349.5 62.8 %collective-permute-start.19 = (bf16[2,576,512]{2,1,0:T(8,128)(2,1)}, bf16[2,576,512]{2,1,0:T(8,128)(2,1)}, u32[]{:S(2)}, u32[]{:S(2)}) collective-permute-start(bf16[2,576,512]{2,1,0:T(8,128)(2,1)} %get-tuple-element.216), channel_id=1, source_target_pairs={{0,1},{1,2},{2,3},{3,4},{4,5},{5,6},{6,7},{7,8},{8,9},{9,10},{10,1... | collective-permute-start | bytes 3538952 | tf_op jit(solution)/shard_map/ppermute | solution.py:706
  367.6 44.7 %collective-permute-start.17 = (bf16[4,4,32,1024]{3,2,1,0:T(8,128)(2,1)}, bf16[4,4,32,1024]{3,2,1,0:T(8,128)(2,1)}, u32[]{:S(2)}, u32[]{:S(2)}) collective-permute-start(bf16[4,4,32,1024]{3,2,1,0:T(8,128)(2,1)} %add_convert_fusion.4), channel_id=1, source_target_pairs={{0,2},{1,3},{2,0},{3,1},{4,6},{5,7},{6,4},{7,5},{8,10},{9,11},{10,... | collective-permute-start | bytes 3145736 | tf_op jit(solution)/shard_map/ppermute | solution.py:607
  368.3 44.0 %collective-permute-start.18 = (bf16[4,4,32,1024]{3,2,1,0:T(8,128)(2,1)}, bf16[4,4,32,1024]{3,2,1,0:T(8,128)(2,1)}, u32[]{:S(2)}, u32[]{:S(2)}) collective-permute-start(bf16[4,4,32,1024]{3,2,1,0:T(8,128)(2,1)} %add_convert_fusion.3), channel_id=1, source_target_pairs={{0,4},{1,5},{2,6},{3,7},{4,0},{5,1},{6,2},{7,3},{8,12},{9,13},{10,... | collective-permute-start | bytes 3145736 | tf_op jit(solution)/shard_map/ppermute | solution.py:607
  417.5 16.6 %collective-permute-start.22 = (bf16[16,32,2560]{2,1,0:T(8,128)(2,1)}, bf16[16,32,2560]{2,1,0:T(8,128)(2,1)}, u32[]{:S(2)}, u32[]{:S(2)}) collective-permute-start(bf16[16,32,2560]{2,1,0:T(8,128)(2,1)} %get-tuple-element.238), channel_id=1, source_target_pairs={{0,1},{1,0},{2,3},{3,2},{4,5},{5,4},{6,7},{7,6},{8,9},{9,8},{10,11... | collective-permute-start | bytes 7864328 | tf_op jit(solution)/shard_map/ppermute | solution.py:607
  434.1 35.7 %collective-permute-start.26 = (bf16[16,32,1536]{2,1,0:T(8,128)(2,1)}, bf16[16,32,1536]{2,1,0:T(8,128)(2,1)}, u32[]{:S(2)}, u32[]{:S(2)}) collective-permute-start(bf16[16,32,1536]{2,1,0:T(8,128)(2,1)} %get-tuple-element.252), channel_id=1, source_target_pairs={{0,1},{1,0},{2,3},{3,2},{4,5},{5,4},{6,7},{7,6},{8,9},{9,8},{10,11... | collective-permute-start | bytes 4718600 | tf_op jit(solution)/shard_map/ppermute | solution.py:607
  434.3 25.8 %collective-permute-start.21 = (bf16[4,4,32,1024]{3,2,1,0:T(8,128)(2,1)}, bf16[4,4,32,1024]{3,2,1,0:T(8,128)(2,1)}, u32[]{:S(2)}, u32[]{:S(2)}) collective-permute-start(bf16[4,4,32,1024]{3,2,1,0:T(8,128)(2,1)} %pad_maximum_fusion.1), channel_id=1, source_target_pairs={{0,8},{1,9},{2,10},{3,11},{4,12},{5,13},{6,14},{7,15},{8,0},{9,1},... | collective-permute-start | bytes 3145736 | tf_op jit(solution)/shard_map/ppermute | solution.py:607
  437.9 22.3 %collective-permute-start.25 = (bf16[4,32,2560]{2,1,0:T(8,128)(2,1)}, bf16[4,32,2560]{2,1,0:T(8,128)(2,1)S(1)}, u32[]{:S(2)}, u32[]{:S(2)}) collective-permute-start(bf16[4,32,2560]{2,1,0:T(8,128)(2,1)} %get-tuple-element.284), channel_id=1, source_target_pairs={{0,6},{1,7},{2,4},{3,5},{4,2},{5,3},{6,0},{7,1},{8,14},{9,15},{10,... | collective-permute-start | bytes 1966088 | tf_op jit(solution)/shard_map/ppermute | solution.py:607
  440.1 29.7 %collective-permute-start.24 = (bf16[4,32,2560]{2,1,0:T(8,128)(2,1)}, bf16[4,32,2560]{2,1,0:T(8,128)(2,1)}, u32[]{:S(2)}, u32[]{:S(2)}) collective-permute-start(bf16[4,32,2560]{2,1,0:T(8,128)(2,1)} %get-tuple-element.285), channel_id=1, source_target_pairs={{0,4},{1,5},{2,6},{3,7},{4,0},{5,1},{6,2},{7,3},{8,12},{9,13},{10,... | collective-permute-start | bytes 1966088 | tf_op jit(solution)/shard_map/ppermute | solution.py:607
  440.1 29.7 %collective-permute-start.23 = (bf16[4,32,2560]{2,1,0:T(8,128)(2,1)}, bf16[4,32,2560]{2,1,0:T(8,128)(2,1)}, u32[]{:S(2)}, u32[]{:S(2)}) collective-permute-start(bf16[4,32,2560]{2,1,0:T(8,128)(2,1)} %get-tuple-element.286), channel_id=1, source_target_pairs={{0,2},{1,3},{2,0},{3,1},{4,6},{5,7},{6,4},{7,5},{8,10},{9,11},{10,... | collective-permute-start | bytes 1966088 | tf_op jit(solution)/shard_map/ppermute | solution.py:607
  472.1 29.1 %collective-permute-start.31 = (bf16[2,4,32,1024]{3,2,1,0:T(8,128)(2,1)S(1)}, bf16[2,4,32,1024]{3,2,1,0:T(8,128)(2,1)S(1)}, u32[]{:S(2)}, u32[]{:S(2)}) collective-permute-start(bf16[2,4,32,1024]{3,2,1,0:T(8,128)(2,1)S(1)} %pad_maximum_fusion.4), channel_id=1, source_target_pairs={{0,16},{1,17},{2,18},{3,19},{4,20},{5,21},{6,22},{7,23},{8,24},{9,... | collective-permute-start | bytes 1572872 | tf_op jit(solution)/shard_map/ppermute | solution.py:607
  475.4 25.8 %collective-permute-start.30 = (bf16[4,32,1536]{2,1,0:T(8,128)(2,1)S(1)}, bf16[4,32,1536]{2,1,0:T(8,128)(2,1)S(1)}, u32[]{:S(2)}, u32[]{:S(2)}) collective-permute-start(bf16[4,32,1536]{2,1,0:T(8,128)(2,1)S(1)} %get-tuple-element.290), channel_id=1, source_target_pairs={{0,6},{1,7},{2,4},{3,5},{4,2},{5,3},{6,0},{7,1},{8,14},{9,15},{10,... | collective-permute-start | bytes 1179656 | tf_op jit(solution)/shard_map/ppermute | solution.py:607
  477.2 24.0 %collective-permute-start.29 = (bf16[4,32,1536]{2,1,0:T(8,128)(2,1)S(1)}, bf16[4,32,1536]{2,1,0:T(8,128)(2,1)S(1)}, u32[]{:S(2)}, u32[]{:S(2)}) collective-permute-start(bf16[4,32,1536]{2,1,0:T(8,128)(2,1)S(1)} %get-tuple-element.291), channel_id=1, source_target_pairs={{0,4},{1,5},{2,6},{3,7},{4,0},{5,1},{6,2},{7,3},{8,12},{9,13},{10,... | collective-permute-start | bytes 1179656 | tf_op jit(solution)/shard_map/ppermute | solution.py:607
  478.2 23.0 %collective-permute-start.28 = (bf16[4,32,1536]{2,1,0:T(8,128)(2,1)S(1)}, bf16[4,32,1536]{2,1,0:T(8,128)(2,1)S(1)}, u32[]{:S(2)}, u32[]{:S(2)}) collective-permute-start(bf16[4,32,1536]{2,1,0:T(8,128)(2,1)S(1)} %get-tuple-element.292), channel_id=1, source_target_pairs={{0,2},{1,3},{2,0},{3,1},{4,6},{5,7},{6,4},{7,5},{8,10},{9,11},{10,... | collective-permute-start | bytes 1179656 | tf_op jit(solution)/shard_map/ppermute | solution.py:607
  480.4 20.8 %collective-permute-start.27 = (bf16[2,32,2560]{2,1,0:T(8,128)(2,1)S(1)}, bf16[2,32,2560]{2,1,0:T(8,128)(2,1)S(1)}, u32[]{:S(2)}, u32[]{:S(2)}) collective-permute-start(bf16[2,32,2560]{2,1,0:T(8,128)(2,1)S(1)} %add_convert_fusion.13), channel_id=1, source_target_pairs={{0,8},{1,9},{2,10},{3,11},{4,12},{5,13},{6,14},{7,15},{8,0},{9,1},... | collective-permute-start | bytes 983048 | tf_op jit(solution)/shard_map/ppermute | solution.py:607
  513.1 14.7 %collective-permute-start.32 = (bf16[1,32,2560]{2,1,0:T(8,128)(2,1)}, bf16[1,32,2560]{2,1,0:T(8,128)(2,1)S(1)}, u32[]{:S(2)}, u32[]{:S(2)}) collective-permute-start(bf16[1,32,2560]{2,1,0:T(8,128)(2,1)} %add_convert_fusion.16), channel_id=1, source_target_pairs={{0,16},{1,17},{2,18},{3,19},{4,20},{5,21},{6,22},{7,23},{8,24},{9,... | collective-permute-start | bytes 491528 | tf_op jit(solution)/shard_map/ppermute | solution.py:607
  (30 other events, 441.9 us)
Sparse Core Ops, SparseCore 0:
  75.4 117.2 all-gather.1

commit v5 on v4

--- a/solution.py
+++ b/solution.py
@@ -268,13 +268,12 @@
 
 
 def feed_kernel(
-    table, home, normed, cot, middle, bias_final, wide, tall, bias_hidden,
-    result, grad_normed, bias_grad, hidden_near, hidden_far, final_near, final_far,
-    total, normed_t, final, active, grad_pre, hidden_grad, final_grad, sems,
+    table, normed, cot, middle, bias_final, wide, tall, bias_hidden,
+    result, grad_normed, bias_grad, hidden_near, hidden_far, active,
+    total, normed_t, final, grad_pre, hidden_grad,
 ):
     step = pl.program_id(0)
     tiles = pl.num_programs(0)
-    slot = lax.rem(step, 2)
     rows, width = normed.shape
     half, _, piece, _ = hidden_near.shape
     devices = tall.shape[0] // 32
@@ -308,6 +307,18 @@
         else:
             hidden_far[place - half, 0] = rows_of
 
+    @pl.when(step == tiles - 1)
+    def _():
+        result[...] = total[...].astype(bf16)
+
+
+def final_kernel(home, active, cot, final_near, final_far, final_grad, sems):
+    step = pl.program_id(0)
+    tiles = pl.num_programs(0)
+    slot = lax.rem(step, 2)
+    half, depth, width = final_near.shape
+    devices = FT // depth
+
     def copy_out(slot, d, target):
         return pltpu.make_async_copy(final_grad.at[slot, d], target, sems.at[slot, d])
 
@@ -333,12 +344,36 @@
 
     @pl.when(step == tiles - 1)
     def _():
-        result[...] = total[...].astype(bf16)
-        wait_out(1 - slot)
-        wait_out(slot)
-
-
-def feed_forward(normed, cot, middle, bias_final, feed, bias_hidden, table, home):
+        for d in range(devices):
+            copy_out(1 - slot, d, final_near.at[0]).wait()
+            copy_out(slot, d, final_near.at[0]).wait()
+
+
+def final_share(active, cot, home):
+    rows, width = cot.shape
+    units = active.shape[1]
+    depth = units // PIECES
+    piece = jax.ShapeDtypeStruct((PIECES // 2, depth, width), bf16)
+    return pl.pallas_call(
+        final_kernel,
+        grid_spec=pltpu.PrefetchScalarGridSpec(
+            num_scalar_prefetch=1,
+            grid=(units // FT,),
+            in_specs=[
+                pl.BlockSpec((rows, FT), lambda t, *_: (0, t)),
+                pl.BlockSpec((rows, width), lambda t, *_: (0, 0), pipeline_mode=pl.Buffered(1)),
+            ],
+            out_specs=[pl.BlockSpec(memory_space=pl.ANY)] * 2,
+            scratch_shapes=[pltpu.VMEM((2, FT // depth, depth, width), bf16), pltpu.SemaphoreType.DMA((2, FT // depth))],
+        ),
+        out_shape=[piece, piece],
+        compiler_params=pltpu.CompilerParams(vmem_limit_bytes=VMEM, dimension_semantics=("arbitrary",)),
+        cost_estimate=spent(14),
+        name="final_share",
+    )(home, active, cot)
+
+
+def feed_forward(normed, cot, middle, bias_final, feed, bias_hidden, table):
     rows, width = normed.shape
     units = bias_hidden.shape[1]
     whole = lambda *shape: pl.BlockSpec(shape, lambda t, *_: (0,) * len(shape), pipeline_mode=pl.Buffered(1))
@@ -348,13 +383,12 @@
     line = pl.BlockSpec((1, FT), lambda t, *_: (0, t))
     square = whole(rows, width)
     wide_piece = sds((PIECES // 2, units // width, width // PIECES, width), bf16)
-    tall_piece = sds((PIECES // 2, depth, width), bf16)
     blocks = width // FT
     edge = pl.BlockSpec((PIECES // 2, 1, width // PIECES, FT), lambda t, *_: (0, t // blocks, 0, t % blocks))
     return pl.pallas_call(
         feed_kernel,
         grid_spec=pltpu.PrefetchScalarGridSpec(
-            num_scalar_prefetch=2,
+            num_scalar_prefetch=1,
             grid=(units // FT,),
             in_specs=[
                 square, square, square, whole(1, width),
@@ -362,21 +396,20 @@
                 pl.BlockSpec((devices * 32, 4 * width), lambda t, *_: (t, 1)),
                 line,
             ],
-            out_specs=[square, square, line, edge, edge] + [pl.BlockSpec(memory_space=pl.ANY)] * 2,
+            out_specs=[square, square, line, edge, edge, pl.BlockSpec((rows, FT), lambda t, *_: (0, t))],
             scratch_shapes=[
                 pltpu.VMEM((rows, width), f32), pltpu.VMEM((width, rows), bf16), pltpu.VMEM((FT, width), bf16),
-                pltpu.VMEM((rows, FT), bf16), pltpu.VMEM((rows, FT), bf16), pltpu.VMEM((width, FT), f32),
-                pltpu.VMEM((2, devices, depth, width), bf16), pltpu.SemaphoreType.DMA((2, devices)),
+                pltpu.VMEM((rows, FT), bf16), pltpu.VMEM((width, FT), f32),
             ],
         ),
         out_shape=[
             sds((rows, width), bf16), sds((rows, width), f32), sds((1, units), f32),
-            wide_piece, wide_piece, tall_piece, tall_piece,
+            wide_piece, wide_piece, sds((rows, units), bf16),
         ],
         compiler_params=pltpu.CompilerParams(vmem_limit_bytes=VMEM, dimension_semantics=("arbitrary",)),
-        cost_estimate=spent(70),
+        cost_estimate=spent(57),
         name="feed_forward",
-    )(table, home, normed, cot, middle, bias_final, feed, feed, bias_hidden)
+    )(table, normed, cot, middle, bias_final, feed, feed, bias_hidden)
 
 
 def project_kernel(
@@ -697,8 +730,8 @@
     half = PIECES // 2
     unit = hidden_width // PIECES
     orders = bit_orders(PIECES)
-    tables = [owners(order, me if direct else 0) for order in orders]
-    home = places(orders[1], me if direct else 0)
+    tables = [owners(order, me) if direct else jnp.arange(PIECES, dtype=jnp.int32) for order in orders]
+    home = places(orders[0], me) if direct else jnp.arange(PIECES, dtype=jnp.int32)
     sync = lax.optimization_barrier
     img = image_starts(segment_ids, me, rows)
     to_right = [(i, i + 1) for i in range(count - 1)]
@@ -748,19 +781,31 @@
     mixed_low, totals = attention_forward(img, queries, key_rows, value_rows, 0, pairs)
     middle = inputs + (jnp.dot(mixed_low, weight_out, preferred_element_type=f32) + bias_out)
     normed_two = layer_norm(middle, gain_two, bias_two).astype(bf16)
-    result, grad_normed_two, hidden_bias_grad, *grads = feed_forward(
-        normed_two, cotangent, middle, bias_final[None], feed, bias_hidden, tables[0], home
+    result, grad_normed_two, hidden_bias_grad, *hidden_grads, active = feed_forward(
+        normed_two, cotangent, middle, bias_final[None], feed, bias_hidden, tables[1]
     )
-    grads = [[g.reshape(g.shape[0], -1, part_rows, width) for g in grads[i : i + 2]] for i in (0, 2)]
     step = pairs // GROUPS
+    blocks = lambda pair: [g.reshape(g.shape[0], -1, part_rows, width) for g in pair]
+    hidden_grads = blocks(hidden_grads)
     if direct:
-        got = [[near, exchange(far, order[0], count)] for (near, far), order in zip(grads, orders)]
+        hidden_got = [hidden_grads[0], exchange(hidden_grads[1], orders[1][0], count)]
+    final_grads = blocks(final_share(active, cotangent, home))
+    if direct:
+        hidden_got, final_grads, grad_normed_two = sync((hidden_got, final_grads, grad_normed_two))
+        final_got = [final_grads[0], exchange(final_grads[1], orders[0][0], count)]
+        away = total([p[8:] for p in hidden_got])
+        away, grad_normed_two = sync((away, grad_normed_two))
+        moving = [exchange(away, orders[1][1], count)]
     middle_grad, grad_branch, grad_mixed, sums_mid = branch_gradient(grad_normed_two, middle, cotangent, weight_out, vectors)
     if direct:
-        got, grad_mixed = sync((got, grad_mixed))
-        away = [total([p[8:] for p in parts]) for parts in got]
+        final_got, grad_mixed = sync((final_got, grad_mixed))
+        away = total([p[8:] for p in final_got])
         away, grad_mixed = sync((away, grad_mixed))
-        moving = [exchange(a, order[1], count) for a, order in zip(away, orders)]
+        moving.append(exchange(away, orders[0][1], count))
+        got = [hidden_got, final_got]
+        turns = orders[1], orders[0]
+    else:
+        grads = [hidden_grads, final_grads]
     first = attention_backward(img, queries, key_rows, value_rows, grad_mixed, totals, 0, step)
     if direct:
         grad_mixed, first = sync((grad_mixed, first))
@@ -771,7 +816,7 @@
         got = [parts + [m] for parts, m in zip(got, moving)]
         away = [total([p[4:8] for p in parts]) for parts in got]
         away, first, second, halo, normed, grad_branch = sync((away, first, second, halo, normed, grad_branch))
-        moving = [exchange(a, order[2], count) for a, order in zip(away, orders)]
+        moving = [exchange(a, order[2], count) for a, order in zip(away, turns)]
     next_halo = send(*second[3:])
     packed_one, sums_one, *share_one = weight_share(normed, *first[:3], *halo, tables[0], (mixed_low, grad_branch))
     if direct:

time: 545 us -> 535 us (0.982)
  starting transfers between devices: 75.6 us -> 59.6 us
    ppermute x3, starting transfers between devices: 28.3 us -> 10.2 us  [per_device(): lax.ppermute(right, 'dev', to_right)]
    pallas_call x0 -> x1, Pallas kernels: none -> 15.2 us  [final_share(): pl.pallas_call(final_kernel, grid_spec=pltpu.PrefetchScalarGridSpec(num_s...]
    pallas_call x1, Pallas kernels: 68.4 us -> 57.7 us  [feed_forward(): pl.pallas_call(feed_kernel, grid_spec=pltpu.PrefetchScalarGridSpec(num_sc...]
  transfers between devices with their start and end apart: 37 -> 37, of which waited for: 13 -> 13; matrix products, arithmetic and copies ran while one was open for 7% -> 9% of each run, Pallas kernels for 28% -> 32%
where the time goes in v5:
time: 535 us; the launch traced here: 527 us
  Pallas kernels  224 us (42%)
  waiting for transfers between devices  119 us (22%)
  starting transfers between devices  59.6 us (11%)
  other arithmetic  50.6 us (9%)
  local copies, waits for them, and re-layouts  29.7 us (6%)
  between operations  20.1 us (4%)
  blocking collectives  19.7 us (4%)
    ppermute x30, waiting for transfers between devices, exchange(): return lax.ppermute(x, 'dev', [(i, i ^ bit) for i in range(count)])  108 us
    pallas_call x1, Pallas kernels, feed_forward(): pl.pallas_call(feed_kernel, grid_spec=pltpu.PrefetchScalarGridSpec(num_sc...  57.7 us
    ppermute x30, starting transfers between devices, exchange(): return lax.ppermute(x, 'dev', [(i, i ^ bit) for i in range(count)])  45.5 us
    pallas_call x2, Pallas kernels, attention_backward(): pl.pallas_call(functools.partial(bwd_kernel, images), grid_spec=pltpu.Pre...  44.3 us
    pallas_call x2, Pallas kernels, weight_share(): pl.pallas_call(functools.partial(share_kernel, bool(extra)), grid_spec=pl...  32 us
    convert_element_type x11, other arithmetic, total(): functools.reduce(lambda a, b: a + b, [p.astype(f32) for p in parts])  30.1 us
    pallas_call x1, Pallas kernels, project(): pl.pallas_call(project_kernel, grid_spec=pltpu.PrefetchScalarGridSpec(num...  26.3 us
    pallas_call x1, Pallas kernels, attention_forward(): pl.pallas_call(functools.partial(fwd_kernel, images), grid_spec=pltpu.Pre...  24.7 us
  transfers between devices with their start and end apart: 37, of which 13 were waited for; matrix products, arithmetic and copies ran while one was open for 9% of the time, Pallas kernels for 32%

profile of v5, /device:TPU:0, one launch (start us, length us, event | category | flops | bytes accessed | tf_op | source)
XLA Modules:
  0.0 527.3 jit_solution(131535855505307699)
XLA Ops:
  16.1 5.1 collective-permute-start.2
  28.9 5.7 %collective-permute-done.1 = bf16[1,32,4224]{2,1,0:T(8,128)(2,1)S(1)} collective-permute-done((bf16[1,32,4224]{2,1,0:T(8,128)(2,1)S(1)}, bf16[1,32,4224]{2,1,0:T(8,128)(2,1)S(1)}, u32[]{:S(2)}, u32[]{:S(2)}) %collective-permute-start.1) | collective-permute-done | bytes 270368 | tf_op jit(solution)/shard_map/ppermute | solution.py:640
  34.6 9.7 %collective-permute-done = bf16[1,32,4224]{2,1,0:T(8,128)(2,1)S(1)} collective-permute-done((bf16[1,32,4224]{2,1,0:T(8,128)(2,1)S(1)}, bf16[1,32,4224]{2,1,0:T(8,128)(2,1)S(1)}, u32[]{:S(2)}, u32[]{:S(2)}) %collective-permute-start) | collective-permute-done | bytes 270368 | tf_op jit(solution)/shard_map/ppermute | solution.py:640
  47.5 13.0 %collective-permute-start.5 = (bf16[4,32,2048]{2,1,0:T(8,128)(2,1)}, bf16[4,32,2048]{2,1,0:T(8,128)(2,1)}, u32[]{:S(2)}, u32[]{:S(2)}) collective-permute-start(bf16[4,32,2048]{2,1,0:T(8,128)(2,1)} %pad_maximum_fusion.3), channel_id=1, source_target_pairs={{0,2},{1,3},{2,0},{3,1},{4,6},{5,7},{6,4},{7,5},{8,10},{9,11},{10,... | collective-permute-start | bytes 1572872 | tf_op jit(solution)/shard_map/ppermute | solution.py:640
  60.7 11.6 %collective-permute-done.5 = bf16[4,32,2048]{2,1,0:T(8,128)(2,1)} collective-permute-done((bf16[4,32,2048]{2,1,0:T(8,128)(2,1)}, bf16[4,32,2048]{2,1,0:T(8,128)(2,1)}, u32[]{:S(2)}, u32[]{:S(2)}) %collective-permute-start.5) | collective-permute-done | bytes 524320 | tf_op jit(solution)/shard_map/ppermute | solution.py:640
  79.6 24.7 %collective-permute-done.9 = bf16[8,32,2176]{2,1,0:T(8,128)(2,1)S(1)} collective-permute-done((bf16[8,32,2176]{2,1,0:T(8,128)(2,1)S(1)}, bf16[8,32,2176]{2,1,0:T(8,128)(2,1)S(1)}, u32[]{:S(2)}, u32[]{:S(2)}) %collective-permute-start.9) | collective-permute-done | bytes 1114144 | tf_op jit(solution)/shard_map/ppermute | solution.py:640
  115.9 3.4 pad_maximum_fusion.x
  119.4 26.3 %project.1 = (bf16[2176,1024]{1,0:T(8,128)(2,1)}, bf16[2176,1024]{1,0:T(8,128)(2,1)}, bf16[2176,1024]{1,0:T(8,128)(2,1)}, bf16[2176,1024]{1,0:T(8,128)(2,1)}, bf...) custom-call(s32[32]{0:T(128)} %broadcast_xor_fusion.table_one.table, ...), custom_call_target="tpu_custom_call" | custom-call | bytes 2400000 | tf_op jit(solution)/shard_map/project/pallas_call | solution.py:463
  147.6 24.7 %attention_forward.1 = (bf16[1024,1024]{1,0:T(8,128)(2,1)}, f32[8,24,768]{2,1,0:T(8,128)}) custom-call(s32[3]{0:T(128)} %pad_add_fusion.img_ref, bf16[2176,1024]{1,0:T(8,128)(2,1)} %get-tuple-element.160.q_ref, bf16[2176,1024]{1,0:T(8,128)(2,1)} %get-tuple-element.161.k_ref, bf16[2176,1024]{1,0:T(8,128)(2,1)} %get-tuple-element.162.v_ref), custom_call_target="tpu_custom_call" | custom-call | bytes 4000000 | tf_op jit(solution)/shard_map/attention_forward/pallas_call | solution.py:159
  173.8 4.7 fusion.18
  182.5 10.2 %all-gather.2.cloned.1.call-done.wide.tall = bf16[1024,8192]{1,0:T(8,128)(2,1)} async-done(((bf16[32,8192]{1,0:T(8,128)(2,1)}), bf16[1024,8192]{1,0:T(8,128)(2,1)}) %all-gather.2.cloned.1.call-update) | async-done | bytes 16777232 | tf_op jit(solution)/shard_map/all_gather | solution.py:766
  192.7 57.7 %feed_forward.1 = (bf16[1024,1024]{1,0:T(8,128)(2,1)}, f32[1024,1024]{1,0:T(8,128)}, f32[1,4096]{1,0:T(1,128)}, bf16[16,4,32,1024]{3,2,1,0:T(8,128)(2,1)}, bf16[...) custom-call(s32[32]{0:T(128)} %broadcast_xor_fusion.1.table_two.table, ...), custom_call_target="tpu_custom_call" | custom-call | bytes 5700000 | tf_op jit(solution)/shard_map/feed_forward/pallas_call | solution.py:388
  251.1 15.2 %final_share.1 = (bf16[16,128,1024]{2,1,0:T(8,128)(2,1)}, bf16[16,128,1024]{2,1,0:T(8,128)(2,1)}) custom-call(s32[32]{0:T(128)} %fusion.4.home, bf16[1024,4096]{1,0:T(8,128)(2,1)} %get-tuple-element.170.active, bf16[1024,1024]{1,0:T(8,128)(2,1)} %cot.5), custom_call_target="tpu_custom_call" | custom-call | bytes 1400000 | tf_op jit(solution)/shard_map/final_share/pallas_call | solution.py:357
  266.7 3.3 add_convert_fusion.1
  271.3 10.2 %branch_gradient.1 = (f32[1024,1024]{1,0:T(8,128)}, bf16[1024,1024]{1,0:T(8,128)(2,1)}, bf16[1024,1024]{1,0:T(8,128)(2,1)}, f32[8,1024]{1,0:T(8,128)}) custom-call(f32[1024,1024]{1,0:T(8,128)} %get-tuple-element.180.grad, f32[1024,1024]{1,0:T(8,128)} %copy-done, bf16[1024,1024]{1,0:T(8,128)(2,1)} %cot.5, bf16[1024,1024]{1,0:T(8,128)(2,1)} %get-tuple-element.164.weight_out, ...), custom_call_target="tpu_custom_call" | custom-call | bytes 1000000 | tf_op jit(solution)/shard_map/branch_gradient/pallas_call | solution.py:609
  281.5 4.6 add_convert_fusion
  286.8 22.3 %attention_backward.2 = (bf16[1024,512]{1,0:T(8,128)(2,1)}, f32[1024,512]{1,0:T(8,128)}, f32[1024,512]{1,0:T(8,128)}, bf16[2,576,512]{2,1,0:T(8,128)(2,1)}, bf16[2,576,512]{2,1,0:T(8,128)(2,1)}) custom-call(s32[3]{0:T(128)} %pad_add_fusion.img_ref, bf16[2176,1024]{1,0:T(8,128)(2,1)} %get-tuple-element.160.q_ref, ...), custom_call_target="tpu_custom_call" | custom-call | bytes 2600000 | tf_op jit(solution)/shard_map/attention_backward/pallas_call | solution.py:243
  310.4 4.0 collective-permute-start.15
  314.4 22.0 %attention_backward.3 = (bf16[1024,512]{1,0:T(8,128)(2,1)}, f32[1024,512]{1,0:T(8,128)}, f32[1024,512]{1,0:T(8,128)}, bf16[2,576,512]{2,1,0:T(8,128)(2,1)}, bf16[2,576,512]{2,1,0:T(8,128)(2,1)}) custom-call(s32[3]{0:T(128)} %pad_add_fusion.img_ref, bf16[2176,1024]{1,0:T(8,128)(2,1)} %get-tuple-element.160.q_ref, ...), custom_call_target="tpu_custom_call" | custom-call | bytes 2600000 | tf_op jit(solution)/shard_map/attention_backward/pallas_call | solution.py:243
  336.5 8.3 %collective-permute-done.14 = bf16[8,4,32,1024]{3,2,1,0:T(8,128)(2,1)} collective-permute-done((bf16[8,4,32,1024]{3,2,1,0:T(8,128)(2,1)}, bf16[8,4,32,1024]{3,2,1,0:T(8,128)(2,1)}, u32[]{:S(2)}, u32[]{:S(2)}) %collective-permute-start.14) | collective-permute-done | bytes 2097184 | tf_op jit(solution)/shard_map/ppermute | solution.py:640
  344.8 5.8 %add_convert_fusion.3 = (bf16[4,4,32,1024]{3,2,1,0:T(8,128)(2,1)}, bf16[4,4,32,1024]{3,2,1,0:T(8,128)(2,1)}) fusion(bf16[8,4,32,1024]{3,2,1,0:T(8,128)(2,1)} %collective-permute-done.14, bf16[16,4,32,1024]{3,2,1,0:T(8,128)(2,1)} %collective-permute-done.13, bf16[16,4,32,1024]{3,2,1,0:T(8,128)(2,1)} %bitcast.41, ...), kind=kLoop, calls=%fused_computation.6 | loop fusion | flops 6291456 | bytes 8388608 | tf_op jit(solution)/shard_map/convert_element_type | solution.py:666
  359.0 18.7 %weight_share.2 = (bf16[1024,1536]{1,0:T(8,128)(2,1)}, f32[1,2560]{1,0:T(1,128)}, bf16[16,32,2560]{2,1,0:T(8,128)(2,1)}, bf16[16,32,2560]{2,1,0:T(8,128)(2,1)}) custom-call(s32[32]{0:T(128)} %broadcast_xor_fusion.table_one.table, bf16[2176,1024]{1,0:T(8,128)(2,1)} %get-tuple-element.249.normed, bf16[1024,512]{1,0:T(8,128)(2,1)} %get-tuple-element.228.dq, ...), custom_call_target="tpu_custom_call" | custom-call | bytes 1000000 | tf_op jit(solution)/shard_map/weight_share/pallas_call | solution.py:548
  377.6 16.3 %collective-permute-done.17 = bf16[4,4,32,1024]{3,2,1,0:T(8,128)(2,1)S(1)} collective-permute-done((bf16[4,4,32,1024]{3,2,1,0:T(8,128)(2,1)}, bf16[4,4,32,1024]{3,2,1,0:T(8,128)(2,1)S(1)}, u32[]{:S(2)}, u32[]{:S(2)}) %collective-permute-start.17) | collective-permute-done | bytes 1048608 | tf_op jit(solution)/shard_map/ppermute | solution.py:640
  393.9 7.7 %collective-permute-done.18 = bf16[4,4,32,1024]{3,2,1,0:T(8,128)(2,1)} collective-permute-done((bf16[4,4,32,1024]{3,2,1,0:T(8,128)(2,1)}, bf16[4,4,32,1024]{3,2,1,0:T(8,128)(2,1)}, u32[]{:S(2)}, u32[]{:S(2)}) %collective-permute-start.18) | collective-permute-done | bytes 1048608 | tf_op jit(solution)/shard_map/ppermute | solution.py:640
  407.2 3.2 collective-permute-start.22
  410.4 13.3 %weight_share.3 = (bf16[1024,1536]{1,0:T(8,128)(2,1)}, f32[1,1536]{1,0:T(1,128)}, bf16[16,32,1536]{2,1,0:T(8,128)(2,1)}, bf16[16,32,1536]{2,1,0:T(8,128)(2,1)}) custom-call(s32[32]{0:T(128)} %broadcast_xor_fusion.table_one.table, bf16[2176,1024]{1,0:T(8,128)(2,1)} %get-tuple-element.249.normed, bf16[1024,512]{1,0:T(8,128)(2,1)} %get-tuple-element.250.dq, ...), custom_call_target="tpu_custom_call" | custom-call | bytes 700000 | tf_op jit(solution)/shard_map/weight_share/pallas_call | solution.py:548
  432.1 14.0 %input_gradient.1 = (bf16[1024,1024]{1,0:T(8,128)(2,1)}, f32[8,1024]{1,0:T(8,128)}) custom-call(bf16[1024,1536]{1,0:T(8,128)(2,1)} %get-tuple-element.263.one, bf16[1024,1536]{1,0:T(8,128)(2,1)} %get-tuple-element.264.two, bf16[1024,1024]{1,0:T(8,128)(2,1)} %tokens.1, f32[1024,1024]{1,0:T(8,128)} %get-tuple-element.265.middle_grad, ...), custom_call_target="tpu_custom_call" | custom-call | bytes 1200000 | tf_op jit(solution)/shard_map/input_gradient/pallas_call | solution.py:609
  449.8 10.6 %collective-permute-done.24 = bf16[4,32,2560]{2,1,0:T(8,128)(2,1)} collective-permute-done((bf16[4,32,2560]{2,1,0:T(8,128)(2,1)}, bf16[4,32,2560]{2,1,0:T(8,128)(2,1)}, u32[]{:S(2)}, u32[]{:S(2)}) %collective-permute-start.24) | collective-permute-done | bytes 655392 | tf_op jit(solution)/shard_map/ppermute | solution.py:640
  471.5 19.7 %all_to_all.12 = f32[32,1,384]{2,1,0:T(1,128)S(1)} all-to-all(f32[32,1,384]{2,1,0:T(1,128)S(1)} %copy.66), channel_id=1, replica_groups=mesh['dev'=32] {'dev'}, dimensions={0} | all-to-all | bytes 98304 | tf_op jit(solution)/shard_map/all_to_all | solution.py:849
  491.3 3.4 add_add_fusion.1
  504.9 4.2 collective-permute-done.33
  511.1 6.4 %collective-permute-done.32 = bf16[1,32,2560]{2,1,0:T(8,128)(2,1)S(1)} collective-permute-done((bf16[1,32,2560]{2,1,0:T(8,128)(2,1)}, bf16[1,32,2560]{2,1,0:T(8,128)(2,1)S(1)}, u32[]{:S(2)}, u32[]{:S(2)}) %collective-permute-start.32) | collective-permute-done | bytes 163872 | tf_op jit(solution)/shard_map/ppermute | solution.py:640
  (205 shorter events, 97.3 us)
Async XLA Ops:
  7.2 185.5 %all-gather.2.cloned.1.call-start = ((), (), s32[]{:S(2)}) async-start(), calls=%async_computation.1 | async-start | bytes 17301504 | tf_op jit(solution)/shard_map/all_gather | solution.py:766
  21.2 13.4 %collective-permute-start.1 = (bf16[1,32,4224]{2,1,0:T(8,128)(2,1)S(1)}, bf16[1,32,4224]{2,1,0:T(8,128)(2,1)S(1)}, u32[]{:S(2)}, u32[]{:S(2)}) collective-permute-start(bf16[1,32,4224]{2,1,0:T(8,128)(2,1)S(1)} %bitcast.49), channel_id=1, source_target_pairs={{0,8},{1,9},{2,10},{3,11},{4,12},{5,13},{6,14},{7,15},{8,0},{9,1},... | collective-permute-start | bytes 811016 | tf_op jit(solution)/shard_map/ppermute | solution.py:640
  21.2 23.1 %collective-permute-start = (bf16[1,32,4224]{2,1,0:T(8,128)(2,1)S(1)}, bf16[1,32,4224]{2,1,0:T(8,128)(2,1)S(1)}, u32[]{:S(2)}, u32[]{:S(2)}) collective-permute-start(bf16[1,32,4224]{2,1,0:T(8,128)(2,1)S(1)} %bitcast.50), channel_id=1, source_target_pairs={{0,16},{1,17},{2,18},{3,19},{4,20},{5,21},{6,22},{7,23},{8,24},{9,... | collective-permute-start | bytes 811016 | tf_op jit(solution)/shard_map/ppermute | solution.py:640
  23.7 20.6 %collective-permute-start.4 = (bf16[576,1024]{1,0:T(8,128)(2,1)S(1)}, bf16[576,1024]{1,0:T(8,128)(2,1)S(1)}, u32[]{:S(2)}, u32[]{:S(2)}) collective-permute-start(bf16[576,1024]{1,0:T(8,128)(2,1)S(1)} %get-tuple-element.303), channel_id=1, source_target_pairs={{1,0},{2,1},{3,2},{4,3},{5,4},{6,5},{7,6},{8,7},{9,8},{10,9},{11,1... | collective-permute-start | bytes 3538952 | tf_op jit(solution)/shard_map/ppermute | solution.py:739
  25.0 19.3 %collective-permute-start.3 = (bf16[576,1024]{1,0:T(8,128)(2,1)S(1)}, bf16[576,1024]{1,0:T(8,128)(2,1)S(1)}, u32[]{:S(2)}, u32[]{:S(2)}) collective-permute-start(bf16[576,1024]{1,0:T(8,128)(2,1)S(1)} %get-tuple-element.304), channel_id=1, source_target_pairs={{0,1},{1,2},{2,3},{3,4},{4,5},{5,6},{6,7},{7,8},{8,9},{9,10},{10,1... | collective-permute-start | bytes 3538952 | tf_op jit(solution)/shard_map/ppermute | solution.py:739
  47.5 24.8 %collective-permute-start.5 = (bf16[4,32,2048]{2,1,0:T(8,128)(2,1)}, bf16[4,32,2048]{2,1,0:T(8,128)(2,1)}, u32[]{:S(2)}, u32[]{:S(2)}) collective-permute-start(bf16[4,32,2048]{2,1,0:T(8,128)(2,1)} %pad_maximum_fusion.3), channel_id=1, source_target_pairs={{0,2},{1,3},{2,0},{3,1},{4,6},{5,7},{6,4},{7,5},{8,10},{9,11},{10,... | collective-permute-start | bytes 1572872 | tf_op jit(solution)/shard_map/ppermute | solution.py:640
  60.6 13.6 %collective-permute-start.6 = (bf16[4,32,2176]{2,1,0:T(8,128)(2,1)S(1)}, bf16[4,32,2176]{2,1,0:T(8,128)(2,1)}, u32[]{:S(2)}, u32[]{:S(2)}) collective-permute-start(bf16[4,32,2176]{2,1,0:T(8,128)(2,1)S(1)} %pad_maximum_fusion.2), channel_id=1, source_target_pairs={{0,4},{1,5},{2,6},{3,7},{4,0},{5,1},{6,2},{7,3},{8,12},{9,13},{10,... | collective-permute-start | bytes 1671176 | tf_op jit(solution)/shard_map/ppermute | solution.py:640
  75.3 29.0 %collective-permute-start.9 = (bf16[8,32,2176]{2,1,0:T(8,128)(2,1)S(1)}, bf16[8,32,2176]{2,1,0:T(8,128)(2,1)S(1)}, u32[]{:S(2)}, u32[]{:S(2)}) collective-permute-start(bf16[8,32,2176]{2,1,0:T(8,128)(2,1)S(1)} %constant_dynamic-update-slice_fusion.13), channel_id=1, source_target_pairs={{0,2},{1,3},{2,0},{3,1},{4,6},{5,7},{6,4},{7,5},{8,10},{9,11},{10,... | collective-permute-start | bytes 3342344 | tf_op jit(solution)/shard_map/ppermute | solution.py:640
  75.9 29.6 %collective-permute-start.7 = (bf16[8,32,2048]{2,1,0:T(8,128)(2,1)}, bf16[8,32,2048]{2,1,0:T(8,128)(2,1)S(1)}, u32[]{:S(2)}, u32[]{:S(2)}) collective-permute-start(bf16[8,32,2048]{2,1,0:T(8,128)(2,1)} %constant_dynamic-update-slice_fusion.8), channel_id=1, source_target_pairs={{0,4},{1,5},{2,6},{3,7},{4,0},{5,1},{6,2},{7,3},{8,12},{9,13},{10,... | collective-permute-start | bytes 3145736 | tf_op jit(solution)/shard_map/ppermute | solution.py:640
  105.4 14.0 %collective-permute-start.10 = (bf16[16,32,2176]{2,1,0:T(8,128)(2,1)}, bf16[16,32,2176]{2,1,0:T(8,128)(2,1)}, u32[]{:S(2)}, u32[]{:S(2)}) collective-permute-start(bf16[16,32,2176]{2,1,0:T(8,128)(2,1)} %constant_dynamic-update-slice_fusion.24.two_near), channel_id=1, source_target_pairs={{0,1},{1,0},{2,3},{3,2},{4,5},{5,4},{6,7},{7,6},{8,9},{9,8},{10,11... | collective-permute-start | bytes 6684680 | tf_op jit(solution)/shard_map/ppermute | solution.py:640
  250.4 16.0 %collective-permute-start.11 = (bf16[16,4,32,1024]{3,2,1,0:T(8,128)(2,1)}, bf16[16,4,32,1024]{3,2,1,0:T(8,128)(2,1)}, u32[]{:S(2)}, u32[]{:S(2)}) collective-permute-start(bf16[16,4,32,1024]{3,2,1,0:T(8,128)(2,1)} %get-tuple-element.169), channel_id=1, source_target_pairs={{0,1},{1,0},{2,3},{3,2},{4,5},{5,4},{6,7},{7,6},{8,9},{9,8},{10,11... | collective-permute-start | bytes 12582920 | tf_op jit(solution)/shard_map/ppermute | solution.py:640
  266.4 15.1 %collective-permute-start.13 = (bf16[16,4,32,1024]{3,2,1,0:T(8,128)(2,1)}, bf16[16,4,32,1024]{3,2,1,0:T(8,128)(2,1)}, u32[]{:S(2)}, u32[]{:S(2)}) collective-permute-start(bf16[16,4,32,1024]{3,2,1,0:T(8,128)(2,1)} %bitcast.67), channel_id=1, source_target_pairs={{0,1},{1,0},{2,3},{3,2},{4,5},{5,4},{6,7},{7,6},{8,9},{9,8},{10,11... | collective-permute-start | bytes 12582920 | tf_op jit(solution)/shard_map/ppermute | solution.py:640
  270.0 66.4 %collective-permute-start.12 = (bf16[8,4,32,1024]{3,2,1,0:T(8,128)(2,1)S(1)}, bf16[8,4,32,1024]{3,2,1,0:T(8,128)(2,1)}, u32[]{:S(2)}, u32[]{:S(2)}) collective-permute-start(bf16[8,4,32,1024]{3,2,1,0:T(8,128)(2,1)S(1)} %add_convert_fusion.1), channel_id=1, source_target_pairs={{0,2},{1,3},{2,0},{3,1},{4,6},{5,7},{6,4},{7,5},{8,10},{9,11},{10,... | collective-permute-start | bytes 6291464 | tf_op jit(solution)/shard_map/ppermute | solution.py:640
  286.1 58.7 %collective-permute-start.14 = (bf16[8,4,32,1024]{3,2,1,0:T(8,128)(2,1)}, bf16[8,4,32,1024]{3,2,1,0:T(8,128)(2,1)}, u32[]{:S(2)}, u32[]{:S(2)}) collective-permute-start(bf16[8,4,32,1024]{3,2,1,0:T(8,128)(2,1)} %add_convert_fusion), channel_id=1, source_target_pairs={{0,4},{1,5},{2,6},{3,7},{4,0},{5,1},{6,2},{7,3},{8,12},{9,13},{10,... | collective-permute-start | bytes 6291464 | tf_op jit(solution)/shard_map/ppermute | solution.py:640
  309.1 27.3 %collective-permute-start.16 = (bf16[2,576,512]{2,1,0:T(8,128)(2,1)}, bf16[2,576,512]{2,1,0:T(8,128)(2,1)S(1)}, u32[]{:S(2)}, u32[]{:S(2)}) collective-permute-start(bf16[2,576,512]{2,1,0:T(8,128)(2,1)} %get-tuple-element.196), channel_id=1, source_target_pairs={{1,0},{2,1},{3,2},{4,3},{5,4},{6,5},{7,6},{8,7},{9,8},{10,9},{11,1... | collective-permute-start | bytes 3538952 | tf_op jit(solution)/shard_map/ppermute | solution.py:739
  310.4 26.1 %collective-permute-start.15 = (bf16[2,576,512]{2,1,0:T(8,128)(2,1)}, bf16[2,576,512]{2,1,0:T(8,128)(2,1)}, u32[]{:S(2)}, u32[]{:S(2)}) collective-permute-start(bf16[2,576,512]{2,1,0:T(8,128)(2,1)} %get-tuple-element.197), channel_id=1, source_target_pairs={{0,1},{1,2},{2,3},{3,4},{4,5},{5,6},{6,7},{7,8},{8,9},{9,10},{10,1... | collective-permute-start | bytes 3538952 | tf_op jit(solution)/shard_map/ppermute | solution.py:739
  350.6 51.0 %collective-permute-start.20 = (bf16[2,576,512]{2,1,0:T(8,128)(2,1)}, bf16[2,576,512]{2,1,0:T(8,128)(2,1)S(1)}, u32[]{:S(2)}, u32[]{:S(2)}) collective-permute-start(bf16[2,576,512]{2,1,0:T(8,128)(2,1)} %get-tuple-element.225), channel_id=1, source_target_pairs={{1,0},{2,1},{3,2},{4,3},{5,4},{6,5},{7,6},{8,7},{9,8},{10,9},{11,1... | collective-permute-start | bytes 3538952 | tf_op jit(solution)/shard_map/ppermute | solution.py:739
  351.9 49.7 %collective-permute-start.19 = (bf16[2,576,512]{2,1,0:T(8,128)(2,1)}, bf16[2,576,512]{2,1,0:T(8,128)(2,1)S(1)}, u32[]{:S(2)}, u32[]{:S(2)}) collective-permute-start(bf16[2,576,512]{2,1,0:T(8,128)(2,1)} %get-tuple-element.226), channel_id=1, source_target_pairs={{0,1},{1,2},{2,3},{3,4},{4,5},{5,6},{6,7},{7,8},{8,9},{9,10},{10,1... | collective-permute-start | bytes 3538952 | tf_op jit(solution)/shard_map/ppermute | solution.py:739
  355.0 38.9 %collective-permute-start.17 = (bf16[4,4,32,1024]{3,2,1,0:T(8,128)(2,1)}, bf16[4,4,32,1024]{3,2,1,0:T(8,128)(2,1)S(1)}, u32[]{:S(2)}, u32[]{:S(2)}) collective-permute-start(bf16[4,4,32,1024]{3,2,1,0:T(8,128)(2,1)} %get-tuple-element.220), channel_id=1, source_target_pairs={{0,4},{1,5},{2,6},{3,7},{4,0},{5,1},{6,2},{7,3},{8,12},{9,13},{10,... | collective-permute-start | bytes 3145736 | tf_op jit(solution)/shard_map/ppermute | solution.py:640
  357.5 44.1 %collective-permute-start.18 = (bf16[4,4,32,1024]{3,2,1,0:T(8,128)(2,1)}, bf16[4,4,32,1024]{3,2,1,0:T(8,128)(2,1)}, u32[]{:S(2)}, u32[]{:S(2)}) collective-permute-start(bf16[4,4,32,1024]{3,2,1,0:T(8,128)(2,1)} %get-tuple-element.221), channel_id=1, source_target_pairs={{0,2},{1,3},{2,0},{3,1},{4,6},{5,7},{6,4},{7,5},{8,10},{9,11},{10,... | collective-permute-start | bytes 3145736 | tf_op jit(solution)/shard_map/ppermute | solution.py:640
  407.2 16.5 %collective-permute-start.22 = (bf16[16,32,2560]{2,1,0:T(8,128)(2,1)}, bf16[16,32,2560]{2,1,0:T(8,128)(2,1)}, u32[]{:S(2)}, u32[]{:S(2)}) collective-permute-start(bf16[16,32,2560]{2,1,0:T(8,128)(2,1)} %get-tuple-element.248), channel_id=1, source_target_pairs={{0,1},{1,0},{2,3},{3,2},{4,5},{5,4},{6,7},{7,6},{8,9},{9,8},{10,11... | collective-permute-start | bytes 7864328 | tf_op jit(solution)/shard_map/ppermute | solution.py:640
  423.7 36.6 %collective-permute-start.26 = (bf16[16,32,1536]{2,1,0:T(8,128)(2,1)}, bf16[16,32,1536]{2,1,0:T(8,128)(2,1)}, u32[]{:S(2)}, u32[]{:S(2)}) collective-permute-start(bf16[16,32,1536]{2,1,0:T(8,128)(2,1)} %get-tuple-element.262), channel_id=1, source_target_pairs={{0,1},{1,0},{2,3},{3,2},{4,5},{5,4},{6,7},{7,6},{8,9},{9,8},{10,11... | collective-permute-start | bytes 4718600 | tf_op jit(solution)/shard_map/ppermute | solution.py:640
  423.9 25.8 %collective-permute-start.21 = (bf16[4,4,32,1024]{3,2,1,0:T(8,128)(2,1)}, bf16[4,4,32,1024]{3,2,1,0:T(8,128)(2,1)}, u32[]{:S(2)}, u32[]{:S(2)}) collective-permute-start(bf16[4,4,32,1024]{3,2,1,0:T(8,128)(2,1)} %pad_maximum_fusion.1), channel_id=1, source_target_pairs={{0,8},{1,9},{2,10},{3,11},{4,12},{5,13},{6,14},{7,15},{8,0},{9,1},... | collective-permute-start | bytes 3145736 | tf_op jit(solution)/shard_map/ppermute | solution.py:640
  428.3 21.5 %collective-permute-start.25 = (bf16[4,32,2560]{2,1,0:T(8,128)(2,1)}, bf16[4,32,2560]{2,1,0:T(8,128)(2,1)S(1)}, u32[]{:S(2)}, u32[]{:S(2)}) collective-permute-start(bf16[4,32,2560]{2,1,0:T(8,128)(2,1)} %get-tuple-element.294), channel_id=1, source_target_pairs={{0,6},{1,7},{2,4},{3,5},{4,2},{5,3},{6,0},{7,1},{8,14},{9,15},{10,... | collective-permute-start | bytes 1966088 | tf_op jit(solution)/shard_map/ppermute | solution.py:640
  429.5 30.8 %collective-permute-start.24 = (bf16[4,32,2560]{2,1,0:T(8,128)(2,1)}, bf16[4,32,2560]{2,1,0:T(8,128)(2,1)}, u32[]{:S(2)}, u32[]{:S(2)}) collective-permute-start(bf16[4,32,2560]{2,1,0:T(8,128)(2,1)} %get-tuple-element.295), channel_id=1, source_target_pairs={{0,4},{1,5},{2,6},{3,7},{4,0},{5,1},{6,2},{7,3},{8,12},{9,13},{10,... | collective-permute-start | bytes 1966088 | tf_op jit(solution)/shard_map/ppermute | solution.py:640
  432.0 28.4 %collective-permute-start.23 = (bf16[4,32,2560]{2,1,0:T(8,128)(2,1)}, bf16[4,32,2560]{2,1,0:T(8,128)(2,1)}, u32[]{:S(2)}, u32[]{:S(2)}) collective-permute-start(bf16[4,32,2560]{2,1,0:T(8,128)(2,1)} %get-tuple-element.296), channel_id=1, source_target_pairs={{0,2},{1,3},{2,0},{3,1},{4,6},{5,7},{6,4},{7,5},{8,10},{9,11},{10,... | collective-permute-start | bytes 1966088 | tf_op jit(solution)/shard_map/ppermute | solution.py:640
  462.7 28.6 %collective-permute-start.31 = (bf16[2,4,32,1024]{3,2,1,0:T(8,128)(2,1)S(1)}, bf16[2,4,32,1024]{3,2,1,0:T(8,128)(2,1)S(1)}, u32[]{:S(2)}, u32[]{:S(2)}) collective-permute-start(bf16[2,4,32,1024]{3,2,1,0:T(8,128)(2,1)S(1)} %pad_maximum_fusion.4), channel_id=1, source_target_pairs={{0,16},{1,17},{2,18},{3,19},{4,20},{5,21},{6,22},{7,23},{8,24},{9,... | collective-permute-start | bytes 1572872 | tf_op jit(solution)/shard_map/ppermute | solution.py:640
  464.8 26.5 %collective-permute-start.30 = (bf16[4,32,1536]{2,1,0:T(8,128)(2,1)S(1)}, bf16[4,32,1536]{2,1,0:T(8,128)(2,1)S(1)}, u32[]{:S(2)}, u32[]{:S(2)}) collective-permute-start(bf16[4,32,1536]{2,1,0:T(8,128)(2,1)S(1)} %get-tuple-element.300), channel_id=1, source_target_pairs={{0,6},{1,7},{2,4},{3,5},{4,2},{5,3},{6,0},{7,1},{8,14},{9,15},{10,... | collective-permute-start | bytes 1179656 | tf_op jit(solution)/shard_map/ppermute | solution.py:640
  467.0 24.2 %collective-permute-start.29 = (bf16[4,32,1536]{2,1,0:T(8,128)(2,1)S(1)}, bf16[4,32,1536]{2,1,0:T(8,128)(2,1)S(1)}, u32[]{:S(2)}, u32[]{:S(2)}) collective-permute-start(bf16[4,32,1536]{2,1,0:T(8,128)(2,1)S(1)} %get-tuple-element.301), channel_id=1, source_target_pairs={{0,4},{1,5},{2,6},{3,7},{4,0},{5,1},{6,2},{7,3},{8,12},{9,13},{10,... | collective-permute-start | bytes 1179656 | tf_op jit(solution)/shard_map/ppermute | solution.py:640
  468.0 23.3 %collective-permute-start.28 = (bf16[4,32,1536]{2,1,0:T(8,128)(2,1)S(1)}, bf16[4,32,1536]{2,1,0:T(8,128)(2,1)S(1)}, u32[]{:S(2)}, u32[]{:S(2)}) collective-permute-start(bf16[4,32,1536]{2,1,0:T(8,128)(2,1)S(1)} %get-tuple-element.302), channel_id=1, source_target_pairs={{0,2},{1,3},{2,0},{3,1},{4,6},{5,7},{6,4},{7,5},{8,10},{9,11},{10,... | collective-permute-start | bytes 1179656 | tf_op jit(solution)/shard_map/ppermute | solution.py:640
  469.7 21.5 %collective-permute-start.27 = (bf16[2,32,2560]{2,1,0:T(8,128)(2,1)S(1)}, bf16[2,32,2560]{2,1,0:T(8,128)(2,1)S(1)}, u32[]{:S(2)}, u32[]{:S(2)}) collective-permute-start(bf16[2,32,2560]{2,1,0:T(8,128)(2,1)S(1)} %add_convert_fusion.13), channel_id=1, source_target_pairs={{0,8},{1,9},{2,10},{3,11},{4,12},{5,13},{6,14},{7,15},{8,0},{9,1},... | collective-permute-start | bytes 983048 | tf_op jit(solution)/shard_map/ppermute | solution.py:640
  503.1 14.4 %collective-permute-start.32 = (bf16[1,32,2560]{2,1,0:T(8,128)(2,1)}, bf16[1,32,2560]{2,1,0:T(8,128)(2,1)S(1)}, u32[]{:S(2)}, u32[]{:S(2)}) collective-permute-start(bf16[1,32,2560]{2,1,0:T(8,128)(2,1)} %add_convert_fusion.16), channel_id=1, source_target_pairs={{0,16},{1,17},{2,18},{3,19},{4,20},{5,21},{6,22},{7,23},{8,24},{9,... | collective-permute-start | bytes 491528 | tf_op jit(solution)/shard_map/ppermute | solution.py:640
  (31 other events, 387.9 us)
Sparse Core Ops, SparseCore 0:
  75.4 117.2 all-gather.1

commit v6 on v5

--- a/solution.py
+++ b/solution.py
@@ -260,6 +260,7 @@
 
 
 FT = 512
+FINAL_TILE = 1024
 ROWS = 1024
 
 
@@ -317,7 +318,7 @@
     tiles = pl.num_programs(0)
     slot = lax.rem(step, 2)
     half, depth, width = final_near.shape
-    devices = FT // depth
+    devices = FINAL_TILE // depth
 
     def copy_out(slot, d, target):
         return pltpu.make_async_copy(final_grad.at[slot, d], target, sems.at[slot, d])
@@ -358,13 +359,13 @@
         final_kernel,
         grid_spec=pltpu.PrefetchScalarGridSpec(
             num_scalar_prefetch=1,
-            grid=(units // FT,),
+            grid=(units // FINAL_TILE,),
             in_specs=[
-                pl.BlockSpec((rows, FT), lambda t, *_: (0, t)),
+                pl.BlockSpec((rows, FINAL_TILE), lambda t, *_: (0, t)),
                 pl.BlockSpec((rows, width), lambda t, *_: (0, 0), pipeline_mode=pl.Buffered(1)),
             ],
             out_specs=[pl.BlockSpec(memory_space=pl.ANY)] * 2,
-            scratch_shapes=[pltpu.VMEM((2, FT // depth, depth, width), bf16), pltpu.SemaphoreType.DMA((2, FT // depth))],
+            scratch_shapes=[pltpu.VMEM((2, FINAL_TILE // depth, depth, width), bf16), pltpu.SemaphoreType.DMA((2, FINAL_TILE // depth))],
         ),
         out_shape=[piece, piece],
         compiler_params=pltpu.CompilerParams(vmem_limit_bytes=VMEM, dimension_semantics=("arbitrary",)),
@@ -482,15 +483,19 @@
 def share_kernel(
     extra, table, normed, dq, dk, dv, left, right, *refs,
 ):
-    mixed, branch = refs[:2] if extra else (None, None)
-    packed, sums, near, far, normed_t, product, x = refs[2 if extra else 0 :]
+    if extra:
+        mixed, branch, packed, sums, near, far, normed_t, mixed_t, product, x = refs
+    else:
+        packed, sums, near, far, product, x = refs
+        normed_t = normed
     step = pl.program_id(0)
     rows = dq.shape[0]
     half, piece, _ = near.shape
 
-    @pl.when(step == 0)
-    def _():
-        normed_t[...] = normed[pl.ds(REACH, rows), :].T
+    if extra:
+        @pl.when(step == 0)
+        def _():
+            normed_t[...] = normed[pl.ds(REACH, rows), :].T
 
     def halo(own, number):
         x[...] = own[...].astype(bf16)
@@ -514,7 +519,7 @@
     if extra:
         @pl.when(step == 6)
         def _():
-            normed_t[...] = mixed[...].T
+            mixed_t[...] = mixed[...].T
 
         @pl.when(step >= 6)
         def _():
@@ -525,7 +530,16 @@
         packed[...] = x[...]
 
     sums[...] = jnp.sum(x[...].astype(f32), axis=0, keepdims=True)
-    product[...] = jnp.dot(normed_t[...], x[...], preferred_element_type=f32)
+    if extra:
+        @pl.when(step < 6)
+        def _():
+            product[...] = jnp.dot(normed_t[...], x[...], preferred_element_type=f32)
+
+        @pl.when(step >= 6)
+        def _():
+            product[...] = jnp.dot(mixed_t[...], x[...], preferred_element_type=f32)
+    else:
+        product[...] = jnp.dot(normed_t[...], x[...], preferred_element_type=f32)
     for place in range(2 * half):
         rows_of = product[pl.ds(pl.multiple_of(table[place] * piece, piece), piece), :].astype(bf16)
         if place < half:
@@ -536,7 +550,7 @@
 
 def weight_share(normed, dq, dk, dv, left, right, table, extra=()):
     rows, cols = dq.shape
-    win, width = normed.shape
+    width = normed.shape[1]
     steps = 6 + (4 if extra else 0)
     whole = lambda *shape: pl.BlockSpec(shape, lambda t, *_: (0,) * len(shape), pipeline_mode=pl.Buffered(1))
     clip = lambda t, low, top: jnp.minimum(jnp.maximum(t - low, 0), top)
@@ -550,13 +564,14 @@
         grid_spec=pltpu.PrefetchScalarGridSpec(
             num_scalar_prefetch=1,
             grid=(steps,),
-            in_specs=[whole(win, width), tall(0, 1), tall(2, 1), tall(4, 1), edge, edge]
+            in_specs=[whole(*normed.shape), tall(0, 1), tall(2, 1), tall(4, 1), edge, edge]
             + ([whole(rows, width), tall(6, 3)] if extra else []),
             out_specs=[tall(0, 5), pl.BlockSpec((1, CW), lambda t, *_: (0, t))]
-            + [piece] * 2,
-            scratch_shapes=[pltpu.VMEM((width, rows), bf16), pltpu.VMEM((width, CW), f32), pltpu.VMEM((rows, CW), bf16)],
+            + [piece] * 2 + ([whole(width, rows)] if extra else []),
+            scratch_shapes=([pltpu.VMEM((width, rows), bf16)] if extra else [])
+            + [pltpu.VMEM((width, CW), f32), pltpu.VMEM((rows, CW), bf16)],
         ),
-        out_shape=[sds((rows, 6 * CW), bf16), sds((1, steps * CW), f32), pieces, pieces],
+        out_shape=[sds((rows, 6 * CW), bf16), sds((1, steps * CW), f32), pieces, pieces] + ([sds((width, rows), bf16)] if extra else []),
         compiler_params=pltpu.CompilerParams(vmem_limit_bytes=VMEM, dimension_semantics=("arbitrary",)),
         cost_estimate=spent(10 if extra else 7),
         name="weight_share",
@@ -818,15 +833,15 @@
         away, first, second, halo, normed, grad_branch = sync((away, first, second, halo, normed, grad_branch))
         moving = [exchange(a, order[2], count) for a, order in zip(away, turns)]
     next_halo = send(*second[3:])
-    packed_one, sums_one, *share_one = weight_share(normed, *first[:3], *halo, tables[0], (mixed_low, grad_branch))
+    packed_one, sums_one, *share_one, turned = weight_share(normed, *first[:3], *halo, tables[0], (mixed_low, grad_branch))
     if direct:
-        moving, second, next_halo, normed, share_one = sync((moving, second, next_halo, normed, share_one))
+        moving, second, next_halo, turned, share_one = sync((moving, second, next_halo, turned, share_one))
         got = [parts + [m] for parts, m in zip(got, moving)]
         away = jnp.concatenate([total([p[2:4] for p in parts]) for parts in got], axis=0)
-        away, second, next_halo, normed, share_one = sync((away, second, next_halo, normed, share_one))
+        away, second, next_halo, turned, share_one = sync((away, second, next_halo, turned, share_one))
         lined = exchange(away, orders[0][3], count)
         share_one = [share_one[0], exchange(share_one[1], orders[0][0], count)]
-    packed_two, sums_two, *share_two = weight_share(normed, *second[:3], *next_halo, tables[0])
+    packed_two, sums_two, *share_two = weight_share(turned, *second[:3], *next_halo, tables[0])
     plane = (orders[0][2], orders[0][1], orders[0][1] | orders[0][2])
     line = (orders[0][4], orders[0][3], orders[0][3] | orders[0][4])
     if direct:
@@ -840,18 +855,19 @@
         [sums.reshape(8, count, part).transpose(1, 0, 2).reshape(count, 8 * part), hidden_bias_grad.reshape(count, -1)], axis=1
     )
     if direct:
+        sums = lax.all_to_all(sums, "dev", 0, 0, tiled=True)
         lined, plane_one, share_one, share_two, input_grad, sums = sync((lined, plane_one, share_one, share_two, input_grad, sums))
         got = [parts + [lined[2 * i : 2 * i + 2]] for i, parts in enumerate(got)]
         ended = exchange(jnp.concatenate([total([p[1:2] for p in parts]) for parts in got], axis=0), orders[0][4], count)
         plane_two = straight(share_two, plane, count)
         share_one = [p[:4] for p in share_one] + plane_one
         lined = exchange(total([p[2:4] for p in share_one]), orders[0][3], count)
-        sums = lax.all_to_all(sums, "dev", 0, 0, tiled=True)
-        lined, plane_two, share_two, sums, ended = sync((lined, plane_two, share_two, sums, ended))
+        lined, plane_two, share_two, sums, ended, got = sync((lined, plane_two, share_two, sums, ended, got))
         share_one = [p[:2] for p in share_one] + [lined]
         share_two = [p[:4] for p in share_two] + plane_two
-        last_one = exchange(total([p[1:2] for p in share_one]), orders[0][4], count)
-        last_two = straight(share_two, line, count)
+        away = [total([p[1:2] for p in share_one])] + [total([p[i : i + 1] for p in share_two]) for i in (1, 2, 3)]
+        away, ended, got = sync((away, ended, got))
+        last_one, *last_two = [exchange(a, bit, count) for a, bit in zip(away, (orders[0][4], *line))]
         finals = [total([p[0] for p in parts] + [ended[i]], f32) for i, parts in enumerate(got)]
         hidden_shard = finals[0].transpose(1, 0, 2).reshape(part, hidden_width)
         final_shard = finals[1].reshape(-1, width)

time: 535 us -> 532 us (level)
  local copies, waits for them, and re-layouts: 29.7 us -> 38.5 us
  waiting for transfers between devices: 119 us -> 112 us
  blocking collectives: 19.7 us -> 13.6 us
    ppermute x30, waiting for transfers between devices: 108 us -> 101 us  [exchange(): return lax.ppermute(x, 'dev', [(i, i ^ bit) for i in range(count)])]
    all_to_all x1, blocking collectives: 19.7 us -> 13.6 us  [per_device(): sums = lax.all_to_all(sums, 'dev', 0, 0, tiled=True)]
  transfers between devices with their start and end apart: 37 -> 37, of which waited for: 13 -> 11; matrix products, arithmetic and copies ran while one was open for 9% -> 10% of each run, Pallas kernels for 32% -> 32%
where the time goes in v6:
time: 532 us; the launch traced here: 524 us
  Pallas kernels  224 us (42%)
  waiting for transfers between devices  112 us (21%)
  starting transfers between devices  61.9 us (12%)
  other arithmetic  49.2 us (9%)
  local copies, waits for them, and re-layouts  38.5 us (7%)
  between operations  20.4 us (4%)
  blocking collectives  13.6 us (3%)
    ppermute x30, waiting for transfers between devices, exchange(): return lax.ppermute(x, 'dev', [(i, i ^ bit) for i in range(count)])  101 us
    pallas_call x1, Pallas kernels, feed_forward(): pl.pallas_call(feed_kernel, grid_spec=pltpu.PrefetchScalarGridSpec(num_sc...  57.9 us
    ppermute x30, starting transfers between devices, exchange(): return lax.ppermute(x, 'dev', [(i, i ^ bit) for i in range(count)])  47.8 us
    pallas_call x2, Pallas kernels, attention_backward(): pl.pallas_call(functools.partial(bwd_kernel, images), grid_spec=pltpu.Pre...  44.1 us
    pallas_call x2, Pallas kernels, weight_share(): pl.pallas_call(functools.partial(share_kernel, bool(extra)), grid_spec=pl...  32.7 us
    convert_element_type x11, other arithmetic, total(): functools.reduce(lambda a, b: a + b, [p.astype(f32) for p in parts])  28.5 us
    pallas_call x1, Pallas kernels, project(): pl.pallas_call(project_kernel, grid_spec=pltpu.PrefetchScalarGridSpec(num...  26.3 us
    pallas_call x1, Pallas kernels, attention_forward(): pl.pallas_call(functools.partial(fwd_kernel, images), grid_spec=pltpu.Pre...  24.7 us
  transfers between devices with their start and end apart: 37, of which 11 were waited for; matrix products, arithmetic and copies ran while one was open for 10% of the time, Pallas kernels for 32%

profile of v6, /device:TPU:0, one launch (start us, length us, event | category | flops | bytes accessed | tf_op | source)
XLA Modules:
  0.0 524.1 jit_solution(12863487437224543652)
XLA Ops:
  16.1 5.1 collective-permute-start.2
  25.0 3.1 collective-permute-start.3
  29.6 5.1 collective-permute-done.1
  34.6 9.7 %collective-permute-done = bf16[1,32,4224]{2,1,0:T(8,128)(2,1)S(1)} collective-permute-done((bf16[1,32,4224]{2,1,0:T(8,128)(2,1)S(1)}, bf16[1,32,4224]{2,1,0:T(8,128)(2,1)S(1)}, u32[]{:S(2)}, u32[]{:S(2)}) %collective-permute-start) | collective-permute-done | bytes 270368 | tf_op jit(solution)/shard_map/ppermute | solution.py:655
  49.4 13.0 %collective-permute-start.5 = (bf16[4,32,2048]{2,1,0:T(8,128)(2,1)}, bf16[4,32,2048]{2,1,0:T(8,128)(2,1)}, u32[]{:S(2)}, u32[]{:S(2)}) collective-permute-start(bf16[4,32,2048]{2,1,0:T(8,128)(2,1)} %pad_maximum_fusion.3), channel_id=1, source_target_pairs={{0,2},{1,3},{2,0},{3,1},{4,6},{5,7},{6,4},{7,5},{8,10},{9,11},{10,... | collective-permute-start | bytes 1572872 | tf_op jit(solution)/shard_map/ppermute | solution.py:655
  63.4 10.8 %collective-permute-done.5 = bf16[4,32,2048]{2,1,0:T(8,128)(2,1)} collective-permute-done((bf16[4,32,2048]{2,1,0:T(8,128)(2,1)}, bf16[4,32,2048]{2,1,0:T(8,128)(2,1)}, u32[]{:S(2)}, u32[]{:S(2)}) %collective-permute-start.5) | collective-permute-done | bytes 524320 | tf_op jit(solution)/shard_map/ppermute | solution.py:655
  84.5 22.8 %collective-permute-done.9 = bf16[8,32,2176]{2,1,0:T(8,128)(2,1)S(1)} collective-permute-done((bf16[8,32,2176]{2,1,0:T(8,128)(2,1)}, bf16[8,32,2176]{2,1,0:T(8,128)(2,1)S(1)}, u32[]{:S(2)}, u32[]{:S(2)}) %collective-permute-start.9) | collective-permute-done | bytes 1114144 | tf_op jit(solution)/shard_map/ppermute | solution.py:655
  118.9 3.6 pad_maximum_fusion.x
  122.5 26.3 %project.1 = (bf16[2176,1024]{1,0:T(8,128)(2,1)}, bf16[2176,1024]{1,0:T(8,128)(2,1)}, bf16[2176,1024]{1,0:T(8,128)(2,1)}, bf16[2176,1024]{1,0:T(8,128)(2,1)}, bf...) custom-call(s32[32]{0:T(128)} %broadcast_xor_fusion.table_one.table, ...), custom_call_target="tpu_custom_call" | custom-call | bytes 2400000 | tf_op jit(solution)/shard_map/project/pallas_call | solution.py:464
  150.7 24.7 %attention_forward.1 = (bf16[1024,1024]{1,0:T(8,128)(2,1)}, f32[8,24,768]{2,1,0:T(8,128)}) custom-call(s32[3]{0:T(128)} %pad_add_fusion.img_ref, bf16[2176,1024]{1,0:T(8,128)(2,1)} %get-tuple-element.186.q_ref, bf16[2176,1024]{1,0:T(8,128)(2,1)} %get-tuple-element.187.k_ref, bf16[2176,1024]{1,0:T(8,128)(2,1)} %get-tuple-element.188.v_ref), custom_call_target="tpu_custom_call" | custom-call | bytes 4000000 | tf_op jit(solution)/shard_map/attention_forward/pallas_call | solution.py:159
  176.9 4.7 fusion.19
  185.7 10.7 %all-gather.2.cloned.1.call-done.wide.tall = bf16[1024,8192]{1,0:T(8,128)(2,1)} async-done(((bf16[32,8192]{1,0:T(8,128)(2,1)}), bf16[1024,8192]{1,0:T(8,128)(2,1)}) %all-gather.2.cloned.1.call-update) | async-done | bytes 16777232 | tf_op jit(solution)/shard_map/all_gather | solution.py:781
  196.3 57.9 %feed_forward.1 = (bf16[1024,1024]{1,0:T(8,128)(2,1)}, f32[1024,1024]{1,0:T(8,128)}, f32[1,4096]{1,0:T(1,128)}, bf16[16,4,32,1024]{3,2,1,0:T(8,128)(2,1)}, bf16[...) custom-call(s32[32]{0:T(128)} %broadcast_xor_fusion.1.table_two.table, ...), custom_call_target="tpu_custom_call" | custom-call | bytes 5700000 | tf_op jit(solution)/shard_map/feed_forward/pallas_call | solution.py:389
  255.0 14.1 %final_share.1 = (bf16[16,128,1024]{2,1,0:T(8,128)(2,1)}, bf16[16,128,1024]{2,1,0:T(8,128)(2,1)}) custom-call(s32[32]{0:T(128)} %fusion.4.home, bf16[1024,4096]{1,0:T(8,128)(2,1)} %get-tuple-element.196.active, bf16[1024,1024]{1,0:T(8,128)(2,1)} %cot.5), custom_call_target="tpu_custom_call" | custom-call | bytes 1400000 | tf_op jit(solution)/shard_map/final_share/pallas_call | solution.py:358
  269.5 3.3 add_convert_fusion.1
  274.1 10.2 %branch_gradient.1 = (f32[1024,1024]{1,0:T(8,128)}, bf16[1024,1024]{1,0:T(8,128)(2,1)}, bf16[1024,1024]{1,0:T(8,128)(2,1)}, f32[8,1024]{1,0:T(8,128)}) custom-call(f32[1024,1024]{1,0:T(8,128)} %get-tuple-element.206.grad, f32[1024,1024]{1,0:T(8,128)} %copy-done, bf16[1024,1024]{1,0:T(8,128)(2,1)} %cot.5, bf16[1024,1024]{1,0:T(8,128)(2,1)} %get-tuple-element.190.weight_out, ...), custom_call_target="tpu_custom_call" | custom-call | bytes 1000000 | tf_op jit(solution)/shard_map/branch_gradient/pallas_call | solution.py:624
  284.2 4.6 add_convert_fusion
  289.7 22.1 %attention_backward.2 = (bf16[1024,512]{1,0:T(8,128)(2,1)}, f32[1024,512]{1,0:T(8,128)}, f32[1024,512]{1,0:T(8,128)}, bf16[2,576,512]{2,1,0:T(8,128)(2,1)}, bf16[2,576,512]{2,1,0:T(8,128)(2,1)}) custom-call(s32[3]{0:T(128)} %pad_add_fusion.img_ref, bf16[2176,1024]{1,0:T(8,128)(2,1)} %get-tuple-element.186.q_ref, ...), custom_call_target="tpu_custom_call" | custom-call | bytes 2600000 | tf_op jit(solution)/shard_map/attention_backward/pallas_call | solution.py:243
  313.0 4.0 collective-permute-start.15
  317.1 22.0 %attention_backward.3 = (bf16[1024,512]{1,0:T(8,128)(2,1)}, f32[1024,512]{1,0:T(8,128)}, f32[1024,512]{1,0:T(8,128)}, bf16[2,576,512]{2,1,0:T(8,128)(2,1)}, bf16[2,576,512]{2,1,0:T(8,128)(2,1)}) custom-call(s32[3]{0:T(128)} %pad_add_fusion.img_ref, bf16[2176,1024]{1,0:T(8,128)(2,1)} %get-tuple-element.186.q_ref, ...), custom_call_target="tpu_custom_call" | custom-call | bytes 2600000 | tf_op jit(solution)/shard_map/attention_backward/pallas_call | solution.py:243
  339.2 8.5 %collective-permute-done.14 = bf16[8,4,32,1024]{3,2,1,0:T(8,128)(2,1)} collective-permute-done((bf16[8,4,32,1024]{3,2,1,0:T(8,128)(2,1)}, bf16[8,4,32,1024]{3,2,1,0:T(8,128)(2,1)}, u32[]{:S(2)}, u32[]{:S(2)}) %collective-permute-start.14) | collective-permute-done | bytes 2097184 | tf_op jit(solution)/shard_map/ppermute | solution.py:655
  347.6 5.8 %add_convert_fusion.3 = (bf16[4,4,32,1024]{3,2,1,0:T(8,128)(2,1)}, bf16[4,4,32,1024]{3,2,1,0:T(8,128)(2,1)}) fusion(bf16[8,4,32,1024]{3,2,1,0:T(8,128)(2,1)} %collective-permute-done.14, bf16[16,4,32,1024]{3,2,1,0:T(8,128)(2,1)} %collective-permute-done.13, bf16[16,4,32,1024]{3,2,1,0:T(8,128)(2,1)} %bitcast.42, ...), kind=kLoop, calls=%fused_computation.6 | loop fusion | flops 6291456 | bytes 8388608 | tf_op jit(solution)/shard_map/convert_element_type | solution.py:681
  354.7 3.1 collective-permute-start.19
  361.8 20.6 %weight_share.2 = (bf16[1024,1536]{1,0:T(8,128)(2,1)}, f32[1,2560]{1,0:T(1,128)}, bf16[16,32,2560]{2,1,0:T(8,128)(2,1)}, bf16[16,32,2560]{2,1,0:T(8,128)(2,1)}, bf16[1024,1024]{1,0:T(8,128)(2,1)}) custom-call(s32[32]{0:T(128)} %broadcast_xor_fusion.table_one.table, bf16[2176,1024]{1,0:T(8,128)(2,1)} %get-tuple-element.253.normed, ...), custom_call_target="tpu_custom_call" | custom-call | bytes 1000000 | tf_op jit(solution)/shard_map/weight_share/pallas_call | solution.py:562
  382.4 14.3 %collective-permute-done.17 = bf16[4,4,32,1024]{3,2,1,0:T(8,128)(2,1)S(1)} collective-permute-done((bf16[4,4,32,1024]{3,2,1,0:T(8,128)(2,1)}, bf16[4,4,32,1024]{3,2,1,0:T(8,128)(2,1)S(1)}, u32[]{:S(2)}, u32[]{:S(2)}) %collective-permute-start.17) | collective-permute-done | bytes 1048608 | tf_op jit(solution)/shard_map/ppermute | solution.py:655
  396.7 7.7 %collective-permute-done.18 = bf16[4,4,32,1024]{3,2,1,0:T(8,128)(2,1)} collective-permute-done((bf16[4,4,32,1024]{3,2,1,0:T(8,128)(2,1)}, bf16[4,4,32,1024]{3,2,1,0:T(8,128)(2,1)}, u32[]{:S(2)}, u32[]{:S(2)}) %collective-permute-start.18) | collective-permute-done | bytes 1048608 | tf_op jit(solution)/shard_map/ppermute | solution.py:655
  410.2 3.2 collective-permute-start.22
  413.4 12.0 %weight_share.3 = (bf16[1024,1536]{1,0:T(8,128)(2,1)}, f32[1,1536]{1,0:T(1,128)}, bf16[16,32,1536]{2,1,0:T(8,128)(2,1)}, bf16[16,32,1536]{2,1,0:T(8,128)(2,1)}) custom-call(s32[32]{0:T(128)} %broadcast_xor_fusion.table_one.table, bf16[1024,1024]{1,0:T(8,128)(2,1)} %get-tuple-element.276.normed, bf16[1024,512]{1,0:T(8,128)(2,1)} %get-tuple-element.277.dq, ...), custom_call_target="tpu_custom_call" | custom-call | bytes 700000 | tf_op jit(solution)/shard_map/weight_share/pallas_call | solution.py:562
  432.7 14.0 %input_gradient.1 = (bf16[1024,1024]{1,0:T(8,128)(2,1)}, f32[8,1024]{1,0:T(8,128)}) custom-call(bf16[1024,1536]{1,0:T(8,128)(2,1)} %get-tuple-element.290.one, bf16[1024,1536]{1,0:T(8,128)(2,1)} %get-tuple-element.291.two, bf16[1024,1024]{1,0:T(8,128)(2,1)} %tokens.1, f32[1024,1024]{1,0:T(8,128)} %get-tuple-element.292.middle_grad, ...), custom_call_target="tpu_custom_call" | custom-call | bytes 1200000 | tf_op jit(solution)/shard_map/input_gradient/pallas_call | solution.py:624
  447.9 13.6 %all_to_all.12 = f32[32,1,384]{2,1,0:T(1,128)S(1)} all-to-all(f32[32,1,384]{2,1,0:T(1,128)S(1)} %copy.66), channel_id=1, replica_groups=mesh['dev'=32] {'dev'}, dimensions={0} | all-to-all | bytes 98304 | tf_op jit(solution)/shard_map/all_to_all | solution.py:858
  476.8 15.2 %collective-permute-done.27 = bf16[2,32,2560]{2,1,0:T(8,128)(2,1)S(1)} collective-permute-done((bf16[2,32,2560]{2,1,0:T(8,128)(2,1)S(1)}, bf16[2,32,2560]{2,1,0:T(8,128)(2,1)S(1)}, u32[]{:S(2)}, u32[]{:S(2)}) %collective-permute-start.27) | collective-permute-done | bytes 327712 | tf_op jit(solution)/shard_map/ppermute | solution.py:655
  505.8 4.7 collective-permute-done.33
  (210 shorter events, 103.2 us)
Async XLA Ops:
  7.2 189.1 %all-gather.2.cloned.1.call-start = ((), (), s32[]{:S(2)}) async-start(), calls=%async_computation.1 | async-start | bytes 17301504 | tf_op jit(solution)/shard_map/all_gather | solution.py:781
  16.1 13.5 %collective-permute-start.2 = (bf16[1,32,4224]{2,1,0:T(8,128)(2,1)S(1)}, bf16[1,32,4224]{2,1,0:T(8,128)(2,1)S(1)}, u32[]{:S(2)}, u32[]{:S(2)}) collective-permute-start(bf16[1,32,4224]{2,1,0:T(8,128)(2,1)S(1)} %bitcast.49), channel_id=1, source_target_pairs={{0,24},{1,25},{2,26},{3,27},{4,28},{5,29},{6,30},{7,31},{8,16},{9,... | collective-permute-start | bytes 811016 | tf_op jit(solution)/shard_map/ppermute | solution.py:655
  21.2 13.4 %collective-permute-start.1 = (bf16[1,32,4224]{2,1,0:T(8,128)(2,1)S(1)}, bf16[1,32,4224]{2,1,0:T(8,128)(2,1)S(1)}, u32[]{:S(2)}, u32[]{:S(2)}) collective-permute-start(bf16[1,32,4224]{2,1,0:T(8,128)(2,1)S(1)} %bitcast.50), channel_id=1, source_target_pairs={{0,8},{1,9},{2,10},{3,11},{4,12},{5,13},{6,14},{7,15},{8,0},{9,1},... | collective-permute-start | bytes 811016 | tf_op jit(solution)/shard_map/ppermute | solution.py:655
  21.2 23.1 %collective-permute-start = (bf16[1,32,4224]{2,1,0:T(8,128)(2,1)S(1)}, bf16[1,32,4224]{2,1,0:T(8,128)(2,1)S(1)}, u32[]{:S(2)}, u32[]{:S(2)}) collective-permute-start(bf16[1,32,4224]{2,1,0:T(8,128)(2,1)S(1)} %bitcast.51), channel_id=1, source_target_pairs={{0,16},{1,17},{2,18},{3,19},{4,20},{5,21},{6,22},{7,23},{8,24},{9,... | collective-permute-start | bytes 811016 | tf_op jit(solution)/shard_map/ppermute | solution.py:655
  23.7 20.6 %collective-permute-start.4 = (bf16[576,1024]{1,0:T(8,128)(2,1)S(1)}, bf16[576,1024]{1,0:T(8,128)(2,1)S(1)}, u32[]{:S(2)}, u32[]{:S(2)}) collective-permute-start(bf16[576,1024]{1,0:T(8,128)(2,1)S(1)} %get-tuple-element.355), channel_id=1, source_target_pairs={{1,0},{2,1},{3,2},{4,3},{5,4},{6,5},{7,6},{8,7},{9,8},{10,9},{11,1... | collective-permute-start | bytes 3538952 | tf_op jit(solution)/shard_map/ppermute | solution.py:754
  25.0 19.3 %collective-permute-start.3 = (bf16[576,1024]{1,0:T(8,128)(2,1)S(1)}, bf16[576,1024]{1,0:T(8,128)(2,1)S(1)}, u32[]{:S(2)}, u32[]{:S(2)}) collective-permute-start(bf16[576,1024]{1,0:T(8,128)(2,1)S(1)} %get-tuple-element.356), channel_id=1, source_target_pairs={{0,1},{1,2},{2,3},{3,4},{4,5},{5,6},{6,7},{7,8},{8,9},{9,10},{10,1... | collective-permute-start | bytes 3538952 | tf_op jit(solution)/shard_map/ppermute | solution.py:754
  49.4 24.8 %collective-permute-start.5 = (bf16[4,32,2048]{2,1,0:T(8,128)(2,1)}, bf16[4,32,2048]{2,1,0:T(8,128)(2,1)}, u32[]{:S(2)}, u32[]{:S(2)}) collective-permute-start(bf16[4,32,2048]{2,1,0:T(8,128)(2,1)} %pad_maximum_fusion.3), channel_id=1, source_target_pairs={{0,2},{1,3},{2,0},{3,1},{4,6},{5,7},{6,4},{7,5},{8,10},{9,11},{10,... | collective-permute-start | bytes 1572872 | tf_op jit(solution)/shard_map/ppermute | solution.py:655
  78.0 29.3 %collective-permute-start.9 = (bf16[8,32,2176]{2,1,0:T(8,128)(2,1)}, bf16[8,32,2176]{2,1,0:T(8,128)(2,1)S(1)}, u32[]{:S(2)}, u32[]{:S(2)}) collective-permute-start(bf16[8,32,2176]{2,1,0:T(8,128)(2,1)} %constant_dynamic-update-slice_fusion.13), channel_id=1, source_target_pairs={{0,2},{1,3},{2,0},{3,1},{4,6},{5,7},{6,4},{7,5},{8,10},{9,11},{10,... | collective-permute-start | bytes 3342344 | tf_op jit(solution)/shard_map/ppermute | solution.py:655
  79.5 28.8 %collective-permute-start.7 = (bf16[8,32,2048]{2,1,0:T(8,128)(2,1)}, bf16[8,32,2048]{2,1,0:T(8,128)(2,1)S(1)}, u32[]{:S(2)}, u32[]{:S(2)}) collective-permute-start(bf16[8,32,2048]{2,1,0:T(8,128)(2,1)} %constant_dynamic-update-slice_fusion.8), channel_id=1, source_target_pairs={{0,4},{1,5},{2,6},{3,7},{4,0},{5,1},{6,2},{7,3},{8,12},{9,13},{10,... | collective-permute-start | bytes 3145736 | tf_op jit(solution)/shard_map/ppermute | solution.py:655
  108.4 14.1 %collective-permute-start.10 = (bf16[16,32,2176]{2,1,0:T(8,128)(2,1)}, bf16[16,32,2176]{2,1,0:T(8,128)(2,1)}, u32[]{:S(2)}, u32[]{:S(2)}) collective-permute-start(bf16[16,32,2176]{2,1,0:T(8,128)(2,1)} %constant_dynamic-update-slice_fusion.24.two_near), channel_id=1, source_target_pairs={{0,1},{1,0},{2,3},{3,2},{4,5},{5,4},{6,7},{7,6},{8,9},{9,8},{10,11... | collective-permute-start | bytes 6684680 | tf_op jit(solution)/shard_map/ppermute | solution.py:655
  254.2 14.9 %collective-permute-start.11 = (bf16[16,4,32,1024]{3,2,1,0:T(8,128)(2,1)}, bf16[16,4,32,1024]{3,2,1,0:T(8,128)(2,1)}, u32[]{:S(2)}, u32[]{:S(2)}) collective-permute-start(bf16[16,4,32,1024]{3,2,1,0:T(8,128)(2,1)} %get-tuple-element.195), channel_id=1, source_target_pairs={{0,1},{1,0},{2,3},{3,2},{4,5},{5,4},{6,7},{7,6},{8,9},{9,8},{10,11... | collective-permute-start | bytes 12582920 | tf_op jit(solution)/shard_map/ppermute | solution.py:655
  269.1 15.1 %collective-permute-start.13 = (bf16[16,4,32,1024]{3,2,1,0:T(8,128)(2,1)}, bf16[16,4,32,1024]{3,2,1,0:T(8,128)(2,1)}, u32[]{:S(2)}, u32[]{:S(2)}) collective-permute-start(bf16[16,4,32,1024]{3,2,1,0:T(8,128)(2,1)} %bitcast.67), channel_id=1, source_target_pairs={{0,1},{1,0},{2,3},{3,2},{4,5},{5,4},{6,7},{7,6},{8,9},{9,8},{10,11... | collective-permute-start | bytes 12582920 | tf_op jit(solution)/shard_map/ppermute | solution.py:655
  272.8 66.4 %collective-permute-start.12 = (bf16[8,4,32,1024]{3,2,1,0:T(8,128)(2,1)S(1)}, bf16[8,4,32,1024]{3,2,1,0:T(8,128)(2,1)}, u32[]{:S(2)}, u32[]{:S(2)}) collective-permute-start(bf16[8,4,32,1024]{3,2,1,0:T(8,128)(2,1)S(1)} %add_convert_fusion.1), channel_id=1, source_target_pairs={{0,2},{1,3},{2,0},{3,1},{4,6},{5,7},{6,4},{7,5},{8,10},{9,11},{10,... | collective-permute-start | bytes 6291464 | tf_op jit(solution)/shard_map/ppermute | solution.py:655
  288.9 58.8 %collective-permute-start.14 = (bf16[8,4,32,1024]{3,2,1,0:T(8,128)(2,1)}, bf16[8,4,32,1024]{3,2,1,0:T(8,128)(2,1)}, u32[]{:S(2)}, u32[]{:S(2)}) collective-permute-start(bf16[8,4,32,1024]{3,2,1,0:T(8,128)(2,1)} %add_convert_fusion), channel_id=1, source_target_pairs={{0,4},{1,5},{2,6},{3,7},{4,0},{5,1},{6,2},{7,3},{8,12},{9,13},{10,... | collective-permute-start | bytes 6291464 | tf_op jit(solution)/shard_map/ppermute | solution.py:655
  311.8 27.4 %collective-permute-start.16 = (bf16[2,576,512]{2,1,0:T(8,128)(2,1)}, bf16[2,576,512]{2,1,0:T(8,128)(2,1)S(1)}, u32[]{:S(2)}, u32[]{:S(2)}) collective-permute-start(bf16[2,576,512]{2,1,0:T(8,128)(2,1)} %get-tuple-element.222), channel_id=1, source_target_pairs={{1,0},{2,1},{3,2},{4,3},{5,4},{6,5},{7,6},{8,7},{9,8},{10,9},{11,1... | collective-permute-start | bytes 3538952 | tf_op jit(solution)/shard_map/ppermute | solution.py:754
  313.0 26.1 %collective-permute-start.15 = (bf16[2,576,512]{2,1,0:T(8,128)(2,1)}, bf16[2,576,512]{2,1,0:T(8,128)(2,1)}, u32[]{:S(2)}, u32[]{:S(2)}) collective-permute-start(bf16[2,576,512]{2,1,0:T(8,128)(2,1)} %get-tuple-element.223), channel_id=1, source_target_pairs={{0,1},{1,2},{2,3},{3,4},{4,5},{5,6},{6,7},{7,8},{8,9},{9,10},{10,1... | collective-permute-start | bytes 3538952 | tf_op jit(solution)/shard_map/ppermute | solution.py:754
  353.4 51.0 %collective-permute-start.20 = (bf16[2,576,512]{2,1,0:T(8,128)(2,1)}, bf16[2,576,512]{2,1,0:T(8,128)(2,1)S(1)}, u32[]{:S(2)}, u32[]{:S(2)}) collective-permute-start(bf16[2,576,512]{2,1,0:T(8,128)(2,1)} %get-tuple-element.251), channel_id=1, source_target_pairs={{1,0},{2,1},{3,2},{4,3},{5,4},{6,5},{7,6},{8,7},{9,8},{10,9},{11,1... | collective-permute-start | bytes 3538952 | tf_op jit(solution)/shard_map/ppermute | solution.py:754
  354.7 49.7 %collective-permute-start.19 = (bf16[2,576,512]{2,1,0:T(8,128)(2,1)}, bf16[2,576,512]{2,1,0:T(8,128)(2,1)S(1)}, u32[]{:S(2)}, u32[]{:S(2)}) collective-permute-start(bf16[2,576,512]{2,1,0:T(8,128)(2,1)} %get-tuple-element.252), channel_id=1, source_target_pairs={{0,1},{1,2},{2,3},{3,4},{4,5},{5,6},{6,7},{7,8},{8,9},{9,10},{10,1... | collective-permute-start | bytes 3538952 | tf_op jit(solution)/shard_map/ppermute | solution.py:754
  357.8 38.9 %collective-permute-start.17 = (bf16[4,4,32,1024]{3,2,1,0:T(8,128)(2,1)}, bf16[4,4,32,1024]{3,2,1,0:T(8,128)(2,1)S(1)}, u32[]{:S(2)}, u32[]{:S(2)}) collective-permute-start(bf16[4,4,32,1024]{3,2,1,0:T(8,128)(2,1)} %get-tuple-element.246), channel_id=1, source_target_pairs={{0,4},{1,5},{2,6},{3,7},{4,0},{5,1},{6,2},{7,3},{8,12},{9,13},{10,... | collective-permute-start | bytes 3145736 | tf_op jit(solution)/shard_map/ppermute | solution.py:655
  360.3 44.1 %collective-permute-start.18 = (bf16[4,4,32,1024]{3,2,1,0:T(8,128)(2,1)}, bf16[4,4,32,1024]{3,2,1,0:T(8,128)(2,1)}, u32[]{:S(2)}, u32[]{:S(2)}) collective-permute-start(bf16[4,4,32,1024]{3,2,1,0:T(8,128)(2,1)} %get-tuple-element.247), channel_id=1, source_target_pairs={{0,2},{1,3},{2,0},{3,1},{4,6},{5,7},{6,4},{7,5},{8,10},{9,11},{10,... | collective-permute-start | bytes 3145736 | tf_op jit(solution)/shard_map/ppermute | solution.py:655
  410.2 15.2 %collective-permute-start.22 = (bf16[16,32,2560]{2,1,0:T(8,128)(2,1)}, bf16[16,32,2560]{2,1,0:T(8,128)(2,1)}, u32[]{:S(2)}, u32[]{:S(2)}) collective-permute-start(bf16[16,32,2560]{2,1,0:T(8,128)(2,1)} %get-tuple-element.275), channel_id=1, source_target_pairs={{0,1},{1,0},{2,3},{3,2},{4,5},{5,4},{6,7},{7,6},{8,9},{9,8},{10,11... | collective-permute-start | bytes 7864328 | tf_op jit(solution)/shard_map/ppermute | solution.py:655
  425.4 36.1 %collective-permute-start.26 = (bf16[16,32,1536]{2,1,0:T(8,128)(2,1)}, bf16[16,32,1536]{2,1,0:T(8,128)(2,1)}, u32[]{:S(2)}, u32[]{:S(2)}) collective-permute-start(bf16[16,32,1536]{2,1,0:T(8,128)(2,1)} %get-tuple-element.289), channel_id=1, source_target_pairs={{0,1},{1,0},{2,3},{3,2},{4,5},{5,4},{6,7},{7,6},{8,9},{9,8},{10,11... | collective-permute-start | bytes 4718600 | tf_op jit(solution)/shard_map/ppermute | solution.py:655
  425.5 36.0 %collective-permute-start.21 = (bf16[4,4,32,1024]{3,2,1,0:T(8,128)(2,1)}, bf16[4,4,32,1024]{3,2,1,0:T(8,128)(2,1)}, u32[]{:S(2)}, u32[]{:S(2)}) collective-permute-start(bf16[4,4,32,1024]{3,2,1,0:T(8,128)(2,1)} %pad_maximum_fusion.1), channel_id=1, source_target_pairs={{0,8},{1,9},{2,10},{3,11},{4,12},{5,13},{6,14},{7,15},{8,0},{9,1},... | collective-permute-start | bytes 3145736 | tf_op jit(solution)/shard_map/ppermute | solution.py:655
  429.0 32.5 %collective-permute-start.25 = (bf16[4,32,2560]{2,1,0:T(8,128)(2,1)}, bf16[4,32,2560]{2,1,0:T(8,128)(2,1)S(1)}, u32[]{:S(2)}, u32[]{:S(2)}) collective-permute-start(bf16[4,32,2560]{2,1,0:T(8,128)(2,1)} %get-tuple-element.346), channel_id=1, source_target_pairs={{0,6},{1,7},{2,4},{3,5},{4,2},{5,3},{6,0},{7,1},{8,14},{9,15},{10,... | collective-permute-start | bytes 1966088 | tf_op jit(solution)/shard_map/ppermute | solution.py:655
  430.3 31.3 %collective-permute-start.24 = (bf16[4,32,2560]{2,1,0:T(8,128)(2,1)}, bf16[4,32,2560]{2,1,0:T(8,128)(2,1)}, u32[]{:S(2)}, u32[]{:S(2)}) collective-permute-start(bf16[4,32,2560]{2,1,0:T(8,128)(2,1)} %get-tuple-element.347), channel_id=1, source_target_pairs={{0,4},{1,5},{2,6},{3,7},{4,0},{5,1},{6,2},{7,3},{8,12},{9,13},{10,... | collective-permute-start | bytes 1966088 | tf_op jit(solution)/shard_map/ppermute | solution.py:655
  432.7 28.9 %collective-permute-start.23 = (bf16[4,32,2560]{2,1,0:T(8,128)(2,1)}, bf16[4,32,2560]{2,1,0:T(8,128)(2,1)}, u32[]{:S(2)}, u32[]{:S(2)}) collective-permute-start(bf16[4,32,2560]{2,1,0:T(8,128)(2,1)} %get-tuple-element.348), channel_id=1, source_target_pairs={{0,2},{1,3},{2,0},{3,1},{4,6},{5,7},{6,4},{7,5},{8,10},{9,11},{10,... | collective-permute-start | bytes 1966088 | tf_op jit(solution)/shard_map/ppermute | solution.py:655
  464.0 28.0 %collective-permute-start.31 = (bf16[2,4,32,1024]{3,2,1,0:T(8,128)(2,1)S(1)}, bf16[2,4,32,1024]{3,2,1,0:T(8,128)(2,1)S(1)}, u32[]{:S(2)}, u32[]{:S(2)}) collective-permute-start(bf16[2,4,32,1024]{3,2,1,0:T(8,128)(2,1)S(1)} %pad_maximum_fusion.4), channel_id=1, source_target_pairs={{0,16},{1,17},{2,18},{3,19},{4,20},{5,21},{6,22},{7,23},{8,24},{9,... | collective-permute-start | bytes 1572872 | tf_op jit(solution)/shard_map/ppermute | solution.py:655
  467.9 24.1 %collective-permute-start.30 = (bf16[4,32,1536]{2,1,0:T(8,128)(2,1)S(1)}, bf16[4,32,1536]{2,1,0:T(8,128)(2,1)S(1)}, u32[]{:S(2)}, u32[]{:S(2)}) collective-permute-start(bf16[4,32,1536]{2,1,0:T(8,128)(2,1)S(1)} %get-tuple-element.352), channel_id=1, source_target_pairs={{0,6},{1,7},{2,4},{3,5},{4,2},{5,3},{6,0},{7,1},{8,14},{9,15},{10,... | collective-permute-start | bytes 1179656 | tf_op jit(solution)/shard_map/ppermute | solution.py:655
  470.2 21.8 %collective-permute-start.29 = (bf16[4,32,1536]{2,1,0:T(8,128)(2,1)S(1)}, bf16[4,32,1536]{2,1,0:T(8,128)(2,1)S(1)}, u32[]{:S(2)}, u32[]{:S(2)}) collective-permute-start(bf16[4,32,1536]{2,1,0:T(8,128)(2,1)S(1)} %get-tuple-element.353), channel_id=1, source_target_pairs={{0,4},{1,5},{2,6},{3,7},{4,0},{5,1},{6,2},{7,3},{8,12},{9,13},{10,... | collective-permute-start | bytes 1179656 | tf_op jit(solution)/shard_map/ppermute | solution.py:655
  471.6 20.4 %collective-permute-start.28 = (bf16[4,32,1536]{2,1,0:T(8,128)(2,1)S(1)}, bf16[4,32,1536]{2,1,0:T(8,128)(2,1)S(1)}, u32[]{:S(2)}, u32[]{:S(2)}) collective-permute-start(bf16[4,32,1536]{2,1,0:T(8,128)(2,1)S(1)} %get-tuple-element.354), channel_id=1, source_target_pairs={{0,2},{1,3},{2,0},{3,1},{4,6},{5,7},{6,4},{7,5},{8,10},{9,11},{10,... | collective-permute-start | bytes 1179656 | tf_op jit(solution)/shard_map/ppermute | solution.py:655
  472.9 19.0 %collective-permute-start.27 = (bf16[2,32,2560]{2,1,0:T(8,128)(2,1)S(1)}, bf16[2,32,2560]{2,1,0:T(8,128)(2,1)S(1)}, u32[]{:S(2)}, u32[]{:S(2)}) collective-permute-start(bf16[2,32,2560]{2,1,0:T(8,128)(2,1)S(1)} %add_convert_fusion.13), channel_id=1, source_target_pairs={{0,8},{1,9},{2,10},{3,11},{4,12},{5,13},{6,14},{7,15},{8,0},{9,1},... | collective-permute-start | bytes 983048 | tf_op jit(solution)/shard_map/ppermute | solution.py:655
  497.2 13.3 %collective-permute-start.33 = (bf16[1,32,1536]{2,1,0:T(8,128)(2,1)S(1)}, bf16[1,32,1536]{2,1,0:T(8,128)(2,1)S(1)}, u32[]{:S(2)}, u32[]{:S(2)}) collective-permute-start(bf16[1,32,1536]{2,1,0:T(8,128)(2,1)S(1)} %get-tuple-element.329), channel_id=1, source_target_pairs={{0,16},{1,17},{2,18},{3,19},{4,20},{5,21},{6,22},{7,23},{8,24},{9,... | collective-permute-start | bytes 294920 | tf_op jit(solution)/shard_map/ppermute | solution.py:655
  (33 other events, 388.0 us)
Sparse Core Ops, SparseCore 0:
  78.1 118.1 all-gather.1

commit v7 on v6

--- a/solution.py
+++ b/solution.py
@@ -754,7 +754,7 @@
     send = lambda left, right: (lax.ppermute(right, "dev", to_right), lax.ppermute(left, "dev", to_left))
 
     vectors = [first_gain, first_bias, query_bias, value_bias, out_bias, second_gain, second_bias, final_bias]
-    small = sync(jnp.concatenate([jnp.stack(vectors, axis=1), hidden_bias.reshape(part, -1)], axis=1)).astype(bf16)
+    small = sync(jnp.concatenate([jnp.stack(vectors), hidden_bias.reshape(-1, part)], axis=0)).T.astype(bf16)
     small = jnp.pad(small, ((0, 0), (0, LANES - small.shape[1])))
     cols = width // GROUPS
     qkv_low = qkv_weight.astype(bf16)
@@ -792,7 +792,7 @@
     inputs = tokens.astype(f32)
     queries, key_rows, value_rows, normed, weight_qkv, weight_out, vectors = project(window, one, two, tables)
     gain_one, bias_one, bias_query, bias_value, bias_out, gain_two, bias_two, bias_final = [vectors[i] for i in range(8)]
-    bias_hidden = vectors[8 : 8 + hidden_width // width].T.reshape(1, hidden_width)
+    bias_hidden = vectors[8 : 8 + hidden_width // width].reshape(-1, count, part).transpose(1, 0, 2).reshape(1, hidden_width)
     mixed_low, totals = attention_forward(img, queries, key_rows, value_rows, 0, pairs)
     middle = inputs + (jnp.dot(mixed_low, weight_out, preferred_element_type=f32) + bias_out)
     normed_two = layer_norm(middle, gain_two, bias_two).astype(bf16)

time: 532 us -> 527 us (level)
  local copies, waits for them, and re-layouts: 38.5 us -> 32.6 us
where the time goes in v7:
time: 527 us; the launch traced here: 520 us
  Pallas kernels  224 us (43%)
  waiting for transfers between devices  113 us (21%)
  starting transfers between devices  62.9 us (12%)
  other arithmetic  49.1 us (9%)
  local copies, waits for them, and re-layouts  32.6 us (6%)
  between operations  20.2 us (4%)
  blocking collectives  13.6 us (3%)
    ppermute x30, waiting for transfers between devices, exchange(): return lax.ppermute(x, 'dev', [(i, i ^ bit) for i in range(count)])  102 us
    pallas_call x1, Pallas kernels, feed_forward(): pl.pallas_call(feed_kernel, grid_spec=pltpu.PrefetchScalarGridSpec(num_sc...  57.7 us
    ppermute x30, starting transfers between devices, exchange(): return lax.ppermute(x, 'dev', [(i, i ^ bit) for i in range(count)])  47 us
    pallas_call x2, Pallas kernels, attention_backward(): pl.pallas_call(functools.partial(bwd_kernel, images), grid_spec=pltpu.Pre...  44.6 us
    pallas_call x2, Pallas kernels, weight_share(): pl.pallas_call(functools.partial(share_kernel, bool(extra)), grid_spec=pl...  32.6 us
    convert_element_type x11, other arithmetic, total(): functools.reduce(lambda a, b: a + b, [p.astype(f32) for p in parts])  29.3 us
    pallas_call x1, Pallas kernels, project(): pl.pallas_call(project_kernel, grid_spec=pltpu.PrefetchScalarGridSpec(num...  26.3 us
    pallas_call x1, Pallas kernels, attention_forward(): pl.pallas_call(functools.partial(fwd_kernel, images), grid_spec=pltpu.Pre...  24.7 us
  transfers between devices with their start and end apart: 37, of which 11 were waited for; matrix products, arithmetic and copies ran while one was open for 10% of the time, Pallas kernels for 32%

profile of v7, /device:TPU:0, one launch (start us, length us, event | category | flops | bytes accessed | tf_op | source)
XLA Modules:
  0.0 520.0 jit_solution(3764151120301232552)
XLA Ops:
  16.2 5.1 collective-permute-start.2
  25.1 3.1 collective-permute-start.3
  29.0 5.7 %collective-permute-done.1 = bf16[1,32,4224]{2,1,0:T(8,128)(2,1)S(1)} collective-permute-done((bf16[1,32,4224]{2,1,0:T(8,128)(2,1)S(1)}, bf16[1,32,4224]{2,1,0:T(8,128)(2,1)S(1)}, u32[]{:S(2)}, u32[]{:S(2)}) %collective-permute-start.1) | collective-permute-done | bytes 270368 | tf_op jit(solution)/shard_map/ppermute | solution.py:655
  34.7 9.7 %collective-permute-done = bf16[1,32,4224]{2,1,0:T(8,128)(2,1)S(1)} collective-permute-done((bf16[1,32,4224]{2,1,0:T(8,128)(2,1)S(1)}, bf16[1,32,4224]{2,1,0:T(8,128)(2,1)S(1)}, u32[]{:S(2)}, u32[]{:S(2)}) %collective-permute-start) | collective-permute-done | bytes 270368 | tf_op jit(solution)/shard_map/ppermute | solution.py:655
  47.5 13.0 %collective-permute-start.5 = (bf16[4,32,2048]{2,1,0:T(8,128)(2,1)}, bf16[4,32,2048]{2,1,0:T(8,128)(2,1)}, u32[]{:S(2)}, u32[]{:S(2)}) collective-permute-start(bf16[4,32,2048]{2,1,0:T(8,128)(2,1)} %pad_maximum_fusion.3), channel_id=1, source_target_pairs={{0,2},{1,3},{2,0},{3,1},{4,6},{5,7},{6,4},{7,5},{8,10},{9,11},{10,... | collective-permute-start | bytes 1572872 | tf_op jit(solution)/shard_map/ppermute | solution.py:655
  60.7 11.6 %collective-permute-done.5 = bf16[4,32,2048]{2,1,0:T(8,128)(2,1)} collective-permute-done((bf16[4,32,2048]{2,1,0:T(8,128)(2,1)}, bf16[4,32,2048]{2,1,0:T(8,128)(2,1)}, u32[]{:S(2)}, u32[]{:S(2)}) %collective-permute-start.5) | collective-permute-done | bytes 524320 | tf_op jit(solution)/shard_map/ppermute | solution.py:655
  79.6 24.8 %collective-permute-done.9 = bf16[8,32,2176]{2,1,0:T(8,128)(2,1)S(1)} collective-permute-done((bf16[8,32,2176]{2,1,0:T(8,128)(2,1)S(1)}, bf16[8,32,2176]{2,1,0:T(8,128)(2,1)S(1)}, u32[]{:S(2)}, u32[]{:S(2)}) %collective-permute-start.9) | collective-permute-done | bytes 1114144 | tf_op jit(solution)/shard_map/ppermute | solution.py:655
  116.0 3.4 pad_maximum_fusion.x
  119.4 26.3 %project.1 = (bf16[2176,1024]{1,0:T(8,128)(2,1)}, bf16[2176,1024]{1,0:T(8,128)(2,1)}, bf16[2176,1024]{1,0:T(8,128)(2,1)}, bf16[2176,1024]{1,0:T(8,128)(2,1)}, bf...) custom-call(s32[32]{0:T(128)} %broadcast_xor_fusion.table_one.table, ...), custom_call_target="tpu_custom_call" | custom-call | bytes 2400000 | tf_op jit(solution)/shard_map/project/pallas_call | solution.py:464
  147.3 24.7 %attention_forward.1 = (bf16[1024,1024]{1,0:T(8,128)(2,1)}, f32[8,24,768]{2,1,0:T(8,128)}) custom-call(s32[3]{0:T(128)} %pad_add_fusion.img_ref, bf16[2176,1024]{1,0:T(8,128)(2,1)} %get-tuple-element.186.q_ref, bf16[2176,1024]{1,0:T(8,128)(2,1)} %get-tuple-element.187.k_ref, bf16[2176,1024]{1,0:T(8,128)(2,1)} %get-tuple-element.188.v_ref), custom_call_target="tpu_custom_call" | custom-call | bytes 4000000 | tf_op jit(solution)/shard_map/attention_forward/pallas_call | solution.py:159
  173.5 4.7 fusion.19
  182.3 10.5 %all-gather.2.cloned.1.call-done.wide.tall = bf16[1024,8192]{1,0:T(8,128)(2,1)} async-done(((bf16[32,8192]{1,0:T(8,128)(2,1)}), bf16[1024,8192]{1,0:T(8,128)(2,1)}) %all-gather.2.cloned.1.call-update) | async-done | bytes 16777232 | tf_op jit(solution)/shard_map/all_gather | solution.py:781
  192.8 57.7 %feed_forward.1 = (bf16[1024,1024]{1,0:T(8,128)(2,1)}, f32[1024,1024]{1,0:T(8,128)}, f32[1,4096]{1,0:T(1,128)}, bf16[16,4,32,1024]{3,2,1,0:T(8,128)(2,1)}, bf16[...) custom-call(s32[32]{0:T(128)} %broadcast_xor_fusion.1.table_two.table, ...), custom_call_target="tpu_custom_call" | custom-call | bytes 5700000 | tf_op jit(solution)/shard_map/feed_forward/pallas_call | solution.py:389
  251.3 14.1 %final_share.1 = (bf16[16,128,1024]{2,1,0:T(8,128)(2,1)}, bf16[16,128,1024]{2,1,0:T(8,128)(2,1)}) custom-call(s32[32]{0:T(128)} %fusion.4.home, bf16[1024,4096]{1,0:T(8,128)(2,1)} %get-tuple-element.196.active, bf16[1024,1024]{1,0:T(8,128)(2,1)} %cot.5), custom_call_target="tpu_custom_call" | custom-call | bytes 1400000 | tf_op jit(solution)/shard_map/final_share/pallas_call | solution.py:358
  265.7 3.3 add_convert_fusion.1
  270.3 10.2 %branch_gradient.1 = (f32[1024,1024]{1,0:T(8,128)}, bf16[1024,1024]{1,0:T(8,128)(2,1)}, bf16[1024,1024]{1,0:T(8,128)(2,1)}, f32[8,1024]{1,0:T(8,128)}) custom-call(f32[1024,1024]{1,0:T(8,128)} %get-tuple-element.206.grad, f32[1024,1024]{1,0:T(8,128)} %copy-done, bf16[1024,1024]{1,0:T(8,128)(2,1)} %cot.5, bf16[1024,1024]{1,0:T(8,128)(2,1)} %get-tuple-element.190.weight_out, ...), custom_call_target="tpu_custom_call" | custom-call | bytes 1000000 | tf_op jit(solution)/shard_map/branch_gradient/pallas_call | solution.py:624
  280.5 4.6 add_convert_fusion
  285.9 22.5 %attention_backward.2 = (bf16[1024,512]{1,0:T(8,128)(2,1)}, f32[1024,512]{1,0:T(8,128)}, f32[1024,512]{1,0:T(8,128)}, bf16[2,576,512]{2,1,0:T(8,128)(2,1)}, bf16[2,576,512]{2,1,0:T(8,128)(2,1)}) custom-call(s32[3]{0:T(128)} %pad_add_fusion.img_ref, bf16[2176,1024]{1,0:T(8,128)(2,1)} %get-tuple-element.186.q_ref, ...), custom_call_target="tpu_custom_call" | custom-call | bytes 2600000 | tf_op jit(solution)/shard_map/attention_backward/pallas_call | solution.py:243
  309.7 5.8 %collective-permute-start.15 = (bf16[2,576,512]{2,1,0:T(8,128)(2,1)}, bf16[2,576,512]{2,1,0:T(8,128)(2,1)}, u32[]{:S(2)}, u32[]{:S(2)}) collective-permute-start(bf16[2,576,512]{2,1,0:T(8,128)(2,1)} %get-tuple-element.223), channel_id=1, source_target_pairs={{0,1},{1,2},{2,3},{3,4},{4,5},{5,6},{6,7},{7,8},{8,9},{9,10},{10,1... | collective-permute-start | bytes 3538952 | tf_op jit(solution)/shard_map/ppermute | solution.py:754
  315.5 22.2 %attention_backward.3 = (bf16[1024,512]{1,0:T(8,128)(2,1)}, f32[1024,512]{1,0:T(8,128)}, f32[1024,512]{1,0:T(8,128)}, bf16[2,576,512]{2,1,0:T(8,128)(2,1)}, bf16[2,576,512]{2,1,0:T(8,128)(2,1)}) custom-call(s32[3]{0:T(128)} %pad_add_fusion.img_ref, bf16[2176,1024]{1,0:T(8,128)(2,1)} %get-tuple-element.186.q_ref, ...), custom_call_target="tpu_custom_call" | custom-call | bytes 2600000 | tf_op jit(solution)/shard_map/attention_backward/pallas_call | solution.py:243
  337.7 6.2 %collective-permute-done.14 = bf16[8,4,32,1024]{3,2,1,0:T(8,128)(2,1)} collective-permute-done((bf16[8,4,32,1024]{3,2,1,0:T(8,128)(2,1)}, bf16[8,4,32,1024]{3,2,1,0:T(8,128)(2,1)}, u32[]{:S(2)}, u32[]{:S(2)}) %collective-permute-start.14) | collective-permute-done | bytes 2097184 | tf_op jit(solution)/shard_map/ppermute | solution.py:655
  343.9 5.7 %add_convert_fusion.3 = (bf16[4,4,32,1024]{3,2,1,0:T(8,128)(2,1)}, bf16[4,4,32,1024]{3,2,1,0:T(8,128)(2,1)}) fusion(bf16[8,4,32,1024]{3,2,1,0:T(8,128)(2,1)} %collective-permute-done.14, bf16[16,4,32,1024]{3,2,1,0:T(8,128)(2,1)} %collective-permute-done.13, bf16[16,4,32,1024]{3,2,1,0:T(8,128)(2,1)} %bitcast.46, ...), kind=kLoop, calls=%fused_computation.6 | loop fusion | flops 6291456 | bytes 8388608 | tf_op jit(solution)/shard_map/convert_element_type | solution.py:681
  358.0 20.6 %weight_share.2 = (bf16[1024,1536]{1,0:T(8,128)(2,1)}, f32[1,2560]{1,0:T(1,128)}, bf16[16,32,2560]{2,1,0:T(8,128)(2,1)}, bf16[16,32,2560]{2,1,0:T(8,128)(2,1)}, bf16[1024,1024]{1,0:T(8,128)(2,1)}) custom-call(s32[32]{0:T(128)} %broadcast_xor_fusion.table_one.table, bf16[2176,1024]{1,0:T(8,128)(2,1)} %get-tuple-element.253.normed, ...), custom_call_target="tpu_custom_call" | custom-call | bytes 1000000 | tf_op jit(solution)/shard_map/weight_share/pallas_call | solution.py:562
  378.6 14.4 %collective-permute-done.17 = bf16[4,4,32,1024]{3,2,1,0:T(8,128)(2,1)S(1)} collective-permute-done((bf16[4,4,32,1024]{3,2,1,0:T(8,128)(2,1)}, bf16[4,4,32,1024]{3,2,1,0:T(8,128)(2,1)S(1)}, u32[]{:S(2)}, u32[]{:S(2)}) %collective-permute-start.17) | collective-permute-done | bytes 1048608 | tf_op jit(solution)/shard_map/ppermute | solution.py:655
  393.0 7.5 %collective-permute-done.18 = bf16[4,4,32,1024]{3,2,1,0:T(8,128)(2,1)} collective-permute-done((bf16[4,4,32,1024]{3,2,1,0:T(8,128)(2,1)}, bf16[4,4,32,1024]{3,2,1,0:T(8,128)(2,1)}, u32[]{:S(2)}, u32[]{:S(2)}) %collective-permute-start.18) | collective-permute-done | bytes 1048608 | tf_op jit(solution)/shard_map/ppermute | solution.py:655
  406.2 3.2 collective-permute-start.22
  409.5 12.0 %weight_share.3 = (bf16[1024,1536]{1,0:T(8,128)(2,1)}, f32[1,1536]{1,0:T(1,128)}, bf16[16,32,1536]{2,1,0:T(8,128)(2,1)}, bf16[16,32,1536]{2,1,0:T(8,128)(2,1)}) custom-call(s32[32]{0:T(128)} %broadcast_xor_fusion.table_one.table, bf16[1024,1024]{1,0:T(8,128)(2,1)} %get-tuple-element.276.normed, bf16[1024,512]{1,0:T(8,128)(2,1)} %get-tuple-element.277.dq, ...), custom_call_target="tpu_custom_call" | custom-call | bytes 700000 | tf_op jit(solution)/shard_map/weight_share/pallas_call | solution.py:562
  428.8 14.0 %input_gradient.1 = (bf16[1024,1024]{1,0:T(8,128)(2,1)}, f32[8,1024]{1,0:T(8,128)}) custom-call(bf16[1024,1536]{1,0:T(8,128)(2,1)} %get-tuple-element.290.one, bf16[1024,1536]{1,0:T(8,128)(2,1)} %get-tuple-element.291.two, bf16[1024,1024]{1,0:T(8,128)(2,1)} %tokens.1, f32[1024,1024]{1,0:T(8,128)} %get-tuple-element.292.middle_grad, ...), custom_call_target="tpu_custom_call" | custom-call | bytes 1200000 | tf_op jit(solution)/shard_map/input_gradient/pallas_call | solution.py:624
  444.0 13.6 %all_to_all.12 = f32[32,1,384]{2,1,0:T(1,128)S(1)} all-to-all(f32[32,1,384]{2,1,0:T(1,128)S(1)} %copy.69), channel_id=1, replica_groups=mesh['dev'=32] {'dev'}, dimensions={0} | all-to-all | bytes 98304 | tf_op jit(solution)/shard_map/all_to_all | solution.py:858
  472.0 15.1 %collective-permute-done.27 = bf16[2,32,2560]{2,1,0:T(8,128)(2,1)S(1)} collective-permute-done((bf16[2,32,2560]{2,1,0:T(8,128)(2,1)S(1)}, bf16[2,32,2560]{2,1,0:T(8,128)(2,1)S(1)}, u32[]{:S(2)}, u32[]{:S(2)}) %collective-permute-start.27) | collective-permute-done | bytes 327712 | tf_op jit(solution)/shard_map/ppermute | solution.py:655
  501.9 3.8 collective-permute-done.33
  506.9 3.3 collective-permute-done.32
  (214 shorter events, 97.2 us)
Async XLA Ops:
  7.2 185.6 %all-gather.2.cloned.1.call-start = ((), (), s32[]{:S(2)}) async-start(), calls=%async_computation.1 | async-start | bytes 17301504 | tf_op jit(solution)/shard_map/all_gather | solution.py:781
  21.3 13.4 %collective-permute-start.1 = (bf16[1,32,4224]{2,1,0:T(8,128)(2,1)S(1)}, bf16[1,32,4224]{2,1,0:T(8,128)(2,1)S(1)}, u32[]{:S(2)}, u32[]{:S(2)}) collective-permute-start(bf16[1,32,4224]{2,1,0:T(8,128)(2,1)S(1)} %bitcast.54), channel_id=1, source_target_pairs={{0,8},{1,9},{2,10},{3,11},{4,12},{5,13},{6,14},{7,15},{8,0},{9,1},... | collective-permute-start | bytes 811016 | tf_op jit(solution)/shard_map/ppermute | solution.py:655
  21.3 23.1 %collective-permute-start = (bf16[1,32,4224]{2,1,0:T(8,128)(2,1)S(1)}, bf16[1,32,4224]{2,1,0:T(8,128)(2,1)S(1)}, u32[]{:S(2)}, u32[]{:S(2)}) collective-permute-start(bf16[1,32,4224]{2,1,0:T(8,128)(2,1)S(1)} %bitcast.55), channel_id=1, source_target_pairs={{0,16},{1,17},{2,18},{3,19},{4,20},{5,21},{6,22},{7,23},{8,24},{9,... | collective-permute-start | bytes 811016 | tf_op jit(solution)/shard_map/ppermute | solution.py:655
  23.8 20.6 %collective-permute-start.4 = (bf16[576,1024]{1,0:T(8,128)(2,1)S(1)}, bf16[576,1024]{1,0:T(8,128)(2,1)S(1)}, u32[]{:S(2)}, u32[]{:S(2)}) collective-permute-start(bf16[576,1024]{1,0:T(8,128)(2,1)S(1)} %get-tuple-element.355), channel_id=1, source_target_pairs={{1,0},{2,1},{3,2},{4,3},{5,4},{6,5},{7,6},{8,7},{9,8},{10,9},{11,1... | collective-permute-start | bytes 3538952 | tf_op jit(solution)/shard_map/ppermute | solution.py:754
  25.1 19.3 %collective-permute-start.3 = (bf16[576,1024]{1,0:T(8,128)(2,1)S(1)}, bf16[576,1024]{1,0:T(8,128)(2,1)S(1)}, u32[]{:S(2)}, u32[]{:S(2)}) collective-permute-start(bf16[576,1024]{1,0:T(8,128)(2,1)S(1)} %get-tuple-element.356), channel_id=1, source_target_pairs={{0,1},{1,2},{2,3},{3,4},{4,5},{5,6},{6,7},{7,8},{8,9},{9,10},{10,1... | collective-permute-start | bytes 3538952 | tf_op jit(solution)/shard_map/ppermute | solution.py:754
  47.5 24.8 %collective-permute-start.5 = (bf16[4,32,2048]{2,1,0:T(8,128)(2,1)}, bf16[4,32,2048]{2,1,0:T(8,128)(2,1)}, u32[]{:S(2)}, u32[]{:S(2)}) collective-permute-start(bf16[4,32,2048]{2,1,0:T(8,128)(2,1)} %pad_maximum_fusion.3), channel_id=1, source_target_pairs={{0,2},{1,3},{2,0},{3,1},{4,6},{5,7},{6,4},{7,5},{8,10},{9,11},{10,... | collective-permute-start | bytes 1572872 | tf_op jit(solution)/shard_map/ppermute | solution.py:655
  60.6 13.6 %collective-permute-start.6 = (bf16[4,32,2176]{2,1,0:T(8,128)(2,1)S(1)}, bf16[4,32,2176]{2,1,0:T(8,128)(2,1)}, u32[]{:S(2)}, u32[]{:S(2)}) collective-permute-start(bf16[4,32,2176]{2,1,0:T(8,128)(2,1)S(1)} %pad_maximum_fusion.2), channel_id=1, source_target_pairs={{0,4},{1,5},{2,6},{3,7},{4,0},{5,1},{6,2},{7,3},{8,12},{9,13},{10,... | collective-permute-start | bytes 1671176 | tf_op jit(solution)/shard_map/ppermute | solution.py:655
  75.3 29.0 %collective-permute-start.9 = (bf16[8,32,2176]{2,1,0:T(8,128)(2,1)S(1)}, bf16[8,32,2176]{2,1,0:T(8,128)(2,1)S(1)}, u32[]{:S(2)}, u32[]{:S(2)}) collective-permute-start(bf16[8,32,2176]{2,1,0:T(8,128)(2,1)S(1)} %constant_dynamic-update-slice_fusion.13), channel_id=1, source_target_pairs={{0,2},{1,3},{2,0},{3,1},{4,6},{5,7},{6,4},{7,5},{8,10},{9,11},{10,... | collective-permute-start | bytes 3342344 | tf_op jit(solution)/shard_map/ppermute | solution.py:655
  75.9 29.5 %collective-permute-start.7 = (bf16[8,32,2048]{2,1,0:T(8,128)(2,1)}, bf16[8,32,2048]{2,1,0:T(8,128)(2,1)S(1)}, u32[]{:S(2)}, u32[]{:S(2)}) collective-permute-start(bf16[8,32,2048]{2,1,0:T(8,128)(2,1)} %constant_dynamic-update-slice_fusion.8), channel_id=1, source_target_pairs={{0,4},{1,5},{2,6},{3,7},{4,0},{5,1},{6,2},{7,3},{8,12},{9,13},{10,... | collective-permute-start | bytes 3145736 | tf_op jit(solution)/shard_map/ppermute | solution.py:655
  105.4 14.0 %collective-permute-start.10 = (bf16[16,32,2176]{2,1,0:T(8,128)(2,1)}, bf16[16,32,2176]{2,1,0:T(8,128)(2,1)}, u32[]{:S(2)}, u32[]{:S(2)}) collective-permute-start(bf16[16,32,2176]{2,1,0:T(8,128)(2,1)} %constant_dynamic-update-slice_fusion.24.two_near), channel_id=1, source_target_pairs={{0,1},{1,0},{2,3},{3,2},{4,5},{5,4},{6,7},{7,6},{8,9},{9,8},{10,11... | collective-permute-start | bytes 6684680 | tf_op jit(solution)/shard_map/ppermute | solution.py:655
  250.5 14.9 %collective-permute-start.11 = (bf16[16,4,32,1024]{3,2,1,0:T(8,128)(2,1)}, bf16[16,4,32,1024]{3,2,1,0:T(8,128)(2,1)}, u32[]{:S(2)}, u32[]{:S(2)}) collective-permute-start(bf16[16,4,32,1024]{3,2,1,0:T(8,128)(2,1)} %get-tuple-element.195), channel_id=1, source_target_pairs={{0,1},{1,0},{2,3},{3,2},{4,5},{5,4},{6,7},{7,6},{8,9},{9,8},{10,11... | collective-permute-start | bytes 12582920 | tf_op jit(solution)/shard_map/ppermute | solution.py:655
  265.4 15.1 %collective-permute-start.13 = (bf16[16,4,32,1024]{3,2,1,0:T(8,128)(2,1)}, bf16[16,4,32,1024]{3,2,1,0:T(8,128)(2,1)}, u32[]{:S(2)}, u32[]{:S(2)}) collective-permute-start(bf16[16,4,32,1024]{3,2,1,0:T(8,128)(2,1)} %bitcast.73), channel_id=1, source_target_pairs={{0,1},{1,0},{2,3},{3,2},{4,5},{5,4},{6,7},{7,6},{8,9},{9,8},{10,11... | collective-permute-start | bytes 12582920 | tf_op jit(solution)/shard_map/ppermute | solution.py:655
  269.0 68.7 %collective-permute-start.12 = (bf16[8,4,32,1024]{3,2,1,0:T(8,128)(2,1)S(1)}, bf16[8,4,32,1024]{3,2,1,0:T(8,128)(2,1)}, u32[]{:S(2)}, u32[]{:S(2)}) collective-permute-start(bf16[8,4,32,1024]{3,2,1,0:T(8,128)(2,1)S(1)} %add_convert_fusion.1), channel_id=1, source_target_pairs={{0,2},{1,3},{2,0},{3,1},{4,6},{5,7},{6,4},{7,5},{8,10},{9,11},{10,... | collective-permute-start | bytes 6291464 | tf_op jit(solution)/shard_map/ppermute | solution.py:655
  285.1 58.8 %collective-permute-start.14 = (bf16[8,4,32,1024]{3,2,1,0:T(8,128)(2,1)}, bf16[8,4,32,1024]{3,2,1,0:T(8,128)(2,1)}, u32[]{:S(2)}, u32[]{:S(2)}) collective-permute-start(bf16[8,4,32,1024]{3,2,1,0:T(8,128)(2,1)} %add_convert_fusion), channel_id=1, source_target_pairs={{0,4},{1,5},{2,6},{3,7},{4,0},{5,1},{6,2},{7,3},{8,12},{9,13},{10,... | collective-permute-start | bytes 6291464 | tf_op jit(solution)/shard_map/ppermute | solution.py:655
  308.4 29.3 %collective-permute-start.16 = (bf16[2,576,512]{2,1,0:T(8,128)(2,1)}, bf16[2,576,512]{2,1,0:T(8,128)(2,1)S(1)}, u32[]{:S(2)}, u32[]{:S(2)}) collective-permute-start(bf16[2,576,512]{2,1,0:T(8,128)(2,1)} %get-tuple-element.222), channel_id=1, source_target_pairs={{1,0},{2,1},{3,2},{4,3},{5,4},{6,5},{7,6},{8,7},{9,8},{10,9},{11,1... | collective-permute-start | bytes 3538952 | tf_op jit(solution)/shard_map/ppermute | solution.py:754
  309.7 28.0 %collective-permute-start.15 = (bf16[2,576,512]{2,1,0:T(8,128)(2,1)}, bf16[2,576,512]{2,1,0:T(8,128)(2,1)}, u32[]{:S(2)}, u32[]{:S(2)}) collective-permute-start(bf16[2,576,512]{2,1,0:T(8,128)(2,1)} %get-tuple-element.223), channel_id=1, source_target_pairs={{0,1},{1,2},{2,3},{3,4},{4,5},{5,6},{6,7},{7,8},{8,9},{9,10},{10,1... | collective-permute-start | bytes 3538952 | tf_op jit(solution)/shard_map/ppermute | solution.py:754
  349.7 50.9 %collective-permute-start.20 = (bf16[2,576,512]{2,1,0:T(8,128)(2,1)}, bf16[2,576,512]{2,1,0:T(8,128)(2,1)S(1)}, u32[]{:S(2)}, u32[]{:S(2)}) collective-permute-start(bf16[2,576,512]{2,1,0:T(8,128)(2,1)} %get-tuple-element.251), channel_id=1, source_target_pairs={{1,0},{2,1},{3,2},{4,3},{5,4},{6,5},{7,6},{8,7},{9,8},{10,9},{11,1... | collective-permute-start | bytes 3538952 | tf_op jit(solution)/shard_map/ppermute | solution.py:754
  351.0 49.6 %collective-permute-start.19 = (bf16[2,576,512]{2,1,0:T(8,128)(2,1)}, bf16[2,576,512]{2,1,0:T(8,128)(2,1)S(1)}, u32[]{:S(2)}, u32[]{:S(2)}) collective-permute-start(bf16[2,576,512]{2,1,0:T(8,128)(2,1)} %get-tuple-element.252), channel_id=1, source_target_pairs={{0,1},{1,2},{2,3},{3,4},{4,5},{5,6},{6,7},{7,8},{8,9},{9,10},{10,1... | collective-permute-start | bytes 3538952 | tf_op jit(solution)/shard_map/ppermute | solution.py:754
  354.1 38.9 %collective-permute-start.17 = (bf16[4,4,32,1024]{3,2,1,0:T(8,128)(2,1)}, bf16[4,4,32,1024]{3,2,1,0:T(8,128)(2,1)S(1)}, u32[]{:S(2)}, u32[]{:S(2)}) collective-permute-start(bf16[4,4,32,1024]{3,2,1,0:T(8,128)(2,1)} %get-tuple-element.246), channel_id=1, source_target_pairs={{0,4},{1,5},{2,6},{3,7},{4,0},{5,1},{6,2},{7,3},{8,12},{9,13},{10,... | collective-permute-start | bytes 3145736 | tf_op jit(solution)/shard_map/ppermute | solution.py:655
  356.6 44.0 %collective-permute-start.18 = (bf16[4,4,32,1024]{3,2,1,0:T(8,128)(2,1)}, bf16[4,4,32,1024]{3,2,1,0:T(8,128)(2,1)}, u32[]{:S(2)}, u32[]{:S(2)}) collective-permute-start(bf16[4,4,32,1024]{3,2,1,0:T(8,128)(2,1)} %get-tuple-element.247), channel_id=1, source_target_pairs={{0,2},{1,3},{2,0},{3,1},{4,6},{5,7},{6,4},{7,5},{8,10},{9,11},{10,... | collective-permute-start | bytes 3145736 | tf_op jit(solution)/shard_map/ppermute | solution.py:655
  406.2 15.3 %collective-permute-start.22 = (bf16[16,32,2560]{2,1,0:T(8,128)(2,1)}, bf16[16,32,2560]{2,1,0:T(8,128)(2,1)}, u32[]{:S(2)}, u32[]{:S(2)}) collective-permute-start(bf16[16,32,2560]{2,1,0:T(8,128)(2,1)} %get-tuple-element.275), channel_id=1, source_target_pairs={{0,1},{1,0},{2,3},{3,2},{4,5},{5,4},{6,7},{7,6},{8,9},{9,8},{10,11... | collective-permute-start | bytes 7864328 | tf_op jit(solution)/shard_map/ppermute | solution.py:655
  421.5 36.1 %collective-permute-start.26 = (bf16[16,32,1536]{2,1,0:T(8,128)(2,1)}, bf16[16,32,1536]{2,1,0:T(8,128)(2,1)}, u32[]{:S(2)}, u32[]{:S(2)}) collective-permute-start(bf16[16,32,1536]{2,1,0:T(8,128)(2,1)} %get-tuple-element.289), channel_id=1, source_target_pairs={{0,1},{1,0},{2,3},{3,2},{4,5},{5,4},{6,7},{7,6},{8,9},{9,8},{10,11... | collective-permute-start | bytes 4718600 | tf_op jit(solution)/shard_map/ppermute | solution.py:655
  421.6 36.0 %collective-permute-start.21 = (bf16[4,4,32,1024]{3,2,1,0:T(8,128)(2,1)}, bf16[4,4,32,1024]{3,2,1,0:T(8,128)(2,1)}, u32[]{:S(2)}, u32[]{:S(2)}) collective-permute-start(bf16[4,4,32,1024]{3,2,1,0:T(8,128)(2,1)} %pad_maximum_fusion.1), channel_id=1, source_target_pairs={{0,8},{1,9},{2,10},{3,11},{4,12},{5,13},{6,14},{7,15},{8,0},{9,1},... | collective-permute-start | bytes 3145736 | tf_op jit(solution)/shard_map/ppermute | solution.py:655
  425.1 32.5 %collective-permute-start.25 = (bf16[4,32,2560]{2,1,0:T(8,128)(2,1)}, bf16[4,32,2560]{2,1,0:T(8,128)(2,1)S(1)}, u32[]{:S(2)}, u32[]{:S(2)}) collective-permute-start(bf16[4,32,2560]{2,1,0:T(8,128)(2,1)} %get-tuple-element.346), channel_id=1, source_target_pairs={{0,6},{1,7},{2,4},{3,5},{4,2},{5,3},{6,0},{7,1},{8,14},{9,15},{10,... | collective-permute-start | bytes 1966088 | tf_op jit(solution)/shard_map/ppermute | solution.py:655
  426.3 31.3 %collective-permute-start.24 = (bf16[4,32,2560]{2,1,0:T(8,128)(2,1)}, bf16[4,32,2560]{2,1,0:T(8,128)(2,1)}, u32[]{:S(2)}, u32[]{:S(2)}) collective-permute-start(bf16[4,32,2560]{2,1,0:T(8,128)(2,1)} %get-tuple-element.347), channel_id=1, source_target_pairs={{0,4},{1,5},{2,6},{3,7},{4,0},{5,1},{6,2},{7,3},{8,12},{9,13},{10,... | collective-permute-start | bytes 1966088 | tf_op jit(solution)/shard_map/ppermute | solution.py:655
  428.7 28.9 %collective-permute-start.23 = (bf16[4,32,2560]{2,1,0:T(8,128)(2,1)}, bf16[4,32,2560]{2,1,0:T(8,128)(2,1)}, u32[]{:S(2)}, u32[]{:S(2)}) collective-permute-start(bf16[4,32,2560]{2,1,0:T(8,128)(2,1)} %get-tuple-element.348), channel_id=1, source_target_pairs={{0,2},{1,3},{2,0},{3,1},{4,6},{5,7},{6,4},{7,5},{8,10},{9,11},{10,... | collective-permute-start | bytes 1966088 | tf_op jit(solution)/shard_map/ppermute | solution.py:655
  460.1 27.1 %collective-permute-start.31 = (bf16[2,4,32,1024]{3,2,1,0:T(8,128)(2,1)S(1)}, bf16[2,4,32,1024]{3,2,1,0:T(8,128)(2,1)S(1)}, u32[]{:S(2)}, u32[]{:S(2)}) collective-permute-start(bf16[2,4,32,1024]{3,2,1,0:T(8,128)(2,1)S(1)} %pad_maximum_fusion.4), channel_id=1, source_target_pairs={{0,16},{1,17},{2,18},{3,19},{4,20},{5,21},{6,22},{7,23},{8,24},{9,... | collective-permute-start | bytes 1572872 | tf_op jit(solution)/shard_map/ppermute | solution.py:655
  463.1 24.1 %collective-permute-start.30 = (bf16[4,32,1536]{2,1,0:T(8,128)(2,1)S(1)}, bf16[4,32,1536]{2,1,0:T(8,128)(2,1)S(1)}, u32[]{:S(2)}, u32[]{:S(2)}) collective-permute-start(bf16[4,32,1536]{2,1,0:T(8,128)(2,1)S(1)} %get-tuple-element.352), channel_id=1, source_target_pairs={{0,6},{1,7},{2,4},{3,5},{4,2},{5,3},{6,0},{7,1},{8,14},{9,15},{10,... | collective-permute-start | bytes 1179656 | tf_op jit(solution)/shard_map/ppermute | solution.py:655
  465.4 21.8 %collective-permute-start.29 = (bf16[4,32,1536]{2,1,0:T(8,128)(2,1)S(1)}, bf16[4,32,1536]{2,1,0:T(8,128)(2,1)S(1)}, u32[]{:S(2)}, u32[]{:S(2)}) collective-permute-start(bf16[4,32,1536]{2,1,0:T(8,128)(2,1)S(1)} %get-tuple-element.353), channel_id=1, source_target_pairs={{0,4},{1,5},{2,6},{3,7},{4,0},{5,1},{6,2},{7,3},{8,12},{9,13},{10,... | collective-permute-start | bytes 1179656 | tf_op jit(solution)/shard_map/ppermute | solution.py:655
  466.8 20.4 %collective-permute-start.28 = (bf16[4,32,1536]{2,1,0:T(8,128)(2,1)S(1)}, bf16[4,32,1536]{2,1,0:T(8,128)(2,1)S(1)}, u32[]{:S(2)}, u32[]{:S(2)}) collective-permute-start(bf16[4,32,1536]{2,1,0:T(8,128)(2,1)S(1)} %get-tuple-element.354), channel_id=1, source_target_pairs={{0,2},{1,3},{2,0},{3,1},{4,6},{5,7},{6,4},{7,5},{8,10},{9,11},{10,... | collective-permute-start | bytes 1179656 | tf_op jit(solution)/shard_map/ppermute | solution.py:655
  468.1 19.0 %collective-permute-start.27 = (bf16[2,32,2560]{2,1,0:T(8,128)(2,1)S(1)}, bf16[2,32,2560]{2,1,0:T(8,128)(2,1)S(1)}, u32[]{:S(2)}, u32[]{:S(2)}) collective-permute-start(bf16[2,32,2560]{2,1,0:T(8,128)(2,1)S(1)} %add_convert_fusion.13), channel_id=1, source_target_pairs={{0,8},{1,9},{2,10},{3,11},{4,12},{5,13},{6,14},{7,15},{8,0},{9,1},... | collective-permute-start | bytes 983048 | tf_op jit(solution)/shard_map/ppermute | solution.py:655
  496.9 13.3 %collective-permute-start.32 = (bf16[1,32,2560]{2,1,0:T(8,128)(2,1)S(1)}, bf16[1,32,2560]{2,1,0:T(8,128)(2,1)S(1)}, u32[]{:S(2)}, u32[]{:S(2)}) collective-permute-start(bf16[1,32,2560]{2,1,0:T(8,128)(2,1)S(1)} %add_convert_fusion.16), channel_id=1, source_target_pairs={{0,16},{1,17},{2,18},{3,19},{4,20},{5,21},{6,22},{7,23},{8,24},{9,... | collective-permute-start | bytes 491528 | tf_op jit(solution)/shard_map/ppermute | solution.py:655
  (34 other events, 369.6 us)
Sparse Core Ops, SparseCore 0:
  75.5 117.2 all-gather.1

commit v8 on v7

--- a/solution.py
+++ b/solution.py
@@ -616,14 +616,14 @@
     sums[1:2, :] += bias_sum
 
 
-def row_blocks(kernel, name, blocked, whole, outs, us):
+def row_blocks(kernel, name, blocked, whole, outs, us, parts):
     rows, width = blocked[0].shape[0], outs[0][0]
-    block = rows // 4
+    block = rows // parts
     strip = lambda cols: pl.BlockSpec((block, cols), lambda t: (t, 0))
     fixed = lambda *shape: pl.BlockSpec(shape, lambda t: (0,) * len(shape), pipeline_mode=pl.Buffered(1))
     return pl.pallas_call(
         kernel,
-        grid=(4,),
+        grid=(parts,),
         in_specs=[strip(a.shape[1]) for a in blocked] + [fixed(*a.shape) for a in whole],
         out_specs=[strip(cols) for cols, _ in outs] + [fixed(8, width)],
         out_shape=[jax.ShapeDtypeStruct((rows, cols), kind) for cols, kind in outs] + [jax.ShapeDtypeStruct((8, width), f32)],
@@ -636,14 +636,14 @@
 def branch_gradient(grad, middle, cot, weight_out, vectors):
     width = middle.shape[1]
     outs = [(width, f32), (width, bf16), (width, bf16)]
-    return row_blocks(branch_kernel, "branch_gradient", [grad, middle, cot], [weight_out, vectors], outs, 10)
+    return row_blocks(branch_kernel, "branch_gradient", [grad, middle, cot], [weight_out, vectors], outs, 10, 4)
 
 
 def input_gradient(one, two, tokens, middle_grad, weight, vectors):
     def kernel(one, two, tokens, middle_grad, weight, vectors, out, sums):
         input_kernel(one, two, weight, tokens, middle_grad, vectors, out, sums)
 
-    return row_blocks(kernel, "input_gradient", [one, two, tokens, middle_grad], [weight, vectors], [(tokens.shape[1], bf16)], 12)
+    return row_blocks(kernel, "input_gradient", [one, two, tokens, middle_grad], [weight, vectors], [(tokens.shape[1], bf16)], 12, 2)
 
 
 def bit_orders(count):

time: 527 us -> 528 us (level)
  Pallas kernels: 224 us -> 234 us
  waiting for transfers between devices: 113 us -> 106 us
  transfers between devices with their start and end apart: 37 -> 37, of which waited for: 11 -> 11; matrix products, arithmetic and copies ran while one was open for 10% -> 10% of each run, Pallas kernels for 32% -> 34%
where the time goes in v8:
time: 528 us; the launch traced here: 520 us
  Pallas kernels  234 us (44%)
  waiting for transfers between devices  106 us (20%)
  starting transfers between devices  61.1 us (12%)
  other arithmetic  49.1 us (9%)
  local copies, waits for them, and re-layouts  32.6 us (6%)
  between operations  20.5 us (4%)
  blocking collectives  12.7 us (2%)
    ppermute x30, waiting for transfers between devices, exchange(): return lax.ppermute(x, 'dev', [(i, i ^ bit) for i in range(count)])  100 us
    pallas_call x1, Pallas kernels, feed_forward(): pl.pallas_call(feed_kernel, grid_spec=pltpu.PrefetchScalarGridSpec(num_sc...  57.9 us
    pallas_call x2, Pallas kernels, attention_backward(): pl.pallas_call(functools.partial(bwd_kernel, images), grid_spec=pltpu.Pre...  48.5 us
    ppermute x30, starting transfers between devices, exchange(): return lax.ppermute(x, 'dev', [(i, i ^ bit) for i in range(count)])  47 us
    pallas_call x2, Pallas kernels, weight_share(): pl.pallas_call(functools.partial(share_kernel, bool(extra)), grid_spec=pl...  32.6 us
    convert_element_type x11, other arithmetic, total(): functools.reduce(lambda a, b: a + b, [p.astype(f32) for p in parts])  29.3 us
    pallas_call x1, Pallas kernels, attention_forward(): pl.pallas_call(functools.partial(fwd_kernel, images), grid_spec=pltpu.Pre...  29.1 us
    pallas_call x1, Pallas kernels, project(): pl.pallas_call(project_kernel, grid_spec=pltpu.PrefetchScalarGridSpec(num...  26.3 us
  transfers between devices with their start and end apart: 37, of which 11 were waited for; matrix products, arithmetic and copies ran while one was open for 10% of the time, Pallas kernels for 34%

profile of v8, /device:TPU:0, one launch (start us, length us, event | category | flops | bytes accessed | tf_op | source)
XLA Modules:
  0.0 520.4 jit_solution(12786842213935618836)
XLA Ops:
  16.2 5.1 collective-permute-start.2
  25.1 3.1 collective-permute-start.3
  29.0 5.7 %collective-permute-done.1 = bf16[1,32,4224]{2,1,0:T(8,128)(2,1)S(1)} collective-permute-done((bf16[1,32,4224]{2,1,0:T(8,128)(2,1)S(1)}, bf16[1,32,4224]{2,1,0:T(8,128)(2,1)S(1)}, u32[]{:S(2)}, u32[]{:S(2)}) %collective-permute-start.1) | collective-permute-done | bytes 270368 | tf_op jit(solution)/shard_map/ppermute | solution.py:655
  34.7 9.7 %collective-permute-done = bf16[1,32,4224]{2,1,0:T(8,128)(2,1)S(1)} collective-permute-done((bf16[1,32,4224]{2,1,0:T(8,128)(2,1)S(1)}, bf16[1,32,4224]{2,1,0:T(8,128)(2,1)S(1)}, u32[]{:S(2)}, u32[]{:S(2)}) %collective-permute-start) | collective-permute-done | bytes 270368 | tf_op jit(solution)/shard_map/ppermute | solution.py:655
  47.5 13.0 %collective-permute-start.5 = (bf16[4,32,2048]{2,1,0:T(8,128)(2,1)}, bf16[4,32,2048]{2,1,0:T(8,128)(2,1)}, u32[]{:S(2)}, u32[]{:S(2)}) collective-permute-start(bf16[4,32,2048]{2,1,0:T(8,128)(2,1)} %pad_maximum_fusion.3), channel_id=1, source_target_pairs={{0,2},{1,3},{2,0},{3,1},{4,6},{5,7},{6,4},{7,5},{8,10},{9,11},{10,... | collective-permute-start | bytes 1572872 | tf_op jit(solution)/shard_map/ppermute | solution.py:655
  60.7 11.6 %collective-permute-done.5 = bf16[4,32,2048]{2,1,0:T(8,128)(2,1)} collective-permute-done((bf16[4,32,2048]{2,1,0:T(8,128)(2,1)}, bf16[4,32,2048]{2,1,0:T(8,128)(2,1)}, u32[]{:S(2)}, u32[]{:S(2)}) %collective-permute-start.5) | collective-permute-done | bytes 524320 | tf_op jit(solution)/shard_map/ppermute | solution.py:655
  79.6 24.8 %collective-permute-done.9 = bf16[8,32,2176]{2,1,0:T(8,128)(2,1)S(1)} collective-permute-done((bf16[8,32,2176]{2,1,0:T(8,128)(2,1)S(1)}, bf16[8,32,2176]{2,1,0:T(8,128)(2,1)S(1)}, u32[]{:S(2)}, u32[]{:S(2)}) %collective-permute-start.9) | collective-permute-done | bytes 1114144 | tf_op jit(solution)/shard_map/ppermute | solution.py:655
  116.0 3.4 pad_maximum_fusion.x
  119.4 26.3 %project.1 = (bf16[2176,1024]{1,0:T(8,128)(2,1)}, bf16[2176,1024]{1,0:T(8,128)(2,1)}, bf16[2176,1024]{1,0:T(8,128)(2,1)}, bf16[2176,1024]{1,0:T(8,128)(2,1)}, bf...) custom-call(s32[32]{0:T(128)} %broadcast_xor_fusion.table_one.table, ...), custom_call_target="tpu_custom_call" | custom-call | bytes 2400000 | tf_op jit(solution)/shard_map/project/pallas_call | solution.py:464
  147.3 29.1 %attention_forward.1 = (bf16[1024,1024]{1,0:T(8,128)(2,1)}, f32[8,24,768]{2,1,0:T(8,128)}) custom-call(s32[3]{0:T(128)} %pad_add_fusion.img_ref, bf16[2176,1024]{1,0:T(8,128)(2,1)} %get-tuple-element.186.q_ref, bf16[2176,1024]{1,0:T(8,128)(2,1)} %get-tuple-element.187.k_ref, bf16[2176,1024]{1,0:T(8,128)(2,1)} %get-tuple-element.188.v_ref), custom_call_target="tpu_custom_call" | custom-call | bytes 4000000 | tf_op jit(solution)/shard_map/attention_forward/pallas_call | solution.py:159
  177.9 4.7 fusion.19
  186.7 6.0 %all-gather.2.cloned.1.call-done.wide.tall = bf16[1024,8192]{1,0:T(8,128)(2,1)} async-done(((bf16[32,8192]{1,0:T(8,128)(2,1)}), bf16[1024,8192]{1,0:T(8,128)(2,1)}) %all-gather.2.cloned.1.call-update) | async-done | bytes 16777232 | tf_op jit(solution)/shard_map/all_gather | solution.py:781
  192.8 57.9 %feed_forward.1 = (bf16[1024,1024]{1,0:T(8,128)(2,1)}, f32[1024,1024]{1,0:T(8,128)}, f32[1,4096]{1,0:T(1,128)}, bf16[16,4,32,1024]{3,2,1,0:T(8,128)(2,1)}, bf16[...) custom-call(s32[32]{0:T(128)} %broadcast_xor_fusion.1.table_two.table, ...), custom_call_target="tpu_custom_call" | custom-call | bytes 5700000 | tf_op jit(solution)/shard_map/feed_forward/pallas_call | solution.py:389
  251.5 14.1 %final_share.1 = (bf16[16,128,1024]{2,1,0:T(8,128)(2,1)}, bf16[16,128,1024]{2,1,0:T(8,128)(2,1)}) custom-call(s32[32]{0:T(128)} %fusion.4.home, bf16[1024,4096]{1,0:T(8,128)(2,1)} %get-tuple-element.196.active, bf16[1024,1024]{1,0:T(8,128)(2,1)} %cot.5), custom_call_target="tpu_custom_call" | custom-call | bytes 1400000 | tf_op jit(solution)/shard_map/final_share/pallas_call | solution.py:358
  265.9 3.3 add_convert_fusion.1
  270.5 10.2 %branch_gradient.1 = (f32[1024,1024]{1,0:T(8,128)}, bf16[1024,1024]{1,0:T(8,128)(2,1)}, bf16[1024,1024]{1,0:T(8,128)(2,1)}, f32[8,1024]{1,0:T(8,128)}) custom-call(f32[1024,1024]{1,0:T(8,128)} %get-tuple-element.206.grad, f32[1024,1024]{1,0:T(8,128)} %copy-done, bf16[1024,1024]{1,0:T(8,128)(2,1)} %cot.5, bf16[1024,1024]{1,0:T(8,128)(2,1)} %get-tuple-element.190.weight_out, ...), custom_call_target="tpu_custom_call" | custom-call | bytes 1000000 | tf_op jit(solution)/shard_map/branch_gradient/pallas_call | solution.py:624
  280.7 4.6 add_convert_fusion
  286.1 24.2 %attention_backward.2 = (bf16[1024,512]{1,0:T(8,128)(2,1)}, f32[1024,512]{1,0:T(8,128)}, f32[1024,512]{1,0:T(8,128)}, bf16[2,576,512]{2,1,0:T(8,128)(2,1)}, bf16[2,576,512]{2,1,0:T(8,128)(2,1)}) custom-call(s32[3]{0:T(128)} %pad_add_fusion.img_ref, bf16[2176,1024]{1,0:T(8,128)(2,1)} %get-tuple-element.186.q_ref, ...), custom_call_target="tpu_custom_call" | custom-call | bytes 2600000 | tf_op jit(solution)/shard_map/attention_backward/pallas_call | solution.py:243
  311.7 4.0 collective-permute-start.15
  315.7 24.2 %attention_backward.3 = (bf16[1024,512]{1,0:T(8,128)(2,1)}, f32[1024,512]{1,0:T(8,128)}, f32[1024,512]{1,0:T(8,128)}, bf16[2,576,512]{2,1,0:T(8,128)(2,1)}, bf16[2,576,512]{2,1,0:T(8,128)(2,1)}) custom-call(s32[3]{0:T(128)} %pad_add_fusion.img_ref, bf16[2176,1024]{1,0:T(8,128)(2,1)} %get-tuple-element.186.q_ref, ...), custom_call_target="tpu_custom_call" | custom-call | bytes 2600000 | tf_op jit(solution)/shard_map/attention_backward/pallas_call | solution.py:243
  340.0 4.2 collective-permute-done.14
  344.1 5.7 %add_convert_fusion.3 = (bf16[4,4,32,1024]{3,2,1,0:T(8,128)(2,1)}, bf16[4,4,32,1024]{3,2,1,0:T(8,128)(2,1)}) fusion(bf16[8,4,32,1024]{3,2,1,0:T(8,128)(2,1)} %collective-permute-done.14, bf16[16,4,32,1024]{3,2,1,0:T(8,128)(2,1)} %collective-permute-done.13, bf16[16,4,32,1024]{3,2,1,0:T(8,128)(2,1)} %bitcast.46, ...), kind=kLoop, calls=%fused_computation.6 | loop fusion | flops 6291456 | bytes 8388608 | tf_op jit(solution)/shard_map/convert_element_type | solution.py:681
  351.2 3.1 collective-permute-start.19
  358.2 20.6 %weight_share.2 = (bf16[1024,1536]{1,0:T(8,128)(2,1)}, f32[1,2560]{1,0:T(1,128)}, bf16[16,32,2560]{2,1,0:T(8,128)(2,1)}, bf16[16,32,2560]{2,1,0:T(8,128)(2,1)}, bf16[1024,1024]{1,0:T(8,128)(2,1)}) custom-call(s32[32]{0:T(128)} %broadcast_xor_fusion.table_one.table, bf16[2176,1024]{1,0:T(8,128)(2,1)} %get-tuple-element.253.normed, ...), custom_call_target="tpu_custom_call" | custom-call | bytes 1000000 | tf_op jit(solution)/shard_map/weight_share/pallas_call | solution.py:562
  378.8 14.4 %collective-permute-done.17 = bf16[4,4,32,1024]{3,2,1,0:T(8,128)(2,1)S(1)} collective-permute-done((bf16[4,4,32,1024]{3,2,1,0:T(8,128)(2,1)}, bf16[4,4,32,1024]{3,2,1,0:T(8,128)(2,1)S(1)}, u32[]{:S(2)}, u32[]{:S(2)}) %collective-permute-start.17) | collective-permute-done | bytes 1048608 | tf_op jit(solution)/shard_map/ppermute | solution.py:655
  393.2 7.5 %collective-permute-done.18 = bf16[4,4,32,1024]{3,2,1,0:T(8,128)(2,1)} collective-permute-done((bf16[4,4,32,1024]{3,2,1,0:T(8,128)(2,1)}, bf16[4,4,32,1024]{3,2,1,0:T(8,128)(2,1)}, u32[]{:S(2)}, u32[]{:S(2)}) %collective-permute-start.18) | collective-permute-done | bytes 1048608 | tf_op jit(solution)/shard_map/ppermute | solution.py:655
  406.4 3.2 collective-permute-start.22
  409.7 12.0 %weight_share.3 = (bf16[1024,1536]{1,0:T(8,128)(2,1)}, f32[1,1536]{1,0:T(1,128)}, bf16[16,32,1536]{2,1,0:T(8,128)(2,1)}, bf16[16,32,1536]{2,1,0:T(8,128)(2,1)}) custom-call(s32[32]{0:T(128)} %broadcast_xor_fusion.table_one.table, bf16[1024,1024]{1,0:T(8,128)(2,1)} %get-tuple-element.276.normed, bf16[1024,512]{1,0:T(8,128)(2,1)} %get-tuple-element.277.dq, ...), custom_call_target="tpu_custom_call" | custom-call | bytes 700000 | tf_op jit(solution)/shard_map/weight_share/pallas_call | solution.py:562
  429.0 14.9 %input_gradient.1 = (bf16[1024,1024]{1,0:T(8,128)(2,1)}, f32[8,1024]{1,0:T(8,128)}) custom-call(bf16[1024,1536]{1,0:T(8,128)(2,1)} %get-tuple-element.290.one, bf16[1024,1536]{1,0:T(8,128)(2,1)} %get-tuple-element.291.two, bf16[1024,1024]{1,0:T(8,128)(2,1)} %tokens.1, f32[1024,1024]{1,0:T(8,128)} %get-tuple-element.292.middle_grad, ...), custom_call_target="tpu_custom_call" | custom-call | bytes 1200000 | tf_op jit(solution)/shard_map/input_gradient/pallas_call | solution.py:624
  445.1 12.7 %all_to_all.12 = f32[32,1,384]{2,1,0:T(1,128)S(1)} all-to-all(f32[32,1,384]{2,1,0:T(1,128)S(1)} %copy.69), channel_id=1, replica_groups=mesh['dev'=32] {'dev'}, dimensions={0} | all-to-all | bytes 98304 | tf_op jit(solution)/shard_map/all_to_all | solution.py:858
  473.1 15.1 %collective-permute-done.27 = bf16[2,32,2560]{2,1,0:T(8,128)(2,1)S(1)} collective-permute-done((bf16[2,32,2560]{2,1,0:T(8,128)(2,1)S(1)}, bf16[2,32,2560]{2,1,0:T(8,128)(2,1)S(1)}, u32[]{:S(2)}, u32[]{:S(2)}) %collective-permute-start.27) | collective-permute-done | bytes 327712 | tf_op jit(solution)/shard_map/ppermute | solution.py:655
  502.1 4.7 collective-permute-done.33
  (214 shorter events, 96.4 us)
Async XLA Ops:
  7.2 185.6 %all-gather.2.cloned.1.call-start = ((), (), s32[]{:S(2)}) async-start(), calls=%async_computation.1 | async-start | bytes 17301504 | tf_op jit(solution)/shard_map/all_gather | solution.py:781
  21.3 13.4 %collective-permute-start.1 = (bf16[1,32,4224]{2,1,0:T(8,128)(2,1)S(1)}, bf16[1,32,4224]{2,1,0:T(8,128)(2,1)S(1)}, u32[]{:S(2)}, u32[]{:S(2)}) collective-permute-start(bf16[1,32,4224]{2,1,0:T(8,128)(2,1)S(1)} %bitcast.54), channel_id=1, source_target_pairs={{0,8},{1,9},{2,10},{3,11},{4,12},{5,13},{6,14},{7,15},{8,0},{9,1},... | collective-permute-start | bytes 811016 | tf_op jit(solution)/shard_map/ppermute | solution.py:655
  21.3 23.1 %collective-permute-start = (bf16[1,32,4224]{2,1,0:T(8,128)(2,1)S(1)}, bf16[1,32,4224]{2,1,0:T(8,128)(2,1)S(1)}, u32[]{:S(2)}, u32[]{:S(2)}) collective-permute-start(bf16[1,32,4224]{2,1,0:T(8,128)(2,1)S(1)} %bitcast.55), channel_id=1, source_target_pairs={{0,16},{1,17},{2,18},{3,19},{4,20},{5,21},{6,22},{7,23},{8,24},{9,... | collective-permute-start | bytes 811016 | tf_op jit(solution)/shard_map/ppermute | solution.py:655
  23.8 20.6 %collective-permute-start.4 = (bf16[576,1024]{1,0:T(8,128)(2,1)S(1)}, bf16[576,1024]{1,0:T(8,128)(2,1)S(1)}, u32[]{:S(2)}, u32[]{:S(2)}) collective-permute-start(bf16[576,1024]{1,0:T(8,128)(2,1)S(1)} %get-tuple-element.355), channel_id=1, source_target_pairs={{1,0},{2,1},{3,2},{4,3},{5,4},{6,5},{7,6},{8,7},{9,8},{10,9},{11,1... | collective-permute-start | bytes 3538952 | tf_op jit(solution)/shard_map/ppermute | solution.py:754
  25.1 19.3 %collective-permute-start.3 = (bf16[576,1024]{1,0:T(8,128)(2,1)S(1)}, bf16[576,1024]{1,0:T(8,128)(2,1)S(1)}, u32[]{:S(2)}, u32[]{:S(2)}) collective-permute-start(bf16[576,1024]{1,0:T(8,128)(2,1)S(1)} %get-tuple-element.356), channel_id=1, source_target_pairs={{0,1},{1,2},{2,3},{3,4},{4,5},{5,6},{6,7},{7,8},{8,9},{9,10},{10,1... | collective-permute-start | bytes 3538952 | tf_op jit(solution)/shard_map/ppermute | solution.py:754
  47.5 24.8 %collective-permute-start.5 = (bf16[4,32,2048]{2,1,0:T(8,128)(2,1)}, bf16[4,32,2048]{2,1,0:T(8,128)(2,1)}, u32[]{:S(2)}, u32[]{:S(2)}) collective-permute-start(bf16[4,32,2048]{2,1,0:T(8,128)(2,1)} %pad_maximum_fusion.3), channel_id=1, source_target_pairs={{0,2},{1,3},{2,0},{3,1},{4,6},{5,7},{6,4},{7,5},{8,10},{9,11},{10,... | collective-permute-start | bytes 1572872 | tf_op jit(solution)/shard_map/ppermute | solution.py:655
  60.6 13.6 %collective-permute-start.6 = (bf16[4,32,2176]{2,1,0:T(8,128)(2,1)S(1)}, bf16[4,32,2176]{2,1,0:T(8,128)(2,1)}, u32[]{:S(2)}, u32[]{:S(2)}) collective-permute-start(bf16[4,32,2176]{2,1,0:T(8,128)(2,1)S(1)} %pad_maximum_fusion.2), channel_id=1, source_target_pairs={{0,4},{1,5},{2,6},{3,7},{4,0},{5,1},{6,2},{7,3},{8,12},{9,13},{10,... | collective-permute-start | bytes 1671176 | tf_op jit(solution)/shard_map/ppermute | solution.py:655
  75.3 29.0 %collective-permute-start.9 = (bf16[8,32,2176]{2,1,0:T(8,128)(2,1)S(1)}, bf16[8,32,2176]{2,1,0:T(8,128)(2,1)S(1)}, u32[]{:S(2)}, u32[]{:S(2)}) collective-permute-start(bf16[8,32,2176]{2,1,0:T(8,128)(2,1)S(1)} %constant_dynamic-update-slice_fusion.13), channel_id=1, source_target_pairs={{0,2},{1,3},{2,0},{3,1},{4,6},{5,7},{6,4},{7,5},{8,10},{9,11},{10,... | collective-permute-start | bytes 3342344 | tf_op jit(solution)/shard_map/ppermute | solution.py:655
  75.9 29.5 %collective-permute-start.7 = (bf16[8,32,2048]{2,1,0:T(8,128)(2,1)}, bf16[8,32,2048]{2,1,0:T(8,128)(2,1)S(1)}, u32[]{:S(2)}, u32[]{:S(2)}) collective-permute-start(bf16[8,32,2048]{2,1,0:T(8,128)(2,1)} %constant_dynamic-update-slice_fusion.8), channel_id=1, source_target_pairs={{0,4},{1,5},{2,6},{3,7},{4,0},{5,1},{6,2},{7,3},{8,12},{9,13},{10,... | collective-permute-start | bytes 3145736 | tf_op jit(solution)/shard_map/ppermute | solution.py:655
  105.4 14.0 %collective-permute-start.10 = (bf16[16,32,2176]{2,1,0:T(8,128)(2,1)}, bf16[16,32,2176]{2,1,0:T(8,128)(2,1)}, u32[]{:S(2)}, u32[]{:S(2)}) collective-permute-start(bf16[16,32,2176]{2,1,0:T(8,128)(2,1)} %constant_dynamic-update-slice_fusion.24.two_near), channel_id=1, source_target_pairs={{0,1},{1,0},{2,3},{3,2},{4,5},{5,4},{6,7},{7,6},{8,9},{9,8},{10,11... | collective-permute-start | bytes 6684680 | tf_op jit(solution)/shard_map/ppermute | solution.py:655
  250.7 14.9 %collective-permute-start.11 = (bf16[16,4,32,1024]{3,2,1,0:T(8,128)(2,1)}, bf16[16,4,32,1024]{3,2,1,0:T(8,128)(2,1)}, u32[]{:S(2)}, u32[]{:S(2)}) collective-permute-start(bf16[16,4,32,1024]{3,2,1,0:T(8,128)(2,1)} %get-tuple-element.195), channel_id=1, source_target_pairs={{0,1},{1,0},{2,3},{3,2},{4,5},{5,4},{6,7},{7,6},{8,9},{9,8},{10,11... | collective-permute-start | bytes 12582920 | tf_op jit(solution)/shard_map/ppermute | solution.py:655
  265.6 15.1 %collective-permute-start.13 = (bf16[16,4,32,1024]{3,2,1,0:T(8,128)(2,1)}, bf16[16,4,32,1024]{3,2,1,0:T(8,128)(2,1)}, u32[]{:S(2)}, u32[]{:S(2)}) collective-permute-start(bf16[16,4,32,1024]{3,2,1,0:T(8,128)(2,1)} %bitcast.73), channel_id=1, source_target_pairs={{0,1},{1,0},{2,3},{3,2},{4,5},{5,4},{6,7},{7,6},{8,9},{9,8},{10,11... | collective-permute-start | bytes 12582920 | tf_op jit(solution)/shard_map/ppermute | solution.py:655
  269.2 70.7 %collective-permute-start.12 = (bf16[8,4,32,1024]{3,2,1,0:T(8,128)(2,1)S(1)}, bf16[8,4,32,1024]{3,2,1,0:T(8,128)(2,1)}, u32[]{:S(2)}, u32[]{:S(2)}) collective-permute-start(bf16[8,4,32,1024]{3,2,1,0:T(8,128)(2,1)S(1)} %add_convert_fusion.1), channel_id=1, source_target_pairs={{0,2},{1,3},{2,0},{3,1},{4,6},{5,7},{6,4},{7,5},{8,10},{9,11},{10,... | collective-permute-start | bytes 6291464 | tf_op jit(solution)/shard_map/ppermute | solution.py:655
  285.3 58.8 %collective-permute-start.14 = (bf16[8,4,32,1024]{3,2,1,0:T(8,128)(2,1)}, bf16[8,4,32,1024]{3,2,1,0:T(8,128)(2,1)}, u32[]{:S(2)}, u32[]{:S(2)}) collective-permute-start(bf16[8,4,32,1024]{3,2,1,0:T(8,128)(2,1)} %add_convert_fusion), channel_id=1, source_target_pairs={{0,4},{1,5},{2,6},{3,7},{4,0},{5,1},{6,2},{7,3},{8,12},{9,13},{10,... | collective-permute-start | bytes 6291464 | tf_op jit(solution)/shard_map/ppermute | solution.py:655
  310.4 29.6 %collective-permute-start.16 = (bf16[2,576,512]{2,1,0:T(8,128)(2,1)}, bf16[2,576,512]{2,1,0:T(8,128)(2,1)S(1)}, u32[]{:S(2)}, u32[]{:S(2)}) collective-permute-start(bf16[2,576,512]{2,1,0:T(8,128)(2,1)} %get-tuple-element.222), channel_id=1, source_target_pairs={{1,0},{2,1},{3,2},{4,3},{5,4},{6,5},{7,6},{8,7},{9,8},{10,9},{11,1... | collective-permute-start | bytes 3538952 | tf_op jit(solution)/shard_map/ppermute | solution.py:754
  311.7 28.3 %collective-permute-start.15 = (bf16[2,576,512]{2,1,0:T(8,128)(2,1)}, bf16[2,576,512]{2,1,0:T(8,128)(2,1)}, u32[]{:S(2)}, u32[]{:S(2)}) collective-permute-start(bf16[2,576,512]{2,1,0:T(8,128)(2,1)} %get-tuple-element.223), channel_id=1, source_target_pairs={{0,1},{1,2},{2,3},{3,4},{4,5},{5,6},{6,7},{7,8},{8,9},{9,10},{10,1... | collective-permute-start | bytes 3538952 | tf_op jit(solution)/shard_map/ppermute | solution.py:754
  349.9 50.9 %collective-permute-start.20 = (bf16[2,576,512]{2,1,0:T(8,128)(2,1)}, bf16[2,576,512]{2,1,0:T(8,128)(2,1)S(1)}, u32[]{:S(2)}, u32[]{:S(2)}) collective-permute-start(bf16[2,576,512]{2,1,0:T(8,128)(2,1)} %get-tuple-element.251), channel_id=1, source_target_pairs={{1,0},{2,1},{3,2},{4,3},{5,4},{6,5},{7,6},{8,7},{9,8},{10,9},{11,1... | collective-permute-start | bytes 3538952 | tf_op jit(solution)/shard_map/ppermute | solution.py:754
  351.2 49.6 %collective-permute-start.19 = (bf16[2,576,512]{2,1,0:T(8,128)(2,1)}, bf16[2,576,512]{2,1,0:T(8,128)(2,1)S(1)}, u32[]{:S(2)}, u32[]{:S(2)}) collective-permute-start(bf16[2,576,512]{2,1,0:T(8,128)(2,1)} %get-tuple-element.252), channel_id=1, source_target_pairs={{0,1},{1,2},{2,3},{3,4},{4,5},{5,6},{6,7},{7,8},{8,9},{9,10},{10,1... | collective-permute-start | bytes 3538952 | tf_op jit(solution)/shard_map/ppermute | solution.py:754
  354.3 38.9 %collective-permute-start.17 = (bf16[4,4,32,1024]{3,2,1,0:T(8,128)(2,1)}, bf16[4,4,32,1024]{3,2,1,0:T(8,128)(2,1)S(1)}, u32[]{:S(2)}, u32[]{:S(2)}) collective-permute-start(bf16[4,4,32,1024]{3,2,1,0:T(8,128)(2,1)} %get-tuple-element.246), channel_id=1, source_target_pairs={{0,4},{1,5},{2,6},{3,7},{4,0},{5,1},{6,2},{7,3},{8,12},{9,13},{10,... | collective-permute-start | bytes 3145736 | tf_op jit(solution)/shard_map/ppermute | solution.py:655
  356.8 44.0 %collective-permute-start.18 = (bf16[4,4,32,1024]{3,2,1,0:T(8,128)(2,1)}, bf16[4,4,32,1024]{3,2,1,0:T(8,128)(2,1)}, u32[]{:S(2)}, u32[]{:S(2)}) collective-permute-start(bf16[4,4,32,1024]{3,2,1,0:T(8,128)(2,1)} %get-tuple-element.247), channel_id=1, source_target_pairs={{0,2},{1,3},{2,0},{3,1},{4,6},{5,7},{6,4},{7,5},{8,10},{9,11},{10,... | collective-permute-start | bytes 3145736 | tf_op jit(solution)/shard_map/ppermute | solution.py:655
  406.4 15.3 %collective-permute-start.22 = (bf16[16,32,2560]{2,1,0:T(8,128)(2,1)}, bf16[16,32,2560]{2,1,0:T(8,128)(2,1)}, u32[]{:S(2)}, u32[]{:S(2)}) collective-permute-start(bf16[16,32,2560]{2,1,0:T(8,128)(2,1)} %get-tuple-element.275), channel_id=1, source_target_pairs={{0,1},{1,0},{2,3},{3,2},{4,5},{5,4},{6,7},{7,6},{8,9},{9,8},{10,11... | collective-permute-start | bytes 7864328 | tf_op jit(solution)/shard_map/ppermute | solution.py:655
  421.7 36.1 %collective-permute-start.26 = (bf16[16,32,1536]{2,1,0:T(8,128)(2,1)}, bf16[16,32,1536]{2,1,0:T(8,128)(2,1)}, u32[]{:S(2)}, u32[]{:S(2)}) collective-permute-start(bf16[16,32,1536]{2,1,0:T(8,128)(2,1)} %get-tuple-element.289), channel_id=1, source_target_pairs={{0,1},{1,0},{2,3},{3,2},{4,5},{5,4},{6,7},{7,6},{8,9},{9,8},{10,11... | collective-permute-start | bytes 4718600 | tf_op jit(solution)/shard_map/ppermute | solution.py:655
  421.8 36.0 %collective-permute-start.21 = (bf16[4,4,32,1024]{3,2,1,0:T(8,128)(2,1)}, bf16[4,4,32,1024]{3,2,1,0:T(8,128)(2,1)}, u32[]{:S(2)}, u32[]{:S(2)}) collective-permute-start(bf16[4,4,32,1024]{3,2,1,0:T(8,128)(2,1)} %pad_maximum_fusion.1), channel_id=1, source_target_pairs={{0,8},{1,9},{2,10},{3,11},{4,12},{5,13},{6,14},{7,15},{8,0},{9,1},... | collective-permute-start | bytes 3145736 | tf_op jit(solution)/shard_map/ppermute | solution.py:655
  425.3 32.5 %collective-permute-start.25 = (bf16[4,32,2560]{2,1,0:T(8,128)(2,1)}, bf16[4,32,2560]{2,1,0:T(8,128)(2,1)S(1)}, u32[]{:S(2)}, u32[]{:S(2)}) collective-permute-start(bf16[4,32,2560]{2,1,0:T(8,128)(2,1)} %get-tuple-element.346), channel_id=1, source_target_pairs={{0,6},{1,7},{2,4},{3,5},{4,2},{5,3},{6,0},{7,1},{8,14},{9,15},{10,... | collective-permute-start | bytes 1966088 | tf_op jit(solution)/shard_map/ppermute | solution.py:655
  426.5 31.3 %collective-permute-start.24 = (bf16[4,32,2560]{2,1,0:T(8,128)(2,1)}, bf16[4,32,2560]{2,1,0:T(8,128)(2,1)}, u32[]{:S(2)}, u32[]{:S(2)}) collective-permute-start(bf16[4,32,2560]{2,1,0:T(8,128)(2,1)} %get-tuple-element.347), channel_id=1, source_target_pairs={{0,4},{1,5},{2,6},{3,7},{4,0},{5,1},{6,2},{7,3},{8,12},{9,13},{10,... | collective-permute-start | bytes 1966088 | tf_op jit(solution)/shard_map/ppermute | solution.py:655
  428.9 28.9 %collective-permute-start.23 = (bf16[4,32,2560]{2,1,0:T(8,128)(2,1)}, bf16[4,32,2560]{2,1,0:T(8,128)(2,1)}, u32[]{:S(2)}, u32[]{:S(2)}) collective-permute-start(bf16[4,32,2560]{2,1,0:T(8,128)(2,1)} %get-tuple-element.348), channel_id=1, source_target_pairs={{0,2},{1,3},{2,0},{3,1},{4,6},{5,7},{6,4},{7,5},{8,10},{9,11},{10,... | collective-permute-start | bytes 1966088 | tf_op jit(solution)/shard_map/ppermute | solution.py:655
  460.3 28.0 %collective-permute-start.31 = (bf16[2,4,32,1024]{3,2,1,0:T(8,128)(2,1)S(1)}, bf16[2,4,32,1024]{3,2,1,0:T(8,128)(2,1)S(1)}, u32[]{:S(2)}, u32[]{:S(2)}) collective-permute-start(bf16[2,4,32,1024]{3,2,1,0:T(8,128)(2,1)S(1)} %pad_maximum_fusion.4), channel_id=1, source_target_pairs={{0,16},{1,17},{2,18},{3,19},{4,20},{5,21},{6,22},{7,23},{8,24},{9,... | collective-permute-start | bytes 1572872 | tf_op jit(solution)/shard_map/ppermute | solution.py:655
  464.1 24.1 %collective-permute-start.30 = (bf16[4,32,1536]{2,1,0:T(8,128)(2,1)S(1)}, bf16[4,32,1536]{2,1,0:T(8,128)(2,1)S(1)}, u32[]{:S(2)}, u32[]{:S(2)}) collective-permute-start(bf16[4,32,1536]{2,1,0:T(8,128)(2,1)S(1)} %get-tuple-element.352), channel_id=1, source_target_pairs={{0,6},{1,7},{2,4},{3,5},{4,2},{5,3},{6,0},{7,1},{8,14},{9,15},{10,... | collective-permute-start | bytes 1179656 | tf_op jit(solution)/shard_map/ppermute | solution.py:655
  466.4 21.8 %collective-permute-start.29 = (bf16[4,32,1536]{2,1,0:T(8,128)(2,1)S(1)}, bf16[4,32,1536]{2,1,0:T(8,128)(2,1)S(1)}, u32[]{:S(2)}, u32[]{:S(2)}) collective-permute-start(bf16[4,32,1536]{2,1,0:T(8,128)(2,1)S(1)} %get-tuple-element.353), channel_id=1, source_target_pairs={{0,4},{1,5},{2,6},{3,7},{4,0},{5,1},{6,2},{7,3},{8,12},{9,13},{10,... | collective-permute-start | bytes 1179656 | tf_op jit(solution)/shard_map/ppermute | solution.py:655
  467.8 20.4 %collective-permute-start.28 = (bf16[4,32,1536]{2,1,0:T(8,128)(2,1)S(1)}, bf16[4,32,1536]{2,1,0:T(8,128)(2,1)S(1)}, u32[]{:S(2)}, u32[]{:S(2)}) collective-permute-start(bf16[4,32,1536]{2,1,0:T(8,128)(2,1)S(1)} %get-tuple-element.354), channel_id=1, source_target_pairs={{0,2},{1,3},{2,0},{3,1},{4,6},{5,7},{6,4},{7,5},{8,10},{9,11},{10,... | collective-permute-start | bytes 1179656 | tf_op jit(solution)/shard_map/ppermute | solution.py:655
  469.2 19.0 %collective-permute-start.27 = (bf16[2,32,2560]{2,1,0:T(8,128)(2,1)S(1)}, bf16[2,32,2560]{2,1,0:T(8,128)(2,1)S(1)}, u32[]{:S(2)}, u32[]{:S(2)}) collective-permute-start(bf16[2,32,2560]{2,1,0:T(8,128)(2,1)S(1)} %add_convert_fusion.13), channel_id=1, source_target_pairs={{0,8},{1,9},{2,10},{3,11},{4,12},{5,13},{6,14},{7,15},{8,0},{9,1},... | collective-permute-start | bytes 983048 | tf_op jit(solution)/shard_map/ppermute | solution.py:655
  493.4 13.3 %collective-permute-start.33 = (bf16[1,32,1536]{2,1,0:T(8,128)(2,1)S(1)}, bf16[1,32,1536]{2,1,0:T(8,128)(2,1)S(1)}, u32[]{:S(2)}, u32[]{:S(2)}) collective-permute-start(bf16[1,32,1536]{2,1,0:T(8,128)(2,1)S(1)} %get-tuple-element.329), channel_id=1, source_target_pairs={{0,16},{1,17},{2,18},{3,19},{4,20},{5,21},{6,22},{7,23},{8,24},{9,... | collective-permute-start | bytes 294920 | tf_op jit(solution)/shard_map/ppermute | solution.py:655
  (34 other events, 369.3 us)
Sparse Core Ops, SparseCore 0:
  75.5 117.2 all-gather.1
